TPU v7x, 32 devices: a whole 2x2x4 slice. The times are simulated.
32 devices in a mesh: dp: 8 (over z, y), mp: 4 (over x, core).
Axes of the slice: x: 2, y: 2, z: 4, core: 2. Of those that a mesh axis runs over, the one named last changes fastest.
Arguments:
- hidden_in: bfloat16 [4096, 1024], P('dp'), may hold values from -6 to 6
- w_query: bfloat16 [1024, 1024], P('dp', 'mp'), may hold values from -0.1875 to 0.1875
- w_key: bfloat16 [1024, 1024], P('dp', 'mp'), may hold values from -0.1875 to 0.1875
- w_value: bfloat16 [1024, 1024], P('dp', 'mp'), may hold values from -0.1875 to 0.1875
- w_out: bfloat16 [1024, 1024], P('mp', 'dp'), may hold values from -1.5 to 1.5
- w_up: bfloat16 [1024, 4096], P('dp', 'mp'), may hold values from -0.1875 to 0.1875
- w_down: bfloat16 [4096, 1024], P('mp', 'dp'), may hold values from -0.09375 to 0.09375
- w_colbert: bfloat16 [1024, 1024], P('dp', 'mp'), may hold values from -0.1875 to 0.1875
- norm1_gain: bfloat16 [1024], P('dp'), may hold values from 0.5 to 1.5
- norm1_shift: bfloat16 [1024], P('dp'), may hold values from -3 to 3
- norm2_gain: bfloat16 [1024], P('dp'), may hold values from 0.5 to 1.5
- norm2_shift: bfloat16 [1024], P('dp'), may hold values from -3 to 3
- queries: bfloat16 [8192, 1024], P('mp'), may hold values from -6 to 6
- passage: int32 [4096], replicated, may hold values from 0 to 14, as said below
- live: int32 [4096], replicated, may hold values from 0 to 1, as said below
- score_grad: float32 [256, 15], P('mp'), may hold values from -6 to 6
Outputs:
- scores: float32 [256, 15], P('mp')
- input_grad: float32 [4096, 1024], P('dp')
- query_grad: float32 [1024, 1024], P('dp', 'mp')
- key_grad: float32 [1024, 1024], P('dp', 'mp')
- value_grad: float32 [1024, 1024], P('dp', 'mp')
- out_grad: float32 [1024, 1024], P('mp', 'dp')
- up_grad: float32 [1024, 4096], P('dp', 'mp')
- down_grad: float32 [4096, 1024], P('mp', 'dp')
- colbert_grad: float32 [1024, 1024], P('dp', 'mp')
- norm1_gain_grad: float32 [1024], P('dp')
- norm1_shift_grad: float32 [1024], P('dp')
- norm2_gain_grad: float32 [1024], P('dp')
- norm2_shift_grad: float32 [1024], P('dp')
Inputs may be any that keep to these rules, and one draw needn't show every extreme that they name: The tokens form 4 aligned groups of 1024, each holding one bucket whose passages all have the same padded length, the group's tokens divided by 1, 2, 4 or 8; which bucket a group holds is drawn. Within a group, token r of its shard d (shards of 512 tokens, d from 0 to 1) is the group's token r * 2 + d in passage order, and each passage is a run of that order. Passages are numbered bucket by bucket, shortest bucket first. In that passage order the live tokens of each passage come first; more than half of every passage's padded length is live, and the first passage of every bucket is live throughout.
All inputs are finite; a program needn't handle non-finite values.
Results may differ from a plain program's by a relative error of at most 0.028.
Values may be sent and summed in bfloat16 or wider, within the bound.
No kernel may reach another device: no remote copies, remote signals or barrier semaphores. Data moves between devices by JAX's collectives and lax.ppermute only.
A program may use at most 128 MiB of HBM per device.

v0:
```python
import jax
import jax.numpy as jnp
from jax import lax
from jax.experimental import pallas as pl
from jax.experimental.pallas import tpu as pltpu
from jax.sharding import PartitionSpec as P

HEAD_DIM = 64
QLEN = 32
NBUCKET = 4
NPASS = 15
LANES = 128
SPARE = 16

neg_big = -1e30
low_type = jnp.bfloat16
full_type = jnp.float32
contract_rows = (((0,), (0,)), ((), ()))
contract_cols = (((1,), (1,)), ((), ()))
contract_inner = (((1,), (0,)), ((), ()))


def room(mebibytes):
    return pltpu.CompilerParams(vmem_limit_bytes=mebibytes * 1024 * 1024)


def room_for_keys(keys):
    return room(min(56, 4 + keys // 128))


brief = pl.CostEstimate(flops=1, bytes_accessed=1, transcendentals=0)


def low_dot(left, right, dims=contract_inner):
    return lax.dot_general(left, right, dims, preferred_element_type=full_type)


def shape_of(shape, dtype=low_type):
    return jax.ShapeDtypeStruct(shape, dtype)


def whole_call(kernel, outs, name, *args):
    vmem = pl.BlockSpec(memory_space=pltpu.VMEM)
    return pl.pallas_call(
        kernel,
        in_specs=[vmem] * len(args),
        out_specs=[vmem] * len(outs),
        out_shape=outs,
        compiler_params=room(12),
        cost_estimate=brief,
        name=name,
    )(*args)


def swap(value, axis, mask):
    pairs = [(source, source ^ mask) for source in range(lax.axis_size(axis))]
    return lax.ppermute(value, axis, pairs)


def bits_of(axis):
    return lax.axis_size(axis).bit_length() - 1


def has_bit(axis, mask):
    return lax.axis_index(axis) // mask % 2 == 1


def upward(axis):
    return [2**level for level in range(bits_of(axis))]


def downward(axis):
    return upward(axis)[::-1]


def offsets_of(masks):
    order = [0]
    for mask in masks:
        order = order + [at ^ mask for at in order]
    return order


def arrange(blocks, axis, masks):
    levels = bits_of(axis)
    cube = blocks.reshape((2,) * levels + blocks.shape[1:])
    for mask in masks:
        at = levels - mask.bit_length()
        cube = jnp.where(has_bit(axis, mask), jnp.flip(cube, at), cube)
    front = [levels - mask.bit_length() for mask in masks]
    cube = jnp.transpose(cube, front + list(range(levels, cube.ndim)))
    return cube.reshape(blocks.shape)


def tie(*values):
    return lax.optimization_barrier(values)


class Gather:
    def __init__(self, value, axis, masks):
        self.axis, self.masks = axis, list(masks)
        self.levels, self.shape = bits_of(axis), value.shape
        self.whole = value.reshape((1,) * self.levels + value.shape)

    def start(self, main):
        if self.masks:
            self.whole, main = tie(self.whole, main)
            self.other = swap(self.whole, self.axis, self.masks[0])
        return main

    def finish(self, main):
        if self.masks:
            mask = self.masks.pop(0)
            other, main = tie(self.other, main)
            at = self.levels - mask.bit_length()
            self.whole = jnp.where(
                has_bit(self.axis, mask),
                jnp.concatenate([other, self.whole], at),
                jnp.concatenate([self.whole, other], at),
            )
        return main

    def step(self, main):
        return self.start(self.finish(main))

    def drain(self, main):
        main = self.finish(main)
        while self.masks:
            main = self.finish(self.start(main))
        return main

    def value(self):
        return self.whole.reshape((-1,) + self.shape)


class Scatter:
    def __init__(self, keep, send, axis, masks):
        self.axis, self.masks = axis, list(masks)
        self.keep, self.send = keep, send

    def start(self, main):
        if self.masks:
            self.send, main = tie(self.send, main)
            self.other = swap(self.send, self.axis, self.masks[0])
        return main

    def finish(self, main):
        if self.masks:
            self.masks.pop(0)
            other, main = tie(self.other, main)
            total = self.keep.astype(full_type) + other.astype(full_type)
            half = total.shape[0] // 2
            if self.masks:
                self.keep, self.send = total[:half], total[half:].astype(low_type)
            else:
                self.keep = total
        return main

    def step(self, main):
        return self.start(self.finish(main))

    def drain(self, main):
        main = self.finish(main)
        while self.masks:
            main = self.finish(self.start(main))
        return main

    def value(self):
        return self.keep[0]


def rows_gather(block):
    blocks = [block]
    for mask in downward("mp"):
        blocks = blocks + [swap(each, "mp", mask) for each in blocks]
    return blocks


def rows_scatter(keep, send, main=None, between=None):
    masks = upward("mp")
    terms = [keep, swap(send, "mp", masks[0])]
    for mask in masks[1:]:
        terms = terms + [swap(rows_fold(*terms), "mp", mask)]
    return terms


def add_up(refs):
    rows = refs[-1].shape[0]
    total = refs[0][0:rows, :].astype(full_type)
    for ref in refs[1:]:
        total = total + ref[0:rows, :].astype(full_type)
    return total


def head_mask(width, head):
    lane = lax.broadcasted_iota(jnp.int32, (1, width), 1)
    return lane // HEAD_DIM == head


def only_head(rows, head):
    return jnp.where(head_mask(rows.shape[1], head), rows, jnp.zeros_like(rows))


def attend_forward_kernel(q_ref, k_ref, v_ref, segq_ref, segk_ref, o_ref, stat_ref):
    tile, width = q_ref.shape
    bias = jnp.where(segq_ref[...] == segk_ref[...], 0.0, neg_big)
    out = jnp.zeros((tile, width), full_type)
    stat = jnp.zeros((tile, LANES), full_type)
    lane = lax.broadcasted_iota(jnp.int32, (1, LANES), 1)
    queries = q_ref[...] * jnp.asarray(0.125, low_type)
    for head in range(width // HEAD_DIM):
        raw = low_dot(only_head(queries, head), k_ref[...], contract_cols) + bias
        top = jnp.max(raw, axis=1, keepdims=True)
        terms = jnp.exp(raw - top)
        total = jnp.sum(terms, axis=1, keepdims=True)
        mixed = low_dot(terms.astype(low_type), v_ref[...]) * (1.0 / total)
        out = jnp.where(head_mask(width, head), mixed, out)
        stat = jnp.where(lane == head, top + jnp.log(total), stat)
    o_ref[...] = out.astype(low_type)
    stat_ref[...] = stat.T[: stat_ref.shape[0]]


def attend_forward(query_key, value_rows, seg_rows, seg_keys):
    rows = seg_rows.shape[0]
    keys, width = value_rows.shape
    tile = LANES
    return pl.pallas_call(
        attend_forward_kernel,
        grid=(rows // tile,),
        in_specs=[
            pl.BlockSpec((tile, width), lambda i: (i, 0)),
            pl.BlockSpec((keys, width), lambda i: (0, 1)),
            pl.BlockSpec((keys, width), lambda i: (0, 0)),
            pl.BlockSpec((tile, 1), lambda i: (i, 0)),
            pl.BlockSpec((1, keys), lambda i: (0, 0)),
        ],
        out_specs=[
            pl.BlockSpec((tile, width), lambda i: (i, 0)),
            pl.BlockSpec((8, tile), lambda i: (0, i)),
        ],
        out_shape=[shape_of((rows, width)), shape_of((8, rows), full_type)],
        compiler_params=room_for_keys(keys),
        cost_estimate=brief,
        name="attend_forward",
    )(query_key, query_key, value_rows, seg_rows, seg_keys)


def attend_terms(q_ref, k_ref, v_ref, do_ref, o_ref, segq_ref, segk_ref, lse_ref):
    tile, width = q_ref.shape
    bias = jnp.where(segq_ref[...] == segk_ref[...], 0.0, neg_big)
    pad = jnp.zeros((LANES - lse_ref.shape[0], tile), full_type)
    lse = jnp.concatenate([lse_ref[...], pad], 0).T
    queries = q_ref[...] * jnp.asarray(0.125, low_type)
    grads = do_ref[...]
    both = grads.astype(full_type) * o_ref[...].astype(full_type)
    for head in range(width // HEAD_DIM):
        q_head = only_head(queries, head)
        g_head = only_head(grads, head)
        delta = jnp.sum(only_head(both, head), axis=1, keepdims=True)
        raw = low_dot(q_head, k_ref[...], contract_cols)
        probs = jnp.exp(raw + (bias - lse[:, head : head + 1]))
        dprobs = low_dot(g_head, v_ref[...], contract_cols)
        dscore = (probs * (dprobs - delta)).astype(low_type)
        yield head, q_head, g_head, probs.astype(low_type), dscore


def attend_own_kernel(
    q_ref, k_ref, v_ref, do_ref, o_ref, segq_ref, segk_ref, lse_ref, dq_ref, dk_ref, dv_ref
):
    tile, width = q_ref.shape
    own = dk_ref.shape[0]

    @pl.when(pl.program_id(0) == 0)
    def _():
        dk_ref[...] = jnp.zeros_like(dk_ref)
        dv_ref[...] = jnp.zeros_like(dv_ref)

    dquery = jnp.zeros((tile, width), full_type)
    for head, q_head, g_head, probs, dscore in attend_terms(
        q_ref, k_ref, v_ref, do_ref, o_ref, segq_ref, segk_ref, lse_ref
    ):
        dquery = jnp.where(head_mask(width, head), low_dot(dscore, k_ref[...]), dquery)
        dk_ref[...] += low_dot(dscore[:, :own], q_head, contract_rows)
        dv_ref[...] += low_dot(probs[:, :own], g_head, contract_rows)
    dq_ref[...] = (dquery * 0.125).astype(low_type)


def attend_own(query_key, value_rows, grads, attended, seg_rows, seg_keys, lse):
    rows, width = grads.shape
    keys = value_rows.shape[0]
    tile = LANES
    return pl.pallas_call(
        attend_own_kernel,
        grid=(rows // tile,),
        in_specs=[
            pl.BlockSpec((tile, width), lambda i: (i, 0)),
            pl.BlockSpec((keys, width), lambda i: (0, 1)),
            pl.BlockSpec((keys, width), lambda i: (0, 0)),
            pl.BlockSpec((tile, width), lambda i: (i, 0)),
            pl.BlockSpec((tile, width), lambda i: (i, 0)),
            pl.BlockSpec((tile, 1), lambda i: (i, 0)),
            pl.BlockSpec((1, keys), lambda i: (0, 0)),
            pl.BlockSpec((8, tile), lambda i: (0, i)),
        ],
        out_specs=[
            pl.BlockSpec((tile, width), lambda i: (i, 0)),
            pl.BlockSpec((rows, width), lambda i: (0, 0)),
            pl.BlockSpec((rows, width), lambda i: (0, 0)),
        ],
        out_shape=[
            shape_of((rows, width)),
            shape_of((rows, width), full_type),
            shape_of((rows, width), full_type),
        ],
        compiler_params=room_for_keys(keys),
        cost_estimate=brief,
        name="attend_own",
    )(query_key, query_key, value_rows, grads, attended, seg_rows, seg_keys, lse)


def attend_other_kernel(
    q_ref,
    k_ref,
    v_ref,
    do_ref,
    o_ref,
    segq_ref,
    segk_ref,
    lse_ref,
    dq_ref,
    dk_ref,
    dv_ref,
    dqk_out,
    dv_out,
    dk_sum,
    dv_sum,
):
    width = q_ref.shape[1]

    @pl.when(pl.program_id(0) == 0)
    def _():
        dk_sum[...] = dk_ref[...]
        dv_sum[...] = dv_ref[...]

    for _, q_head, g_head, probs, dscore in attend_terms(
        q_ref, k_ref, v_ref, do_ref, o_ref, segq_ref, segk_ref, lse_ref
    ):
        dk_sum[...] += low_dot(dscore, q_head, contract_rows)
        dv_sum[...] += low_dot(probs, g_head, contract_rows)

    @pl.when(pl.program_id(0) == pl.num_programs(0) - 1)
    def _():
        dqk_out[:, :width] = dq_ref[...]
        dqk_out[:, width:] = dk_sum[...].astype(low_type)
        dv_out[...] = dv_sum[...].astype(low_type)


def attend_other(query_key, value_rows, grads, attended, seg_rows, seg_keys, lse, dq, dk, dv):
    rows, width = grads.shape
    own = dq.shape[0]
    tile = LANES
    first = own // tile
    held = pl.BlockSpec((own, width), lambda i: (0, 0))
    return pl.pallas_call(
        attend_other_kernel,
        grid=(rows // tile,),
        in_specs=[
            pl.BlockSpec((tile, width), lambda i: (i + first, 0)),
            pl.BlockSpec((own, width), lambda i: (0, 1)),
            held,
            pl.BlockSpec((tile, width), lambda i: (i, 0)),
            pl.BlockSpec((tile, width), lambda i: (i, 0)),
            pl.BlockSpec((tile, 1), lambda i: (i, 0)),
            pl.BlockSpec((1, own), lambda i: (0, 0)),
            pl.BlockSpec((8, tile), lambda i: (0, i)),
            held,
            held,
            held,
        ],
        out_specs=[pl.BlockSpec((own, 2 * width), lambda i: (0, 0)), held],
        out_shape=[shape_of((own, 2 * width)), shape_of((own, width))],
        scratch_shapes=[pltpu.VMEM((own, width), full_type)] * 2,
        compiler_params=room_for_keys(own),
        cost_estimate=brief,
        name="attend_other",
    )(query_key, query_key, value_rows, grads, attended, seg_rows, seg_keys, lse, dq, dk, dv)


def lanes_of(ref):
    return jnp.concatenate([ref[at] for at in range(ref.shape[0])], axis=1)


def rows_of(refs):
    return jnp.concatenate([ref[...] for ref in refs], axis=0)


def feed_up_kernel(*refs):
    *row_refs, up_ref, g_ref, slope_ref = refs
    for at, ref in enumerate(row_refs):
        place = pl.ds(at * ref.shape[0], ref.shape[0])
        inner = low_dot(ref[...], up_ref[...])
        normal = 0.5 * (1.0 + lax.erf(inner * 0.7071067811865476))
        g_ref[place, :] = (inner * normal).astype(low_type)
        slope = normal + inner * jnp.exp(-0.5 * inner * inner) * 0.3989422804014327
        slope_ref[place, :] = slope.astype(low_type)


def feed_up(blocks, w_up, units):
    own, width = blocks[0].shape
    rows = own * len(blocks)
    tile = 256
    return pl.pallas_call(
        feed_up_kernel,
        grid=(units // tile,),
        in_specs=[pl.BlockSpec((own, width), lambda i: (0, 0))] * len(blocks)
        + [pl.BlockSpec((width, tile), lambda i: (0, i))],
        out_specs=[pl.BlockSpec((rows, tile), lambda i: (0, i))] * 2,
        out_shape=[shape_of((rows, units))] * 2,
        compiler_params=room(10),
        cost_estimate=brief,
        name="feed_up",
    )(*blocks, w_up)


def store_halves(total, keep_ref, send_ref):
    half = total.shape[0] // 2
    keep_ref[...] = total[:half]
    send_ref[...] = total[half:].astype(low_type)


def halves_of(rows, width):
    return [shape_of((rows // 2, width), full_type), shape_of((rows // 2, width))]


def feed_down_kernel(g_ref, down_ref, keep_ref, send_ref):
    store_halves(low_dot(g_ref[...], lanes_of(down_ref)), keep_ref, send_ref)


def feed_down(active, w_down):
    rows, units = active.shape
    blocks, _, lanes = w_down.shape
    tile = 2
    return pl.pallas_call(
        feed_down_kernel,
        grid=(blocks // tile,),
        in_specs=[
            pl.BlockSpec((rows, units), lambda i: (0, 0)),
            pl.BlockSpec((tile, units, lanes), lambda i: (i, 0, 0)),
        ],
        out_specs=[pl.BlockSpec((rows // 2, tile * lanes), lambda i: (0, i))] * 2,
        out_shape=halves_of(rows, blocks * lanes),
        compiler_params=room(10),
        cost_estimate=brief,
        name="feed_down",
    )(active, w_down)


def feed_inner_kernel(*refs):
    *row_refs, down_ref, slope_ref, dz_ref = refs
    weight = lanes_of(down_ref)
    for at, ref in enumerate(row_refs):
        place = pl.ds(at * ref.shape[0], ref.shape[0])
        dactive = low_dot(ref[...], weight, contract_cols)
        dz_ref[place, :] = (dactive * slope_ref[place, :].astype(full_type)).astype(low_type)


def feed_inner(blocks, w_down, slope):
    own, width = blocks[0].shape
    rows, units = slope.shape
    tile = 256
    lanes = w_down.shape[2]
    return pl.pallas_call(
        feed_inner_kernel,
        grid=(units // tile,),
        in_specs=[pl.BlockSpec((own, width), lambda i: (0, 0))] * len(blocks)
        + [
            pl.BlockSpec((w_down.shape[0], tile, lanes), lambda i: (0, i, 0)),
            pl.BlockSpec((rows, tile), lambda i: (0, i)),
        ],
        out_specs=pl.BlockSpec((rows, tile), lambda i: (0, i)),
        out_shape=shape_of((rows, units)),
        compiler_params=room(10),
        cost_estimate=brief,
        name="feed_inner",
    )(*blocks, w_down, slope)


def feed_back_kernel(dz_ref, up_ref, keep_ref, send_ref):
    store_halves(low_dot(dz_ref[...], up_ref[...], contract_cols), keep_ref, send_ref)


def feed_back(dinner, w_up):
    rows, units = dinner.shape
    width = w_up.shape[0]
    tile = 256
    return pl.pallas_call(
        feed_back_kernel,
        grid=(width // tile,),
        in_specs=[
            pl.BlockSpec((rows, units), lambda i: (0, 0)),
            pl.BlockSpec((tile, units), lambda i: (i, 0)),
        ],
        out_specs=[pl.BlockSpec((rows // 2, tile), lambda i: (0, i))] * 2,
        out_shape=halves_of(rows, width),
        compiler_params=room(10),
        cost_estimate=brief,
        name="feed_back",
    )(dinner, w_up)


def late_forward_kernel(*refs):
    *e_refs, q_ref, live_ref, sharp_ref, soft_ref = refs
    blocks = soft_ref.shape[0]
    per = blocks // len(e_refs)
    for at, e_ref in enumerate(e_refs):
        rows = e_ref.shape[0]
        place = pl.ds(at * rows, rows)
        sharp = low_dot(e_ref[...], q_ref[...], contract_cols) * 2.0 + live_ref[place, :]
        sharp_ref[place, :] = sharp
        cube = sharp.reshape(per, rows // per, sharp.shape[1])
        top = jnp.max(cube, axis=1)
        total = jnp.sum(jnp.exp(cube - top[:, None, :]), axis=1)
        soft = jnp.where(top > 0.5 * neg_big, top + jnp.log(total), neg_big)
        soft_ref[pl.ds(at * per, per), :] = soft


def late_forward(e_blocks, queries, live_bias, blocks):
    own, width = e_blocks[0].shape
    rows = own * len(e_blocks)
    count = queries.shape[0]
    tile = 512
    return pl.pallas_call(
        late_forward_kernel,
        grid=(count // tile,),
        in_specs=[pl.BlockSpec((own, width), lambda i: (0, 0))] * len(e_blocks)
        + [
            pl.BlockSpec((tile, width), lambda i: (i, 0)),
            pl.BlockSpec((rows, 1), lambda i: (0, 0)),
        ],
        out_specs=[
            pl.BlockSpec((rows, tile), lambda i: (0, i)),
            pl.BlockSpec((blocks, tile), lambda i: (0, i)),
        ],
        out_shape=[shape_of((rows, count), full_type), shape_of((blocks, count), full_type)],
        compiler_params=room(14),
        cost_estimate=brief,
        name="late_forward",
    )(*e_blocks, queries, live_bias)


def late_backward_kernel(sharp_ref, soft_ref, weight_ref, q_ref, keep_ref, send_ref, total):
    step = pl.program_id(0)
    blocks = soft_ref.shape[0]
    rows, tile = sharp_ref.shape
    cube = sharp_ref[...].reshape(blocks, rows // blocks, tile)
    pulled = weight_ref[...][:, None, :] * jnp.exp(cube - soft_ref[...][:, None, :])
    term = low_dot(pulled.reshape(rows, tile).astype(low_type), q_ref[...])

    @pl.when(step == 0)
    def _():
        total[...] = term

    @pl.when(step > 0)
    def _():
        total[...] += term

    @pl.when(step == pl.num_programs(0) - 1)
    def _():
        store_halves(total[...], keep_ref, send_ref)


def late_backward(sharp, soft, weight, queries):
    rows, count = sharp.shape
    width = queries.shape[1]
    blocks = soft.shape[0]
    tile = 512
    held = pl.BlockSpec((rows // 2, width), lambda i: (0, 0))
    return pl.pallas_call(
        late_backward_kernel,
        grid=(count // tile,),
        in_specs=[
            pl.BlockSpec((rows, tile), lambda i: (0, i)),
            pl.BlockSpec((blocks, tile), lambda i: (0, i)),
            pl.BlockSpec((blocks, tile), lambda i: (0, i)),
            pl.BlockSpec((tile, width), lambda i: (i, 0)),
        ],
        out_specs=[held, held],
        out_shape=halves_of(rows, width),
        scratch_shapes=[pltpu.VMEM((rows, width), full_type)],
        compiler_params=room(16),
        cost_estimate=brief,
        name="late_backward",
    )(sharp, soft, weight, queries)


def norm_stats(values):
    centre = values - jnp.mean(values, axis=-1, keepdims=True)
    spread = jnp.mean(centre * centre, axis=-1, keepdims=True)
    scale = lax.rsqrt(spread + 1e-05)
    return centre * scale, scale


def norm_backward(unit, scale, gain, grad):
    dunit = grad * gain
    dvalues = scale * (
        dunit
        - jnp.mean(dunit, axis=-1, keepdims=True)
        - unit * jnp.mean(dunit * unit, axis=-1, keepdims=True)
    )
    return (
        dvalues,
        jnp.sum(grad * unit, axis=0, keepdims=True),
        jnp.sum(grad, axis=0, keepdims=True),
    )


def norm_one_kernel(*refs):
    *terms, norm_ref, h_ref, low_ref, unit_ref, scale_ref = refs
    unit, scale = norm_stats(add_up(terms))
    normed = unit * norm_ref[0:1] + norm_ref[1:2]
    h_ref[...] = normed
    low_ref[...] = normed.astype(low_type)
    unit_ref[...] = unit
    scale_ref[...] = scale


def lanes_at(order_ref, at, span):
    return pl.ds(pl.multiple_of(order_ref[at] * span, span), span)


def norm_two_kernel(order_ref, *refs):
    *rest, low_ref, unit_ref, scale_ref, e_ref, elow_ref, inv_ref = refs
    parts = order_ref.shape[0]
    *terms, norm_ref = rest[:-parts]
    col_refs = rest[-parts:]
    unit, scale = norm_stats(add_up(terms))
    normed_low = (unit * norm_ref[2:3] + norm_ref[3:4]).astype(low_type)
    low_ref[...] = normed_low
    unit_ref[...] = unit
    scale_ref[...] = scale
    span = col_refs[0].shape[1]
    squares = 0.0
    for at, ref in enumerate(col_refs):
        projected = low_dot(normed_low, ref[...])
        e_ref[:, lanes_at(order_ref, at, span)] = projected
        squares = squares + jnp.sum(projected * projected, axis=-1, keepdims=True)
    inv = lax.rsqrt(squares + 1e-06)
    embedded = e_ref[...] * inv
    e_ref[...] = embedded
    elow_ref[...] = embedded.astype(low_type)
    inv_ref[...] = inv


def norm_two_back_kernel(order_ref, *refs):
    *rest, du_ref, dr_ref, low_ref, g_ref = refs
    parts = order_ref.shape[0]
    *terms, norm_ref, unit_ref, scale_ref, e_ref, inv_ref = rest[:-parts]
    col_refs = rest[-parts:]
    dembed = add_up(terms)
    embedded = e_ref[...]
    along = jnp.sum(embedded * dembed, axis=-1, keepdims=True)
    du_ref[...] = (inv_ref[...] * (dembed - embedded * along)).astype(low_type)
    span = col_refs[0].shape[1]
    dnormed = 0.0
    for at, ref in enumerate(col_refs):
        dproj = du_ref[:, lanes_at(order_ref, at, span)]
        dnormed = dnormed + low_dot(dproj, ref[...], contract_cols)
    dresid, dgain, dshift = norm_backward(
        unit_ref[...], scale_ref[...], norm_ref[2:3], dnormed
    )
    dr_ref[...] = dresid
    low_ref[...] = dresid.astype(low_type)
    g_ref[...] = jnp.concatenate([dgain, dshift], 0)


def split_sums(sums):
    high = sums.astype(low_type).astype(full_type)
    zeros = jnp.zeros((SPARE - 8, sums.shape[1]), full_type)
    return jnp.concatenate([high, sums - high, zeros], 0).astype(low_type)


def norm_one_back_kernel(*refs):
    *terms, norm_ref, unit_ref, scale_ref, two_ref, dr_ref, pack_ref = refs
    dresid, dgain, dshift = norm_backward(
        unit_ref[...], scale_ref[...], norm_ref[0:1], add_up(terms)
    )
    dr_ref[...] = dresid
    rows = dresid.shape[0]
    pack_ref[0:rows, :] = dresid.astype(low_type)
    pack_ref[rows : rows + SPARE, :] = split_sums(
        jnp.concatenate([dgain, dshift, two_ref[...]], 0)
    )


def fold_kernel(keep_ref, got_ref, low_ref):
    half = low_ref.shape[0]
    total = keep_ref[half:, :] + got_ref[half:, :].astype(full_type)
    low_ref[...] = total.astype(low_type)


def rows_fold(keep, got):
    return whole_call(fold_kernel, [shape_of((got.shape[0] // 2, got.shape[1]))], "fold", keep, got)[0]


def mix_kernel(o_ref, out_ref, keep_ref, send_ref):
    rows = o_ref.shape[1]
    weight = jnp.concatenate([out_ref[at, 0:rows, :] for at in range(out_ref.shape[0])], axis=1)
    store_halves(low_dot(o_ref[...], weight), keep_ref, send_ref)


def unmix_kernel(*refs):
    *packs, out_ref, do_ref, sums_ref = refs
    rows = do_ref.shape[1]
    weight = jnp.concatenate([out_ref[at, 0:rows, :] for at in range(out_ref.shape[0])], axis=1)
    own = packs[0].shape[0] - SPARE
    sums = jnp.zeros((8, weight.shape[1]), full_type)
    for at, ref in enumerate(packs):
        do = low_dot(ref[0:own, :], weight, contract_cols)
        do_ref[at * own : (at + 1) * own, :] = do.astype(low_type)
        sums = sums + ref[own : own + SPARE, :].astype(full_type)[:8]
    sums_ref[...] = split_sums(sums[:4] + sums[4:])


def block_order(masks):
    return lax.axis_index("dp") ^ jnp.asarray(offsets_of(masks[::-1]), jnp.int32)


def ordered_call(kernel, outs, scratch, name, order, *args):
    vmem = pl.BlockSpec(memory_space=pltpu.VMEM)
    return pl.pallas_call(
        kernel,
        in_specs=[pl.BlockSpec(memory_space=pltpu.SMEM)] + [vmem] * len(args),
        out_specs=[vmem] * len(outs),
        out_shape=outs,
        scratch_shapes=[pltpu.VMEM(*each) for each in scratch],
        compiler_params=room(12),
        cost_estimate=brief,
        name=name,
    )(order, *args)


def stored(place_ref, left, right):
    turned = left.T
    cols = right.shape[1]
    for start in range(0, cols, 256):
        stop = min(start + 256, cols)
        place_ref[:, start:stop] = low_dot(turned, right[:, start:stop]).astype(low_type)


def deal(order_ref, keep_ref, send_ref, write):
    half = keep_ref.shape[0]
    for at in range(2 * half):
        write(keep_ref.at[at] if at < half else send_ref.at[at - half], order_ref[at])


def rows_in(ref, block, count):
    return ref[pl.ds(pl.multiple_of(block * count, count), count), :]


def lanes_in(ref, block):
    return ref[:, pl.ds(pl.multiple_of(block * LANES, LANES), LANES)]


def halves_like(count, block):
    return [shape_of((count // 2,) + block)] * 2


def grad_down_kernel(order_ref, active_ref, *refs):
    *row_refs, keep_ref, send_ref, total = refs
    stored(total, active_ref[...], rows_of(row_refs))

    def write(ref, block):
        ref[...] = lanes_in(total, block)

    deal(order_ref, keep_ref, send_ref, write)


def grad_down(active, row_blocks, masks):
    count = lax.axis_size("dp")
    units, width = active.shape[1], row_blocks[0].shape[1]
    if width // count == LANES:
        return ordered_call(
            grad_down_kernel,
            halves_like(count, (units, LANES)),
            [((units, width), low_type)],
            "grad_down",
            block_order(masks),
            active,
            *row_blocks,
        )
    whole = low_dot(active, jnp.concatenate(row_blocks, 0), contract_rows).astype(low_type)
    return halves(arrange(jnp.swapaxes(whole.reshape(units, count, -1), 0, 1), "dp", masks))


def halves(blocks):
    half = blocks.shape[0] // 2
    return blocks[:half], blocks[half:]


def grad_up_kernel(order_ref, dinner_ref, *refs):
    *row_refs, keep_ref, send_ref, total = refs
    parts = len(row_refs) // 3
    units = dinner_ref.shape[1]
    block_rows = keep_ref.shape[1]
    cols = keep_ref.shape[2] - units
    stored(total.at[:, 0:units], rows_of(row_refs[:parts]), dinner_ref[...])
    mine = pl.ds(pl.multiple_of(order_ref[order_ref.shape[0] - 1] * cols, cols), cols)
    dproj = jnp.concatenate([ref[:, mine] for ref in row_refs[2 * parts :]], axis=0)
    stored(total.at[:, units:], rows_of(row_refs[parts : 2 * parts]), dproj)

    def write(ref, block):
        ref[...] = rows_in(total, block, block_rows)

    deal(order_ref, keep_ref, send_ref, write)


def grad_up(dinner, one_blocks, two_blocks, du_blocks, col_width, masks):
    count = lax.axis_size("dp")
    units, width = dinner.shape[1], one_blocks[0].shape[1]
    column = lax.axis_index("mp")
    rows = width // count
    if rows == LANES:
        order = jnp.concatenate([block_order(masks), column.reshape(1)])
        return ordered_call(
            grad_up_kernel,
            halves_like(count, (rows, units + col_width)),
            [((width, units + col_width), low_type)],
            "grad_up",
            order,
            dinner,
            *one_blocks,
            *two_blocks,
            *du_blocks,
        )
    dproj = lax.dynamic_slice_in_dim(
        jnp.concatenate(du_blocks, 0), column * col_width, col_width, 1
    )
    up = low_dot(jnp.concatenate(one_blocks, 0), dinner, contract_rows)
    col = low_dot(jnp.concatenate(two_blocks, 0), dproj, contract_rows)
    whole = jnp.concatenate([up, col], 1).astype(low_type)
    return halves(arrange(whole.reshape(count, rows, -1), "dp", masks))


def grad_qk_kernel(order_ref, left_ref, right_ref, keep_ref, send_ref, total):
    block_rows = keep_ref.shape[1]
    stored(total, left_ref[...], right_ref[...])

    def write(ref, block):
        ref[...] = rows_in(total, block, block_rows)

    deal(order_ref, keep_ref, send_ref, write)


def grad_qk(left, right, masks):
    count = lax.axis_size("dp")
    width, cols = left.shape[1], right.shape[1]
    rows = width // count
    if rows == LANES:
        return ordered_call(
            grad_qk_kernel,
            halves_like(count, (rows, cols)),
            [((width, cols), low_type)],
            "grad_qk",
            block_order(masks),
            left,
            right,
        )
    whole = low_dot(left, right, contract_rows).astype(low_type)
    return halves(arrange(whole.reshape(count, rows, cols), "dp", masks))


def grad_vo_kernel(order_ref, hidden_ref, dv_ref, o_ref, *refs):
    *packs, sums_ref, keep_ref, send_ref, total_v, total_o = refs
    rows = packs[0].shape[0] - SPARE
    cols = dv_ref.shape[1]
    heads = o_ref.shape[1]
    stored(total_v, hidden_ref[...], dv_ref[...])
    mixed = jnp.concatenate([ref[0:rows, :] for ref in packs], axis=0)
    stored(total_o.at[0:heads, :], o_ref[...], mixed)
    total_o[heads : heads + SPARE, :] = sums_ref[...]

    def write(ref, block):
        value = rows_in(total_v, block, LANES)
        for at in range(cols // LANES):
            ref[at * LANES : (at + 1) * LANES, :] = value[:, at * LANES : (at + 1) * LANES]
        ref[cols:, :] = lanes_in(total_o, block)

    deal(order_ref, keep_ref, send_ref, write)


def pack_vo(value, out):
    cols = value.shape[-1]
    parts = [value[..., at : at + LANES] for at in range(0, cols, LANES)]
    return jnp.concatenate(parts + [out.reshape(out.shape[:-2] + (-1, LANES))], axis=-2)


def unpack_vo(packed, rows, cols, out_shape):
    high = rows * cols // LANES
    value = jnp.concatenate(
        [packed[..., at : at + rows, :] for at in range(0, high, rows)], axis=-1
    )
    return value, packed[..., high:, :].reshape(packed.shape[:-2] + out_shape)


def grad_vo(hidden, dvalue, attended, packs, sums, masks):
    count = lax.axis_size("dp")
    width, cols = hidden.shape[1], dvalue.shape[1]
    heads = attended.shape[1]
    rows = width // count
    if rows == LANES:
        block = (cols * rows // LANES + heads + SPARE, LANES)
        return ordered_call(
            grad_vo_kernel,
            halves_like(count, block),
            [((width, cols), low_type), ((heads + SPARE, width), low_type)],
            "grad_vo",
            block_order(masks),
            hidden,
            dvalue,
            attended,
            *packs,
            sums,
        )
    value = low_dot(hidden, dvalue, contract_rows).astype(low_type).reshape(count, rows, cols)
    mixed = jnp.concatenate([each[:-SPARE] for each in packs], 0)
    out = low_dot(attended, mixed, contract_rows).astype(low_type)
    out = jnp.concatenate([out, sums], 0).reshape(heads + SPARE, count, rows)
    return halves(arrange(pack_vo(value, jnp.swapaxes(out, 0, 1)), "dp", masks))


def to_lanes(blocks):
    if blocks.shape[2] == LANES:
        return blocks
    whole = jnp.swapaxes(blocks, 0, 1).reshape(blocks.shape[1], -1, LANES)
    return jnp.swapaxes(whole, 0, 1)


def place_kernel(at_ref, *refs):
    *blocks, out_ref = refs
    rows = blocks[0].shape[0]
    for at, ref in enumerate(blocks):
        start = pl.multiple_of(at_ref[at] * rows, rows)
        out_ref[pl.ds(start, rows), :] = ref[...].astype(full_type)


def place_rows(order, blocks):
    rows, width = blocks[0].shape
    outs = [shape_of((rows * len(blocks), width), full_type)]
    return ordered_call(place_kernel, outs, [], "place_rows", order, *blocks)[0]


def unproject_kernel(dqk_ref, dv_ref, a_ref, b_ref, keep_ref, send_ref):
    total = low_dot(dqk_ref[...], a_ref[...], contract_cols)
    store_halves(total + low_dot(dv_ref[...], b_ref[...], contract_cols), keep_ref, send_ref)


def unproject(dqk, dvalue, w_qk, w_v):
    outs = halves_of(dqk.shape[0], w_qk.shape[0])
    return whole_call(unproject_kernel, outs, "unproject", dqk, dvalue, w_qk, w_v)


def close_kernel(*refs):
    *terms, out_ref = refs
    out_ref[...] = add_up(terms).astype(low_type)


def pack_kernel(
    order_ref,
    hidden_ref,
    q_ref,
    k_ref,
    v_ref,
    o_ref,
    norm_ref,
    up_ref,
    col_ref,
    a_out,
    u_out,
    b_out,
    own_out,
):
    heads = q_ref.shape[1]
    a_out[:, :heads] = q_ref[...]
    a_out[:, heads:] = k_ref[...]
    units = up_ref.shape[1]
    u_out[:, :units] = up_ref[...]
    u_out[:, units:] = col_ref[...]
    for at in range(heads // LANES):
        b_out[at * LANES : (at + 1) * LANES, :] = v_ref[:, at * LANES : (at + 1) * LANES]
    rest = v_ref.shape[0] * heads // LANES
    b_out[rest : rest + o_ref.shape[0], :] = o_ref[...]
    b_out[rest + o_ref.shape[0] :, :] = norm_ref[...]
    parts = order_ref.shape[0]
    rows = hidden_ref.shape[0] // parts
    for at in range(parts):
        own_out[at * rows : (at + 1) * rows, :] = rows_in(hidden_ref, order_ref[at], rows)


def pack_inputs(order, hidden, w_query, w_key, w_value, w_out, norms, w_up, w_colbert):
    rows, heads = w_query.shape
    if w_out.shape[1] == LANES and rows == LANES:
        packed = (rows * heads // LANES + w_out.shape[0] + SPARE, LANES)
        outs = [
            shape_of((rows, 2 * heads)),
            shape_of((rows, w_up.shape[1] + w_colbert.shape[1])),
            shape_of(packed),
            shape_of(hidden.shape),
        ]
        args = (hidden, w_query, w_key, w_value, w_out, norms, w_up, w_colbert)
        return ordered_call(pack_kernel, outs, [], "pack", order, *args)
    span = hidden.shape[0] // order.shape[0]
    return (
        jnp.concatenate([w_query, w_key], axis=1),
        jnp.concatenate([w_up, w_colbert], axis=1),
        pack_vo(w_value, jnp.concatenate([w_out, norms], axis=0)),
        jnp.concatenate(
            [
                lax.dynamic_slice_in_dim(hidden, order[at] * span, span, 0)
                for at in range(order.shape[0])
            ]
        ),
    )


def body(
    hidden_in,
    w_query,
    w_key,
    w_value,
    w_out,
    w_up,
    w_down,
    w_colbert,
    norm1_gain,
    norm1_shift,
    norm2_gain,
    norm2_shift,
    queries,
    passage,
    live,
    score_grad,
):
    tok_rows, width = hidden_in.shape
    device = lax.axis_index("dp")
    column = lax.axis_index("mp")
    dp_size = lax.axis_size("dp")
    mp_size = lax.axis_size("mp")
    group_size = dp_size // NBUCKET
    group_levels = group_size.bit_length() - 1
    own_rows = tok_rows // mp_size
    head_width = w_query.shape[1]
    dp_up, dp_down = upward("dp"), downward("dp")
    turned = dp_up[:1] + dp_down[:-1]
    row_order = offsets_of(downward("mp"))

    def ordered(value, owner, span=own_rows):
        return jnp.concatenate(
            [
                lax.dynamic_slice_in_dim(value, (owner * mp_size + (column ^ at)) * span, span, 0)
                for at in row_order
            ]
        )

    def group_gather(value):
        for level in range(group_levels):
            value = jnp.concatenate([value, swap(value, "dp", 2**level)], 0)
        return value

    across = dp_up[-1:] + dp_up[:-1]
    turned_back, across_back = turned[::-1], across[::-1]
    col_order = column ^ jnp.asarray(row_order, jnp.int32)
    norms = jnp.stack([norm1_gain, norm1_shift, norm2_gain, norm2_shift])
    norms = jnp.concatenate([norms, jnp.zeros((SPARE - 4, w_out.shape[1]), low_type)], 0)
    out_shape = (w_out.shape[0] + SPARE, w_out.shape[1])
    packed_a, packed_u, packed_b, hidden_own = pack_inputs(
        col_order, hidden_in, w_query, w_key, w_value, w_out, norms, w_up, w_colbert
    )
    own_hidden = hidden_own[:own_rows]
    pack_a = Gather(packed_a, "dp", dp_down)
    pack_u = Gather(packed_u, "dp", dp_down)
    pack_b = Gather(packed_b, "dp", turned)
    pack_d = Gather(w_down, "dp", dp_down)

    main = (hidden_own, own_hidden)
    main = pack_a.start(main)
    main = pack_u.start(main)
    main = pack_b.start(main)
    others = group_gather(main[1][None])[1:]
    seg_own = ordered(passage, device)
    live_own = ordered(live, device)
    seg_others = jnp.concatenate([ordered(passage, device ^ at) for at in range(1, group_size)])
    live_others = jnp.concatenate([ordered(live, device ^ at) for at in range(1, group_size)])
    slot_own = jnp.where(live_own == 1, seg_own, -1)
    slot_keys = jnp.concatenate([slot_own, jnp.where(live_others == 1, seg_others, -1)])
    seg_column, seg_far, slot_row = seg_own[:, None], seg_others[:, None], slot_keys[None, :]
    blocks = 2 ** (NBUCKET - 1)
    seg_block = seg_own.reshape(blocks, -1)[:, 0]
    live_bias = jnp.where(live_own == 1, 0.0, neg_big)[:, None]
    same = seg_block[:, None] == seg_block[None, :]
    passages = jnp.arange(NPASS, dtype=jnp.int32)
    place = (seg_block[:, None] == passages[None, :]).astype(full_type)
    grad_block = jnp.sum(place[:, None, :] * score_grad[None], axis=2)
    weight = jnp.repeat(grad_block / QLEN, QLEN, axis=1)
    early = (seg_column, seg_far, slot_own, slot_row, live_bias, weight, same, place)
    early, main = tie(early, main)
    seg_column, seg_far, slot_own, slot_row, live_bias, weight, same, place = early
    main = pack_a.step(main)
    others, main = tie(others, main)
    far_others = swap(others, "mp", 2)
    main = pack_u.step(main)
    main = pack_b.step(main)
    main = pack_a.step(main)
    main = pack_d.start(main)
    far_others, main = tie(far_others, main)
    others = [others, far_others]
    others = others + [swap(each, "mp", 1) for each in others]
    others = jnp.stack(others, 1).reshape(-1, width)
    hidden_own, own_hidden = main
    hidden_all = jnp.concatenate([hidden_own, others], 0)
    main = (hidden_own, own_hidden, hidden_all)
    main = pack_b.step(main)
    main = pack_u.step(main)
    main = pack_a.drain(main)
    full_a = pack_a.value().reshape(width, -1)
    full_a, main = tie(full_a, main)
    hidden_own, own_hidden, hidden_all = main

    query_key = low_dot(hidden_all, full_a).astype(low_type)
    main = (query_key, hidden_all)
    main = pack_d.step(main)
    main = pack_b.drain(main)
    full_b, full_out = unpack_vo(pack_b.value(), w_value.shape[0], head_width, out_shape)
    full_b = full_b.reshape(width, head_width)
    full_out = to_lanes(full_out)
    (full_b, full_out), main = tie((full_b, full_out), main)
    query_key, hidden_all = main
    value_rows = low_dot(hidden_all, full_b).astype(low_type)
    norm_rows = jnp.swapaxes(full_out[:, head_width : head_width + 4], 0, 1).reshape(4, width)
    norm_rows = norm_rows.astype(full_type)
    attended, lse = attend_forward(query_key, value_rows, seg_column, slot_row)
    norm_rows, attended = tie(norm_rows, attended)
    attended = pack_d.step(attended)
    terms = rows_scatter(*whole_call(mix_kernel, halves_of(tok_rows, width), "mix", attended, full_out))
    terms = pack_u.drain(terms)
    square = shape_of((own_rows, width), full_type)
    low_square = shape_of((own_rows, width))
    narrow = shape_of((own_rows, 1), full_type)
    normed_one, normed_low, unit_one, scale_one = whole_call(
        norm_one_kernel,
        [square, low_square, square, narrow],
        "norm_one",
        own_hidden,
        *terms,
        norm_rows,
    )

    units = w_up.shape[1]
    rows_one = rows_gather(normed_low)
    full_up = pack_u.value().reshape(width, -1)
    col_own = full_up[:, units:]
    (full_up, col_own), rows_one = tie((full_up, col_own), rows_one)
    far_col = swap(col_own, "mp", 2)
    active, slope = feed_up(rows_one, full_up, units)
    main = pack_d.drain((active, slope))
    full_down = to_lanes(pack_d.value())
    full_down, (active, slope) = tie(full_down, main)
    keep, send = feed_down(active, full_down)
    far_col, (keep, send) = tie(far_col, (keep, send))
    terms = rows_scatter(keep, send)
    col_blocks = [col_own, far_col]
    col_blocks = col_blocks + [swap(each, "mp", 1) for each in col_blocks]
    normed_two_low, unit_two, scale_two, embedded, embed_low, inv_length = ordered_call(
        norm_two_kernel,
        [low_square, square, narrow, square, low_square, narrow],
        [],
        "norm_two",
        col_order,
        normed_one,
        *terms,
        norm_rows,
        *col_blocks,
    )

    e_blocks = rows_gather(embed_low)
    sharp, soft_block = late_forward(e_blocks, queries, live_bias, blocks)
    two_blocks, soft_block = tie(normed_two_low, soft_block)
    soft_group = group_gather(soft_block[None])
    terms = jnp.where(same[:, None, :, None], soft_group[None], neg_big)
    top = jnp.max(terms, axis=(1, 2))
    soft = top + jnp.log(jnp.sum(jnp.exp(terms - top[:, None, None]), axis=(1, 2)))
    two_blocks = rows_gather(two_blocks)
    far = group_gather(jnp.stack([attended]))[1:]
    far_lse = group_gather(lse[None])[1:]
    keep, send = late_backward(sharp, soft, weight, queries)
    (far, far_lse, two_blocks), (keep, send) = tie((far, far_lse, two_blocks), (keep, send))
    far_attended = far.reshape(-1, head_width)
    far_lse = jnp.swapaxes(far_lse, 0, 1).reshape(8, -1)

    query_means = jnp.mean(soft.reshape(blocks, -1, QLEN), axis=2) * 0.5
    shared = jnp.sum(same.astype(full_type), axis=1)
    scores = jnp.sum(query_means[:, :, None] * (place / shared[:, None])[:, None, :], axis=0)
    scores, keep = tie(scores, keep)

    terms = rows_scatter(keep, send)
    dproj_low, dresid_two, dresid_low, two_sums = ordered_call(
        norm_two_back_kernel,
        [low_square, square, low_square, shape_of((2, width), full_type)],
        [],
        "norm_two_back",
        col_order,
        *terms,
        norm_rows,
        unit_two,
        scale_two,
        embedded,
        inv_length,
        *col_blocks,
    )
    dresid_blocks = rows_gather(dresid_low)

    dproj_low, dresid_blocks = tie(dproj_low, dresid_blocks)
    du_far = swap(dproj_low, "mp", 2)
    if group_size < dp_size:
        masks = dp_up[group_levels:]
        scores = scores + swap(scores, "dp", masks[0])
    dinner = feed_inner(dresid_blocks, full_down, slope)
    (scores, keep_up), dinner = tie((scores, full_up), dinner)
    for mask in masks[1:]:
        scores = scores + swap(scores, "dp", mask)
    keep, send = feed_back(dinner, keep_up)
    got = swap(send, "mp", 1)
    du_blocks = [dproj_low, du_far]
    du_blocks = du_blocks + [swap(each, "mp", 1) for each in du_blocks]
    terms = [keep, got]
    low = rows_fold(*terms)
    (scores, active, dinner), low = tie((scores, active, dinner), low)
    far_low = swap(low, "mp", 2)
    grad_d = Scatter(*grad_down(active, dresid_blocks, across_back), "dp", across_back)
    dinner = grad_d.start(dinner)
    grad_u = Scatter(
        *grad_up(dinner, rows_one, two_blocks, du_blocks, w_colbert.shape[1], dp_up), "dp", dp_up
    )
    far_low = grad_u.start(far_low)
    dresid_one, mixed_pack = whole_call(
        norm_one_back_kernel,
        [square, shape_of((own_rows + SPARE, width))],
        "norm_one_back",
        dresid_two,
        *terms,
        far_low,
        norm_rows,
        unit_one,
        scale_one,
        two_sums,
    )
    packs = rows_gather(mixed_pack)

    dattended, norm_sums = whole_call(
        unmix_kernel,
        [shape_of((tok_rows, head_width)), shape_of((SPARE, width))],
        "unmix",
        *packs,
        full_out,
    )
    far_grads = group_gather(dattended[None])[1:].reshape(-1, head_width)
    main = grad_d.step(dattended)
    dquery, dkey, dvalue = attend_own(
        query_key, value_rows, main, attended, seg_column, slot_row, lse
    )
    far_grads, dquery = tie(far_grads, dquery)
    main = (far_grads, dquery)
    main = grad_u.step(main)
    main = grad_d.step(main)
    far_grads, dquery = main
    dqk, dvalue_low = attend_other(
        query_key,
        value_rows,
        far_grads,
        far_attended,
        seg_far,
        slot_own[None, :],
        far_lse,
        dquery,
        dkey,
        dvalue,
    )
    main = grad_d.finish((dqk, dvalue_low))
    main = grad_u.step(main)
    dqk, dvalue_low = main
    grad_b = Scatter(
        *grad_vo(hidden_own, dvalue_low, attended, packs, norm_sums, turned_back), "dp", turned_back
    )
    dqk = grad_b.start(dqk)
    grad_a = Scatter(*grad_qk(hidden_own, dqk, dp_up), "dp", dp_up)
    dqk = grad_a.start(dqk)
    keep, send = unproject(dqk, dvalue_low, full_a, full_b)
    terms = rows_scatter(keep, send)
    terms = grad_a.step(terms)
    terms = grad_b.step(terms)
    input_own = whole_call(close_kernel, [low_square], "close", dresid_one, *terms)[0]
    input_own = grad_u.finish(input_own)
    input_blocks = rows_gather(input_own)
    input_blocks = grad_a.step(input_blocks)
    input_grad = place_rows(col_order, input_blocks)
    input_grad = grad_b.step(input_grad)
    input_grad = grad_b.drain(grad_a.drain(input_grad))

    grad_qk_rows = grad_a.value()
    value_grad, out_rows = unpack_vo(grad_b.value(), w_value.shape[0], head_width, out_shape)
    norm_grads = out_rows[head_width : head_width + 4] + out_rows[head_width + 4 : head_width + 8]
    up_rows = grad_u.value()
    return (
        scores,
        input_grad,
        grad_qk_rows[:, :head_width],
        grad_qk_rows[:, head_width:],
        value_grad,
        out_rows[:head_width],
        up_rows[:, :units],
        grad_d.value(),
        up_rows[:, units:],
        norm_grads[0],
        norm_grads[1],
        norm_grads[2],
        norm_grads[3],
    )


def solution(mesh):
    rows, both, across = P("dp", None), P("dp", "mp"), P("mp", "dp")
    return jax.shard_map(
        body,
        mesh=mesh,
        in_specs=(
            (rows, both, both, both, across, both, across, both)
            + (P("dp"),) * 4
            + (P("mp", None), P(), P(), P("mp", None))
        ),
        out_specs=(
            (P("mp", None), rows, both, both, both, across, both, across, both)
            + (P("dp"),) * 4
        ),
        check_vma=False,
    )
```

profile of v0, /device:TPU:0, one launch (start us, length us, event | category | flops | bytes accessed | tf_op | source)
XLA Modules:
  0.0 356.9 jit_solution(17521918600612572030)
XLA Ops:
  9.2 4.1 %collective-permute-start = (bf16[1,1,1,128,512]{4,3,2,1,0:T(8,128)(2,1)S(1)}, bf16[1,1,1,128,512]{4,3,2,1,0:T(8,128)(2,1)S(1)}, u32[]{:S(2)}, u32[]{:S(2)}) collective-permute-start(bf16[1,1,1,128,512]{4,3,2,1,0:T(8,128)(2,1)S(1)} %bitcast.81), channel_id=1, source_target_pairs={{0,16},{4,20},{8,24},{12,28},{16,0},{20,4},{24,8},{28,12},{1,17},{... | collective-permute-start | bytes 393224 | tf_op jit(solution)/shard_map/ppermute | solution.py:57
  19.7 7.8 %collective-permute-done = bf16[1,1,1,128,512]{4,3,2,1,0:T(8,128)(2,1)S(1)} collective-permute-done((bf16[1,1,1,128,512]{4,3,2,1,0:T(8,128)(2,1)S(1)}, bf16[1,1,1,128,512]{4,3,2,1,0:T(8,128)(2,1)S(1)}, u32[]{:S(2)}, u32[]{:S(2)}) %collective-permute-start) | collective-permute-done | bytes 131104 | tf_op jit(solution)/shard_map/ppermute | solution.py:57
  27.6 1.9 collective-permute-start.8
  29.5 4.3 %collective-permute-done.3 = bf16[1,1,1,128,1280]{4,3,2,1,0:T(8,128)(2,1)S(1)} collective-permute-done((bf16[1,1,1,128,1280]{4,3,2,1,0:T(8,128)(2,1)S(1)}, bf16[1,1,1,128,1280]{4,3,2,1,0:T(8,128)(2,1)S(1)}, u32[]{:S(2)}, u32[]{:S(2)}) %collective-permute-start.3) | collective-permute-done | bytes 327712 | tf_op jit(solution)/shard_map/ppermute | solution.py:57
  33.9 1.7 maximum_select_fusion.10
  35.7 3.7 %collective-permute-done.1 = bf16[2,1,1,128,512]{4,3,2,1,0:T(8,128)(2,1)S(1)} collective-permute-done((bf16[2,1,1,128,512]{4,3,2,1,0:T(8,128)(2,1)S(1)}, bf16[2,1,1,128,512]{4,3,2,1,0:T(8,128)(2,1)S(1)}, u32[]{:S(2)}, u32[]{:S(2)}) %collective-permute-start.1) | collective-permute-done | bytes 262176 | tf_op jit(solution)/shard_map/ppermute | solution.py:57
  40.5 4.2 %collective-permute-start.7 = (bf16[1,1,2,528,128]{4,3,2,1,0:T(8,128)(2,1)}, bf16[1,1,2,528,128]{4,3,2,1,0:T(8,128)(2,1)S(1)}, u32[]{:S(2)}, u32[]{:S(2)}) collective-permute-start(bf16[1,1,2,528,128]{4,3,2,1,0:T(8,128)(2,1)} %maximum_select_fusion.10), channel_id=1, source_target_pairs={{0,16},{4,20},{8,24},{12,28},{16,0},{20,4},{24,8},{28,12},{1,17},{... | collective-permute-start | bytes 811016 | tf_op jit(solution)/shard_map/ppermute | solution.py:57
  47.8 13.6 %collective-permute-done.7 = bf16[1,1,2,528,128]{4,3,2,1,0:T(8,128)(2,1)S(1)} collective-permute-done((bf16[1,1,2,528,128]{4,3,2,1,0:T(8,128)(2,1)}, bf16[1,1,2,528,128]{4,3,2,1,0:T(8,128)(2,1)S(1)}, u32[]{:S(2)}, u32[]{:S(2)}) %collective-permute-start.7) | collective-permute-done | bytes 270368 | tf_op jit(solution)/shard_map/ppermute | solution.py:57
  62.5 4.5 %collective-permute-start.14 = (bf16[2,1,2,528,128]{4,3,2,1,0:T(8,128)(2,1)S(1)}, bf16[2,1,2,528,128]{4,3,2,1,0:T(8,128)(2,1)S(1)}, u32[]{:S(2)}, u32[]{:S(2)}) collective-permute-start(bf16[2,1,2,528,128]{4,3,2,1,0:T(8,128)(2,1)S(1)} %maximum_select_fusion.7), channel_id=1, source_target_pairs={{0,8},{4,12},{8,0},{12,4},{16,24},{20,28},{24,16},{28,20},{1,9},{5... | collective-permute-start | bytes 1622024 | tf_op jit(solution)/shard_map/ppermute | solution.py:57
  67.0 2.4 collective-permute-done.6
  75.4 5.5 %collective-permute-done.14 = bf16[2,1,2,528,128]{4,3,2,1,0:T(8,128)(2,1)S(1)} collective-permute-done((bf16[2,1,2,528,128]{4,3,2,1,0:T(8,128)(2,1)S(1)}, bf16[2,1,2,528,128]{4,3,2,1,0:T(8,128)(2,1)S(1)}, u32[]{:S(2)}, u32[]{:S(2)}) %collective-permute-start.14) | collective-permute-done | bytes 540704 | tf_op jit(solution)/shard_map/ppermute | solution.py:57
  82.1 7.8 %attend_forward.1 = (bf16[512,256]{1,0:T(8,128)(2,1)S(1)}, f32[8,512]{1,0:T(8,128)S(1)}) custom-call(bf16[1024,512]{1,0:T(8,128)(2,1)S(1)} %convolution_convert_fusion.q_ref.k_ref, bf16[1024,512]{1,0:T(8,128)(2,1)S(1)} %convolution_convert_fusion.q_ref.k_ref, bf16[1024,256]{1,0:T(8,128)(2,1)S(1)} %convolution_convert_fusion.1.v_ref, ...), custom_call_target="tpu_custom_call" | custom-call | flops 1 | bytes 1 | tf_op jit(solution)/shard_map/attend_forward/pallas_call | solution.py:226
  92.3 1.9 collective-permute-done.15.got_ref.refs_2_
  97.4 5.3 %collective-permute-done.16.refs_3_ = bf16[128,1024]{1,0:T(8,128)(2,1)S(1)} collective-permute-done((bf16[128,1024]{1,0:T(8,128)(2,1)S(1)}, bf16[128,1024]{1,0:T(8,128)(2,1)S(1)}, u32[]{:S(2)}, u32[]{:S(2)}) %collective-permute-start.16) | collective-permute-done | bytes 262176 | tf_op jit(solution)/shard_map/ppermute | solution.py:57
  102.7 2.8 collective-permute-done.11
  108.2 4.8 %collective-permute-done.17.refs_1_ = bf16[128,1024]{1,0:T(8,128)(2,1)S(1)} collective-permute-done((bf16[128,1024]{1,0:T(8,128)(2,1)S(1)}, bf16[128,1024]{1,0:T(8,128)(2,1)S(1)}, u32[]{:S(2)}, u32[]{:S(2)}) %collective-permute-start.17) | collective-permute-done | bytes 262176 | tf_op jit(solution)/shard_map/ppermute | solution.py:57
  116.1 2.9 feed_up.1
  120.0 6.1 %collective-permute-done.21 = bf16[2,2,1,1024,128]{4,3,2,1,0:T(8,128)(2,1)S(1)} collective-permute-done((bf16[2,2,1,1024,128]{4,3,2,1,0:T(8,128)(2,1)S(1)}, bf16[2,2,1,1024,128]{4,3,2,1,0:T(8,128)(2,1)S(1)}, u32[]{:S(2)}, u32[]{:S(2)}) %collective-permute-start.21) | collective-permute-done | bytes 1048608 | tf_op jit(solution)/shard_map/ppermute | solution.py:57
  126.5 1.9 feed_down.1
  132.1 6.8 %collective-permute-done.23.refs_3_ = bf16[128,1024]{1,0:T(8,128)(2,1)S(1)} collective-permute-done((bf16[128,1024]{1,0:T(8,128)(2,1)S(1)}, bf16[128,1024]{1,0:T(8,128)(2,1)S(1)}, u32[]{:S(2)}, u32[]{:S(2)}) %collective-permute-start.23) | collective-permute-done | bytes 262176 | tf_op jit(solution)/shard_map/ppermute | solution.py:57
  141.9 6.0 %collective-permute-done.26.refs_1_ = bf16[128,1024]{1,0:T(8,128)(2,1)S(1)} collective-permute-done((bf16[128,1024]{1,0:T(8,128)(2,1)S(1)}, bf16[128,1024]{1,0:T(8,128)(2,1)S(1)}, u32[]{:S(2)}, u32[]{:S(2)}) %collective-permute-start.26) | collective-permute-done | bytes 262176 | tf_op jit(solution)/shard_map/ppermute | solution.py:57
  149.4 6.7 %late_forward.1 = (f32[512,2048]{1,0:T(8,128)S(1)}, f32[8,2048]{1,0:T(8,128)S(1)}) custom-call(bf16[128,1024]{1,0:T(8,128)(2,1)S(1)} %get-tuple-element.394.refs_0_, bf16[128,1024]{1,0:T(8,128)(2,1)S(1)} %collective-permute-done.26.refs_1_, bf16[128,1024]{1,0:T(8,128)(2,1)S(1)} %collective-permute-done.27.refs_2_, ...), custom_call_target="tpu_custom_call" | custom-call | flops 1 | bytes 1 | tf_op jit(solution)/shard_map/late_forward/pallas_call | solution.py:531
  162.2 5.4 %collective-permute-done.32.refs_5_ = bf16[128,1024]{1,0:T(8,128)(2,1)S(1)} collective-permute-done((bf16[128,1024]{1,0:T(8,128)(2,1)S(1)}, bf16[128,1024]{1,0:T(8,128)(2,1)S(1)}, u32[]{:S(2)}, u32[]{:S(2)}) %collective-permute-start.32) | collective-permute-done | bytes 262176 | tf_op jit(solution)/shard_map/ppermute | solution.py:57
  167.6 4.9 %late_backward.1 = (f32[256,1024]{1,0:T(8,128)S(1)}, bf16[256,1024]{1,0:T(8,128)(2,1)}) custom-call(f32[512,2048]{1,0:T(8,128)S(1)} %get-tuple-element.401.sharp_ref, f32[8,2048]{1,0:T(8,128)S(1)} %log_add_fusion.soft_ref, f32[8,2048]{1,0:T(8,128)S(1)} %reshape.605.weight_ref, bf16[2048,1024]{1,0:T(8,128)(2,1)S(1)} %copy-done.2), custom_call_target="tpu_custom_call" | custom-call | flops 1 | bytes 1 | tf_op jit(solution)/shard_map/late_backward/pallas_call | solution.py:577
  185.4 6.7 %collective-permute-done.37.refs_2_ = bf16[128,1024]{1,0:T(8,128)(2,1)S(1)} collective-permute-done((bf16[128,1024]{1,0:T(8,128)(2,1)S(1)}, bf16[128,1024]{1,0:T(8,128)(2,1)S(1)}, u32[]{:S(2)}, u32[]{:S(2)}) %collective-permute-start.37) | collective-permute-done | bytes 262176 | tf_op jit(solution)/shard_map/ppermute | solution.py:57
  198.0 2.3 norm_two_back.1
  201.8 5.9 %collective-permute-done.38.refs_1_ = bf16[128,1024]{1,0:T(8,128)(2,1)S(1)} collective-permute-done((bf16[128,1024]{1,0:T(8,128)(2,1)S(1)}, bf16[128,1024]{1,0:T(8,128)(2,1)S(1)}, u32[]{:S(2)}, u32[]{:S(2)}) %collective-permute-start.38) | collective-permute-done | bytes 262176 | tf_op jit(solution)/shard_map/ppermute | solution.py:57
  207.7 1.9 collective-permute-start.35
  211.4 3.6 %feed_inner.1.dz_ref.dinner_ref = bf16[512,1024]{1,0:T(8,128)(2,1)S(1)} custom-call(bf16[128,1024]{1,0:T(8,128)(2,1)S(1)} %get-tuple-element.415.refs_0_, bf16[128,1024]{1,0:T(8,128)(2,1)S(1)} %collective-permute-done.38.refs_1_, bf16[128,1024]{1,0:T(8,128)(2,1)S(1)} %collective-permute-done.39.refs_2_, ...), custom_call_target="tpu_custom_call" | custom-call | flops 1 | bytes 1 | tf_op jit(solution)/shard_map/feed_inner/pallas_call | solution.py:471
  215.1 2.2 feed_back.1
  219.0 4.0 %collective-permute-start.41 = (f32[64,15]{0,1:T(8,128)S(1)}, f32[64,15]{0,1:T(8,128)S(1)}, u32[]{:S(2)}, u32[]{:S(2)}) collective-permute-start(f32[64,15]{0,1:T(8,128)S(1)} %add.158), channel_id=1, source_target_pairs={{0,16},{4,20},{8,24},{12,28},{16,0},{20,4},{24,8},{28,12},{1,17},{... | collective-permute-start | bytes 11528 | tf_op jit(solution)/shard_map/ppermute | solution.py:57
  227.8 2.4 grad_down.1
  230.2 2.0 collective-permute-start.52
  232.3 2.3 grad_up.1
  237.5 6.9 %collective-permute-done.48.refs_1_ = bf16[144,1024]{1,0:T(8,128)(2,1)S(1)} collective-permute-done((bf16[144,1024]{1,0:T(8,128)(2,1)S(1)}, bf16[144,1024]{1,0:T(8,128)(2,1)S(1)}, u32[]{:S(2)}, u32[]{:S(2)}) %collective-permute-start.48) | collective-permute-done | bytes 294944 | tf_op jit(solution)/shard_map/ppermute | solution.py:57
  248.3 7.4 %collective-permute-done.52 = bf16[4,1024,128]{2,1,0:T(8,128)(2,1)S(1)} collective-permute-done((bf16[4,1024,128]{2,1,0:T(8,128)(2,1)S(1)}, bf16[4,1024,128]{2,1,0:T(8,128)(2,1)S(1)}, u32[]{:S(2)}, u32[]{:S(2)}) %collective-permute-start.52) | collective-permute-done | bytes 1048608 | tf_op jit(solution)/shard_map/ppermute | solution.py:57
  256.9 10.2 %attend_own.1 = (bf16[512,256]{1,0:T(8,128)(2,1)S(1)}, f32[512,256]{1,0:T(8,128)S(1)}, f32[512,256]{1,0:T(8,128)S(1)}) custom-call(bf16[1024,512]{1,0:T(8,128)(2,1)S(1)} %convolution_convert_fusion.q_ref.k_ref, bf16[1024,512]{1,0:T(8,128)(2,1)S(1)} %convolution_convert_fusion.q_ref.k_ref, bf16[1024,256]{1,0:T(8,128)(2,1)S(1)} %copy-done.8, ...), custom_call_target="tpu_custom_call" | custom-call | flops 1 | bytes 1 | tf_op jit(solution)/shard_map/attend_own/pallas_call | solution.py:291
  273.1 1.9 collective-permute-start.53
  275.0 7.9 %collective-permute-done.54 = bf16[2,1024,128]{2,1,0:T(8,128)(2,1)S(1)} collective-permute-done((bf16[2,1024,128]{2,1,0:T(8,128)(2,1)S(1)}, bf16[2,1024,128]{2,1,0:T(8,128)(2,1)S(1)}, u32[]{:S(2)}, u32[]{:S(2)}) %collective-permute-start.54) | collective-permute-done | bytes 524320 | tf_op jit(solution)/shard_map/ppermute | solution.py:57
  284.1 3.6 collective-permute-start.55
  290.8 8.0 %attend_other.1 = (bf16[512,512]{1,0:T(8,128)(2,1)S(1)}, bf16[512,256]{1,0:T(8,128)(2,1)S(1)}) custom-call(bf16[1024,512]{1,0:T(8,128)(2,1)S(1)} %convolution_convert_fusion.q_ref.k_ref, bf16[1024,512]{1,0:T(8,128)(2,1)S(1)} %convolution_convert_fusion.q_ref.k_ref, bf16[1024,256]{1,0:T(8,128)(2,1)S(1)} %copy-done.8, bf16[512,256]{1,0:T(8,128)(2,1)S(1)} %bitcast.77, ...), custom_call_target="tpu_custom_call" | custom-call | flops 1 | bytes 1 | tf_op jit(solution)/shard_map/attend_other/pallas_call | solution.py:363
  309.3 9.6 %collective-permute-done.57 = bf16[4,128,512]{2,1,0:T(8,128)(2,1)S(1)} collective-permute-done((bf16[4,128,512]{2,1,0:T(8,128)(2,1)S(1)}, bf16[4,128,512]{2,1,0:T(8,128)(2,1)S(1)}, u32[]{:S(2)}, u32[]{:S(2)}) %collective-permute-start.57) | collective-permute-done | bytes 524320 | tf_op jit(solution)/shard_map/ppermute | solution.py:57
  319.0 7.4 %collective-permute-done.56 = bf16[4,528,128]{2,1,0:T(8,128)(2,1)S(1)} collective-permute-done((bf16[4,528,128]{2,1,0:T(8,128)(2,1)S(1)}, bf16[4,528,128]{2,1,0:T(8,128)(2,1)S(1)}, u32[]{:S(2)}, u32[]{:S(2)}) %collective-permute-start.56) | collective-permute-done | bytes 540704 | tf_op jit(solution)/shard_map/ppermute | solution.py:57
  328.4 1.8 fusion.3
  330.6 2.1 collective-permute-start.60
  335.9 7.8 %collective-permute-done.61 = bf16[2,128,512]{2,1,0:T(8,128)(2,1)S(1)} collective-permute-done((bf16[2,128,512]{2,1,0:T(8,128)(2,1)S(1)}, bf16[2,128,512]{2,1,0:T(8,128)(2,1)S(1)}, u32[]{:S(2)}, u32[]{:S(2)}) %collective-permute-start.61) | collective-permute-done | bytes 262176 | tf_op jit(solution)/shard_map/ppermute | solution.py:57
  343.9 2.0 place_rows.1
  347.7 6.5 %collective-permute-done.67 = bf16[1,128,512]{2,1,0:T(8,128)(2,1)S(1)} collective-permute-done((bf16[1,128,512]{2,1,0:T(8,128)(2,1)S(1)}, bf16[1,128,512]{2,1,0:T(8,128)(2,1)S(1)}, u32[]{:S(2)}, u32[]{:S(2)}) %collective-permute-start.67) | collective-permute-done | bytes 131104 | tf_op jit(solution)/shard_map/ppermute | solution.py:57
  (428 shorter events, 121.3 us)
Async XLA Ops:
  9.2 18.3 %collective-permute-start = (bf16[1,1,1,128,512]{4,3,2,1,0:T(8,128)(2,1)S(1)}, bf16[1,1,1,128,512]{4,3,2,1,0:T(8,128)(2,1)S(1)}, u32[]{:S(2)}, u32[]{:S(2)}) collective-permute-start(bf16[1,1,1,128,512]{4,3,2,1,0:T(8,128)(2,1)S(1)} %bitcast.81), channel_id=1, source_target_pairs={{0,16},{4,20},{8,24},{12,28},{16,0},{20,4},{24,8},{28,12},{1,17},{... | collective-permute-start | bytes 393224 | tf_op jit(solution)/shard_map/ppermute | solution.py:57
  13.4 14.3 %collective-permute-start.4 = (bf16[1,128,1024]{2,1,0:T(8,128)(2,1)S(1)}, bf16[1,128,1024]{2,1,0:T(8,128)(2,1)}, u32[]{:S(2)}, u32[]{:S(2)}) collective-permute-start(bf16[1,128,1024]{2,1,0:T(8,128)(2,1)S(1)} %bitcast.73), channel_id=1, source_target_pairs={{0,4},{4,0},{8,12},{12,8},{16,20},{20,16},{24,28},{28,24},{1,5},{5... | collective-permute-start | bytes 786440 | tf_op jit(solution)/shard_map/ppermute | solution.py:57
  14.9 18.9 %collective-permute-start.3 = (bf16[1,1,1,128,1280]{4,3,2,1,0:T(8,128)(2,1)S(1)}, bf16[1,1,1,128,1280]{4,3,2,1,0:T(8,128)(2,1)S(1)}, u32[]{:S(2)}, u32[]{:S(2)}) collective-permute-start(bf16[1,1,1,128,1280]{4,3,2,1,0:T(8,128)(2,1)S(1)} %bitcast.74), channel_id=1, source_target_pairs={{0,16},{4,20},{8,24},{12,28},{16,0},{20,4},{24,8},{28,12},{1,17},{... | collective-permute-start | bytes 983048 | tf_op jit(solution)/shard_map/ppermute | solution.py:57
  15.2 18.7 %collective-permute-start.2 = (bf16[1,1,1,528,128]{4,3,2,1,0:T(8,128)(2,1)S(1)}, bf16[1,1,1,528,128]{4,3,2,1,0:T(8,128)(2,1)}, u32[]{:S(2)}, u32[]{:S(2)}) collective-permute-start(bf16[1,1,1,528,128]{4,3,2,1,0:T(8,128)(2,1)S(1)} %bitcast.79), channel_id=1, source_target_pairs={{0,4},{4,0},{8,12},{12,8},{16,20},{20,16},{24,28},{28,24},{1,5},{5... | collective-permute-start | bytes 405512 | tf_op jit(solution)/shard_map/ppermute | solution.py:57
  27.5 11.8 %collective-permute-start.1 = (bf16[2,1,1,128,512]{4,3,2,1,0:T(8,128)(2,1)S(1)}, bf16[2,1,1,128,512]{4,3,2,1,0:T(8,128)(2,1)S(1)}, u32[]{:S(2)}, u32[]{:S(2)}) collective-permute-start(bf16[2,1,1,128,512]{4,3,2,1,0:T(8,128)(2,1)S(1)} %maximum_select_fusion.11), channel_id=1, source_target_pairs={{0,8},{4,12},{8,0},{12,4},{16,24},{20,28},{24,16},{28,20},{1,9},{5... | collective-permute-start | bytes 786440 | tf_op jit(solution)/shard_map/ppermute | solution.py:57
  27.6 12.5 %collective-permute-start.8 = (bf16[1,128,1024]{2,1,0:T(8,128)(2,1)}, bf16[1,128,1024]{2,1,0:T(8,128)(2,1)}, u32[]{:S(2)}, u32[]{:S(2)}) collective-permute-start(bf16[1,128,1024]{2,1,0:T(8,128)(2,1)} %collective-permute-done.4), channel_id=1, source_target_pairs={{0,2},{1,3},{2,0},{3,1},{4,6},{5,7},{6,4},{7,5},{8,10},{9,11},{10,... | collective-permute-start | bytes 786440 | tf_op jit(solution)/shard_map/ppermute | solution.py:57
  29.5 16.6 %collective-permute-start.9 = (bf16[1,128,1024]{2,1,0:T(8,128)(2,1)}, bf16[1,128,1024]{2,1,0:T(8,128)(2,1)}, u32[]{:S(2)}, u32[]{:S(2)}) collective-permute-start(bf16[1,128,1024]{2,1,0:T(8,128)(2,1)} %collective-permute-done.4), channel_id=1, source_target_pairs={{0,1},{1,0},{2,3},{3,2},{4,5},{5,4},{6,7},{7,6},{8,9},{9,8},{10,11... | collective-permute-start | bytes 786440 | tf_op jit(solution)/shard_map/ppermute | solution.py:57
  40.3 29.1 %collective-permute-start.6 = (bf16[2,1,1,128,1280]{4,3,2,1,0:T(8,128)(2,1)S(1)}, bf16[2,1,1,128,1280]{4,3,2,1,0:T(8,128)(2,1)}, u32[]{:S(2)}, u32[]{:S(2)}) collective-permute-start(bf16[2,1,1,128,1280]{4,3,2,1,0:T(8,128)(2,1)S(1)} %maximum_select_fusion.6), channel_id=1, source_target_pairs={{0,8},{4,12},{8,0},{12,4},{16,24},{20,28},{24,16},{28,20},{1,9},{5... | collective-permute-start | bytes 1966088 | tf_op jit(solution)/shard_map/ppermute | solution.py:57
  40.5 20.9 %collective-permute-start.7 = (bf16[1,1,2,528,128]{4,3,2,1,0:T(8,128)(2,1)}, bf16[1,1,2,528,128]{4,3,2,1,0:T(8,128)(2,1)S(1)}, u32[]{:S(2)}, u32[]{:S(2)}) collective-permute-start(bf16[1,1,2,528,128]{4,3,2,1,0:T(8,128)(2,1)} %maximum_select_fusion.10), channel_id=1, source_target_pairs={{0,16},{4,20},{8,24},{12,28},{16,0},{20,4},{24,8},{28,12},{1,17},{... | collective-permute-start | bytes 811016 | tf_op jit(solution)/shard_map/ppermute | solution.py:57
  44.6 26.2 %collective-permute-start.5 = (bf16[2,2,1,128,512]{4,3,2,1,0:T(8,128)(2,1)}, bf16[2,2,1,128,512]{4,3,2,1,0:T(8,128)(2,1)S(1)}, u32[]{:S(2)}, u32[]{:S(2)}) collective-permute-start(bf16[2,2,1,128,512]{4,3,2,1,0:T(8,128)(2,1)} %maximum_select_fusion.8), channel_id=1, source_target_pairs={{0,4},{4,0},{8,12},{12,8},{16,20},{20,16},{24,28},{28,24},{1,5},{5... | collective-permute-start | bytes 1572872 | tf_op jit(solution)/shard_map/ppermute | solution.py:57
  46.2 27.4 %collective-permute-start.12 = (bf16[1,1,1,1024,128]{4,3,2,1,0:T(8,128)(2,1)}, bf16[1,1,1,1024,128]{4,3,2,1,0:T(8,128)(2,1)S(1)}, u32[]{:S(2)}, u32[]{:S(2)}) collective-permute-start(bf16[1,1,1,1024,128]{4,3,2,1,0:T(8,128)(2,1)} %bitcast.93), channel_id=1, source_target_pairs={{0,16},{4,20},{8,24},{12,28},{16,0},{20,4},{24,8},{28,12},{1,17},{... | collective-permute-start | bytes 786440 | tf_op jit(solution)/shard_map/ppermute | solution.py:57
  62.5 18.3 %collective-permute-start.14 = (bf16[2,1,2,528,128]{4,3,2,1,0:T(8,128)(2,1)S(1)}, bf16[2,1,2,528,128]{4,3,2,1,0:T(8,128)(2,1)S(1)}, u32[]{:S(2)}, u32[]{:S(2)}) collective-permute-start(bf16[2,1,2,528,128]{4,3,2,1,0:T(8,128)(2,1)S(1)} %maximum_select_fusion.7), channel_id=1, source_target_pairs={{0,8},{4,12},{8,0},{12,4},{16,24},{20,28},{24,16},{28,20},{1,9},{5... | collective-permute-start | bytes 1622024 | tf_op jit(solution)/shard_map/ppermute | solution.py:57
  73.6 18.0 %collective-permute-start.13 = (bf16[2,1,1,1024,128]{4,3,2,1,0:T(8,128)(2,1)S(1)}, bf16[2,1,1,1024,128]{4,3,2,1,0:T(8,128)(2,1)S(1)}, u32[]{:S(2)}, u32[]{:S(2)}) collective-permute-start(bf16[2,1,1,1024,128]{4,3,2,1,0:T(8,128)(2,1)S(1)} %maximum_select_fusion.9), channel_id=1, source_target_pairs={{0,8},{4,12},{8,0},{12,4},{16,24},{20,28},{24,16},{28,20},{1,9},{5... | collective-permute-start | bytes 1572872 | tf_op jit(solution)/shard_map/ppermute | solution.py:57
  73.7 31.8 %collective-permute-start.11 = (bf16[2,2,1,128,1280]{4,3,2,1,0:T(8,128)(2,1)S(1)}, bf16[2,2,1,128,1280]{4,3,2,1,0:T(8,128)(2,1)S(1)}, u32[]{:S(2)}, u32[]{:S(2)}) collective-permute-start(bf16[2,2,1,128,1280]{4,3,2,1,0:T(8,128)(2,1)S(1)} %maximum_select_fusion.2), channel_id=1, source_target_pairs={{0,4},{4,0},{8,12},{12,8},{16,20},{20,16},{24,28},{28,24},{1,5},{5... | collective-permute-start | bytes 3932168 | tf_op jit(solution)/shard_map/ppermute | solution.py:57
  94.3 8.4 %collective-permute-start.16 = (bf16[128,1024]{1,0:T(8,128)(2,1)S(1)}, bf16[128,1024]{1,0:T(8,128)(2,1)S(1)}, u32[]{:S(2)}, u32[]{:S(2)}) collective-permute-start(bf16[128,1024]{1,0:T(8,128)(2,1)S(1)} %fold.5), channel_id=1, source_target_pairs={{0,2},{1,3},{2,0},{3,1},{4,6},{5,7},{6,4},{7,5},{8,10},{9,11},{10,... | collective-permute-start | bytes 786440 | tf_op jit(solution)/shard_map/ppermute | solution.py:57
  95.9 30.3 %collective-permute-start.21 = (bf16[2,2,1,1024,128]{4,3,2,1,0:T(8,128)(2,1)S(1)}, bf16[2,2,1,1024,128]{4,3,2,1,0:T(8,128)(2,1)S(1)}, u32[]{:S(2)}, u32[]{:S(2)}) collective-permute-start(bf16[2,2,1,1024,128]{4,3,2,1,0:T(8,128)(2,1)S(1)} %maximum_select_fusion.5), channel_id=1, source_target_pairs={{0,4},{4,0},{8,12},{12,8},{16,20},{20,16},{24,28},{28,24},{1,5},{5... | collective-permute-start | bytes 3145736 | tf_op jit(solution)/shard_map/ppermute | solution.py:57
  114.5 14.0 %collective-permute-start.20 = (bf16[1024,256]{1,0:T(8,128)(2,1)S(1)}, bf16[1024,256]{1,0:T(8,128)(2,1)S(1)}, u32[]{:S(2)}, u32[]{:S(2)}) collective-permute-start(bf16[1024,256]{1,0:T(8,128)(2,1)S(1)} %slice.178.refs_5_.refs_8_), channel_id=1, source_target_pairs={{0,2},{1,3},{2,0},{3,1},{4,6},{5,7},{6,4},{7,5},{8,10},{9,11},{10,... | collective-permute-start | bytes 1572872 | tf_op jit(solution)/shard_map/ppermute | solution.py:57
  130.5 8.4 %collective-permute-start.23 = (bf16[128,1024]{1,0:T(8,128)(2,1)S(1)}, bf16[128,1024]{1,0:T(8,128)(2,1)S(1)}, u32[]{:S(2)}, u32[]{:S(2)}) collective-permute-start(bf16[128,1024]{1,0:T(8,128)(2,1)S(1)} %fold.6), channel_id=1, source_target_pairs={{0,2},{1,3},{2,0},{3,1},{4,6},{5,7},{6,4},{7,5},{8,10},{9,11},{10,... | collective-permute-start | bytes 786440 | tf_op jit(solution)/shard_map/ppermute | solution.py:57
  140.3 7.6 %collective-permute-start.26 = (bf16[128,1024]{1,0:T(8,128)(2,1)S(1)}, bf16[128,1024]{1,0:T(8,128)(2,1)S(1)}, u32[]{:S(2)}, u32[]{:S(2)}) collective-permute-start(bf16[128,1024]{1,0:T(8,128)(2,1)S(1)} %get-tuple-element.394.refs_0_), channel_id=1, source_target_pairs={{0,2},{1,3},{2,0},{3,1},{4,6},{5,7},{6,4},{7,5},{8,10},{9,11},{10,... | collective-permute-start | bytes 786440 | tf_op jit(solution)/shard_map/ppermute | solution.py:57
  158.0 15.5 %collective-permute-start.31 = (f32[1,8,512]{2,1,0:T(8,128)S(1)}, f32[1,8,512]{2,1,0:T(8,128)S(1)}, u32[]{:S(2)}, u32[]{:S(2)}) collective-permute-start(f32[1,8,512]{2,1,0:T(8,128)S(1)} %bitcast.88), channel_id=1, source_target_pairs={{0,4},{4,0},{8,12},{12,8},{16,20},{20,16},{24,28},{28,24},{1,5},{5... | collective-permute-start | bytes 49160 | tf_op jit(solution)/shard_map/ppermute | solution.py:57
  158.5 15.6 %collective-permute-start.30 = (bf16[1,512,256]{2,1,0:T(8,128)(2,1)S(1)}, bf16[1,512,256]{2,1,0:T(8,128)(2,1)S(1)}, u32[]{:S(2)}, u32[]{:S(2)}) collective-permute-start(bf16[1,512,256]{2,1,0:T(8,128)(2,1)S(1)} %bitcast.70), channel_id=1, source_target_pairs={{0,4},{4,0},{8,12},{12,8},{16,20},{20,16},{24,28},{28,24},{1,5},{5... | collective-permute-start | bytes 786440 | tf_op jit(solution)/shard_map/ppermute | solution.py:57
  160.1 7.5 %collective-permute-start.32 = (bf16[128,1024]{1,0:T(8,128)(2,1)S(1)}, bf16[128,1024]{1,0:T(8,128)(2,1)S(1)}, u32[]{:S(2)}, u32[]{:S(2)}) collective-permute-start(bf16[128,1024]{1,0:T(8,128)(2,1)S(1)} %get-tuple-element.431.refs_4_), channel_id=1, source_target_pairs={{0,2},{1,3},{2,0},{3,1},{4,6},{5,7},{6,4},{7,5},{8,10},{9,11},{10,... | collective-permute-start | bytes 786440 | tf_op jit(solution)/shard_map/ppermute | solution.py:57
  161.6 13.2 %collective-permute-start.33 = (bf16[128,1024]{1,0:T(8,128)(2,1)S(1)}, bf16[128,1024]{1,0:T(8,128)(2,1)S(1)}, u32[]{:S(2)}, u32[]{:S(2)}) collective-permute-start(bf16[128,1024]{1,0:T(8,128)(2,1)S(1)} %get-tuple-element.431.refs_4_), channel_id=1, source_target_pairs={{0,1},{1,0},{2,3},{3,2},{4,5},{5,4},{6,7},{7,6},{8,9},{9,8},{10,11... | collective-permute-start | bytes 786440 | tf_op jit(solution)/shard_map/ppermute | solution.py:57
  167.6 7.9 %collective-permute-start.34 = (bf16[128,1024]{1,0:T(8,128)(2,1)S(1)}, bf16[128,1024]{1,0:T(8,128)(2,1)S(1)}, u32[]{:S(2)}, u32[]{:S(2)}) collective-permute-start(bf16[128,1024]{1,0:T(8,128)(2,1)S(1)} %collective-permute-done.32.refs_5_), channel_id=1, source_target_pairs={{0,1},{1,0},{2,3},{3,2},{4,5},{5,4},{6,7},{7,6},{8,9},{9,8},{10,11... | collective-permute-start | bytes 786440 | tf_op jit(solution)/shard_map/ppermute | solution.py:57
  183.8 8.3 %collective-permute-start.37 = (bf16[128,1024]{1,0:T(8,128)(2,1)S(1)}, bf16[128,1024]{1,0:T(8,128)(2,1)S(1)}, u32[]{:S(2)}, u32[]{:S(2)}) collective-permute-start(bf16[128,1024]{1,0:T(8,128)(2,1)S(1)} %fold.7), channel_id=1, source_target_pairs={{0,2},{1,3},{2,0},{3,1},{4,6},{5,7},{6,4},{7,5},{8,10},{9,11},{10,... | collective-permute-start | bytes 786440 | tf_op jit(solution)/shard_map/ppermute | solution.py:57
  200.3 7.4 %collective-permute-start.38 = (bf16[128,1024]{1,0:T(8,128)(2,1)S(1)}, bf16[128,1024]{1,0:T(8,128)(2,1)S(1)}, u32[]{:S(2)}, u32[]{:S(2)}) collective-permute-start(bf16[128,1024]{1,0:T(8,128)(2,1)S(1)} %get-tuple-element.415.refs_0_), channel_id=1, source_target_pairs={{0,2},{1,3},{2,0},{3,1},{4,6},{5,7},{6,4},{7,5},{8,10},{9,11},{10,... | collective-permute-start | bytes 786440 | tf_op jit(solution)/shard_map/ppermute | solution.py:57
  201.8 9.5 %collective-permute-start.39 = (bf16[128,1024]{1,0:T(8,128)(2,1)S(1)}, bf16[128,1024]{1,0:T(8,128)(2,1)S(1)}, u32[]{:S(2)}, u32[]{:S(2)}) collective-permute-start(bf16[128,1024]{1,0:T(8,128)(2,1)S(1)} %get-tuple-element.415.refs_0_), channel_id=1, source_target_pairs={{0,1},{1,0},{2,3},{3,2},{4,5},{5,4},{6,7},{7,6},{8,9},{9,8},{10,11... | collective-permute-start | bytes 786440 | tf_op jit(solution)/shard_map/ppermute | solution.py:57
  217.3 8.8 %collective-permute-start.42 = (bf16[256,1024]{1,0:T(8,128)(2,1)S(1)}, bf16[256,1024]{1,0:T(8,128)(2,1)S(1)}, u32[]{:S(2)}, u32[]{:S(2)}) collective-permute-start(bf16[256,1024]{1,0:T(8,128)(2,1)S(1)} %get-tuple-element.424), channel_id=1, source_target_pairs={{0,1},{1,0},{2,3},{3,2},{4,5},{5,4},{6,7},{7,6},{8,9},{9,8},{10,11... | collective-permute-start | bytes 1572872 | tf_op jit(solution)/shard_map/ppermute | solution.py:57
  217.4 8.7 %collective-permute-start.43 = (bf16[128,1024]{1,0:T(8,128)(2,1)S(1)}, bf16[128,1024]{1,0:T(8,128)(2,1)S(1)}, u32[]{:S(2)}, u32[]{:S(2)}) collective-permute-start(bf16[128,1024]{1,0:T(8,128)(2,1)S(1)} %get-tuple-element.435.refs_8_), channel_id=1, source_target_pairs={{0,2},{1,3},{2,0},{3,1},{4,6},{5,7},{6,4},{7,5},{8,10},{9,11},{10,... | collective-permute-start | bytes 786440 | tf_op jit(solution)/shard_map/ppermute | solution.py:57
  223.0 9.3 %collective-permute-start.44 = (bf16[128,1024]{1,0:T(8,128)(2,1)S(1)}, bf16[128,1024]{1,0:T(8,128)(2,1)S(1)}, u32[]{:S(2)}, u32[]{:S(2)}) collective-permute-start(bf16[128,1024]{1,0:T(8,128)(2,1)S(1)} %get-tuple-element.435.refs_8_), channel_id=1, source_target_pairs={{0,1},{1,0},{2,3},{3,2},{4,5},{5,4},{6,7},{7,6},{8,9},{9,8},{10,11... | collective-permute-start | bytes 786440 | tf_op jit(solution)/shard_map/ppermute | solution.py:57
  226.2 8.8 %collective-permute-start.46 = (bf16[128,1024]{1,0:T(8,128)(2,1)S(1)}, bf16[128,1024]{1,0:T(8,128)(2,1)S(1)}, u32[]{:S(2)}, u32[]{:S(2)}) collective-permute-start(bf16[128,1024]{1,0:T(8,128)(2,1)S(1)} %fold.8), channel_id=1, source_target_pairs={{0,2},{1,3},{2,0},{3,1},{4,6},{5,7},{6,4},{7,5},{8,10},{9,11},{10,... | collective-permute-start | bytes 786440 | tf_op jit(solution)/shard_map/ppermute | solution.py:57
  230.2 25.6 %collective-permute-start.52 = (bf16[4,1024,128]{2,1,0:T(8,128)(2,1)S(1)}, bf16[4,1024,128]{2,1,0:T(8,128)(2,1)S(1)}, u32[]{:S(2)}, u32[]{:S(2)}) collective-permute-start(bf16[4,1024,128]{2,1,0:T(8,128)(2,1)S(1)} %get-tuple-element.448), channel_id=1, source_target_pairs={{0,8},{4,12},{8,0},{12,4},{16,24},{20,28},{24,16},{28,20},{1,9},{5... | collective-permute-start | bytes 3145736 | tf_op jit(solution)/shard_map/ppermute | solution.py:57
  235.0 36.8 %collective-permute-start.47 = (bf16[4,128,1280]{2,1,0:T(8,128)(2,1)S(1)}, bf16[4,128,1280]{2,1,0:T(8,128)(2,1)S(1)}, u32[]{:S(2)}, u32[]{:S(2)}) collective-permute-start(bf16[4,128,1280]{2,1,0:T(8,128)(2,1)S(1)} %get-tuple-element.439), channel_id=1, source_target_pairs={{0,4},{4,0},{8,12},{12,8},{16,20},{20,16},{24,28},{28,24},{1,5},{5... | collective-permute-start | bytes 3932168 | tf_op jit(solution)/shard_map/ppermute | solution.py:57
  235.9 8.5 %collective-permute-start.48 = (bf16[144,1024]{1,0:T(8,128)(2,1)S(1)}, bf16[144,1024]{1,0:T(8,128)(2,1)S(1)}, u32[]{:S(2)}, u32[]{:S(2)}) collective-permute-start(bf16[144,1024]{1,0:T(8,128)(2,1)S(1)} %get-tuple-element.445.refs_0_), channel_id=1, source_target_pairs={{0,2},{1,3},{2,0},{3,1},{4,6},{5,7},{6,4},{7,5},{8,10},{9,11},{10,... | collective-permute-start | bytes 884744 | tf_op jit(solution)/shard_map/ppermute | solution.py:57
  246.8 24.2 %collective-permute-start.51 = (bf16[1,512,256]{2,1,0:T(8,128)(2,1)S(1)}, bf16[1,512,256]{2,1,0:T(8,128)(2,1)S(1)}, u32[]{:S(2)}, u32[]{:S(2)}) collective-permute-start(bf16[1,512,256]{2,1,0:T(8,128)(2,1)S(1)} %bitcast.78), channel_id=1, source_target_pairs={{0,4},{4,0},{8,12},{12,8},{16,20},{20,16},{24,28},{28,24},{1,5},{5... | collective-permute-start | bytes 786440 | tf_op jit(solution)/shard_map/ppermute | solution.py:57
  269.4 13.5 %collective-permute-start.54 = (bf16[2,1024,128]{2,1,0:T(8,128)(2,1)S(1)}, bf16[2,1024,128]{2,1,0:T(8,128)(2,1)S(1)}, u32[]{:S(2)}, u32[]{:S(2)}) collective-permute-start(bf16[2,1024,128]{2,1,0:T(8,128)(2,1)S(1)} %slice.238), channel_id=1, source_target_pairs={{0,4},{4,0},{8,12},{12,8},{16,20},{20,16},{24,28},{28,24},{1,5},{5... | collective-permute-start | bytes 1572872 | tf_op jit(solution)/shard_map/ppermute | solution.py:57
  273.1 25.7 %collective-permute-start.53 = (bf16[2,128,1280]{2,1,0:T(8,128)(2,1)}, bf16[2,128,1280]{2,1,0:T(8,128)(2,1)}, u32[]{:S(2)}, u32[]{:S(2)}) collective-permute-start(bf16[2,128,1280]{2,1,0:T(8,128)(2,1)} %slice.237), channel_id=1, source_target_pairs={{0,8},{4,12},{8,0},{12,4},{16,24},{20,28},{24,16},{28,20},{1,9},{5... | collective-permute-start | bytes 1966088 | tf_op jit(solution)/shard_map/ppermute | solution.py:57
  284.1 14.7 %collective-permute-start.55 = (bf16[1,1024,128]{2,1,0:T(8,128)(2,1)}, bf16[1,1024,128]{2,1,0:T(8,128)(2,1)}, u32[]{:S(2)}, u32[]{:S(2)}) collective-permute-start(bf16[1,1024,128]{2,1,0:T(8,128)(2,1)} %slice.242), channel_id=1, source_target_pairs={{0,16},{4,20},{8,24},{12,28},{16,0},{20,4},{24,8},{28,12},{1,17},{... | collective-permute-start | bytes 786440 | tf_op jit(solution)/shard_map/ppermute | solution.py:57
  304.5 14.3 %collective-permute-start.57 = (bf16[4,128,512]{2,1,0:T(8,128)(2,1)S(1)}, bf16[4,128,512]{2,1,0:T(8,128)(2,1)S(1)}, u32[]{:S(2)}, u32[]{:S(2)}) collective-permute-start(bf16[4,128,512]{2,1,0:T(8,128)(2,1)S(1)} %get-tuple-element.490), channel_id=1, source_target_pairs={{0,4},{4,0},{8,12},{12,8},{16,20},{20,16},{24,28},{28,24},{1,5},{5... | collective-permute-start | bytes 1572872 | tf_op jit(solution)/shard_map/ppermute | solution.py:57
  305.0 21.4 %collective-permute-start.56 = (bf16[4,528,128]{2,1,0:T(8,128)(2,1)S(1)}, bf16[4,528,128]{2,1,0:T(8,128)(2,1)S(1)}, u32[]{:S(2)}, u32[]{:S(2)}) collective-permute-start(bf16[4,528,128]{2,1,0:T(8,128)(2,1)S(1)} %get-tuple-element.486), channel_id=1, source_target_pairs={{0,8},{4,12},{8,0},{12,4},{16,24},{20,28},{24,16},{28,20},{1,9},{5... | collective-permute-start | bytes 1622024 | tf_op jit(solution)/shard_map/ppermute | solution.py:57
  306.4 12.4 %collective-permute-start.59 = (bf16[128,1024]{1,0:T(8,128)(2,1)S(1)}, bf16[128,1024]{1,0:T(8,128)(2,1)S(1)}, u32[]{:S(2)}, u32[]{:S(2)}) collective-permute-start(bf16[128,1024]{1,0:T(8,128)(2,1)S(1)} %fold.9), channel_id=1, source_target_pairs={{0,2},{1,3},{2,0},{3,1},{4,6},{5,7},{6,4},{7,5},{8,10},{9,11},{10,... | collective-permute-start | bytes 786440 | tf_op jit(solution)/shard_map/ppermute | solution.py:57
  308.0 18.7 %collective-permute-start.62 = (bf16[1,128,1280]{2,1,0:T(8,128)(2,1)S(1)}, bf16[1,128,1280]{2,1,0:T(8,128)(2,1)S(1)}, u32[]{:S(2)}, u32[]{:S(2)}) collective-permute-start(bf16[1,128,1280]{2,1,0:T(8,128)(2,1)S(1)} %slice.239), channel_id=1, source_target_pairs={{0,16},{4,20},{8,24},{12,28},{16,0},{20,4},{24,8},{28,12},{1,17},{... | collective-permute-start | bytes 983048 | tf_op jit(solution)/shard_map/ppermute | solution.py:57
  326.7 7.6 %collective-permute-start.63 = (bf16[128,1024]{1,0:T(8,128)(2,1)S(1)}, bf16[128,1024]{1,0:T(8,128)(2,1)S(1)}, u32[]{:S(2)}, u32[]{:S(2)}) collective-permute-start(bf16[128,1024]{1,0:T(8,128)(2,1)S(1)} %close.1.refs_0_), channel_id=1, source_target_pairs={{0,2},{1,3},{2,0},{3,1},{4,6},{5,7},{6,4},{7,5},{8,10},{9,11},{10,... | collective-permute-start | bytes 786440 | tf_op jit(solution)/shard_map/ppermute | solution.py:57
  330.2 13.6 %collective-permute-start.61 = (bf16[2,128,512]{2,1,0:T(8,128)(2,1)S(1)}, bf16[2,128,512]{2,1,0:T(8,128)(2,1)S(1)}, u32[]{:S(2)}, u32[]{:S(2)}) collective-permute-start(bf16[2,128,512]{2,1,0:T(8,128)(2,1)S(1)} %slice.241), channel_id=1, source_target_pairs={{0,8},{4,12},{8,0},{12,4},{16,24},{20,28},{24,16},{28,20},{1,9},{5... | collective-permute-start | bytes 786440 | tf_op jit(solution)/shard_map/ppermute | solution.py:57
  330.6 15.4 %collective-permute-start.60 = (bf16[2,528,128]{2,1,0:T(8,128)(2,1)S(1)}, bf16[2,528,128]{2,1,0:T(8,128)(2,1)S(1)}, u32[]{:S(2)}, u32[]{:S(2)}) collective-permute-start(bf16[2,528,128]{2,1,0:T(8,128)(2,1)S(1)} %slice.240), channel_id=1, source_target_pairs={{0,16},{4,20},{8,24},{12,28},{16,0},{20,4},{24,8},{28,12},{1,17},{... | collective-permute-start | bytes 811016 | tf_op jit(solution)/shard_map/ppermute | solution.py:57
  334.4 9.4 %collective-permute-start.65 = (bf16[128,1024]{1,0:T(8,128)(2,1)S(1)}, bf16[128,1024]{1,0:T(8,128)(2,1)S(1)}, u32[]{:S(2)}, u32[]{:S(2)}) collective-permute-start(bf16[128,1024]{1,0:T(8,128)(2,1)S(1)} %collective-permute-done.63.refs_1_), channel_id=1, source_target_pairs={{0,1},{1,0},{2,3},{3,2},{4,5},{5,4},{6,7},{7,6},{8,9},{9,8},{10,11... | collective-permute-start | bytes 786440 | tf_op jit(solution)/shard_map/ppermute | solution.py:57
  345.9 8.3 %collective-permute-start.67 = (bf16[1,128,512]{2,1,0:T(8,128)(2,1)S(1)}, bf16[1,128,512]{2,1,0:T(8,128)(2,1)S(1)}, u32[]{:S(2)}, u32[]{:S(2)}) collective-permute-start(bf16[1,128,512]{2,1,0:T(8,128)(2,1)S(1)} %slice.244), channel_id=1, source_target_pairs={{0,16},{4,20},{8,24},{12,28},{16,0},{20,4},{24,8},{28,12},{1,17},{... | collective-permute-start | bytes 393224 | tf_op jit(solution)/shard_map/ppermute | solution.py:57
  346.2 8.8 %collective-permute-start.66 = (bf16[1,528,128]{2,1,0:T(8,128)(2,1)S(1)}, bf16[1,528,128]{2,1,0:T(8,128)(2,1)S(1)}, u32[]{:S(2)}, u32[]{:S(2)}) collective-permute-start(bf16[1,528,128]{2,1,0:T(8,128)(2,1)S(1)} %slice.243), channel_id=1, source_target_pairs={{0,4},{4,0},{8,12},{12,8},{16,20},{20,16},{24,28},{28,24},{1,5},{5... | collective-permute-start | bytes 405512 | tf_op jit(solution)/shard_map/ppermute | solution.py:57
  (131 other events, 1157.7 us)
where the time goes:
time: 358 us; the launch traced here: 357 us
  waiting for transfers between devices  157 us (44%)
  starting transfers between devices  69.8 us (19%)
  Pallas kernels  66.4 us (19%)
  local copies, waits for them, and re-layouts  37 us (10%)
  other arithmetic  22.4 us (6%)
    ppermute x68, waiting for transfers between devices, swap(): return lax.ppermute(value, axis, pairs)  157 us
    ppermute x68, starting transfers between devices, swap(): return lax.ppermute(value, axis, pairs)  69.8 us
    unnamed x222, local copies, waits for them, and re-layouts  27.5 us
    pallas_call x8, Pallas kernels, ordered_call(): pl.pallas_call(kernel, in_specs=[pl.BlockSpec(memory_space=pltpu.SMEM)] +...  13.9 us
    pallas_call x1, Pallas kernels, attend_own(): pl.pallas_call(attend_own_kernel, grid=(rows // tile,), in_specs=[pl.Bloc...  10.2 us
    pallas_call x1, Pallas kernels, attend_other(): pl.pallas_call(attend_other_kernel, grid=(rows // tile,), in_specs=[pl.Bl...  7.95 us
    select_n x12, other arithmetic, finish(): jnp.where(has_bit(self.axis, mask), jnp.concatenate([other, self.whole],...  7.82 us
    pallas_call x1, Pallas kernels, attend_forward(): pl.pallas_call(attend_forward_kernel, grid=(rows // tile,), in_specs=[pl....  7.79 us
  transfers between devices with their start and end apart: 68, of which 36 were waited for; matrix products, arithmetic and copies ran while one was open for 8% of the time, Pallas kernels for 12%

commit v1 on v0

--- a/solution.py
+++ b/solution.py
@@ -39,12 +39,16 @@
     return jax.ShapeDtypeStruct(shape, dtype)
 
 
+def whole_block(shape):
+    return pl.BlockSpec(shape, lambda i: (0,) * len(shape))
+
+
 def whole_call(kernel, outs, name, *args):
-    vmem = pl.BlockSpec(memory_space=pltpu.VMEM)
     return pl.pallas_call(
         kernel,
-        in_specs=[vmem] * len(args),
-        out_specs=[vmem] * len(outs),
+        grid=(1,),
+        in_specs=[whole_block(each.shape) for each in args],
+        out_specs=[whole_block(each.shape) for each in outs],
         out_shape=outs,
         compiler_params=room(12),
         cost_estimate=brief,
@@ -147,12 +151,10 @@
         if self.masks:
             self.masks.pop(0)
             other, main = tie(self.other, main)
-            total = self.keep.astype(full_type) + other.astype(full_type)
-            half = total.shape[0] // 2
             if self.masks:
-                self.keep, self.send = total[:half], total[half:].astype(low_type)
+                self.keep, self.send = halve(self.keep, other)
             else:
-                self.keep = total
+                self.other = other
         return main
 
     def step(self, main):
@@ -165,7 +167,33 @@
         return main
 
     def value(self):
-        return self.keep[0]
+        return self.keep[0].astype(full_type) + self.other[0].astype(full_type)
+
+
+def halve_kernel(keep_low, keep_high, other_low, other_high, low_ref, high_ref):
+    for keep, other, out in (
+        (keep_low, other_low, low_ref),
+        (keep_high, other_high, high_ref),
+    ):
+        total = keep[...].astype(full_type) + other[...].astype(full_type)
+        out[...] = total.astype(low_type)
+
+
+def halve(keep, other):
+    half = keep.shape[0] // 2
+    block = (1,) + keep.shape[1:]
+    low = pl.BlockSpec(block, lambda i: (i, 0, 0))
+    high = pl.BlockSpec(block, lambda i: (half + i, 0, 0))
+    return pl.pallas_call(
+        halve_kernel,
+        grid=(half,),
+        in_specs=[low, high, low, high],
+        out_specs=[low, low],
+        out_shape=[shape_of((half,) + keep.shape[1:])] * 2,
+        compiler_params=room(8),
+        cost_estimate=brief,
+        name="halve",
+    )(keep, keep, other, other)
 
 
 def rows_gather(block):
@@ -263,126 +291,89 @@
         yield head, q_head, g_head, probs.astype(low_type), dscore
 
 
-def attend_own_kernel(
-    q_ref, k_ref, v_ref, do_ref, o_ref, segq_ref, segk_ref, lse_ref, dq_ref, dk_ref, dv_ref
-):
-    tile, width = q_ref.shape
-    own = dk_ref.shape[0]
-
-    @pl.when(pl.program_id(0) == 0)
-    def _():
-        dk_ref[...] = jnp.zeros_like(dk_ref)
-        dv_ref[...] = jnp.zeros_like(dv_ref)
-
-    dquery = jnp.zeros((tile, width), full_type)
-    for head, q_head, g_head, probs, dscore in attend_terms(
-        q_ref, k_ref, v_ref, do_ref, o_ref, segq_ref, segk_ref, lse_ref
-    ):
-        dquery = jnp.where(head_mask(width, head), low_dot(dscore, k_ref[...]), dquery)
-        dk_ref[...] += low_dot(dscore[:, :own], q_head, contract_rows)
-        dv_ref[...] += low_dot(probs[:, :own], g_head, contract_rows)
-    dq_ref[...] = (dquery * 0.125).astype(low_type)
-
-
-def attend_own(query_key, value_rows, grads, attended, seg_rows, seg_keys, lse):
-    rows, width = grads.shape
-    keys = value_rows.shape[0]
+def attend_back(rows_of_q, part, keys, masks, sums, wants_dq, dq_parts=()):
+    query_key, first_row, grads, attended, lse, seg_rows = rows_of_q
+    value_rows, seg_keys, own = masks
+    width = value_rows.shape[1]
     tile = LANES
+    parts_of = 1 if part is None else 2
+    steps = grads.shape[0] // tile // parts_of
+    shift = steps if part == 1 else 0
+    first = first_row // tile + shift
+    closing = len(dq_parts) > 0
+
+    def kernel(*refs):
+        base, refs = refs[:8], refs[8:]
+        q_ref, k_ref = base[:2]
+        before, refs = (refs[:2], refs[2:]) if sums else (None, refs)
+        parts, refs = refs[: len(dq_parts)], refs[len(dq_parts) :]
+        if closing:
+            dqk_out, dv_out, dk_sum, dv_sum = refs
+        else:
+            dk_sum, dv_sum = refs[:2]
+        step = pl.program_id(0)
+
+        @pl.when(step == 0)
+        def _():
+            dk_sum[...] = before[0][...] if sums else jnp.zeros_like(dk_sum)
+            dv_sum[...] = before[1][...] if sums else jnp.zeros_like(dv_sum)
+
+        dquery = jnp.zeros((tile, width), full_type)
+        for head, q_head, g_head, probs, dscore in attend_terms(*base):
+            if wants_dq:
+                dquery = jnp.where(head_mask(width, head), low_dot(dscore, k_ref[...]), dquery)
+            dk_sum[...] += low_dot(dscore[:, :own], q_head, contract_rows)
+            dv_sum[...] += low_dot(probs[:, :own], g_head, contract_rows)
+        if wants_dq:
+            refs[2][...] = (dquery * 0.125).astype(low_type)
+        if closing:
+
+            @pl.when(step == steps - 1)
+            def _():
+                rows = own // len(parts)
+                for at, ref in enumerate(parts):
+                    dqk_out[at * rows : (at + 1) * rows, :width] = ref[...]
+                dqk_out[:, width:] = dk_sum[...].astype(low_type)
+                dv_out[...] = dv_sum[...].astype(low_type)
+
+    tile_rows = pl.BlockSpec((tile, width), lambda i: (shift + i, 0))
+    held = whole_block((own, width))
+    in_specs = [
+        pl.BlockSpec((tile, width), lambda i: (first + i, 0)),
+        pl.BlockSpec((keys, width), lambda i: (0, 1)),
+        pl.BlockSpec((keys, width), lambda i: (0, 0)),
+        tile_rows,
+        tile_rows,
+        pl.BlockSpec((tile, 1), lambda i: (shift + i, 0)),
+        pl.BlockSpec((1, keys), lambda i: (0, 0)),
+        pl.BlockSpec((8, tile), lambda i: (0, shift + i)),
+    ]
+    args = [query_key, query_key, value_rows, grads, attended, seg_rows, seg_keys, lse]
+    if sums:
+        in_specs, args = in_specs + [held, held], args + list(sums)
+    in_specs = in_specs + [whole_block(each.shape) for each in dq_parts]
+    args = args + list(dq_parts)
+    if closing:
+        outs = [shape_of((own, 2 * width)), shape_of((own, width))]
+        out_specs = [whole_block(each.shape) for each in outs]
+        scratch = [pltpu.VMEM((own, width), full_type)] * 2
+    else:
+        outs = [shape_of((own, width), full_type)] * 2
+        out_specs, scratch = [held, held], []
+        if wants_dq:
+            outs = outs + [shape_of((steps * tile, width))]
+            out_specs = out_specs + [pl.BlockSpec((tile, width), lambda i: (i, 0))]
     return pl.pallas_call(
-        attend_own_kernel,
-        grid=(rows // tile,),
-        in_specs=[
-            pl.BlockSpec((tile, width), lambda i: (i, 0)),
-            pl.BlockSpec((keys, width), lambda i: (0, 1)),
-            pl.BlockSpec((keys, width), lambda i: (0, 0)),
-            pl.BlockSpec((tile, width), lambda i: (i, 0)),
-            pl.BlockSpec((tile, width), lambda i: (i, 0)),
-            pl.BlockSpec((tile, 1), lambda i: (i, 0)),
-            pl.BlockSpec((1, keys), lambda i: (0, 0)),
-            pl.BlockSpec((8, tile), lambda i: (0, i)),
-        ],
-        out_specs=[
-            pl.BlockSpec((tile, width), lambda i: (i, 0)),
-            pl.BlockSpec((rows, width), lambda i: (0, 0)),
-            pl.BlockSpec((rows, width), lambda i: (0, 0)),
-        ],
-        out_shape=[
-            shape_of((rows, width)),
-            shape_of((rows, width), full_type),
-            shape_of((rows, width), full_type),
-        ],
+        kernel,
+        grid=(steps,),
+        in_specs=in_specs,
+        out_specs=out_specs,
+        out_shape=outs,
+        scratch_shapes=scratch,
         compiler_params=room_for_keys(keys),
         cost_estimate=brief,
-        name="attend_own",
-    )(query_key, query_key, value_rows, grads, attended, seg_rows, seg_keys, lse)
-
-
-def attend_other_kernel(
-    q_ref,
-    k_ref,
-    v_ref,
-    do_ref,
-    o_ref,
-    segq_ref,
-    segk_ref,
-    lse_ref,
-    dq_ref,
-    dk_ref,
-    dv_ref,
-    dqk_out,
-    dv_out,
-    dk_sum,
-    dv_sum,
-):
-    width = q_ref.shape[1]
-
-    @pl.when(pl.program_id(0) == 0)
-    def _():
-        dk_sum[...] = dk_ref[...]
-        dv_sum[...] = dv_ref[...]
-
-    for _, q_head, g_head, probs, dscore in attend_terms(
-        q_ref, k_ref, v_ref, do_ref, o_ref, segq_ref, segk_ref, lse_ref
-    ):
-        dk_sum[...] += low_dot(dscore, q_head, contract_rows)
-        dv_sum[...] += low_dot(probs, g_head, contract_rows)
-
-    @pl.when(pl.program_id(0) == pl.num_programs(0) - 1)
-    def _():
-        dqk_out[:, :width] = dq_ref[...]
-        dqk_out[:, width:] = dk_sum[...].astype(low_type)
-        dv_out[...] = dv_sum[...].astype(low_type)
-
-
-def attend_other(query_key, value_rows, grads, attended, seg_rows, seg_keys, lse, dq, dk, dv):
-    rows, width = grads.shape
-    own = dq.shape[0]
-    tile = LANES
-    first = own // tile
-    held = pl.BlockSpec((own, width), lambda i: (0, 0))
-    return pl.pallas_call(
-        attend_other_kernel,
-        grid=(rows // tile,),
-        in_specs=[
-            pl.BlockSpec((tile, width), lambda i: (i + first, 0)),
-            pl.BlockSpec((own, width), lambda i: (0, 1)),
-            held,
-            pl.BlockSpec((tile, width), lambda i: (i, 0)),
-            pl.BlockSpec((tile, width), lambda i: (i, 0)),
-            pl.BlockSpec((tile, 1), lambda i: (i, 0)),
-            pl.BlockSpec((1, own), lambda i: (0, 0)),
-            pl.BlockSpec((8, tile), lambda i: (0, i)),
-            held,
-            held,
-            held,
-        ],
-        out_specs=[pl.BlockSpec((own, 2 * width), lambda i: (0, 0)), held],
-        out_shape=[shape_of((own, 2 * width)), shape_of((own, width))],
-        scratch_shapes=[pltpu.VMEM((own, width), full_type)] * 2,
-        compiler_params=room_for_keys(own),
-        cost_estimate=brief,
-        name="attend_other",
-    )(query_key, query_key, value_rows, grads, attended, seg_rows, seg_keys, lse, dq, dk, dv)
+        name="attend_back",
+    )(*args)
 
 
 def lanes_of(ref):
@@ -547,13 +538,43 @@
     )(*e_blocks, queries, live_bias)
 
 
-def late_backward_kernel(sharp_ref, soft_ref, weight_ref, q_ref, keep_ref, send_ref, total):
+def join_soft(soft, far, same):
+    top = soft
+    for at in range(far.shape[0]):
+        top = jnp.maximum(top, far[at])
+    total = jnp.exp(soft - top)
+    for at in range(far.shape[0]):
+        total = total + jnp.exp(far[at] - top)
+    blocks = soft.shape[0]
+    most = jnp.full(soft.shape, neg_big, full_type)
+    for at in range(blocks):
+        shared = same[:, at : at + 1] > 0.0
+        most = jnp.maximum(most, jnp.where(shared, top[at : at + 1], neg_big))
+    sums = jnp.zeros(soft.shape, full_type)
+    for at in range(blocks):
+        shared = same[:, at : at + 1] > 0.0
+        term = jnp.where(shared, top[at : at + 1], neg_big)
+        sums = sums + jnp.exp(term - most) * total[at : at + 1]
+    return most + jnp.log(sums)
+
+
+def late_backward_kernel(
+    sharp_ref, soft_ref, far_ref, same_ref, place_ref, weight_ref, q_ref, *refs
+):
+    keep_ref, send_ref, score_ref, total = refs
     step = pl.program_id(0)
     blocks = soft_ref.shape[0]
     rows, tile = sharp_ref.shape
+    soft = join_soft(soft_ref[...], far_ref[...], same_ref[...])
     cube = sharp_ref[...].reshape(blocks, rows // blocks, tile)
-    pulled = weight_ref[...][:, None, :] * jnp.exp(cube - soft_ref[...][:, None, :])
+    pulled = weight_ref[...][:, None, :] * jnp.exp(cube - soft[:, None, :])
     term = low_dot(pulled.reshape(rows, tile).astype(low_type), q_ref[...])
+    query = lax.broadcasted_iota(jnp.int32, (tile, score_ref.shape[0]), 0) // QLEN
+    count = lax.broadcasted_iota(jnp.int32, (tile, score_ref.shape[0]), 1)
+    pool = jnp.where(query == count, 0.5 / QLEN, 0.0)
+    exact = lax.Precision.HIGHEST
+    means = lax.dot_general(pool, soft, (((0,), (1,)), ((), ())), precision=exact)
+    score_ref[...] = lax.dot_general(means, place_ref[...], contract_inner, precision=exact)
 
     @pl.when(step == 0)
     def _():
@@ -568,28 +589,31 @@
         store_halves(total[...], keep_ref, send_ref)
 
 
-def late_backward(sharp, soft, weight, queries):
+def late_backward(sharp, soft, far, same, place, weight, queries):
     rows, count = sharp.shape
     width = queries.shape[1]
     blocks = soft.shape[0]
     tile = 512
-    held = pl.BlockSpec((rows // 2, width), lambda i: (0, 0))
+    held = whole_block((rows // 2, width))
     return pl.pallas_call(
         late_backward_kernel,
         grid=(count // tile,),
         in_specs=[
             pl.BlockSpec((rows, tile), lambda i: (0, i)),
             pl.BlockSpec((blocks, tile), lambda i: (0, i)),
+            pl.BlockSpec((far.shape[0], blocks, tile), lambda i: (0, 0, i)),
+            whole_block(same.shape),
+            whole_block(place.shape),
             pl.BlockSpec((blocks, tile), lambda i: (0, i)),
             pl.BlockSpec((tile, width), lambda i: (i, 0)),
         ],
-        out_specs=[held, held],
-        out_shape=halves_of(rows, width),
+        out_specs=[held, held, pl.BlockSpec((tile // QLEN, NPASS), lambda i: (i, 0))],
+        out_shape=halves_of(rows, width) + [shape_of((count // QLEN, NPASS), full_type)],
         scratch_shapes=[pltpu.VMEM((rows, width), full_type)],
         compiler_params=room(16),
         cost_estimate=brief,
         name="late_backward",
-    )(sharp, soft, weight, queries)
+    )(sharp, soft, far, same, place, weight, queries)
 
 
 def norm_stats(values):
@@ -724,15 +748,16 @@
     return lax.axis_index("dp") ^ jnp.asarray(offsets_of(masks[::-1]), jnp.int32)
 
 
-def ordered_call(kernel, outs, scratch, name, order, *args):
-    vmem = pl.BlockSpec(memory_space=pltpu.VMEM)
+def ordered_call(kernel, outs, scratch, name, order, *args, grant=20):
     return pl.pallas_call(
         kernel,
-        in_specs=[pl.BlockSpec(memory_space=pltpu.SMEM)] + [vmem] * len(args),
-        out_specs=[vmem] * len(outs),
+        grid=(1,),
+        in_specs=[pl.BlockSpec(memory_space=pltpu.SMEM)]
+        + [whole_block(each.shape) for each in args],
+        out_specs=[whole_block(each.shape) for each in outs],
         out_shape=outs,
         scratch_shapes=[pltpu.VMEM(*each) for each in scratch],
-        compiler_params=room(12),
+        compiler_params=room(grant),
         cost_estimate=brief,
         name=name,
     )(order, *args)
@@ -885,6 +910,44 @@
         ref[cols:, :] = lanes_in(total_o, block)
 
     deal(order_ref, keep_ref, send_ref, write)
+
+
+def finish_pair_kernel(keep_ref, other_ref, left_ref, right_ref):
+    total = keep_ref[...].astype(full_type) + other_ref[...].astype(full_type)
+    cols = left_ref.shape[1]
+    left_ref[...] = total[:, :cols]
+    right_ref[...] = total[:, cols:]
+
+
+def finish_pair(scatter, cols):
+    rows, both = scatter.keep.shape[1:]
+    outs = [shape_of((rows, cols), full_type), shape_of((rows, both - cols), full_type)]
+    return whole_call(finish_pair_kernel, outs, "finish_pair", scatter.keep[0], scatter.other[0])
+
+
+def finish_vo_kernel(keep_ref, other_ref, value_ref, out_ref, *norm_refs):
+    total = keep_ref[...].astype(full_type) + other_ref[...].astype(full_type)
+    rows, cols = value_ref.shape
+    row = 0
+    for at in range(0, cols, LANES):
+        value_ref[:, at : at + LANES] = total[row : row + rows]
+        row += rows
+    out_ref[...] = total[row : row + out_ref.shape[0]]
+    row += out_ref.shape[0]
+    for at, ref in enumerate(norm_refs):
+        ref[...] = total[row + at : row + at + 1] + total[row + 4 + at : row + 5 + at]
+
+
+def finish_vo(keep, other, value_shape, out_shape):
+    rows, cols = out_shape
+    if cols == LANES:
+        outs = [shape_of(value_shape, full_type), shape_of(out_shape, full_type)]
+        outs = outs + [shape_of((1, cols), full_type)] * 4
+        value, out, *norms = whole_call(finish_vo_kernel, outs, "finish_vo", keep, other)
+        return value, out, norms
+    total = keep.astype(full_type) + other.astype(full_type)
+    value, out = unpack_vo(total, *value_shape, (rows + SPARE, cols))
+    return value, out[:rows], out[rows : rows + 4] + out[rows + 4 : rows + 8]
 
 
 def pack_vo(value, out):
@@ -963,40 +1026,33 @@
     out_ref[...] = add_up(terms).astype(low_type)
 
 
-def pack_kernel(
-    order_ref,
-    hidden_ref,
-    q_ref,
-    k_ref,
-    v_ref,
-    o_ref,
-    norm_ref,
-    up_ref,
-    col_ref,
-    a_out,
-    u_out,
-    b_out,
-    own_out,
-):
-    heads = q_ref.shape[1]
+def pack_kernel(order_ref, *refs):
+    hidden_ref, q_ref, k_ref, v_ref, o_ref, up_ref, col_ref, *norm_refs = refs[:11]
+    a_out, u_out, b_out, own_out, block_out = refs[11:]
+    heads, units = q_ref.shape[1], up_ref.shape[1]
     a_out[:, :heads] = q_ref[...]
     a_out[:, heads:] = k_ref[...]
-    units = up_ref.shape[1]
     u_out[:, :units] = up_ref[...]
     u_out[:, units:] = col_ref[...]
-    for at in range(heads // LANES):
-        b_out[at * LANES : (at + 1) * LANES, :] = v_ref[:, at * LANES : (at + 1) * LANES]
-    rest = v_ref.shape[0] * heads // LANES
-    b_out[rest : rest + o_ref.shape[0], :] = o_ref[...]
-    b_out[rest + o_ref.shape[0] :, :] = norm_ref[...]
+    row = 0
+    for at in range(0, heads, LANES):
+        b_out[row : row + v_ref.shape[0], :] = v_ref[:, at : at + LANES]
+        row += v_ref.shape[0]
+    b_out[row : row + o_ref.shape[0], :] = o_ref[...]
+    row += o_ref.shape[0]
+    norms = [ref[...].astype(full_type).reshape(1, -1) for ref in norm_refs]
+    norms = jnp.concatenate(norms + [jnp.zeros((SPARE - 4, LANES), full_type)], axis=0)
+    b_out[row : row + SPARE, :] = norms.astype(low_type)
     parts = order_ref.shape[0]
     rows = hidden_ref.shape[0] // parts
     for at in range(parts):
         own_out[at * rows : (at + 1) * rows, :] = rows_in(hidden_ref, order_ref[at], rows)
-
-
-def pack_inputs(order, hidden, w_query, w_key, w_value, w_out, norms, w_up, w_colbert):
+    block_out[...] = own_out[0:rows, :]
+
+
+def pack_inputs(order, hidden, w_query, w_key, w_value, w_out, w_up, w_colbert, *norms):
     rows, heads = w_query.shape
+    span = hidden.shape[0] // order.shape[0]
     if w_out.shape[1] == LANES and rows == LANES:
         packed = (rows * heads // LANES + w_out.shape[0] + SPARE, LANES)
         outs = [
@@ -1004,20 +1060,21 @@
             shape_of((rows, w_up.shape[1] + w_colbert.shape[1])),
             shape_of(packed),
             shape_of(hidden.shape),
+            shape_of((span, hidden.shape[1])),
         ]
-        args = (hidden, w_query, w_key, w_value, w_out, norms, w_up, w_colbert)
-        return ordered_call(pack_kernel, outs, [], "pack", order, *args)
-    span = hidden.shape[0] // order.shape[0]
+        args = (hidden, w_query, w_key, w_value, w_out, w_up, w_colbert) + norms
+        return ordered_call(pack_kernel, outs, [], "pack", order, *args, grant=60)
+    norms = jnp.concatenate([jnp.stack(norms), jnp.zeros((SPARE - 4, w_out.shape[1]), low_type)], 0)
+    blocks = [
+        lax.dynamic_slice_in_dim(hidden, order[at] * span, span, 0)
+        for at in range(order.shape[0])
+    ]
     return (
         jnp.concatenate([w_query, w_key], axis=1),
         jnp.concatenate([w_up, w_colbert], axis=1),
         pack_vo(w_value, jnp.concatenate([w_out, norms], axis=0)),
-        jnp.concatenate(
-            [
-                lax.dynamic_slice_in_dim(hidden, order[at] * span, span, 0)
-                for at in range(order.shape[0])
-            ]
-        ),
+        jnp.concatenate(blocks),
+        blocks[0],
     )
 
 
@@ -1068,13 +1125,11 @@
     across = dp_up[-1:] + dp_up[:-1]
     turned_back, across_back = turned[::-1], across[::-1]
     col_order = column ^ jnp.asarray(row_order, jnp.int32)
-    norms = jnp.stack([norm1_gain, norm1_shift, norm2_gain, norm2_shift])
-    norms = jnp.concatenate([norms, jnp.zeros((SPARE - 4, w_out.shape[1]), low_type)], 0)
+    norms = (norm1_gain, norm1_shift, norm2_gain, norm2_shift)
     out_shape = (w_out.shape[0] + SPARE, w_out.shape[1])
-    packed_a, packed_u, packed_b, hidden_own = pack_inputs(
-        col_order, hidden_in, w_query, w_key, w_value, w_out, norms, w_up, w_colbert
-    )
-    own_hidden = hidden_own[:own_rows]
+    packed_a, packed_u, packed_b, hidden_own, own_hidden = pack_inputs(
+        col_order, hidden_in, w_query, w_key, w_value, w_out, w_up, w_colbert, *norms
+    )
     pack_a = Gather(packed_a, "dp", dp_down)
     pack_u = Gather(packed_u, "dp", dp_down)
     pack_b = Gather(packed_b, "dp", turned)
@@ -1100,6 +1155,9 @@
     place = (seg_block[:, None] == passages[None, :]).astype(full_type)
     grad_block = jnp.sum(place[:, None, :] * score_grad[None], axis=2)
     weight = jnp.repeat(grad_block / QLEN, QLEN, axis=1)
+    same = same.astype(full_type)
+    place = place / jnp.sum(same, axis=1, keepdims=True)
+    slot_own = slot_own[None, :]
     early = (seg_column, seg_far, slot_own, slot_row, live_bias, weight, same, place)
     early, main = tie(early, main)
     seg_column, seg_far, slot_own, slot_row, live_bias, weight, same, place = early
@@ -1107,9 +1165,9 @@
     others, main = tie(others, main)
     far_others = swap(others, "mp", 2)
     main = pack_u.step(main)
-    main = pack_b.step(main)
+    main = pack_b.finish(main)
     main = pack_a.step(main)
-    main = pack_d.start(main)
+    main = pack_b.start(main)
     far_others, main = tie(far_others, main)
     others = [others, far_others]
     others = others + [swap(each, "mp", 1) for each in others]
@@ -1117,8 +1175,9 @@
     hidden_own, own_hidden = main
     hidden_all = jnp.concatenate([hidden_own, others], 0)
     main = (hidden_own, own_hidden, hidden_all)
+    main = pack_u.step(main)
     main = pack_b.step(main)
-    main = pack_u.step(main)
+    main = pack_d.start(main)
     main = pack_a.drain(main)
     full_a = pack_a.value().reshape(width, -1)
     full_a, main = tie(full_a, main)
@@ -1126,7 +1185,6 @@
 
     query_key = low_dot(hidden_all, full_a).astype(low_type)
     main = (query_key, hidden_all)
-    main = pack_d.step(main)
     main = pack_b.drain(main)
     full_b, full_out = unpack_vo(pack_b.value(), w_value.shape[0], head_width, out_shape)
     full_b = full_b.reshape(width, head_width)
@@ -1134,13 +1192,15 @@
     (full_b, full_out), main = tie((full_b, full_out), main)
     query_key, hidden_all = main
     value_rows = low_dot(hidden_all, full_b).astype(low_type)
+    value_rows = pack_d.step(value_rows)
     norm_rows = jnp.swapaxes(full_out[:, head_width : head_width + 4], 0, 1).reshape(4, width)
     norm_rows = norm_rows.astype(full_type)
     attended, lse = attend_forward(query_key, value_rows, seg_column, slot_row)
     norm_rows, attended = tie(norm_rows, attended)
-    attended = pack_d.step(attended)
-    terms = rows_scatter(*whole_call(mix_kernel, halves_of(tok_rows, width), "mix", attended, full_out))
-    terms = pack_u.drain(terms)
+    attended = pack_u.drain(attended)
+    keep, send = whole_call(mix_kernel, halves_of(tok_rows, width), "mix", attended, full_out)
+    keep, send = pack_d.step((keep, send))
+    terms = rows_scatter(keep, send)
     square = shape_of((own_rows, width), full_type)
     low_square = shape_of((own_rows, width))
     narrow = shape_of((own_rows, 1), full_type)
@@ -1164,8 +1224,11 @@
     full_down = to_lanes(pack_d.value())
     full_down, (active, slope) = tie(full_down, main)
     keep, send = feed_down(active, full_down)
-    far_col, (keep, send) = tie(far_col, (keep, send))
+    (far, far_lse), send = tie((attended, lse), send)
+    far = group_gather(far[None])[1:]
+    far_lse = group_gather(far_lse[None])[1:]
     terms = rows_scatter(keep, send)
+    (far, far_lse), terms = tie((far, far_lse), terms)
     col_blocks = [col_own, far_col]
     col_blocks = col_blocks + [swap(each, "mp", 1) for each in col_blocks]
     normed_two_low, unit_two, scale_two, embedded, embed_low, inv_length = ordered_call(
@@ -1181,26 +1244,24 @@
     )
 
     e_blocks = rows_gather(embed_low)
+    two_low, e_blocks = tie(normed_two_low, e_blocks)
+    far_two = swap(two_low, "mp", 2)
     sharp, soft_block = late_forward(e_blocks, queries, live_bias, blocks)
-    two_blocks, soft_block = tie(normed_two_low, soft_block)
-    soft_group = group_gather(soft_block[None])
-    terms = jnp.where(same[:, None, :, None], soft_group[None], neg_big)
-    top = jnp.max(terms, axis=(1, 2))
-    soft = top + jnp.log(jnp.sum(jnp.exp(terms - top[:, None, None]), axis=(1, 2)))
-    two_blocks = rows_gather(two_blocks)
-    far = group_gather(jnp.stack([attended]))[1:]
-    far_lse = group_gather(lse[None])[1:]
-    keep, send = late_backward(sharp, soft, weight, queries)
-    (far, far_lse, two_blocks), (keep, send) = tie((far, far_lse, two_blocks), (keep, send))
+    soft_far = group_gather(soft_block[None])[1:]
+    keep, send, scores = late_backward(
+        sharp, soft_block, soft_far, same, place, weight, queries
+    )
+    far_two, (keep, send) = tie(far_two, (keep, send))
     far_attended = far.reshape(-1, head_width)
     far_lse = jnp.swapaxes(far_lse, 0, 1).reshape(8, -1)
 
-    query_means = jnp.mean(soft.reshape(blocks, -1, QLEN), axis=2) * 0.5
-    shared = jnp.sum(same.astype(full_type), axis=1)
-    scores = jnp.sum(query_means[:, :, None] * (place / shared[:, None])[:, None, :], axis=0)
-    scores, keep = tie(scores, keep)
-
+    score_masks = dp_up[group_levels:]
+    scores, send = tie(scores, send)
+    scores_far = swap(scores, "dp", score_masks[0])
     terms = rows_scatter(keep, send)
+    scores_far, terms = tie(scores_far, terms)
+    scores, terms = tie(scores + scores_far, terms)
+    scores_far = swap(scores, "dp", score_masks[1])
     dproj_low, dresid_two, dresid_low, two_sums = ordered_call(
         norm_two_back_kernel,
         [low_square, square, low_square, shape_of((2, width), full_type)],
@@ -1215,29 +1276,34 @@
         inv_length,
         *col_blocks,
     )
-    dresid_blocks = rows_gather(dresid_low)
+    dresid_blocks = [dresid_low, swap(dresid_low, "mp", 2)]
+    scores_far, dresid_blocks = tie(scores_far, dresid_blocks)
+    dresid_blocks = dresid_blocks + [swap(each, "mp", 1) for each in dresid_blocks]
+    two_blocks = [normed_two_low, far_two]
+    two_blocks = two_blocks + [swap(each, "mp", 1) for each in two_blocks]
+    two_blocks, dresid_blocks = tie(two_blocks, dresid_blocks)
+    scores = scores + scores_far
+    for mask in score_masks[2:]:
+        scores = scores + swap(scores, "dp", mask)
 
     dproj_low, dresid_blocks = tie(dproj_low, dresid_blocks)
     du_far = swap(dproj_low, "mp", 2)
-    if group_size < dp_size:
-        masks = dp_up[group_levels:]
-        scores = scores + swap(scores, "dp", masks[0])
     dinner = feed_inner(dresid_blocks, full_down, slope)
-    (scores, keep_up), dinner = tie((scores, full_up), dinner)
-    for mask in masks[1:]:
-        scores = scores + swap(scores, "dp", mask)
-    keep, send = feed_back(dinner, keep_up)
+    du_far, dinner = tie(du_far, dinner)
+    keep, send = feed_back(dinner, full_up)
     got = swap(send, "mp", 1)
     du_blocks = [dproj_low, du_far]
     du_blocks = du_blocks + [swap(each, "mp", 1) for each in du_blocks]
     terms = [keep, got]
     low = rows_fold(*terms)
-    (scores, active, dinner), low = tie((scores, active, dinner), low)
+    (active, dinner), low = tie((active, dinner), low)
     far_low = swap(low, "mp", 2)
-    grad_d = Scatter(*grad_down(active, dresid_blocks, across_back), "dp", across_back)
+    grad_d = Scatter(*grad_down(active, dresid_blocks, dp_up), "dp", dp_up)
     dinner = grad_d.start(dinner)
     grad_u = Scatter(
-        *grad_up(dinner, rows_one, two_blocks, du_blocks, w_colbert.shape[1], dp_up), "dp", dp_up
+        *grad_up(dinner, rows_one, two_blocks, du_blocks, w_colbert.shape[1], across_back),
+        "dp",
+        across_back,
     )
     far_low = grad_u.start(far_low)
     dresid_one, mixed_pack = whole_call(
@@ -1262,66 +1328,64 @@
         full_out,
     )
     far_grads = group_gather(dattended[None])[1:].reshape(-1, head_width)
-    main = grad_d.step(dattended)
-    dquery, dkey, dvalue = attend_own(
-        query_key, value_rows, main, attended, seg_column, slot_row, lse
-    )
+    own_q = (query_key, 0, dattended, attended, lse, seg_column)
+    all_keys = (value_rows, slot_row, tok_rows)
+    keys = value_rows.shape[0]
+    *sums, dquery = attend_back(own_q, None, keys, all_keys, None, True)
+    dquery = grad_d.step(dquery)
     far_grads, dquery = tie(far_grads, dquery)
-    main = (far_grads, dquery)
-    main = grad_u.step(main)
-    main = grad_d.step(main)
-    far_grads, dquery = main
-    dqk, dvalue_low = attend_other(
-        query_key,
-        value_rows,
-        far_grads,
-        far_attended,
-        seg_far,
-        slot_own[None, :],
-        far_lse,
-        dquery,
-        dkey,
-        dvalue,
-    )
-    main = grad_d.finish((dqk, dvalue_low))
-    main = grad_u.step(main)
-    dqk, dvalue_low = main
+    far_q = (query_key, tok_rows, far_grads, far_attended, far_lse, seg_far)
+    own_keys = (value_rows, slot_own, tok_rows)
+    sums = attend_back(far_q, 0, tok_rows, own_keys, sums, False)
+    sums = grad_u.step(sums)
+    dqk, dvalue_low = attend_back(far_q, 1, tok_rows, own_keys, sums, False, (dquery,))
     grad_b = Scatter(
-        *grad_vo(hidden_own, dvalue_low, attended, packs, norm_sums, turned_back), "dp", turned_back
+        *grad_vo(hidden_own, dvalue_low, attended, packs, norm_sums, across_back),
+        "dp",
+        across_back,
     )
     dqk = grad_b.start(dqk)
     grad_a = Scatter(*grad_qk(hidden_own, dqk, dp_up), "dp", dp_up)
     dqk = grad_a.start(dqk)
     keep, send = unproject(dqk, dvalue_low, full_a, full_b)
-    terms = rows_scatter(keep, send)
-    terms = grad_a.step(terms)
-    terms = grad_b.step(terms)
+    got = swap(send, "mp", 1)
+    low = rows_fold(keep, got)
+    terms = [keep, got, swap(low, "mp", 2)]
+    terms = grad_d.step(terms)
     input_own = whole_call(close_kernel, [low_square], "close", dresid_one, *terms)[0]
-    input_own = grad_u.finish(input_own)
-    input_blocks = rows_gather(input_own)
-    input_blocks = grad_a.step(input_blocks)
+    far_own = swap(input_own, "mp", 2)
+    far_own = grad_u.step(grad_a.step(far_own))
+    far_own = grad_b.step(far_own)
+    input_blocks = [input_own, far_own]
+    input_blocks = input_blocks + [swap(each, "mp", 1) for each in input_blocks]
     input_grad = place_rows(col_order, input_blocks)
+    input_grad = grad_d.finish(grad_a.step(input_grad))
+    down_grad = grad_d.value()
     input_grad = grad_b.step(input_grad)
-    input_grad = grad_b.drain(grad_a.drain(input_grad))
-
-    grad_qk_rows = grad_a.value()
-    value_grad, out_rows = unpack_vo(grad_b.value(), w_value.shape[0], head_width, out_shape)
-    norm_grads = out_rows[head_width : head_width + 4] + out_rows[head_width + 4 : head_width + 8]
-    up_rows = grad_u.value()
+    input_grad = grad_u.finish(input_grad)
+    up_grad, colbert_grad = finish_pair(grad_u, units)
+    ends = (input_grad, down_grad, up_grad, colbert_grad)
+    ends = grad_a.finish(ends)
+    query_grad, key_grad = finish_pair(grad_a, head_width)
+    ends, (query_grad, key_grad) = grad_b.finish((ends, (query_grad, key_grad)))
+    input_grad, down_grad, up_grad, colbert_grad = ends
+    value_grad, out_grad, norm_grads = finish_vo(
+        grad_b.keep[0], grad_b.other[0], w_value.shape, w_out.shape
+    )
     return (
         scores,
         input_grad,
-        grad_qk_rows[:, :head_width],
-        grad_qk_rows[:, head_width:],
+        query_grad,
+        key_grad,
         value_grad,
-        out_rows[:head_width],
-        up_rows[:, :units],
-        grad_d.value(),
-        up_rows[:, units:],
-        norm_grads[0],
-        norm_grads[1],
-        norm_grads[2],
-        norm_grads[3],
+        out_grad,
+        up_grad,
+        down_grad,
+        colbert_grad,
+        norm_grads[0].reshape(-1),
+        norm_grads[1].reshape(-1),
+        norm_grads[2].reshape(-1),
+        norm_grads[3].reshape(-1),
     )
 
 

time: 358 us -> 332 us (0.927)
  local copies, waits for them, and re-layouts: 37 us -> 8.32 us
  Pallas kernels: 66.4 us -> 79.1 us
  starting transfers between devices: 69.8 us -> 62.9 us
  other arithmetic: 22.4 us -> 15.8 us
  waiting for transfers between devices: 157 us -> 161 us
    unnamed x222 -> x79, local copies, waits for them, and re-layouts: 27.5 us -> 5.13 us
    pallas_call x21 -> x33, Pallas kernels: 36.5 us -> 48.5 us  [the longest x3 19.3 us: attend_back(): pl.pallas_call(kernel, grid=(steps,), in_specs=in_specs, out_specs=out_sp...]
    ppermute x68, starting transfers between devices: 69.8 us -> 62.9 us  [swap(): return lax.ppermute(value, axis, pairs)]
    slice x13 -> x0, local copies, waits for them, and re-layouts: 4.92 us -> none  [the longest x8 2 us: finish(): self.keep, self.send = (total[:half], total[half:].astype(low_type))]
    ppermute x68, waiting for transfers between devices: 157 us -> 161 us  [swap(): return lax.ppermute(value, axis, pairs)]
  transfers between devices with their start and end apart: 68 -> 68, of which waited for: 36 -> 35; matrix products, arithmetic and copies ran while one was open for 8% -> 6% of each run, Pallas kernels for 12% -> 18%
where the time goes in v1:
time: 332 us; the launch traced here: 331 us
  waiting for transfers between devices  161 us (48%)
  Pallas kernels  79.1 us (24%)
  starting transfers between devices  62.9 us (19%)
  other arithmetic  15.8 us (5%)
  local copies, waits for them, and re-layouts  8.32 us (3%)
    ppermute x68, waiting for transfers between devices, swap(): return lax.ppermute(value, axis, pairs)  161 us
    ppermute x68, starting transfers between devices, swap(): return lax.ppermute(value, axis, pairs)  62.9 us
    pallas_call x3, Pallas kernels, attend_back(): pl.pallas_call(kernel, grid=(steps,), in_specs=in_specs, out_specs=out_sp...  19.3 us
    pallas_call x8, Pallas kernels, ordered_call(): pl.pallas_call(kernel, grid=(1,), in_specs=[pl.BlockSpec(memory_space=plt...  17.4 us
    select_n x12, other arithmetic, finish(): jnp.where(has_bit(self.axis, mask), jnp.concatenate([other, self.whole],...  9.78 us
    pallas_call x1, Pallas kernels, attend_forward(): pl.pallas_call(attend_forward_kernel, grid=(rows // tile,), in_specs=[pl....  7.79 us
    pallas_call x1, Pallas kernels, late_forward(): pl.pallas_call(late_forward_kernel, grid=(count // tile,), in_specs=[pl.B...  6.81 us
  transfers between devices with their start and end apart: 68, of which 35 were waited for; matrix products, arithmetic and copies ran while one was open for 6% of the time, Pallas kernels for 18%

profile of v1, /device:TPU:0, one launch (start us, length us, event | category | flops | bytes accessed | tf_op | source)
XLA Modules:
  0.0 331.0 jit_solution(10440219480825143701)
XLA Ops:
  1.8 2.7 pack.1
  4.5 4.0 %collective-permute-start = (bf16[1,1,1,128,512]{4,3,2,1,0:T(8,128)(2,1)}, bf16[1,1,1,128,512]{4,3,2,1,0:T(8,128)(2,1)S(1)}, u32[]{:S(2)}, u32[]{:S(2)}) collective-permute-start(bf16[1,1,1,128,512]{4,3,2,1,0:T(8,128)(2,1)} %bitcast.98), channel_id=1, source_target_pairs={{0,16},{4,20},{8,24},{12,28},{16,0},{20,4},{24,8},{28,12},{1,17},{... | collective-permute-start | bytes 393224 | tf_op jit(solution)/shard_map/ppermute | solution.py:61
  15.4 7.6 %collective-permute-done = bf16[1,1,1,128,512]{4,3,2,1,0:T(8,128)(2,1)S(1)} collective-permute-done((bf16[1,1,1,128,512]{4,3,2,1,0:T(8,128)(2,1)}, bf16[1,1,1,128,512]{4,3,2,1,0:T(8,128)(2,1)S(1)}, u32[]{:S(2)}, u32[]{:S(2)}) %collective-permute-start) | collective-permute-done | bytes 131104 | tf_op jit(solution)/shard_map/ppermute | solution.py:61
  24.1 1.8 collective-permute-start.8
  26.0 3.3 collective-permute-done.3
  31.4 3.5 %collective-permute-done.1 = bf16[2,1,1,128,512]{4,3,2,1,0:T(8,128)(2,1)S(1)} collective-permute-done((bf16[2,1,1,128,512]{4,3,2,1,0:T(8,128)(2,1)S(1)}, bf16[2,1,1,128,512]{4,3,2,1,0:T(8,128)(2,1)S(1)}, u32[]{:S(2)}, u32[]{:S(2)}) %collective-permute-start.1) | collective-permute-done | bytes 262176 | tf_op jit(solution)/shard_map/ppermute | solution.py:61
  38.5 16.1 %collective-permute-done.7 = bf16[2,1,1,128,1280]{4,3,2,1,0:T(8,128)(2,1)S(1)} collective-permute-done((bf16[2,1,1,128,1280]{4,3,2,1,0:T(8,128)(2,1)S(1)}, bf16[2,1,1,128,1280]{4,3,2,1,0:T(8,128)(2,1)S(1)}, u32[]{:S(2)}, u32[]{:S(2)}) %collective-permute-start.7) | collective-permute-done | bytes 655392 | tf_op jit(solution)/shard_map/ppermute | solution.py:61
  56.8 3.5 %collective-permute-start.11 = (bf16[1,1,1,1024,128]{4,3,2,1,0:T(8,128)(2,1)S(1)}, bf16[1,1,1,1024,128]{4,3,2,1,0:T(8,128)(2,1)S(1)}, u32[]{:S(2)}, u32[]{:S(2)}) collective-permute-start(bf16[1,1,1,1024,128]{4,3,2,1,0:T(8,128)(2,1)S(1)} %bitcast.90), channel_id=1, source_target_pairs={{0,16},{4,20},{8,24},{12,28},{16,0},{20,4},{24,8},{28,12},{1,17},{... | collective-permute-start | bytes 786440 | tf_op jit(solution)/shard_map/ppermute | solution.py:61
  63.1 12.7 %collective-permute-done.12 = bf16[2,1,2,528,128]{4,3,2,1,0:T(8,128)(2,1)S(1)} collective-permute-done((bf16[2,1,2,528,128]{4,3,2,1,0:T(8,128)(2,1)S(1)}, bf16[2,1,2,528,128]{4,3,2,1,0:T(8,128)(2,1)S(1)}, u32[]{:S(2)}, u32[]{:S(2)}) %collective-permute-start.12) | collective-permute-done | bytes 540704 | tf_op jit(solution)/shard_map/ppermute | solution.py:61
  80.9 7.8 %attend_forward.1 = (bf16[512,256]{1,0:T(8,128)(2,1)S(1)}, f32[8,512]{1,0:T(8,128)S(1)}) custom-call(bf16[1024,512]{1,0:T(8,128)(2,1)S(1)} %convolution_convert_fusion.q_ref.k_ref.refs_0_.refs_1_, bf16[1024,512]{1,0:T(8,128)(2,1)S(1)} %convolution_convert_fusion.q_ref.k_ref.refs_0_.refs_1_, bf16[1024,256]{1,0:T(8,128)(2,1)S(1)} %convolution_convert_fusion.1.v_ref.refs_2_, ...), custom_call_target="tpu_custom_call" | custom-call | flops 1 | bytes 1 | tf_op jit(solution)/shard_map/attend_forward/pallas_call | solution.py:254
  88.7 2.1 collective-permute-done.14
  96.6 6.8 %collective-permute-done.16.refs_3_ = bf16[128,1024]{1,0:T(8,128)(2,1)S(1)} collective-permute-done((bf16[128,1024]{1,0:T(8,128)(2,1)S(1)}, bf16[128,1024]{1,0:T(8,128)(2,1)S(1)}, u32[]{:S(2)}, u32[]{:S(2)}) %collective-permute-start.16) | collective-permute-done | bytes 262176 | tf_op jit(solution)/shard_map/ppermute | solution.py:61
  105.4 6.0 %collective-permute-done.18.refs_1_ = bf16[128,1024]{1,0:T(8,128)(2,1)S(1)} collective-permute-done((bf16[128,1024]{1,0:T(8,128)(2,1)S(1)}, bf16[128,1024]{1,0:T(8,128)(2,1)S(1)}, u32[]{:S(2)}, u32[]{:S(2)}) %collective-permute-start.18) | collective-permute-done | bytes 262176 | tf_op jit(solution)/shard_map/ppermute | solution.py:61
  111.3 3.0 maximum_select_fusion
  116.0 2.9 feed_up.1
  119.2 1.9 feed_down.1
  121.7 7.1 %collective-permute-done.25.refs_6_.refs_9_ = bf16[1024,256]{1,0:T(8,128)(2,1)S(1)} collective-permute-done((bf16[1024,256]{1,0:T(8,128)(2,1)S(1)}, bf16[1024,256]{1,0:T(8,128)(2,1)S(1)}, u32[]{:S(2)}, u32[]{:S(2)}) %collective-permute-start.25) | collective-permute-done | bytes 524320 | tf_op jit(solution)/shard_map/ppermute | solution.py:61
  132.5 5.4 %collective-permute-done.22 = f32[1,8,512]{2,1,0:T(8,128)S(1)} collective-permute-done((f32[1,8,512]{2,1,0:T(8,128)S(1)}, f32[1,8,512]{2,1,0:T(8,128)S(1)}, u32[]{:S(2)}, u32[]{:S(2)}) %collective-permute-start.22) | collective-permute-done | bytes 16416 | tf_op jit(solution)/shard_map/ppermute | solution.py:61
  141.9 6.1 %collective-permute-done.28.refs_1_ = bf16[128,1024]{1,0:T(8,128)(2,1)S(1)} collective-permute-done((bf16[128,1024]{1,0:T(8,128)(2,1)S(1)}, bf16[128,1024]{1,0:T(8,128)(2,1)S(1)}, u32[]{:S(2)}, u32[]{:S(2)}) %collective-permute-start.28) | collective-permute-done | bytes 262176 | tf_op jit(solution)/shard_map/ppermute | solution.py:61
  151.1 6.8 %late_forward.1 = (f32[512,2048]{1,0:T(8,128)S(1)}, f32[8,2048]{1,0:T(8,128)S(1)}) custom-call(bf16[128,1024]{1,0:T(8,128)(2,1)S(1)} %get-tuple-element.440.refs_0_, bf16[128,1024]{1,0:T(8,128)(2,1)S(1)} %collective-permute-done.28.refs_1_, bf16[128,1024]{1,0:T(8,128)(2,1)S(1)} %collective-permute-done.29.refs_2_, ...), custom_call_target="tpu_custom_call" | custom-call | flops 1 | bytes 1 | tf_op jit(solution)/shard_map/late_forward/pallas_call | solution.py:522
  159.5 2.7 collective-permute-done.31.far_ref
  162.2 5.2 %late_backward.1 = (f32[256,1024]{1,0:T(8,128)S(1)}, bf16[256,1024]{1,0:T(8,128)(2,1)S(1)}, f32[64,15]{1,0:T(8,128)S(1)}) custom-call(f32[512,2048]{1,0:T(8,128)S(1)} %get-tuple-element.445.sharp_ref, f32[8,2048]{1,0:T(8,128)S(1)} %get-tuple-element.446.soft_ref, f32[1,8,2048]{2,1,0:T(8,128)S(1)} %collective-permute-done.31.far_ref, ...), custom_call_target="tpu_custom_call" | custom-call | flops 1 | bytes 1 | tf_op jit(solution)/shard_map/late_backward/pallas_call | solution.py:598
  167.5 1.9 collective-permute-done.34.got_ref.refs_1_
  171.4 2.5 collective-permute-done.33
  173.9 3.9 %collective-permute-done.35.refs_2_ = bf16[128,1024]{1,0:T(8,128)(2,1)S(1)} collective-permute-done((bf16[128,1024]{1,0:T(8,128)(2,1)S(1)}, bf16[128,1024]{1,0:T(8,128)(2,1)S(1)}, u32[]{:S(2)}, u32[]{:S(2)}) %collective-permute-start.35) | collective-permute-done | bytes 262176 | tf_op jit(solution)/shard_map/ppermute | solution.py:61
  180.2 2.3 collective-permute-start.36
  183.0 2.0 collective-permute-done.36
  185.0 2.2 collective-permute-done.37.refs_1_
  189.6 3.6 %feed_inner.1.dz_ref.dinner_ref = bf16[512,1024]{1,0:T(8,128)(2,1)S(1)} custom-call(bf16[128,1024]{1,0:T(8,128)(2,1)S(1)} %get-tuple-element.483.refs_0_, bf16[128,1024]{1,0:T(8,128)(2,1)S(1)} %collective-permute-done.37.refs_1_, bf16[128,1024]{1,0:T(8,128)(2,1)S(1)} %collective-permute-done.40.refs_2_, ...), custom_call_target="tpu_custom_call" | custom-call | flops 1 | bytes 1 | tf_op jit(solution)/shard_map/feed_inner/pallas_call | solution.py:462
  193.2 4.2 %collective-permute-done.42.refs_9_ = bf16[128,1024]{1,0:T(8,128)(2,1)S(1)} collective-permute-done((bf16[128,1024]{1,0:T(8,128)(2,1)S(1)}, bf16[128,1024]{1,0:T(8,128)(2,1)S(1)}, u32[]{:S(2)}, u32[]{:S(2)}) %collective-permute-start.42) | collective-permute-done | bytes 262176 | tf_op jit(solution)/shard_map/ppermute | solution.py:61
  197.4 2.4 feed_back.1
  202.5 3.4 %grad_down.1 = (bf16[4,1024,128]{2,1,0:T(8,128)(2,1)S(1)}, bf16[4,1024,128]{2,1,0:T(8,128)(2,1)}) custom-call(s32[8]{0:T(128)S(1)} %broadcast_xor_fusion.order_ref, bf16[512,1024]{1,0:T(8,128)(2,1)S(1)} %get-tuple-element.491.g_ref.active_ref, bf16[128,1024]{1,0:T(8,128)(2,1)S(1)} %get-tuple-element.483.refs_0_, ...), custom_call_target="tpu_custom_call" | custom-call | flops 1 | bytes 1 | tf_op jit(solution)/shard_map/grad_down/pallas_call | solution.py:752
  206.8 3.4 %grad_up.1 = (bf16[4,128,1280]{2,1,0:T(8,128)(2,1)S(1)}, bf16[4,128,1280]{2,1,0:T(8,128)(2,1)}) custom-call(s32[9]{0:T(128)S(1)} %pad_add_fusion.4.order_ref, bf16[512,1024]{1,0:T(8,128)(2,1)S(1)} %feed_inner.1.dz_ref.dinner_ref, bf16[128,1024]{1,0:T(8,128)(2,1)S(1)} %get-tuple-element.417.refs_0_, bf16[128,1024]{1,0:T(8,128)(2,1)S(1)} %collective-permute-done.18.refs_1_, ...), custom_call_target="tpu_custom_call" | custom-call | flops 1 | bytes 1 | tf_op jit(solution)/shard_map/grad_up/pallas_call | solution.py:752
  215.2 6.7 %collective-permute-done.47.refs_1_ = bf16[144,1024]{1,0:T(8,128)(2,1)S(1)} collective-permute-done((bf16[144,1024]{1,0:T(8,128)(2,1)S(1)}, bf16[144,1024]{1,0:T(8,128)(2,1)S(1)}, u32[]{:S(2)}, u32[]{:S(2)}) %collective-permute-start.47) | collective-permute-done | bytes 294944 | tf_op jit(solution)/shard_map/ppermute | solution.py:61
  226.7 10.9 %attend_back.3 = (f32[512,256]{1,0:T(8,128)S(1)}, f32[512,256]{1,0:T(8,128)S(1)}, bf16[512,256]{1,0:T(8,128)(2,1)S(1)}) custom-call(bf16[1024,512]{1,0:T(8,128)(2,1)S(1)} %convolution_convert_fusion.q_ref.k_ref.refs_0_.refs_1_, bf16[1024,512]{1,0:T(8,128)(2,1)S(1)} %convolution_convert_fusion.q_ref.k_ref.refs_0_.refs_1_, ...), custom_call_target="tpu_custom_call" | custom-call | flops 1 | bytes 1 | tf_op jit(solution)/shard_map/attend_back/pallas_call | solution.py:366
  239.5 2.7 collective-permute-done.50
  242.1 4.0 %attend_back.4 = (f32[512,256]{1,0:T(8,128)S(1)}, f32[512,256]{1,0:T(8,128)S(1)}) custom-call(bf16[1024,512]{1,0:T(8,128)(2,1)S(1)} %convolution_convert_fusion.q_ref.k_ref.refs_0_.refs_1_, bf16[1024,512]{1,0:T(8,128)(2,1)S(1)} %convolution_convert_fusion.q_ref.k_ref.refs_0_.refs_1_, bf16[1024,256]{1,0:T(8,128)(2,1)S(1)} %convolution_convert_fusion.1.v_ref.refs_2_, ...), custom_call_target="tpu_custom_call" | custom-call | flops 1 | bytes 1 | tf_op jit(solution)/shard_map/attend_back/pallas_call | solution.py:366
  247.8 4.4 %attend_back.5 = (bf16[512,512]{1,0:T(8,128)(2,1)S(1)}, bf16[512,256]{1,0:T(8,128)(2,1)S(1)}) custom-call(bf16[1024,512]{1,0:T(8,128)(2,1)S(1)} %convolution_convert_fusion.q_ref.k_ref.refs_0_.refs_1_, bf16[1024,512]{1,0:T(8,128)(2,1)S(1)} %convolution_convert_fusion.q_ref.k_ref.refs_0_.refs_1_, ...), custom_call_target="tpu_custom_call" | custom-call | flops 1 | bytes 1 | tf_op jit(solution)/shard_map/attend_back/pallas_call | solution.py:366
  261.9 9.1 %collective-permute-done.56.other_low.other_high = bf16[2,1024,128]{2,1,0:T(8,128)(2,1)S(1)} collective-permute-done((bf16[2,1024,128]{2,1,0:T(8,128)(2,1)S(1)}, bf16[2,1024,128]{2,1,0:T(8,128)(2,1)S(1)}, u32[]{:S(2)}, u32[]{:S(2)}) %collective-permute-start.56) | collective-permute-done | bytes 524320 | tf_op jit(solution)/shard_map/ppermute | solution.py:61
  273.4 11.5 %collective-permute-done.55.other_low.other_high = bf16[4,128,512]{2,1,0:T(8,128)(2,1)S(1)} collective-permute-done((bf16[4,128,512]{2,1,0:T(8,128)(2,1)S(1)}, bf16[4,128,512]{2,1,0:T(8,128)(2,1)S(1)}, u32[]{:S(2)}, u32[]{:S(2)}) %collective-permute-start.55) | collective-permute-done | bytes 524320 | tf_op jit(solution)/shard_map/ppermute | solution.py:61
  289.6 2.7 collective-permute-start.61
  293.2 2.0 place_rows.1
  295.2 7.4 %collective-permute-done.62.other_low.other_high = bf16[2,128,512]{2,1,0:T(8,128)(2,1)S(1)} collective-permute-done((bf16[2,128,512]{2,1,0:T(8,128)(2,1)}, bf16[2,128,512]{2,1,0:T(8,128)(2,1)S(1)}, u32[]{:S(2)}, u32[]{:S(2)}) %collective-permute-start.62) | collective-permute-done | bytes 262176 | tf_op jit(solution)/shard_map/ppermute | solution.py:61
  302.7 10.0 %collective-permute-done.61 = bf16[1,1024,128]{2,1,0:T(8,128)(2,1)} collective-permute-done((bf16[1,1024,128]{2,1,0:T(8,128)(2,1)}, bf16[1,1024,128]{2,1,0:T(8,128)(2,1)}, u32[]{:S(2)}, u32[]{:S(2)}) %collective-permute-start.61) | collective-permute-done | bytes 262176 | tf_op jit(solution)/shard_map/ppermute | solution.py:61
  312.7 3.0 collective-permute-start.65
  315.7 1.8 add_bitcast_fusion
  317.5 7.8 %collective-permute-done.67 = bf16[1,128,1280]{2,1,0:T(8,128)(2,1)S(1)} collective-permute-done((bf16[1,128,1280]{2,1,0:T(8,128)(2,1)S(1)}, bf16[1,128,1280]{2,1,0:T(8,128)(2,1)S(1)}, u32[]{:S(2)}, u32[]{:S(2)}) %collective-permute-start.67) | collective-permute-done | bytes 327712 | tf_op jit(solution)/shard_map/ppermute | solution.py:61
  326.2 1.9 collective-permute-done.66
  (260 shorter events, 93.1 us)
Async XLA Ops:
  4.5 18.4 %collective-permute-start = (bf16[1,1,1,128,512]{4,3,2,1,0:T(8,128)(2,1)}, bf16[1,1,1,128,512]{4,3,2,1,0:T(8,128)(2,1)S(1)}, u32[]{:S(2)}, u32[]{:S(2)}) collective-permute-start(bf16[1,1,1,128,512]{4,3,2,1,0:T(8,128)(2,1)} %bitcast.98), channel_id=1, source_target_pairs={{0,16},{4,20},{8,24},{12,28},{16,0},{20,4},{24,8},{28,12},{1,17},{... | collective-permute-start | bytes 393224 | tf_op jit(solution)/shard_map/ppermute | solution.py:61
  8.6 15.5 %collective-permute-start.4 = (bf16[1,128,1024]{2,1,0:T(8,128)(2,1)}, bf16[1,128,1024]{2,1,0:T(8,128)(2,1)S(1)}, u32[]{:S(2)}, u32[]{:S(2)}) collective-permute-start(bf16[1,128,1024]{2,1,0:T(8,128)(2,1)} %bitcast.74), channel_id=1, source_target_pairs={{0,4},{4,0},{8,12},{12,8},{16,20},{20,16},{24,28},{28,24},{1,5},{5... | collective-permute-start | bytes 786440 | tf_op jit(solution)/shard_map/ppermute | solution.py:61
  10.1 19.1 %collective-permute-start.3 = (bf16[1,1,1,128,1280]{4,3,2,1,0:T(8,128)(2,1)}, bf16[1,1,1,128,1280]{4,3,2,1,0:T(8,128)(2,1)S(1)}, u32[]{:S(2)}, u32[]{:S(2)}) collective-permute-start(bf16[1,1,1,128,1280]{4,3,2,1,0:T(8,128)(2,1)} %bitcast.88), channel_id=1, source_target_pairs={{0,16},{4,20},{8,24},{12,28},{16,0},{20,4},{24,8},{28,12},{1,17},{... | collective-permute-start | bytes 983048 | tf_op jit(solution)/shard_map/ppermute | solution.py:61
  10.4 18.9 %collective-permute-start.2 = (bf16[1,1,1,528,128]{4,3,2,1,0:T(8,128)(2,1)}, bf16[1,1,1,528,128]{4,3,2,1,0:T(8,128)(2,1)}, u32[]{:S(2)}, u32[]{:S(2)}) collective-permute-start(bf16[1,1,1,528,128]{4,3,2,1,0:T(8,128)(2,1)} %bitcast.96), channel_id=1, source_target_pairs={{0,4},{4,0},{8,12},{12,8},{16,20},{20,16},{24,28},{28,24},{1,5},{5... | collective-permute-start | bytes 405512 | tf_op jit(solution)/shard_map/ppermute | solution.py:61
  24.0 10.9 %collective-permute-start.1 = (bf16[2,1,1,128,512]{4,3,2,1,0:T(8,128)(2,1)S(1)}, bf16[2,1,1,128,512]{4,3,2,1,0:T(8,128)(2,1)S(1)}, u32[]{:S(2)}, u32[]{:S(2)}) collective-permute-start(bf16[2,1,1,128,512]{4,3,2,1,0:T(8,128)(2,1)S(1)} %maximum_select_fusion.11), channel_id=1, source_target_pairs={{0,8},{4,12},{8,0},{12,4},{16,24},{20,28},{24,16},{28,20},{1,9},{5... | collective-permute-start | bytes 786440 | tf_op jit(solution)/shard_map/ppermute | solution.py:61
  24.1 10.8 %collective-permute-start.8 = (bf16[1,128,1024]{2,1,0:T(8,128)(2,1)S(1)}, bf16[1,128,1024]{2,1,0:T(8,128)(2,1)S(1)}, u32[]{:S(2)}, u32[]{:S(2)}) collective-permute-start(bf16[1,128,1024]{2,1,0:T(8,128)(2,1)S(1)} %collective-permute-done.4), channel_id=1, source_target_pairs={{0,2},{1,3},{2,0},{3,1},{4,6},{5,7},{6,4},{7,5},{8,10},{9,11},{10,... | collective-permute-start | bytes 786440 | tf_op jit(solution)/shard_map/ppermute | solution.py:61
  26.0 12.2 %collective-permute-start.9 = (bf16[1,128,1024]{2,1,0:T(8,128)(2,1)S(1)}, bf16[1,128,1024]{2,1,0:T(8,128)(2,1)S(1)}, u32[]{:S(2)}, u32[]{:S(2)}) collective-permute-start(bf16[1,128,1024]{2,1,0:T(8,128)(2,1)S(1)} %collective-permute-done.4), channel_id=1, source_target_pairs={{0,1},{1,0},{2,3},{3,2},{4,5},{5,4},{6,7},{7,6},{8,9},{9,8},{10,11... | collective-permute-start | bytes 786440 | tf_op jit(solution)/shard_map/ppermute | solution.py:61
  29.4 25.2 %collective-permute-start.7 = (bf16[2,1,1,128,1280]{4,3,2,1,0:T(8,128)(2,1)S(1)}, bf16[2,1,1,128,1280]{4,3,2,1,0:T(8,128)(2,1)S(1)}, u32[]{:S(2)}, u32[]{:S(2)}) collective-permute-start(bf16[2,1,1,128,1280]{4,3,2,1,0:T(8,128)(2,1)S(1)} %maximum_select_fusion.6), channel_id=1, source_target_pairs={{0,8},{4,12},{8,0},{12,4},{16,24},{20,28},{24,16},{28,20},{1,9},{5... | collective-permute-start | bytes 1966088 | tf_op jit(solution)/shard_map/ppermute | solution.py:61
  35.0 20.9 %collective-permute-start.6 = (bf16[1,1,2,528,128]{4,3,2,1,0:T(8,128)(2,1)S(1)}, bf16[1,1,2,528,128]{4,3,2,1,0:T(8,128)(2,1)S(1)}, u32[]{:S(2)}, u32[]{:S(2)}) collective-permute-start(bf16[1,1,2,528,128]{4,3,2,1,0:T(8,128)(2,1)S(1)} %maximum_select_fusion.10), channel_id=1, source_target_pairs={{0,16},{4,20},{8,24},{12,28},{16,0},{20,4},{24,8},{28,12},{1,17},{... | collective-permute-start | bytes 811016 | tf_op jit(solution)/shard_map/ppermute | solution.py:61
  36.7 19.3 %collective-permute-start.5 = (bf16[2,2,1,128,512]{4,3,2,1,0:T(8,128)(2,1)S(1)}, bf16[2,2,1,128,512]{4,3,2,1,0:T(8,128)(2,1)S(1)}, u32[]{:S(2)}, u32[]{:S(2)}) collective-permute-start(bf16[2,2,1,128,512]{4,3,2,1,0:T(8,128)(2,1)S(1)} %maximum_select_fusion.8), channel_id=1, source_target_pairs={{0,4},{4,0},{8,12},{12,8},{16,20},{20,16},{24,28},{28,24},{1,5},{5... | collective-permute-start | bytes 1572872 | tf_op jit(solution)/shard_map/ppermute | solution.py:61
  55.9 19.9 %collective-permute-start.12 = (bf16[2,1,2,528,128]{4,3,2,1,0:T(8,128)(2,1)S(1)}, bf16[2,1,2,528,128]{4,3,2,1,0:T(8,128)(2,1)S(1)}, u32[]{:S(2)}, u32[]{:S(2)}) collective-permute-start(bf16[2,1,2,528,128]{4,3,2,1,0:T(8,128)(2,1)S(1)} %maximum_select_fusion.7), channel_id=1, source_target_pairs={{0,8},{4,12},{8,0},{12,4},{16,24},{20,28},{24,16},{28,20},{1,9},{5... | collective-permute-start | bytes 1622024 | tf_op jit(solution)/shard_map/ppermute | solution.py:61
  56.8 20.1 %collective-permute-start.11 = (bf16[1,1,1,1024,128]{4,3,2,1,0:T(8,128)(2,1)S(1)}, bf16[1,1,1,1024,128]{4,3,2,1,0:T(8,128)(2,1)S(1)}, u32[]{:S(2)}, u32[]{:S(2)}) collective-permute-start(bf16[1,1,1,1024,128]{4,3,2,1,0:T(8,128)(2,1)S(1)} %bitcast.90), channel_id=1, source_target_pairs={{0,16},{4,20},{8,24},{12,28},{16,0},{20,4},{24,8},{28,12},{1,17},{... | collective-permute-start | bytes 786440 | tf_op jit(solution)/shard_map/ppermute | solution.py:61
  60.3 30.5 %collective-permute-start.14 = (bf16[2,2,1,128,1280]{4,3,2,1,0:T(8,128)(2,1)}, bf16[2,2,1,128,1280]{4,3,2,1,0:T(8,128)(2,1)}, u32[]{:S(2)}, u32[]{:S(2)}) collective-permute-start(bf16[2,2,1,128,1280]{4,3,2,1,0:T(8,128)(2,1)} %maximum_select_fusion.2), channel_id=1, source_target_pairs={{0,4},{4,0},{8,12},{12,8},{16,20},{20,16},{24,28},{28,24},{1,5},{5... | collective-permute-start | bytes 3932168 | tf_op jit(solution)/shard_map/ppermute | solution.py:61
  77.8 13.4 %collective-permute-start.13 = (bf16[2,1,1,1024,128]{4,3,2,1,0:T(8,128)(2,1)}, bf16[2,1,1,1024,128]{4,3,2,1,0:T(8,128)(2,1)}, u32[]{:S(2)}, u32[]{:S(2)}) collective-permute-start(bf16[2,1,1,1024,128]{4,3,2,1,0:T(8,128)(2,1)} %maximum_select_fusion.9), channel_id=1, source_target_pairs={{0,8},{4,12},{8,0},{12,4},{16,24},{20,28},{24,16},{28,20},{1,9},{5... | collective-permute-start | bytes 1572872 | tf_op jit(solution)/shard_map/ppermute | solution.py:61
  93.1 25.8 %collective-permute-start.17 = (bf16[2,2,1,1024,128]{4,3,2,1,0:T(8,128)(2,1)S(1)}, bf16[2,2,1,1024,128]{4,3,2,1,0:T(8,128)(2,1)S(1)}, u32[]{:S(2)}, u32[]{:S(2)}) collective-permute-start(bf16[2,2,1,1024,128]{4,3,2,1,0:T(8,128)(2,1)S(1)} %maximum_select_fusion.5), channel_id=1, source_target_pairs={{0,4},{4,0},{8,12},{12,8},{16,20},{20,16},{24,28},{28,24},{1,5},{5... | collective-permute-start | bytes 3145736 | tf_op jit(solution)/shard_map/ppermute | solution.py:61
  95.0 8.4 %collective-permute-start.16 = (bf16[128,1024]{1,0:T(8,128)(2,1)S(1)}, bf16[128,1024]{1,0:T(8,128)(2,1)S(1)}, u32[]{:S(2)}, u32[]{:S(2)}) collective-permute-start(bf16[128,1024]{1,0:T(8,128)(2,1)S(1)} %fold.5), channel_id=1, source_target_pairs={{0,2},{1,3},{2,0},{3,1},{4,6},{5,7},{6,4},{7,5},{8,10},{9,11},{10,... | collective-permute-start | bytes 786440 | tf_op jit(solution)/shard_map/ppermute | solution.py:61
  103.8 7.6 %collective-permute-start.18 = (bf16[128,1024]{1,0:T(8,128)(2,1)S(1)}, bf16[128,1024]{1,0:T(8,128)(2,1)S(1)}, u32[]{:S(2)}, u32[]{:S(2)}) collective-permute-start(bf16[128,1024]{1,0:T(8,128)(2,1)S(1)} %get-tuple-element.417.refs_0_), channel_id=1, source_target_pairs={{0,2},{1,3},{2,0},{3,1},{4,6},{5,7},{6,4},{7,5},{8,10},{9,11},{10,... | collective-permute-start | bytes 786440 | tf_op jit(solution)/shard_map/ppermute | solution.py:61
  105.4 9.0 %collective-permute-start.19 = (bf16[128,1024]{1,0:T(8,128)(2,1)S(1)}, bf16[128,1024]{1,0:T(8,128)(2,1)S(1)}, u32[]{:S(2)}, u32[]{:S(2)}) collective-permute-start(bf16[128,1024]{1,0:T(8,128)(2,1)S(1)} %get-tuple-element.417.refs_0_), channel_id=1, source_target_pairs={{0,1},{1,0},{2,3},{3,2},{4,5},{5,4},{6,7},{7,6},{8,9},{9,8},{10,11... | collective-permute-start | bytes 786440 | tf_op jit(solution)/shard_map/ppermute | solution.py:61
  114.4 14.4 %collective-permute-start.25 = (bf16[1024,256]{1,0:T(8,128)(2,1)S(1)}, bf16[1024,256]{1,0:T(8,128)(2,1)S(1)}, u32[]{:S(2)}, u32[]{:S(2)}) collective-permute-start(bf16[1024,256]{1,0:T(8,128)(2,1)S(1)} %slice.27.refs_5_.refs_8_), channel_id=1, source_target_pairs={{0,2},{1,3},{2,0},{3,1},{4,6},{5,7},{6,4},{7,5},{8,10},{9,11},{10,... | collective-permute-start | bytes 1572872 | tf_op jit(solution)/shard_map/ppermute | solution.py:61
  121.1 9.2 %collective-permute-start.23 = (bf16[256,1024]{1,0:T(8,128)(2,1)S(1)}, bf16[256,1024]{1,0:T(8,128)(2,1)S(1)}, u32[]{:S(2)}, u32[]{:S(2)}) collective-permute-start(bf16[256,1024]{1,0:T(8,128)(2,1)S(1)} %get-tuple-element.433), channel_id=1, source_target_pairs={{0,1},{1,0},{2,3},{3,2},{4,5},{5,4},{6,7},{7,6},{8,9},{9,8},{10,11... | collective-permute-start | bytes 1572872 | tf_op jit(solution)/shard_map/ppermute | solution.py:61
  121.4 17.5 %collective-permute-start.26 = (bf16[1024,256]{1,0:T(8,128)(2,1)S(1)}, bf16[1024,256]{1,0:T(8,128)(2,1)S(1)}, u32[]{:S(2)}, u32[]{:S(2)}) collective-permute-start(bf16[1024,256]{1,0:T(8,128)(2,1)S(1)} %slice.27.refs_5_.refs_8_), channel_id=1, source_target_pairs={{0,1},{1,0},{2,3},{3,2},{4,5},{5,4},{6,7},{7,6},{8,9},{9,8},{10,11... | collective-permute-start | bytes 1572872 | tf_op jit(solution)/shard_map/ppermute | solution.py:61
  128.8 10.2 %collective-permute-start.27 = (bf16[1024,256]{1,0:T(8,128)(2,1)S(1)}, bf16[1024,256]{1,0:T(8,128)(2,1)S(1)}, u32[]{:S(2)}, u32[]{:S(2)}) collective-permute-start(bf16[1024,256]{1,0:T(8,128)(2,1)S(1)} %collective-permute-done.25.refs_6_.refs_9_), channel_id=1, source_target_pairs={{0,1},{1,0},{2,3},{3,2},{4,5},{5,4},{6,7},{7,6},{8,9},{9,8},{10,11... | collective-permute-start | bytes 1572872 | tf_op jit(solution)/shard_map/ppermute | solution.py:61
  128.8 9.1 %collective-permute-start.21 = (bf16[1,512,256]{2,1,0:T(8,128)(2,1)S(1)}, bf16[1,512,256]{2,1,0:T(8,128)(2,1)S(1)}, u32[]{:S(2)}, u32[]{:S(2)}) collective-permute-start(bf16[1,512,256]{2,1,0:T(8,128)(2,1)S(1)} %bitcast.65), channel_id=1, source_target_pairs={{0,4},{4,0},{8,12},{12,8},{16,20},{20,16},{24,28},{28,24},{1,5},{5... | collective-permute-start | bytes 786440 | tf_op jit(solution)/shard_map/ppermute | solution.py:61
  130.4 8.5 %collective-permute-start.24 = (bf16[128,1024]{1,0:T(8,128)(2,1)S(1)}, bf16[128,1024]{1,0:T(8,128)(2,1)S(1)}, u32[]{:S(2)}, u32[]{:S(2)}) collective-permute-start(bf16[128,1024]{1,0:T(8,128)(2,1)S(1)} %fold.6), channel_id=1, source_target_pairs={{0,2},{1,3},{2,0},{3,1},{4,6},{5,7},{6,4},{7,5},{8,10},{9,11},{10,... | collective-permute-start | bytes 786440 | tf_op jit(solution)/shard_map/ppermute | solution.py:61
  140.3 7.7 %collective-permute-start.28 = (bf16[128,1024]{1,0:T(8,128)(2,1)S(1)}, bf16[128,1024]{1,0:T(8,128)(2,1)S(1)}, u32[]{:S(2)}, u32[]{:S(2)}) collective-permute-start(bf16[128,1024]{1,0:T(8,128)(2,1)S(1)} %get-tuple-element.440.refs_0_), channel_id=1, source_target_pairs={{0,2},{1,3},{2,0},{3,1},{4,6},{5,7},{6,4},{7,5},{8,10},{9,11},{10,... | collective-permute-start | bytes 786440 | tf_op jit(solution)/shard_map/ppermute | solution.py:61
  149.5 17.9 %collective-permute-start.32 = (bf16[128,1024]{1,0:T(8,128)(2,1)S(1)}, bf16[128,1024]{1,0:T(8,128)(2,1)S(1)}, u32[]{:S(2)}, u32[]{:S(2)}) collective-permute-start(bf16[128,1024]{1,0:T(8,128)(2,1)S(1)} %get-tuple-element.495.refs_4_), channel_id=1, source_target_pairs={{0,2},{1,3},{2,0},{3,1},{4,6},{5,7},{6,4},{7,5},{8,10},{9,11},{10,... | collective-permute-start | bytes 786440 | tf_op jit(solution)/shard_map/ppermute | solution.py:61
  169.5 8.4 %collective-permute-start.35 = (bf16[128,1024]{1,0:T(8,128)(2,1)S(1)}, bf16[128,1024]{1,0:T(8,128)(2,1)S(1)}, u32[]{:S(2)}, u32[]{:S(2)}) collective-permute-start(bf16[128,1024]{1,0:T(8,128)(2,1)S(1)} %fold.7), channel_id=1, source_target_pairs={{0,2},{1,3},{2,0},{3,1},{4,6},{5,7},{6,4},{7,5},{8,10},{9,11},{10,... | collective-permute-start | bytes 786440 | tf_op jit(solution)/shard_map/ppermute | solution.py:61
  179.6 7.6 %collective-permute-start.37 = (bf16[128,1024]{1,0:T(8,128)(2,1)S(1)}, bf16[128,1024]{1,0:T(8,128)(2,1)S(1)}, u32[]{:S(2)}, u32[]{:S(2)}) collective-permute-start(bf16[128,1024]{1,0:T(8,128)(2,1)S(1)} %get-tuple-element.483.refs_0_), channel_id=1, source_target_pairs={{0,2},{1,3},{2,0},{3,1},{4,6},{5,7},{6,4},{7,5},{8,10},{9,11},{10,... | collective-permute-start | bytes 786440 | tf_op jit(solution)/shard_map/ppermute | solution.py:61
  189.1 8.3 %collective-permute-start.42 = (bf16[128,1024]{1,0:T(8,128)(2,1)S(1)}, bf16[128,1024]{1,0:T(8,128)(2,1)S(1)}, u32[]{:S(2)}, u32[]{:S(2)}) collective-permute-start(bf16[128,1024]{1,0:T(8,128)(2,1)S(1)} %get-tuple-element.482.refs_8_), channel_id=1, source_target_pairs={{0,2},{1,3},{2,0},{3,1},{4,6},{5,7},{6,4},{7,5},{8,10},{9,11},{10,... | collective-permute-start | bytes 786440 | tf_op jit(solution)/shard_map/ppermute | solution.py:61
  199.9 6.9 %collective-permute-start.44 = (bf16[128,1024]{1,0:T(8,128)(2,1)S(1)}, bf16[128,1024]{1,0:T(8,128)(2,1)S(1)}, u32[]{:S(2)}, u32[]{:S(2)}) collective-permute-start(bf16[128,1024]{1,0:T(8,128)(2,1)S(1)} %get-tuple-element.482.refs_8_), channel_id=1, source_target_pairs={{0,1},{1,0},{2,3},{3,2},{4,5},{5,4},{6,7},{7,6},{8,9},{9,8},{10,11... | collective-permute-start | bytes 786440 | tf_op jit(solution)/shard_map/ppermute | solution.py:61
  201.8 8.4 %collective-permute-start.46 = (bf16[128,1024]{1,0:T(8,128)(2,1)S(1)}, bf16[128,1024]{1,0:T(8,128)(2,1)S(1)}, u32[]{:S(2)}, u32[]{:S(2)}) collective-permute-start(bf16[128,1024]{1,0:T(8,128)(2,1)S(1)} %fold.8), channel_id=1, source_target_pairs={{0,2},{1,3},{2,0},{3,1},{4,6},{5,7},{6,4},{7,5},{8,10},{9,11},{10,... | collective-permute-start | bytes 786440 | tf_op jit(solution)/shard_map/ppermute | solution.py:61
  210.3 35.9 %collective-permute-start.52 = (bf16[4,128,1280]{2,1,0:T(8,128)(2,1)}, bf16[4,128,1280]{2,1,0:T(8,128)(2,1)}, u32[]{:S(2)}, u32[]{:S(2)}) collective-permute-start(bf16[4,128,1280]{2,1,0:T(8,128)(2,1)} %get-tuple-element.521), channel_id=1, source_target_pairs={{0,8},{4,12},{8,0},{12,4},{16,24},{20,28},{24,16},{28,20},{1,9},{5... | collective-permute-start | bytes 3932168 | tf_op jit(solution)/shard_map/ppermute | solution.py:61
  211.7 26.4 %collective-permute-start.51 = (bf16[4,1024,128]{2,1,0:T(8,128)(2,1)}, bf16[4,1024,128]{2,1,0:T(8,128)(2,1)}, u32[]{:S(2)}, u32[]{:S(2)}) collective-permute-start(bf16[4,1024,128]{2,1,0:T(8,128)(2,1)} %get-tuple-element.509), channel_id=1, source_target_pairs={{0,4},{4,0},{8,12},{12,8},{16,20},{20,16},{24,28},{28,24},{1,5},{5... | collective-permute-start | bytes 3145736 | tf_op jit(solution)/shard_map/ppermute | solution.py:61
  213.6 8.3 %collective-permute-start.47 = (bf16[144,1024]{1,0:T(8,128)(2,1)S(1)}, bf16[144,1024]{1,0:T(8,128)(2,1)S(1)}, u32[]{:S(2)}, u32[]{:S(2)}) collective-permute-start(bf16[144,1024]{1,0:T(8,128)(2,1)S(1)} %get-tuple-element.506.refs_0_), channel_id=1, source_target_pairs={{0,2},{1,3},{2,0},{3,1},{4,6},{5,7},{6,4},{7,5},{8,10},{9,11},{10,... | collective-permute-start | bytes 884744 | tf_op jit(solution)/shard_map/ppermute | solution.py:61
  225.0 17.1 %collective-permute-start.50 = (bf16[1,512,256]{2,1,0:T(8,128)(2,1)}, bf16[1,512,256]{2,1,0:T(8,128)(2,1)S(1)}, u32[]{:S(2)}, u32[]{:S(2)}) collective-permute-start(bf16[1,512,256]{2,1,0:T(8,128)(2,1)} %bitcast.36), channel_id=1, source_target_pairs={{0,4},{4,0},{8,12},{12,8},{16,20},{20,16},{24,28},{28,24},{1,5},{5... | collective-permute-start | bytes 786440 | tf_op jit(solution)/shard_map/ppermute | solution.py:61
  256.2 14.8 %collective-permute-start.56 = (bf16[2,1024,128]{2,1,0:T(8,128)(2,1)S(1)}, bf16[2,1024,128]{2,1,0:T(8,128)(2,1)S(1)}, u32[]{:S(2)}, u32[]{:S(2)}) collective-permute-start(bf16[2,1024,128]{2,1,0:T(8,128)(2,1)S(1)} %get-tuple-element.547), channel_id=1, source_target_pairs={{0,8},{4,12},{8,0},{12,4},{16,24},{20,28},{24,16},{28,20},{1,9},{5... | collective-permute-start | bytes 1572872 | tf_op jit(solution)/shard_map/ppermute | solution.py:61
  256.9 28.8 %collective-permute-start.54 = (bf16[2,128,1280]{2,1,0:T(8,128)(2,1)S(1)}, bf16[2,128,1280]{2,1,0:T(8,128)(2,1)S(1)}, u32[]{:S(2)}, u32[]{:S(2)}) collective-permute-start(bf16[2,128,1280]{2,1,0:T(8,128)(2,1)S(1)} %get-tuple-element.540), channel_id=1, source_target_pairs={{0,4},{4,0},{8,12},{12,8},{16,20},{20,16},{24,28},{28,24},{1,5},{5... | collective-permute-start | bytes 1966088 | tf_op jit(solution)/shard_map/ppermute | solution.py:61
  258.4 27.4 %collective-permute-start.53 = (bf16[4,528,128]{2,1,0:T(8,128)(2,1)S(1)}, bf16[4,528,128]{2,1,0:T(8,128)(2,1)S(1)}, u32[]{:S(2)}, u32[]{:S(2)}) collective-permute-start(bf16[4,528,128]{2,1,0:T(8,128)(2,1)S(1)} %get-tuple-element.538), channel_id=1, source_target_pairs={{0,8},{4,12},{8,0},{12,4},{16,24},{20,28},{24,16},{28,20},{1,9},{5... | collective-permute-start | bytes 1622024 | tf_op jit(solution)/shard_map/ppermute | solution.py:61
  259.9 11.1 %collective-permute-start.58 = (bf16[128,1024]{1,0:T(8,128)(2,1)S(1)}, bf16[128,1024]{1,0:T(8,128)(2,1)S(1)}, u32[]{:S(2)}, u32[]{:S(2)}) collective-permute-start(bf16[128,1024]{1,0:T(8,128)(2,1)S(1)} %fold.9), channel_id=1, source_target_pairs={{0,2},{1,3},{2,0},{3,1},{4,6},{5,7},{6,4},{7,5},{8,10},{9,11},{10,... | collective-permute-start | bytes 786440 | tf_op jit(solution)/shard_map/ppermute | solution.py:61
  261.4 23.5 %collective-permute-start.55 = (bf16[4,128,512]{2,1,0:T(8,128)(2,1)S(1)}, bf16[4,128,512]{2,1,0:T(8,128)(2,1)S(1)}, u32[]{:S(2)}, u32[]{:S(2)}) collective-permute-start(bf16[4,128,512]{2,1,0:T(8,128)(2,1)S(1)} %get-tuple-element.544), channel_id=1, source_target_pairs={{0,4},{4,0},{8,12},{12,8},{16,20},{20,16},{24,28},{28,24},{1,5},{5... | collective-permute-start | bytes 1572872 | tf_op jit(solution)/shard_map/ppermute | solution.py:61
  271.8 13.1 %collective-permute-start.59 = (bf16[128,1024]{1,0:T(8,128)(2,1)S(1)}, bf16[128,1024]{1,0:T(8,128)(2,1)S(1)}, u32[]{:S(2)}, u32[]{:S(2)}) collective-permute-start(bf16[128,1024]{1,0:T(8,128)(2,1)S(1)} %close.1.refs_0_), channel_id=1, source_target_pairs={{0,2},{1,3},{2,0},{3,1},{4,6},{5,7},{6,4},{7,5},{8,10},{9,11},{10,... | collective-permute-start | bytes 786440 | tf_op jit(solution)/shard_map/ppermute | solution.py:61
  273.4 18.9 %collective-permute-start.63 = (bf16[128,1024]{1,0:T(8,128)(2,1)S(1)}, bf16[128,1024]{1,0:T(8,128)(2,1)S(1)}, u32[]{:S(2)}, u32[]{:S(2)}) collective-permute-start(bf16[128,1024]{1,0:T(8,128)(2,1)S(1)} %close.1.refs_0_), channel_id=1, source_target_pairs={{0,1},{1,0},{2,3},{3,2},{4,5},{5,4},{6,7},{7,6},{8,9},{9,8},{10,11... | collective-permute-start | bytes 786440 | tf_op jit(solution)/shard_map/ppermute | solution.py:61
  286.7 26.0 %collective-permute-start.60 = (bf16[2,528,128]{2,1,0:T(8,128)(2,1)}, bf16[2,528,128]{2,1,0:T(8,128)(2,1)S(1)}, u32[]{:S(2)}, u32[]{:S(2)}) collective-permute-start(bf16[2,528,128]{2,1,0:T(8,128)(2,1)} %get-tuple-element.571), channel_id=1, source_target_pairs={{0,4},{4,0},{8,12},{12,8},{16,20},{20,16},{24,28},{28,24},{1,5},{5... | collective-permute-start | bytes 811016 | tf_op jit(solution)/shard_map/ppermute | solution.py:61
  288.2 14.4 %collective-permute-start.62 = (bf16[2,128,512]{2,1,0:T(8,128)(2,1)}, bf16[2,128,512]{2,1,0:T(8,128)(2,1)S(1)}, u32[]{:S(2)}, u32[]{:S(2)}) collective-permute-start(bf16[2,128,512]{2,1,0:T(8,128)(2,1)} %get-tuple-element.574), channel_id=1, source_target_pairs={{0,8},{4,12},{8,0},{12,4},{16,24},{20,28},{24,16},{28,20},{1,9},{5... | collective-permute-start | bytes 786440 | tf_op jit(solution)/shard_map/ppermute | solution.py:61
  289.6 23.0 %collective-permute-start.61 = (bf16[1,1024,128]{2,1,0:T(8,128)(2,1)}, bf16[1,1024,128]{2,1,0:T(8,128)(2,1)}, u32[]{:S(2)}, u32[]{:S(2)}) collective-permute-start(bf16[1,1024,128]{2,1,0:T(8,128)(2,1)} %get-tuple-element.572), channel_id=1, source_target_pairs={{0,16},{4,20},{8,24},{12,28},{16,0},{20,4},{24,8},{28,12},{1,17},{... | collective-permute-start | bytes 786440 | tf_op jit(solution)/shard_map/ppermute | solution.py:61
  292.3 33.0 %collective-permute-start.67 = (bf16[1,128,1280]{2,1,0:T(8,128)(2,1)S(1)}, bf16[1,128,1280]{2,1,0:T(8,128)(2,1)S(1)}, u32[]{:S(2)}, u32[]{:S(2)}) collective-permute-start(bf16[1,128,1280]{2,1,0:T(8,128)(2,1)S(1)} %get-tuple-element.586), channel_id=1, source_target_pairs={{0,16},{4,20},{8,24},{12,28},{16,0},{20,4},{24,8},{28,12},{1,17},{... | collective-permute-start | bytes 983048 | tf_op jit(solution)/shard_map/ppermute | solution.py:61
  312.7 15.4 %collective-permute-start.66 = (bf16[1,128,512]{2,1,0:T(8,128)(2,1)S(1)}, bf16[1,128,512]{2,1,0:T(8,128)(2,1)S(1)}, u32[]{:S(2)}, u32[]{:S(2)}) collective-permute-start(bf16[1,128,512]{2,1,0:T(8,128)(2,1)S(1)} %get-tuple-element.585), channel_id=1, source_target_pairs={{0,16},{4,20},{8,24},{12,28},{16,0},{20,4},{24,8},{28,12},{1,17},{... | collective-permute-start | bytes 393224 | tf_op jit(solution)/shard_map/ppermute | solution.py:61
  312.7 17.6 %collective-permute-start.65 = (bf16[1,528,128]{2,1,0:T(8,128)(2,1)S(1)}, bf16[1,528,128]{2,1,0:T(8,128)(2,1)S(1)}, u32[]{:S(2)}, u32[]{:S(2)}) collective-permute-start(bf16[1,528,128]{2,1,0:T(8,128)(2,1)S(1)} %get-tuple-element.584), channel_id=1, source_target_pairs={{0,16},{4,20},{8,24},{12,28},{16,0},{20,4},{24,8},{28,12},{1,17},{... | collective-permute-start | bytes 405512 | tf_op jit(solution)/shard_map/ppermute | solution.py:61
  (59 other events, 347.9 us)

commit v2 on v1

--- a/solution.py
+++ b/solution.py
@@ -203,19 +203,22 @@
     return blocks
 
 
-def rows_scatter(keep, send, main=None, between=None):
+def rows_scatter(blocks):
     masks = upward("mp")
-    terms = [keep, swap(send, "mp", masks[0])]
-    for mask in masks[1:]:
-        terms = terms + [swap(rows_fold(*terms), "mp", mask)]
-    return terms
+    terms = [[block] for block in blocks]
+    for mask in masks:
+        half = len(terms) // 2
+        sends = [each[0] if len(each) == 1 else rows_fold(each) for each in terms[half:]]
+        order = range(half)[::-1]
+        got = {at: swap(sends[at], "mp", mask) for at in order}
+        terms = [terms[at] + [got[at]] for at in range(half)]
+    return terms[0]
 
 
 def add_up(refs):
-    rows = refs[-1].shape[0]
-    total = refs[0][0:rows, :].astype(full_type)
+    total = refs[0][...].astype(full_type)
     for ref in refs[1:]:
-        total = total + ref[0:rows, :].astype(full_type)
+        total = total + ref[...].astype(full_type)
     return total
 
 
@@ -412,18 +415,20 @@
     )(*blocks, w_up)
 
 
-def store_halves(total, keep_ref, send_ref):
-    half = total.shape[0] // 2
-    keep_ref[...] = total[:half]
-    send_ref[...] = total[half:].astype(low_type)
-
-
-def halves_of(rows, width):
-    return [shape_of((rows // 2, width), full_type), shape_of((rows // 2, width))]
-
-
-def feed_down_kernel(g_ref, down_ref, keep_ref, send_ref):
-    store_halves(low_dot(g_ref[...], lanes_of(down_ref)), keep_ref, send_ref)
+def store_blocks(total, block_refs):
+    rows = total.shape[0] // len(block_refs)
+    for at, ref in enumerate(block_refs):
+        ref[...] = total[at * rows : (at + 1) * rows].astype(ref.dtype)
+
+
+def blocks_of(rows, width):
+    count = lax.axis_size("mp")
+    kept = [shape_of((rows // count, width), full_type)] * (count // 2)
+    return kept + [shape_of((rows // count, width))] * (count // 2)
+
+
+def feed_down_kernel(g_ref, down_ref, *block_refs):
+    store_blocks(low_dot(g_ref[...], lanes_of(down_ref)), block_refs)
 
 
 def feed_down(active, w_down):
@@ -437,8 +442,11 @@
             pl.BlockSpec((rows, units), lambda i: (0, 0)),
             pl.BlockSpec((tile, units, lanes), lambda i: (i, 0, 0)),
         ],
-        out_specs=[pl.BlockSpec((rows // 2, tile * lanes), lambda i: (0, i))] * 2,
-        out_shape=halves_of(rows, blocks * lanes),
+        out_specs=[
+            pl.BlockSpec((each.shape[0], tile * lanes), lambda i: (0, i))
+            for each in blocks_of(rows, blocks * lanes)
+        ],
+        out_shape=blocks_of(rows, blocks * lanes),
         compiler_params=room(10),
         cost_estimate=brief,
         name="feed_down",
@@ -475,8 +483,8 @@
     )(*blocks, w_down, slope)
 
 
-def feed_back_kernel(dz_ref, up_ref, keep_ref, send_ref):
-    store_halves(low_dot(dz_ref[...], up_ref[...], contract_cols), keep_ref, send_ref)
+def feed_back_kernel(dz_ref, up_ref, *block_refs):
+    store_blocks(low_dot(dz_ref[...], up_ref[...], contract_cols), block_refs)
 
 
 def feed_back(dinner, w_up):
@@ -490,8 +498,11 @@
             pl.BlockSpec((rows, units), lambda i: (0, 0)),
             pl.BlockSpec((tile, units), lambda i: (i, 0)),
         ],
-        out_specs=[pl.BlockSpec((rows // 2, tile), lambda i: (0, i))] * 2,
-        out_shape=halves_of(rows, width),
+        out_specs=[
+            pl.BlockSpec((each.shape[0], tile), lambda i: (0, i))
+            for each in blocks_of(rows, width)
+        ],
+        out_shape=blocks_of(rows, width),
         compiler_params=room(10),
         cost_estimate=brief,
         name="feed_back",
@@ -561,7 +572,7 @@
 def late_backward_kernel(
     sharp_ref, soft_ref, far_ref, same_ref, place_ref, weight_ref, q_ref, *refs
 ):
-    keep_ref, send_ref, score_ref, total = refs
+    *block_refs, score_ref, total = refs
     step = pl.program_id(0)
     blocks = soft_ref.shape[0]
     rows, tile = sharp_ref.shape
@@ -586,7 +597,7 @@
 
     @pl.when(step == pl.num_programs(0) - 1)
     def _():
-        store_halves(total[...], keep_ref, send_ref)
+        store_blocks(total[...], block_refs)
 
 
 def late_backward(sharp, soft, far, same, place, weight, queries):
@@ -594,7 +605,7 @@
     width = queries.shape[1]
     blocks = soft.shape[0]
     tile = 512
-    held = whole_block((rows // 2, width))
+    outs = blocks_of(rows, width)
     return pl.pallas_call(
         late_backward_kernel,
         grid=(count // tile,),
@@ -607,8 +618,9 @@
             pl.BlockSpec((blocks, tile), lambda i: (0, i)),
             pl.BlockSpec((tile, width), lambda i: (i, 0)),
         ],
-        out_specs=[held, held, pl.BlockSpec((tile // QLEN, NPASS), lambda i: (i, 0))],
-        out_shape=halves_of(rows, width) + [shape_of((count // QLEN, NPASS), full_type)],
+        out_specs=[whole_block(each.shape) for each in outs]
+        + [pl.BlockSpec((tile // QLEN, NPASS), lambda i: (i, 0))],
+        out_shape=outs + [shape_of((count // QLEN, NPASS), full_type)],
         scratch_shapes=[pltpu.VMEM((rows, width), full_type)],
         compiler_params=room(16),
         cost_estimate=brief,
@@ -675,7 +687,7 @@
 
 
 def norm_two_back_kernel(order_ref, *refs):
-    *rest, du_ref, dr_ref, low_ref, g_ref = refs
+    *rest, own_ref, far_ref, dr_ref, low_ref, g_ref, du_ref = refs
     parts = order_ref.shape[0]
     *terms, norm_ref, unit_ref, scale_ref, e_ref, inv_ref = rest[:-parts]
     col_refs = rest[-parts:]
@@ -688,6 +700,10 @@
     for at, ref in enumerate(col_refs):
         dproj = du_ref[:, lanes_at(order_ref, at, span)]
         dnormed = dnormed + low_dot(dproj, ref[...], contract_cols)
+    half = own_ref.shape[1]
+    mine = order_ref[0] // (parts // 2)
+    own_ref[...] = du_ref[:, pl.ds(pl.multiple_of(mine * half, half), half)]
+    far_ref[...] = du_ref[:, pl.ds(pl.multiple_of((1 - mine) * half, half), half)]
     dresid, dgain, dshift = norm_backward(
         unit_ref[...], scale_ref[...], norm_ref[2:3], dnormed
     )
@@ -715,20 +731,19 @@
     )
 
 
-def fold_kernel(keep_ref, got_ref, low_ref):
-    half = low_ref.shape[0]
-    total = keep_ref[half:, :] + got_ref[half:, :].astype(full_type)
-    low_ref[...] = total.astype(low_type)
-
-
-def rows_fold(keep, got):
-    return whole_call(fold_kernel, [shape_of((got.shape[0] // 2, got.shape[1]))], "fold", keep, got)[0]
-
-
-def mix_kernel(o_ref, out_ref, keep_ref, send_ref):
+def fold_kernel(*refs):
+    *terms, low_ref = refs
+    low_ref[...] = add_up(terms).astype(low_type)
+
+
+def rows_fold(terms):
+    return whole_call(fold_kernel, [shape_of(terms[0].shape)], "fold", *terms)[0]
+
+
+def mix_kernel(o_ref, out_ref, *block_refs):
     rows = o_ref.shape[1]
     weight = jnp.concatenate([out_ref[at, 0:rows, :] for at in range(out_ref.shape[0])], axis=1)
-    store_halves(low_dot(o_ref[...], weight), keep_ref, send_ref)
+    store_blocks(low_dot(o_ref[...], weight), block_refs)
 
 
 def unmix_kernel(*refs):
@@ -828,7 +843,8 @@
     block_rows = keep_ref.shape[1]
     cols = keep_ref.shape[2] - units
     stored(total.at[:, 0:units], rows_of(row_refs[:parts]), dinner_ref[...])
-    mine = pl.ds(pl.multiple_of(order_ref[order_ref.shape[0] - 1] * cols, cols), cols)
+    mine = order_ref[order_ref.shape[0] - 1] % (row_refs[-1].shape[1] // cols)
+    mine = pl.ds(pl.multiple_of(mine * cols, cols), cols)
     dproj = jnp.concatenate([ref[:, mine] for ref in row_refs[2 * parts :]], axis=0)
     stored(total.at[:, units:], rows_of(row_refs[parts : 2 * parts]), dproj)
 
@@ -856,6 +872,7 @@
             *two_blocks,
             *du_blocks,
         )
+    column = column % (du_blocks[0].shape[1] // col_width)
     dproj = lax.dynamic_slice_in_dim(
         jnp.concatenate(du_blocks, 0), column * col_width, col_width, 1
     )
@@ -1011,13 +1028,13 @@
     return ordered_call(place_kernel, outs, [], "place_rows", order, *blocks)[0]
 
 
-def unproject_kernel(dqk_ref, dv_ref, a_ref, b_ref, keep_ref, send_ref):
+def unproject_kernel(dqk_ref, dv_ref, a_ref, b_ref, *block_refs):
     total = low_dot(dqk_ref[...], a_ref[...], contract_cols)
-    store_halves(total + low_dot(dv_ref[...], b_ref[...], contract_cols), keep_ref, send_ref)
+    store_blocks(total + low_dot(dv_ref[...], b_ref[...], contract_cols), block_refs)
 
 
 def unproject(dqk, dvalue, w_qk, w_v):
-    outs = halves_of(dqk.shape[0], w_qk.shape[0])
+    outs = blocks_of(dqk.shape[0], w_qk.shape[0])
     return whole_call(unproject_kernel, outs, "unproject", dqk, dvalue, w_qk, w_v)
 
 
@@ -1132,13 +1149,14 @@
     )
     pack_a = Gather(packed_a, "dp", dp_down)
     pack_u = Gather(packed_u, "dp", dp_down)
-    pack_b = Gather(packed_b, "dp", turned)
-    pack_d = Gather(w_down, "dp", dp_down)
+    pack_b = Gather(packed_b, "dp", dp_down)
+    pack_d = Gather(w_down, "dp", turned)
 
     main = (hidden_own, own_hidden)
     main = pack_a.start(main)
+    main = pack_b.start(main)
     main = pack_u.start(main)
-    main = pack_b.start(main)
+    main = pack_d.start(main)
     others = group_gather(main[1][None])[1:]
     seg_own = ordered(passage, device)
     live_own = ordered(live, device)
@@ -1162,22 +1180,22 @@
     early, main = tie(early, main)
     seg_column, seg_far, slot_own, slot_row, live_bias, weight, same, place = early
     main = pack_a.step(main)
+    main = pack_b.step(main)
     others, main = tie(others, main)
     far_others = swap(others, "mp", 2)
+    main = pack_d.finish(main)
     main = pack_u.step(main)
-    main = pack_b.finish(main)
+    main = pack_d.start(main)
     main = pack_a.step(main)
-    main = pack_b.start(main)
+    main = pack_b.step(main)
     far_others, main = tie(far_others, main)
+    main = pack_u.step(main)
     others = [others, far_others]
     others = others + [swap(each, "mp", 1) for each in others]
     others = jnp.stack(others, 1).reshape(-1, width)
     hidden_own, own_hidden = main
     hidden_all = jnp.concatenate([hidden_own, others], 0)
     main = (hidden_own, own_hidden, hidden_all)
-    main = pack_u.step(main)
-    main = pack_b.step(main)
-    main = pack_d.start(main)
     main = pack_a.drain(main)
     full_a = pack_a.value().reshape(width, -1)
     full_a, main = tie(full_a, main)
@@ -1190,17 +1208,20 @@
     full_b = full_b.reshape(width, head_width)
     full_out = to_lanes(full_out)
     (full_b, full_out), main = tie((full_b, full_out), main)
+    main = pack_d.step(main)
     query_key, hidden_all = main
     value_rows = low_dot(hidden_all, full_b).astype(low_type)
-    value_rows = pack_d.step(value_rows)
     norm_rows = jnp.swapaxes(full_out[:, head_width : head_width + 4], 0, 1).reshape(4, width)
     norm_rows = norm_rows.astype(full_type)
     attended, lse = attend_forward(query_key, value_rows, seg_column, slot_row)
     norm_rows, attended = tie(norm_rows, attended)
-    attended = pack_u.drain(attended)
-    keep, send = whole_call(mix_kernel, halves_of(tok_rows, width), "mix", attended, full_out)
-    keep, send = pack_d.step((keep, send))
-    terms = rows_scatter(keep, send)
+    parts = whole_call(mix_kernel, blocks_of(tok_rows, width), "mix", attended, full_out)
+    terms = rows_scatter(parts)
+    terms = pack_u.drain(terms)
+    full_up = pack_u.value().reshape(width, -1)
+    units = w_up.shape[1]
+    col_own = full_up[:, units:]
+    col_own, terms = tie(col_own, terms)
     square = shape_of((own_rows, width), full_type)
     low_square = shape_of((own_rows, width))
     narrow = shape_of((own_rows, 1), full_type)
@@ -1213,21 +1234,18 @@
         norm_rows,
     )
 
-    units = w_up.shape[1]
-    rows_one = rows_gather(normed_low)
-    full_up = pack_u.value().reshape(width, -1)
-    col_own = full_up[:, units:]
-    (full_up, col_own), rows_one = tie((full_up, col_own), rows_one)
+    rows_one = [normed_low, swap(normed_low, "mp", 2)]
+    rows_one = pack_d.drain(rows_one)
+    rows_one = rows_one + [swap(each, "mp", 1) for each in rows_one]
+    full_down = to_lanes(pack_d.value())
     far_col = swap(col_own, "mp", 2)
     active, slope = feed_up(rows_one, full_up, units)
-    main = pack_d.drain((active, slope))
-    full_down = to_lanes(pack_d.value())
-    full_down, (active, slope) = tie(full_down, main)
-    keep, send = feed_down(active, full_down)
-    (far, far_lse), send = tie((attended, lse), send)
+    parts = feed_down(active, full_down)
+    (far, far_lse), parts = tie((attended, lse), parts)
     far = group_gather(far[None])[1:]
     far_lse = group_gather(far_lse[None])[1:]
-    terms = rows_scatter(keep, send)
+    far_col, parts = tie(far_col, parts)
+    terms = rows_scatter(parts)
     (far, far_lse), terms = tie((far, far_lse), terms)
     col_blocks = [col_own, far_col]
     col_blocks = col_blocks + [swap(each, "mp", 1) for each in col_blocks]
@@ -1248,24 +1266,25 @@
     far_two = swap(two_low, "mp", 2)
     sharp, soft_block = late_forward(e_blocks, queries, live_bias, blocks)
     soft_far = group_gather(soft_block[None])[1:]
-    keep, send, scores = late_backward(
+    *parts, scores = late_backward(
         sharp, soft_block, soft_far, same, place, weight, queries
     )
-    far_two, (keep, send) = tie(far_two, (keep, send))
+    far_two, parts = tie(far_two, parts)
     far_attended = far.reshape(-1, head_width)
     far_lse = jnp.swapaxes(far_lse, 0, 1).reshape(8, -1)
 
     score_masks = dp_up[group_levels:]
-    scores, send = tie(scores, send)
+    scores, parts = tie(scores, parts)
     scores_far = swap(scores, "dp", score_masks[0])
-    terms = rows_scatter(keep, send)
+    terms = rows_scatter(parts)
     scores_far, terms = tie(scores_far, terms)
     scores, terms = tie(scores + scores_far, terms)
     scores_far = swap(scores, "dp", score_masks[1])
-    dproj_low, dresid_two, dresid_low, two_sums = ordered_call(
+    low_half = shape_of((own_rows, width // 2))
+    du_own, du_far, dresid_two, dresid_low, two_sums = ordered_call(
         norm_two_back_kernel,
-        [low_square, square, low_square, shape_of((2, width), full_type)],
-        [],
+        [low_half, low_half, square, low_square, shape_of((2, width), full_type)],
+        [((own_rows, width), low_type)],
         "norm_two_back",
         col_order,
         *terms,
@@ -1286,19 +1305,18 @@
     for mask in score_masks[2:]:
         scores = scores + swap(scores, "dp", mask)
 
-    dproj_low, dresid_blocks = tie(dproj_low, dresid_blocks)
-    du_far = swap(dproj_low, "mp", 2)
+    (du_own, du_far), dresid_blocks = tie((du_own, du_far), dresid_blocks)
+    du_far = swap(du_far, "mp", 2)
     dinner = feed_inner(dresid_blocks, full_down, slope)
     du_far, dinner = tie(du_far, dinner)
-    keep, send = feed_back(dinner, full_up)
-    got = swap(send, "mp", 1)
-    du_blocks = [dproj_low, du_far]
+    parts = feed_back(dinner, full_up)
+    got_far, got = swap(parts[3], "mp", 1), swap(parts[2], "mp", 1)
+    du_blocks = [du_own, du_far]
     du_blocks = du_blocks + [swap(each, "mp", 1) for each in du_blocks]
-    terms = [keep, got]
-    low = rows_fold(*terms)
+    low = rows_fold([parts[1], got_far])
     (active, dinner), low = tie((active, dinner), low)
     far_low = swap(low, "mp", 2)
-    grad_d = Scatter(*grad_down(active, dresid_blocks, dp_up), "dp", dp_up)
+    grad_d = Scatter(*grad_down(active, dresid_blocks, turned), "dp", turned)
     dinner = grad_d.start(dinner)
     grad_u = Scatter(
         *grad_up(dinner, rows_one, two_blocks, du_blocks, w_colbert.shape[1], across_back),
@@ -1311,7 +1329,8 @@
         [square, shape_of((own_rows + SPARE, width))],
         "norm_one_back",
         dresid_two,
-        *terms,
+        parts[0],
+        got,
         far_low,
         norm_rows,
         unit_one,
@@ -1339,30 +1358,31 @@
     sums = attend_back(far_q, 0, tok_rows, own_keys, sums, False)
     sums = grad_u.step(sums)
     dqk, dvalue_low = attend_back(far_q, 1, tok_rows, own_keys, sums, False, (dquery,))
+    parts = unproject(dqk, dvalue_low, full_a, full_b)
+    got_far, got = swap(parts[3], "mp", 1), swap(parts[2], "mp", 1)
+    low = rows_fold([parts[1], got_far])
+    (dqk, dvalue_low), low = tie((dqk, dvalue_low), low)
+    far_low = swap(low, "mp", 2)
     grad_b = Scatter(
         *grad_vo(hidden_own, dvalue_low, attended, packs, norm_sums, across_back),
         "dp",
         across_back,
     )
     dqk = grad_b.start(dqk)
+    dqk = grad_d.step(dqk)
     grad_a = Scatter(*grad_qk(hidden_own, dqk, dp_up), "dp", dp_up)
-    dqk = grad_a.start(dqk)
-    keep, send = unproject(dqk, dvalue_low, full_a, full_b)
-    got = swap(send, "mp", 1)
-    low = rows_fold(keep, got)
-    terms = [keep, got, swap(low, "mp", 2)]
-    terms = grad_d.step(terms)
-    input_own = whole_call(close_kernel, [low_square], "close", dresid_one, *terms)[0]
+    last = grad_a.start(parts[0])
+    last = grad_u.step(last)
+    terms = [dresid_one, last, got, far_low]
+    input_own = whole_call(close_kernel, [low_square], "close", *terms)[0]
     far_own = swap(input_own, "mp", 2)
-    far_own = grad_u.step(grad_a.step(far_own))
-    far_own = grad_b.step(far_own)
+    far_own = grad_a.step(grad_b.step(far_own))
     input_blocks = [input_own, far_own]
     input_blocks = input_blocks + [swap(each, "mp", 1) for each in input_blocks]
     input_grad = place_rows(col_order, input_blocks)
-    input_grad = grad_d.finish(grad_a.step(input_grad))
+    input_grad = grad_a.step(grad_b.step(input_grad))
+    input_grad = grad_d.finish(grad_u.finish(input_grad))
     down_grad = grad_d.value()
-    input_grad = grad_b.step(input_grad)
-    input_grad = grad_u.finish(input_grad)
     up_grad, colbert_grad = finish_pair(grad_u, units)
     ends = (input_grad, down_grad, up_grad, colbert_grad)
     ends = grad_a.finish(ends)

time: 332 us -> 313 us (0.943)
  waiting for transfers between devices: 161 us -> 146 us
  starting transfers between devices: 62.9 us -> 58 us
    ppermute x68 -> x73, waiting for transfers between devices: 161 us -> 146 us  [swap(): return lax.ppermute(value, axis, pairs)]
    ppermute x68 -> x73, starting transfers between devices: 62.9 us -> 58 us  [swap(): return lax.ppermute(value, axis, pairs)]
  transfers between devices with their start and end apart: 68 -> 73, of which waited for: 35 -> 43; matrix products, arithmetic and copies ran while one was open for 6% -> 6% of each run, Pallas kernels for 18% -> 23%
where the time goes in v2:
time: 313 us; the launch traced here: 312 us
  waiting for transfers between devices  146 us (47%)
  Pallas kernels  80.6 us (26%)
  starting transfers between devices  58 us (19%)
  other arithmetic  16.3 us (5%)
  local copies, waits for them, and re-layouts  8.26 us (3%)
    ppermute x73, waiting for transfers between devices, swap(): return lax.ppermute(value, axis, pairs)  146 us
    ppermute x73, starting transfers between devices, swap(): return lax.ppermute(value, axis, pairs)  58 us
    pallas_call x3, Pallas kernels, attend_back(): pl.pallas_call(kernel, grid=(steps,), in_specs=in_specs, out_specs=out_sp...  20.9 us
    pallas_call x8, Pallas kernels, ordered_call(): pl.pallas_call(kernel, grid=(1,), in_specs=[pl.BlockSpec(memory_space=plt...  16.3 us
    select_n x12, other arithmetic, finish(): jnp.where(has_bit(self.axis, mask), jnp.concatenate([other, self.whole],...  10.3 us
    pallas_call x1, Pallas kernels, attend_forward(): pl.pallas_call(attend_forward_kernel, grid=(rows // tile,), in_specs=[pl....  8.01 us
    pallas_call x1, Pallas kernels, late_forward(): pl.pallas_call(late_forward_kernel, grid=(count // tile,), in_specs=[pl.B...  6.71 us
    pallas_call x14, Pallas kernels, whole_call(): pl.pallas_call(kernel, grid=(1,), in_specs=[whole_block(each.shape) for e...  6.33 us
  transfers between devices with their start and end apart: 73, of which 43 were waited for; matrix products, arithmetic and copies ran while one was open for 6% of the time, Pallas kernels for 23%

profile of v2, /device:TPU:0, one launch (start us, length us, event | category | flops | bytes accessed | tf_op | source)
XLA Modules:
  0.0 312.4 jit_solution(9860084444768501297)
XLA Ops:
  1.8 2.7 pack.1
  4.5 4.0 %collective-permute-start = (bf16[1,1,1,128,512]{4,3,2,1,0:T(8,128)(2,1)}, bf16[1,1,1,128,512]{4,3,2,1,0:T(8,128)(2,1)S(1)}, u32[]{:S(2)}, u32[]{:S(2)}) collective-permute-start(bf16[1,1,1,128,512]{4,3,2,1,0:T(8,128)(2,1)} %bitcast.93), channel_id=1, source_target_pairs={{0,16},{4,20},{8,24},{12,28},{16,0},{20,4},{24,8},{28,12},{1,17},{... | collective-permute-start | bytes 393224 | tf_op jit(solution)/shard_map/ppermute | solution.py:61
  10.7 2.8 collective-permute-start.5
  17.0 8.8 %collective-permute-done = bf16[1,1,1,128,512]{4,3,2,1,0:T(8,128)(2,1)S(1)} collective-permute-done((bf16[1,1,1,128,512]{4,3,2,1,0:T(8,128)(2,1)}, bf16[1,1,1,128,512]{4,3,2,1,0:T(8,128)(2,1)S(1)}, u32[]{:S(2)}, u32[]{:S(2)}) %collective-permute-start) | collective-permute-done | bytes 131104 | tf_op jit(solution)/shard_map/ppermute | solution.py:61
  31.9 3.1 %collective-permute-done.5 = bf16[1,1,1,128,1280]{4,3,2,1,0:T(8,128)(2,1)S(1)} collective-permute-done((bf16[1,1,1,128,1280]{4,3,2,1,0:T(8,128)(2,1)}, bf16[1,1,1,128,1280]{4,3,2,1,0:T(8,128)(2,1)S(1)}, u32[]{:S(2)}, u32[]{:S(2)}) %collective-permute-start.5) | collective-permute-done | bytes 327712 | tf_op jit(solution)/shard_map/ppermute | solution.py:61
  37.3 3.4 %collective-permute-done.1 = bf16[2,1,1,128,512]{4,3,2,1,0:T(8,128)(2,1)S(1)} collective-permute-done((bf16[2,1,1,128,512]{4,3,2,1,0:T(8,128)(2,1)S(1)}, bf16[2,1,1,128,512]{4,3,2,1,0:T(8,128)(2,1)S(1)}, u32[]{:S(2)}, u32[]{:S(2)}) %collective-permute-start.1) | collective-permute-done | bytes 262176 | tf_op jit(solution)/shard_map/ppermute | solution.py:61
  41.5 4.9 %collective-permute-done.9 = bf16[2,1,1,528,128]{4,3,2,1,0:T(8,128)(2,1)S(1)} collective-permute-done((bf16[2,1,1,528,128]{4,3,2,1,0:T(8,128)(2,1)S(1)}, bf16[2,1,1,528,128]{4,3,2,1,0:T(8,128)(2,1)S(1)}, u32[]{:S(2)}, u32[]{:S(2)}) %collective-permute-start.9) | collective-permute-done | bytes 270368 | tf_op jit(solution)/shard_map/ppermute | solution.py:61
  52.5 12.5 %collective-permute-done.7 = bf16[2,1,1,128,1280]{4,3,2,1,0:T(8,128)(2,1)} collective-permute-done((bf16[2,1,1,128,1280]{4,3,2,1,0:T(8,128)(2,1)S(1)}, bf16[2,1,1,128,1280]{4,3,2,1,0:T(8,128)(2,1)}, u32[]{:S(2)}, u32[]{:S(2)}) %collective-permute-start.7) | collective-permute-done | bytes 655392 | tf_op jit(solution)/shard_map/ppermute | solution.py:61
  69.4 5.6 %collective-permute-done.13 = bf16[2,2,1,528,128]{4,3,2,1,0:T(8,128)(2,1)S(1)} collective-permute-done((bf16[2,2,1,528,128]{4,3,2,1,0:T(8,128)(2,1)}, bf16[2,2,1,528,128]{4,3,2,1,0:T(8,128)(2,1)S(1)}, u32[]{:S(2)}, u32[]{:S(2)}) %collective-permute-start.13) | collective-permute-done | bytes 540704 | tf_op jit(solution)/shard_map/ppermute | solution.py:61
  79.0 8.0 %attend_forward.1 = (bf16[512,256]{1,0:T(8,128)(2,1)S(1)}, f32[8,512]{1,0:T(8,128)S(1)}) custom-call(bf16[1024,512]{1,0:T(8,128)(2,1)S(1)} %convolution_convert_fusion.q_ref.k_ref.refs_0_.refs_1_, bf16[1024,512]{1,0:T(8,128)(2,1)S(1)} %convolution_convert_fusion.q_ref.k_ref.refs_0_.refs_1_, bf16[1024,256]{1,0:T(8,128)(2,1)S(1)} %convolution_convert_fusion.1.v_ref.refs_2_, ...), custom_call_target="tpu_custom_call" | custom-call | flops 1 | bytes 1 | tf_op jit(solution)/shard_map/attend_forward/pallas_call | solution.py:257
  87.6 2.6 collective-permute-start.18
  91.9 7.1 %collective-permute-done.17.refs_3_ = bf16[128,1024]{1,0:T(8,128)(2,1)S(1)} collective-permute-done((bf16[128,1024]{1,0:T(8,128)(2,1)S(1)}, bf16[128,1024]{1,0:T(8,128)(2,1)S(1)}, u32[]{:S(2)}, u32[]{:S(2)}) %collective-permute-start.17) | collective-permute-done | bytes 262176 | tf_op jit(solution)/shard_map/ppermute | solution.py:61
  99.0 7.6 %collective-permute-done.12 = bf16[2,2,1,128,1280]{4,3,2,1,0:T(8,128)(2,1)S(1)} collective-permute-done((bf16[2,2,1,128,1280]{4,3,2,1,0:T(8,128)(2,1)S(1)}, bf16[2,2,1,128,1280]{4,3,2,1,0:T(8,128)(2,1)S(1)}, u32[]{:S(2)}, u32[]{:S(2)}) %collective-permute-start.12) | collective-permute-done | bytes 1310752 | tf_op jit(solution)/shard_map/ppermute | solution.py:61
  109.9 4.0 %collective-permute-done.18 = bf16[2,1,2,1024,128]{4,3,2,1,0:T(8,128)(2,1)S(1)} collective-permute-done((bf16[2,1,2,1024,128]{4,3,2,1,0:T(8,128)(2,1)S(1)}, bf16[2,1,2,1024,128]{4,3,2,1,0:T(8,128)(2,1)S(1)}, u32[]{:S(2)}, u32[]{:S(2)}) %collective-permute-start.18) | collective-permute-done | bytes 1048608 | tf_op jit(solution)/shard_map/ppermute | solution.py:61
  113.9 3.2 %collective-permute-done.19.refs_1_ = bf16[128,1024]{1,0:T(8,128)(2,1)S(1)} collective-permute-done((bf16[128,1024]{1,0:T(8,128)(2,1)S(1)}, bf16[128,1024]{1,0:T(8,128)(2,1)S(1)}, u32[]{:S(2)}, u32[]{:S(2)}) %collective-permute-start.19) | collective-permute-done | bytes 262176 | tf_op jit(solution)/shard_map/ppermute | solution.py:61
  119.0 2.9 feed_up.1
  121.9 1.9 feed_down.1
  123.8 2.0 collective-permute-done.24.refs_6_.refs_9_
  131.5 4.7 %collective-permute-done.22 = bf16[1,512,256]{2,1,0:T(8,128)(2,1)S(1)} collective-permute-done((bf16[1,512,256]{2,1,0:T(8,128)(2,1)S(1)}, bf16[1,512,256]{2,1,0:T(8,128)(2,1)S(1)}, u32[]{:S(2)}, u32[]{:S(2)}) %collective-permute-start.22) | collective-permute-done | bytes 262176 | tf_op jit(solution)/shard_map/ppermute | solution.py:61
  140.5 5.5 %collective-permute-done.30.refs_1_ = bf16[128,1024]{1,0:T(8,128)(2,1)S(1)} collective-permute-done((bf16[128,1024]{1,0:T(8,128)(2,1)S(1)}, bf16[128,1024]{1,0:T(8,128)(2,1)S(1)}, u32[]{:S(2)}, u32[]{:S(2)}) %collective-permute-start.30) | collective-permute-done | bytes 262176 | tf_op jit(solution)/shard_map/ppermute | solution.py:61
  149.1 6.7 %late_forward.1 = (f32[512,2048]{1,0:T(8,128)S(1)}, f32[8,2048]{1,0:T(8,128)S(1)}) custom-call(bf16[128,1024]{1,0:T(8,128)(2,1)S(1)} %get-tuple-element.464.refs_0_, bf16[128,1024]{1,0:T(8,128)(2,1)S(1)} %collective-permute-done.30.refs_1_, bf16[128,1024]{1,0:T(8,128)(2,1)S(1)} %collective-permute-done.31.refs_2_, ...), custom_call_target="tpu_custom_call" | custom-call | flops 1 | bytes 1 | tf_op jit(solution)/shard_map/late_forward/pallas_call | solution.py:533
  156.8 3.3 %collective-permute-done.33.far_ref = f32[1,8,2048]{2,1,0:T(8,128)S(1)} collective-permute-done((f32[1,8,2048]{2,1,0:T(8,128)S(1)}, f32[1,8,2048]{2,1,0:T(8,128)S(1)}, u32[]{:S(2)}, u32[]{:S(2)}) %collective-permute-start.33) | collective-permute-done | bytes 65568 | tf_op jit(solution)/shard_map/ppermute | solution.py:61
  160.1 5.1 %late_backward.1 = (f32[128,1024]{1,0:T(8,128)S(1)}, f32[128,1024]{1,0:T(8,128)S(1)}, bf16[128,1024]{1,0:T(8,128)(2,1)S(1)}, bf16[128,1024]{1,0:T(8,128)(2,1)S(1)}, f32[64,15]{1,0:T(8,128)S(1)}) custom-call(f32[512,2048]{1,0:T(8,128)S(1)} %get-tuple-element.469.sharp_ref, f32[8,2048]{1,0:T(8,128)S(1)} %get-tuple-element.470.soft_ref, ...), custom_call_target="tpu_custom_call" | custom-call | flops 1 | bytes 1 | tf_op jit(solution)/shard_map/late_backward/pallas_call | solution.py:609
  167.5 2.5 collective-permute-start.35
  170.0 1.9 collective-permute-done.35
  171.9 3.4 %collective-permute-done.38.refs_2_ = bf16[128,1024]{1,0:T(8,128)(2,1)S(1)} collective-permute-done((bf16[128,1024]{1,0:T(8,128)(2,1)S(1)}, bf16[128,1024]{1,0:T(8,128)(2,1)S(1)}, u32[]{:S(2)}, u32[]{:S(2)}) %collective-permute-start.38) | collective-permute-done | bytes 262176 | tf_op jit(solution)/shard_map/ppermute | solution.py:61
  179.5 3.3 %collective-permute-done.39 = f32[64,15]{1,0:T(8,128)S(1)} collective-permute-done((f32[64,15]{1,0:T(8,128)S(1)}, f32[64,15]{1,0:T(8,128)S(1)}, u32[]{:S(2)}, u32[]{:S(2)}) %collective-permute-start.39) | collective-permute-done | bytes 3872 | tf_op jit(solution)/shard_map/ppermute | solution.py:61
  182.8 1.8 collective-permute-done.40.refs_1_
  187.1 3.6 %feed_inner.1.dz_ref.dinner_ref = bf16[512,1024]{1,0:T(8,128)(2,1)S(1)} custom-call(bf16[128,1024]{1,0:T(8,128)(2,1)S(1)} %get-tuple-element.515.refs_0_, bf16[128,1024]{1,0:T(8,128)(2,1)S(1)} %collective-permute-done.40.refs_1_, bf16[128,1024]{1,0:T(8,128)(2,1)S(1)} %collective-permute-done.43.refs_2_, ...), custom_call_target="tpu_custom_call" | custom-call | flops 1 | bytes 1 | tf_op jit(solution)/shard_map/feed_inner/pallas_call | solution.py:470
  192.1 2.4 feed_back.1
  196.8 2.4 grad_down.1
  199.3 3.4 %grad_up.1 = (bf16[4,128,1280]{2,1,0:T(8,128)(2,1)S(1)}, bf16[4,128,1280]{2,1,0:T(8,128)(2,1)}) custom-call(s32[9]{0:T(128)S(1)} %pad_add_fusion.4.order_ref, bf16[512,1024]{1,0:T(8,128)(2,1)S(1)} %feed_inner.1.dz_ref.dinner_ref, bf16[128,1024]{1,0:T(8,128)(2,1)S(1)} %get-tuple-element.439.refs_0_, bf16[128,1024]{1,0:T(8,128)(2,1)S(1)} %collective-permute-done.19.refs_1_, ...), custom_call_target="tpu_custom_call" | custom-call | flops 1 | bytes 1 | tf_op jit(solution)/shard_map/grad_up/pallas_call | solution.py:767
  202.6 1.9 collective-permute-done.50.refs_3_
  204.6 2.5 collective-permute-start.56
  210.6 8.5 %collective-permute-done.51.refs_1_ = bf16[144,1024]{1,0:T(8,128)(2,1)S(1)} collective-permute-done((bf16[144,1024]{1,0:T(8,128)(2,1)S(1)}, bf16[144,1024]{1,0:T(8,128)(2,1)S(1)}, u32[]{:S(2)}, u32[]{:S(2)}) %collective-permute-start.51) | collective-permute-done | bytes 294944 | tf_op jit(solution)/shard_map/ppermute | solution.py:61
  223.2 10.8 %attend_back.3 = (f32[512,256]{1,0:T(8,128)S(1)}, f32[512,256]{1,0:T(8,128)S(1)}, bf16[512,256]{1,0:T(8,128)(2,1)S(1)}) custom-call(bf16[1024,512]{1,0:T(8,128)(2,1)S(1)} %convolution_convert_fusion.q_ref.k_ref.refs_0_.refs_1_, bf16[1024,512]{1,0:T(8,128)(2,1)S(1)} %convolution_convert_fusion.q_ref.k_ref.refs_0_.refs_1_, ...), custom_call_target="tpu_custom_call" | custom-call | flops 1 | bytes 1 | tf_op jit(solution)/shard_map/attend_back/pallas_call | solution.py:369
  240.4 4.9 %attend_back.4 = (f32[512,256]{1,0:T(8,128)S(1)}, f32[512,256]{1,0:T(8,128)S(1)}) custom-call(bf16[1024,512]{1,0:T(8,128)(2,1)S(1)} %convolution_convert_fusion.q_ref.k_ref.refs_0_.refs_1_, bf16[1024,512]{1,0:T(8,128)(2,1)S(1)} %convolution_convert_fusion.q_ref.k_ref.refs_0_.refs_1_, bf16[1024,256]{1,0:T(8,128)(2,1)S(1)} %convolution_convert_fusion.1.v_ref.refs_2_, ...), custom_call_target="tpu_custom_call" | custom-call | flops 1 | bytes 1 | tf_op jit(solution)/shard_map/attend_back/pallas_call | solution.py:369
  247.9 5.1 %attend_back.5 = (bf16[512,512]{1,0:T(8,128)(2,1)S(1)}, bf16[512,256]{1,0:T(8,128)(2,1)S(1)}) custom-call(bf16[1024,512]{1,0:T(8,128)(2,1)S(1)} %convolution_convert_fusion.q_ref.k_ref.refs_0_.refs_1_, bf16[1024,512]{1,0:T(8,128)(2,1)S(1)} %convolution_convert_fusion.q_ref.k_ref.refs_0_.refs_1_, ...), custom_call_target="tpu_custom_call" | custom-call | flops 1 | bytes 1 | tf_op jit(solution)/shard_map/attend_back/pallas_call | solution.py:369
  258.2 3.6 %collective-permute-done.60.other_low.other_high = bf16[2,1024,128]{2,1,0:T(8,128)(2,1)} collective-permute-done((bf16[2,1024,128]{2,1,0:T(8,128)(2,1)}, bf16[2,1024,128]{2,1,0:T(8,128)(2,1)}, u32[]{:S(2)}, u32[]{:S(2)}) %collective-permute-start.60) | collective-permute-done | bytes 524320 | tf_op jit(solution)/shard_map/ppermute | solution.py:61
  268.8 5.7 %collective-permute-done.58.other_low.other_high = bf16[4,528,128]{2,1,0:T(8,128)(2,1)S(1)} collective-permute-done((bf16[4,528,128]{2,1,0:T(8,128)(2,1)S(1)}, bf16[4,528,128]{2,1,0:T(8,128)(2,1)S(1)}, u32[]{:S(2)}, u32[]{:S(2)}) %collective-permute-start.58) | collective-permute-done | bytes 540704 | tf_op jit(solution)/shard_map/ppermute | solution.py:61
  276.7 2.7 collective-permute-done.65.other_low.other_high
  279.7 2.0 collective-permute-start.71
  282.4 2.0 place_rows.1
  284.7 6.9 %collective-permute-done.69.other_low.other_high = bf16[2,128,512]{2,1,0:T(8,128)(2,1)S(1)} collective-permute-done((bf16[2,128,512]{2,1,0:T(8,128)(2,1)S(1)}, bf16[2,128,512]{2,1,0:T(8,128)(2,1)S(1)}, u32[]{:S(2)}, u32[]{:S(2)}) %collective-permute-start.69) | collective-permute-done | bytes 262176 | tf_op jit(solution)/shard_map/ppermute | solution.py:61
  291.6 5.6 %collective-permute-done.71 = bf16[1,1024,128]{2,1,0:T(8,128)(2,1)} collective-permute-done((bf16[1,1024,128]{2,1,0:T(8,128)(2,1)}, bf16[1,1024,128]{2,1,0:T(8,128)(2,1)}, u32[]{:S(2)}, u32[]{:S(2)}) %collective-permute-start.71) | collective-permute-done | bytes 262176 | tf_op jit(solution)/shard_map/ppermute | solution.py:61
  297.4 2.7 collective-permute-start.68
  302.8 6.1 %collective-permute-done.70 = bf16[1,128,512]{2,1,0:T(8,128)(2,1)S(1)} collective-permute-done((bf16[1,128,512]{2,1,0:T(8,128)(2,1)S(1)}, bf16[1,128,512]{2,1,0:T(8,128)(2,1)S(1)}, u32[]{:S(2)}, u32[]{:S(2)}) %collective-permute-start.70) | collective-permute-done | bytes 131104 | tf_op jit(solution)/shard_map/ppermute | solution.py:61
  309.6 2.1 collective-permute-done.68
  (262 shorter events, 100.4 us)
Async XLA Ops:
  4.5 21.3 %collective-permute-start = (bf16[1,1,1,128,512]{4,3,2,1,0:T(8,128)(2,1)}, bf16[1,1,1,128,512]{4,3,2,1,0:T(8,128)(2,1)S(1)}, u32[]{:S(2)}, u32[]{:S(2)}) collective-permute-start(bf16[1,1,1,128,512]{4,3,2,1,0:T(8,128)(2,1)} %bitcast.93), channel_id=1, source_target_pairs={{0,16},{4,20},{8,24},{12,28},{16,0},{20,4},{24,8},{28,12},{1,17},{... | collective-permute-start | bytes 393224 | tf_op jit(solution)/shard_map/ppermute | solution.py:61
  8.6 20.2 %collective-permute-start.4 = (bf16[1,1,1,528,128]{4,3,2,1,0:T(8,128)(2,1)}, bf16[1,1,1,528,128]{4,3,2,1,0:T(8,128)(2,1)S(1)}, u32[]{:S(2)}, u32[]{:S(2)}) collective-permute-start(bf16[1,1,1,528,128]{4,3,2,1,0:T(8,128)(2,1)} %bitcast.91), channel_id=1, source_target_pairs={{0,16},{4,20},{8,24},{12,28},{16,0},{20,4},{24,8},{28,12},{1,17},{... | collective-permute-start | bytes 405512 | tf_op jit(solution)/shard_map/ppermute | solution.py:61
  8.6 21.4 %collective-permute-start.3 = (bf16[1,128,1024]{2,1,0:T(8,128)(2,1)}, bf16[1,128,1024]{2,1,0:T(8,128)(2,1)}, u32[]{:S(2)}, u32[]{:S(2)}) collective-permute-start(bf16[1,128,1024]{2,1,0:T(8,128)(2,1)} %bitcast.72), channel_id=1, source_target_pairs={{0,4},{4,0},{8,12},{12,8},{16,20},{20,16},{24,28},{28,24},{1,5},{5... | collective-permute-start | bytes 786440 | tf_op jit(solution)/shard_map/ppermute | solution.py:61
  10.4 21.5 %collective-permute-start.2 = (bf16[1,1,1,1024,128]{4,3,2,1,0:T(8,128)(2,1)}, bf16[1,1,1,1024,128]{4,3,2,1,0:T(8,128)(2,1)}, u32[]{:S(2)}, u32[]{:S(2)}) collective-permute-start(bf16[1,1,1,1024,128]{4,3,2,1,0:T(8,128)(2,1)} %bitcast.88), channel_id=1, source_target_pairs={{0,4},{4,0},{8,12},{12,8},{16,20},{20,16},{24,28},{28,24},{1,5},{5... | collective-permute-start | bytes 786440 | tf_op jit(solution)/shard_map/ppermute | solution.py:61
  10.7 24.4 %collective-permute-start.5 = (bf16[1,1,1,128,1280]{4,3,2,1,0:T(8,128)(2,1)}, bf16[1,1,1,128,1280]{4,3,2,1,0:T(8,128)(2,1)S(1)}, u32[]{:S(2)}, u32[]{:S(2)}) collective-permute-start(bf16[1,1,1,128,1280]{4,3,2,1,0:T(8,128)(2,1)} %bitcast.86), channel_id=1, source_target_pairs={{0,16},{4,20},{8,24},{12,28},{16,0},{20,4},{24,8},{28,12},{1,17},{... | collective-permute-start | bytes 983048 | tf_op jit(solution)/shard_map/ppermute | solution.py:61
  26.9 13.8 %collective-permute-start.1 = (bf16[2,1,1,128,512]{4,3,2,1,0:T(8,128)(2,1)S(1)}, bf16[2,1,1,128,512]{4,3,2,1,0:T(8,128)(2,1)S(1)}, u32[]{:S(2)}, u32[]{:S(2)}) collective-permute-start(bf16[2,1,1,128,512]{4,3,2,1,0:T(8,128)(2,1)S(1)} %maximum_select_fusion.11), channel_id=1, source_target_pairs={{0,8},{4,12},{8,0},{12,4},{16,24},{20,28},{24,16},{28,20},{1,9},{5... | collective-permute-start | bytes 786440 | tf_op jit(solution)/shard_map/ppermute | solution.py:61
  29.8 16.6 %collective-permute-start.9 = (bf16[2,1,1,528,128]{4,3,2,1,0:T(8,128)(2,1)S(1)}, bf16[2,1,1,528,128]{4,3,2,1,0:T(8,128)(2,1)S(1)}, u32[]{:S(2)}, u32[]{:S(2)}) collective-permute-start(bf16[2,1,1,528,128]{4,3,2,1,0:T(8,128)(2,1)S(1)} %maximum_select_fusion.10), channel_id=1, source_target_pairs={{0,8},{4,12},{8,0},{12,4},{16,24},{20,28},{24,16},{28,20},{1,9},{5... | collective-permute-start | bytes 811016 | tf_op jit(solution)/shard_map/ppermute | solution.py:61
  30.0 17.3 %collective-permute-start.8 = (bf16[1,128,1024]{2,1,0:T(8,128)(2,1)}, bf16[1,128,1024]{2,1,0:T(8,128)(2,1)}, u32[]{:S(2)}, u32[]{:S(2)}) collective-permute-start(bf16[1,128,1024]{2,1,0:T(8,128)(2,1)} %collective-permute-done.3), channel_id=1, source_target_pairs={{0,2},{1,3},{2,0},{3,1},{4,6},{5,7},{6,4},{7,5},{8,10},{9,11},{10,... | collective-permute-start | bytes 786440 | tf_op jit(solution)/shard_map/ppermute | solution.py:61
  31.9 18.8 %collective-permute-start.10 = (bf16[1,128,1024]{2,1,0:T(8,128)(2,1)}, bf16[1,128,1024]{2,1,0:T(8,128)(2,1)}, u32[]{:S(2)}, u32[]{:S(2)}) collective-permute-start(bf16[1,128,1024]{2,1,0:T(8,128)(2,1)} %collective-permute-done.3), channel_id=1, source_target_pairs={{0,1},{1,0},{2,3},{3,2},{4,5},{5,4},{6,7},{7,6},{8,9},{9,8},{10,11... | collective-permute-start | bytes 786440 | tf_op jit(solution)/shard_map/ppermute | solution.py:61
  35.1 29.8 %collective-permute-start.7 = (bf16[2,1,1,128,1280]{4,3,2,1,0:T(8,128)(2,1)S(1)}, bf16[2,1,1,128,1280]{4,3,2,1,0:T(8,128)(2,1)}, u32[]{:S(2)}, u32[]{:S(2)}) collective-permute-start(bf16[2,1,1,128,1280]{4,3,2,1,0:T(8,128)(2,1)S(1)} %maximum_select_fusion.6), channel_id=1, source_target_pairs={{0,8},{4,12},{8,0},{12,4},{16,24},{20,28},{24,16},{28,20},{1,9},{5... | collective-permute-start | bytes 1966088 | tf_op jit(solution)/shard_map/ppermute | solution.py:61
  47.4 30.7 %collective-permute-start.14 = (bf16[1,1,2,1024,128]{4,3,2,1,0:T(8,128)(2,1)S(1)}, bf16[1,1,2,1024,128]{4,3,2,1,0:T(8,128)(2,1)S(1)}, u32[]{:S(2)}, u32[]{:S(2)}) collective-permute-start(bf16[1,1,2,1024,128]{4,3,2,1,0:T(8,128)(2,1)S(1)} %maximum_select_fusion.8), channel_id=1, source_target_pairs={{0,16},{4,20},{8,24},{12,28},{16,0},{20,4},{24,8},{28,12},{1,17},{... | collective-permute-start | bytes 1572872 | tf_op jit(solution)/shard_map/ppermute | solution.py:61
  49.1 17.6 %collective-permute-start.6 = (bf16[2,2,1,128,512]{4,3,2,1,0:T(8,128)(2,1)}, bf16[2,2,1,128,512]{4,3,2,1,0:T(8,128)(2,1)S(1)}, u32[]{:S(2)}, u32[]{:S(2)}) collective-permute-start(bf16[2,2,1,128,512]{4,3,2,1,0:T(8,128)(2,1)} %maximum_select_fusion.9), channel_id=1, source_target_pairs={{0,4},{4,0},{8,12},{12,8},{16,20},{20,16},{24,28},{28,24},{1,5},{5... | collective-permute-start | bytes 1572872 | tf_op jit(solution)/shard_map/ppermute | solution.py:61
  50.7 24.3 %collective-permute-start.13 = (bf16[2,2,1,528,128]{4,3,2,1,0:T(8,128)(2,1)}, bf16[2,2,1,528,128]{4,3,2,1,0:T(8,128)(2,1)S(1)}, u32[]{:S(2)}, u32[]{:S(2)}) collective-permute-start(bf16[2,2,1,528,128]{4,3,2,1,0:T(8,128)(2,1)} %maximum_select_fusion.7), channel_id=1, source_target_pairs={{0,4},{4,0},{8,12},{12,8},{16,20},{20,16},{24,28},{28,24},{1,5},{5... | collective-permute-start | bytes 1622024 | tf_op jit(solution)/shard_map/ppermute | solution.py:61
  76.4 30.2 %collective-permute-start.12 = (bf16[2,2,1,128,1280]{4,3,2,1,0:T(8,128)(2,1)S(1)}, bf16[2,2,1,128,1280]{4,3,2,1,0:T(8,128)(2,1)S(1)}, u32[]{:S(2)}, u32[]{:S(2)}) collective-permute-start(bf16[2,2,1,128,1280]{4,3,2,1,0:T(8,128)(2,1)S(1)} %maximum_select_fusion.2), channel_id=1, source_target_pairs={{0,4},{4,0},{8,12},{12,8},{16,20},{20,16},{24,28},{28,24},{1,5},{5... | collective-permute-start | bytes 3932168 | tf_op jit(solution)/shard_map/ppermute | solution.py:61
  87.6 26.3 %collective-permute-start.18 = (bf16[2,1,2,1024,128]{4,3,2,1,0:T(8,128)(2,1)S(1)}, bf16[2,1,2,1024,128]{4,3,2,1,0:T(8,128)(2,1)S(1)}, u32[]{:S(2)}, u32[]{:S(2)}) collective-permute-start(bf16[2,1,2,1024,128]{4,3,2,1,0:T(8,128)(2,1)S(1)} %maximum_select_fusion.5), channel_id=1, source_target_pairs={{0,8},{4,12},{8,0},{12,4},{16,24},{20,28},{24,16},{28,20},{1,9},{5... | collective-permute-start | bytes 3145736 | tf_op jit(solution)/shard_map/ppermute | solution.py:61
  90.3 8.6 %collective-permute-start.17 = (bf16[128,1024]{1,0:T(8,128)(2,1)S(1)}, bf16[128,1024]{1,0:T(8,128)(2,1)S(1)}, u32[]{:S(2)}, u32[]{:S(2)}) collective-permute-start(bf16[128,1024]{1,0:T(8,128)(2,1)S(1)} %fold.5), channel_id=1, source_target_pairs={{0,2},{1,3},{2,0},{3,1},{4,6},{5,7},{6,4},{7,5},{8,10},{9,11},{10,... | collective-permute-start | bytes 786440 | tf_op jit(solution)/shard_map/ppermute | solution.py:61
  107.8 9.3 %collective-permute-start.19 = (bf16[128,1024]{1,0:T(8,128)(2,1)S(1)}, bf16[128,1024]{1,0:T(8,128)(2,1)S(1)}, u32[]{:S(2)}, u32[]{:S(2)}) collective-permute-start(bf16[128,1024]{1,0:T(8,128)(2,1)S(1)} %get-tuple-element.439.refs_0_), channel_id=1, source_target_pairs={{0,2},{1,3},{2,0},{3,1},{4,6},{5,7},{6,4},{7,5},{8,10},{9,11},{10,... | collective-permute-start | bytes 786440 | tf_op jit(solution)/shard_map/ppermute | solution.py:61
  109.3 16.4 %collective-permute-start.24 = (bf16[1024,256]{1,0:T(8,128)(2,1)S(1)}, bf16[1024,256]{1,0:T(8,128)(2,1)S(1)}, u32[]{:S(2)}, u32[]{:S(2)}) collective-permute-start(bf16[1024,256]{1,0:T(8,128)(2,1)S(1)} %slice.27.refs_5_.refs_8_), channel_id=1, source_target_pairs={{0,2},{1,3},{2,0},{3,1},{4,6},{5,7},{6,4},{7,5},{8,10},{9,11},{10,... | collective-permute-start | bytes 1572872 | tf_op jit(solution)/shard_map/ppermute | solution.py:61
  125.8 11.8 %collective-permute-start.28 = (bf16[1024,256]{1,0:T(8,128)(2,1)S(1)}, bf16[1024,256]{1,0:T(8,128)(2,1)S(1)}, u32[]{:S(2)}, u32[]{:S(2)}) collective-permute-start(bf16[1024,256]{1,0:T(8,128)(2,1)S(1)} %slice.27.refs_5_.refs_8_), channel_id=1, source_target_pairs={{0,1},{1,0},{2,3},{3,2},{4,5},{5,4},{6,7},{7,6},{8,9},{9,8},{10,11... | collective-permute-start | bytes 1572872 | tf_op jit(solution)/shard_map/ppermute | solution.py:61
  126.3 11.3 %collective-permute-start.29 = (bf16[1024,256]{1,0:T(8,128)(2,1)S(1)}, bf16[1024,256]{1,0:T(8,128)(2,1)S(1)}, u32[]{:S(2)}, u32[]{:S(2)}) collective-permute-start(bf16[1024,256]{1,0:T(8,128)(2,1)S(1)} %collective-permute-done.24.refs_6_.refs_9_), channel_id=1, source_target_pairs={{0,1},{1,0},{2,3},{3,2},{4,5},{5,4},{6,7},{7,6},{8,9},{9,8},{10,11... | collective-permute-start | bytes 1572872 | tf_op jit(solution)/shard_map/ppermute | solution.py:61
  127.8 8.4 %collective-permute-start.22 = (bf16[1,512,256]{2,1,0:T(8,128)(2,1)S(1)}, bf16[1,512,256]{2,1,0:T(8,128)(2,1)S(1)}, u32[]{:S(2)}, u32[]{:S(2)}) collective-permute-start(bf16[1,512,256]{2,1,0:T(8,128)(2,1)S(1)} %bitcast.65), channel_id=1, source_target_pairs={{0,4},{4,0},{8,12},{12,8},{16,20},{20,16},{24,28},{28,24},{1,5},{5... | collective-permute-start | bytes 786440 | tf_op jit(solution)/shard_map/ppermute | solution.py:61
  128.3 8.6 %collective-permute-start.25 = (bf16[128,1024]{1,0:T(8,128)(2,1)S(1)}, bf16[128,1024]{1,0:T(8,128)(2,1)S(1)}, u32[]{:S(2)}, u32[]{:S(2)}) collective-permute-start(bf16[128,1024]{1,0:T(8,128)(2,1)S(1)} %get-tuple-element.455), channel_id=1, source_target_pairs={{0,1},{1,0},{2,3},{3,2},{4,5},{5,4},{6,7},{7,6},{8,9},{9,8},{10,11... | collective-permute-start | bytes 786440 | tf_op jit(solution)/shard_map/ppermute | solution.py:61
  130.0 7.6 %collective-permute-start.27 = (bf16[128,1024]{1,0:T(8,128)(2,1)S(1)}, bf16[128,1024]{1,0:T(8,128)(2,1)S(1)}, u32[]{:S(2)}, u32[]{:S(2)}) collective-permute-start(bf16[128,1024]{1,0:T(8,128)(2,1)S(1)} %fold.6), channel_id=1, source_target_pairs={{0,2},{1,3},{2,0},{3,1},{4,6},{5,7},{6,4},{7,5},{8,10},{9,11},{10,... | collective-permute-start | bytes 786440 | tf_op jit(solution)/shard_map/ppermute | solution.py:61
  139.0 7.1 %collective-permute-start.30 = (bf16[128,1024]{1,0:T(8,128)(2,1)S(1)}, bf16[128,1024]{1,0:T(8,128)(2,1)S(1)}, u32[]{:S(2)}, u32[]{:S(2)}) collective-permute-start(bf16[128,1024]{1,0:T(8,128)(2,1)S(1)} %get-tuple-element.464.refs_0_), channel_id=1, source_target_pairs={{0,2},{1,3},{2,0},{3,1},{4,6},{5,7},{6,4},{7,5},{8,10},{9,11},{10,... | collective-permute-start | bytes 786440 | tf_op jit(solution)/shard_map/ppermute | solution.py:61
  147.6 17.7 %collective-permute-start.34 = (bf16[128,1024]{1,0:T(8,128)(2,1)S(1)}, bf16[128,1024]{1,0:T(8,128)(2,1)S(1)}, u32[]{:S(2)}, u32[]{:S(2)}) collective-permute-start(bf16[128,1024]{1,0:T(8,128)(2,1)S(1)} %get-tuple-element.529.refs_4_), channel_id=1, source_target_pairs={{0,2},{1,3},{2,0},{3,1},{4,6},{5,7},{6,4},{7,5},{8,10},{9,11},{10,... | collective-permute-start | bytes 786440 | tf_op jit(solution)/shard_map/ppermute | solution.py:61
  165.3 6.5 %collective-permute-start.36 = (bf16[128,1024]{1,0:T(8,128)(2,1)S(1)}, bf16[128,1024]{1,0:T(8,128)(2,1)S(1)}, u32[]{:S(2)}, u32[]{:S(2)}) collective-permute-start(bf16[128,1024]{1,0:T(8,128)(2,1)S(1)} %get-tuple-element.486), channel_id=1, source_target_pairs={{0,1},{1,0},{2,3},{3,2},{4,5},{5,4},{6,7},{7,6},{8,9},{9,8},{10,11... | collective-permute-start | bytes 786440 | tf_op jit(solution)/shard_map/ppermute | solution.py:61
  166.9 8.4 %collective-permute-start.38 = (bf16[128,1024]{1,0:T(8,128)(2,1)S(1)}, bf16[128,1024]{1,0:T(8,128)(2,1)S(1)}, u32[]{:S(2)}, u32[]{:S(2)}) collective-permute-start(bf16[128,1024]{1,0:T(8,128)(2,1)S(1)} %fold.7), channel_id=1, source_target_pairs={{0,2},{1,3},{2,0},{3,1},{4,6},{5,7},{6,4},{7,5},{8,10},{9,11},{10,... | collective-permute-start | bytes 786440 | tf_op jit(solution)/shard_map/ppermute | solution.py:61
  177.0 7.6 %collective-permute-start.40 = (bf16[128,1024]{1,0:T(8,128)(2,1)S(1)}, bf16[128,1024]{1,0:T(8,128)(2,1)S(1)}, u32[]{:S(2)}, u32[]{:S(2)}) collective-permute-start(bf16[128,1024]{1,0:T(8,128)(2,1)S(1)} %get-tuple-element.515.refs_0_), channel_id=1, source_target_pairs={{0,2},{1,3},{2,0},{3,1},{4,6},{5,7},{6,4},{7,5},{8,10},{9,11},{10,... | collective-permute-start | bytes 786440 | tf_op jit(solution)/shard_map/ppermute | solution.py:61
  196.2 8.4 %collective-permute-start.50 = (bf16[128,1024]{1,0:T(8,128)(2,1)S(1)}, bf16[128,1024]{1,0:T(8,128)(2,1)S(1)}, u32[]{:S(2)}, u32[]{:S(2)}) collective-permute-start(bf16[128,1024]{1,0:T(8,128)(2,1)S(1)} %fold.8), channel_id=1, source_target_pairs={{0,2},{1,3},{2,0},{3,1},{4,6},{5,7},{6,4},{7,5},{8,10},{9,11},{10,... | collective-permute-start | bytes 786440 | tf_op jit(solution)/shard_map/ppermute | solution.py:61
  204.6 40.7 %collective-permute-start.56 = (bf16[4,128,1280]{2,1,0:T(8,128)(2,1)}, bf16[4,128,1280]{2,1,0:T(8,128)(2,1)}, u32[]{:S(2)}, u32[]{:S(2)}) collective-permute-start(bf16[4,128,1280]{2,1,0:T(8,128)(2,1)} %get-tuple-element.556), channel_id=1, source_target_pairs={{0,8},{4,12},{8,0},{12,4},{16,24},{20,28},{24,16},{28,20},{1,9},{5... | collective-permute-start | bytes 3932168 | tf_op jit(solution)/shard_map/ppermute | solution.py:61
  207.1 27.1 %collective-permute-start.55 = (bf16[4,1024,128]{2,1,0:T(8,128)(2,1)S(1)}, bf16[4,1024,128]{2,1,0:T(8,128)(2,1)S(1)}, u32[]{:S(2)}, u32[]{:S(2)}) collective-permute-start(bf16[4,1024,128]{2,1,0:T(8,128)(2,1)S(1)} %get-tuple-element.544), channel_id=1, source_target_pairs={{0,4},{4,0},{8,12},{12,8},{16,20},{20,16},{24,28},{28,24},{1,5},{5... | collective-permute-start | bytes 3145736 | tf_op jit(solution)/shard_map/ppermute | solution.py:61
  210.0 9.1 %collective-permute-start.51 = (bf16[144,1024]{1,0:T(8,128)(2,1)S(1)}, bf16[144,1024]{1,0:T(8,128)(2,1)S(1)}, u32[]{:S(2)}, u32[]{:S(2)}) collective-permute-start(bf16[144,1024]{1,0:T(8,128)(2,1)S(1)} %get-tuple-element.541.refs_0_), channel_id=1, source_target_pairs={{0,2},{1,3},{2,0},{3,1},{4,6},{5,7},{6,4},{7,5},{8,10},{9,11},{10,... | collective-permute-start | bytes 884744 | tf_op jit(solution)/shard_map/ppermute | solution.py:61
  210.6 8.5 %collective-permute-start.52 = (bf16[144,1024]{1,0:T(8,128)(2,1)S(1)}, bf16[144,1024]{1,0:T(8,128)(2,1)S(1)}, u32[]{:S(2)}, u32[]{:S(2)}) collective-permute-start(bf16[144,1024]{1,0:T(8,128)(2,1)S(1)} %get-tuple-element.541.refs_0_), channel_id=1, source_target_pairs={{0,1},{1,0},{2,3},{3,2},{4,5},{5,4},{6,7},{7,6},{8,9},{9,8},{10,11... | collective-permute-start | bytes 884744 | tf_op jit(solution)/shard_map/ppermute | solution.py:61
  222.2 15.1 %collective-permute-start.54 = (bf16[1,512,256]{2,1,0:T(8,128)(2,1)}, bf16[1,512,256]{2,1,0:T(8,128)(2,1)}, u32[]{:S(2)}, u32[]{:S(2)}) collective-permute-start(bf16[1,512,256]{2,1,0:T(8,128)(2,1)} %bitcast.36), channel_id=1, source_target_pairs={{0,4},{4,0},{8,12},{12,8},{16,20},{20,16},{24,28},{28,24},{1,5},{5... | collective-permute-start | bytes 786440 | tf_op jit(solution)/shard_map/ppermute | solution.py:61
  236.1 25.7 %collective-permute-start.60 = (bf16[2,1024,128]{2,1,0:T(8,128)(2,1)}, bf16[2,1024,128]{2,1,0:T(8,128)(2,1)}, u32[]{:S(2)}, u32[]{:S(2)}) collective-permute-start(bf16[2,1024,128]{2,1,0:T(8,128)(2,1)} %get-tuple-element.582), channel_id=1, source_target_pairs={{0,16},{4,20},{8,24},{12,28},{16,0},{20,4},{24,8},{28,12},{1,17},{... | collective-permute-start | bytes 1572872 | tf_op jit(solution)/shard_map/ppermute | solution.py:61
  246.9 19.2 %collective-permute-start.59 = (bf16[2,128,1280]{2,1,0:T(8,128)(2,1)S(1)}, bf16[2,128,1280]{2,1,0:T(8,128)(2,1)S(1)}, u32[]{:S(2)}, u32[]{:S(2)}) collective-permute-start(bf16[2,128,1280]{2,1,0:T(8,128)(2,1)S(1)} %get-tuple-element.580), channel_id=1, source_target_pairs={{0,4},{4,0},{8,12},{12,8},{16,20},{20,16},{24,28},{28,24},{1,5},{5... | collective-permute-start | bytes 1966088 | tf_op jit(solution)/shard_map/ppermute | solution.py:61
  257.3 17.2 %collective-permute-start.58 = (bf16[4,528,128]{2,1,0:T(8,128)(2,1)S(1)}, bf16[4,528,128]{2,1,0:T(8,128)(2,1)S(1)}, u32[]{:S(2)}, u32[]{:S(2)}) collective-permute-start(bf16[4,528,128]{2,1,0:T(8,128)(2,1)S(1)} %get-tuple-element.577), channel_id=1, source_target_pairs={{0,8},{4,12},{8,0},{12,4},{16,24},{20,28},{24,16},{28,20},{1,9},{5... | collective-permute-start | bytes 1622024 | tf_op jit(solution)/shard_map/ppermute | solution.py:61
  257.4 9.4 %collective-permute-start.61 = (bf16[128,1024]{1,0:T(8,128)(2,1)S(1)}, bf16[128,1024]{1,0:T(8,128)(2,1)S(1)}, u32[]{:S(2)}, u32[]{:S(2)}) collective-permute-start(bf16[128,1024]{1,0:T(8,128)(2,1)S(1)} %get-tuple-element.595), channel_id=1, source_target_pairs={{0,1},{1,0},{2,3},{3,2},{4,5},{5,4},{6,7},{7,6},{8,9},{9,8},{10,11... | collective-permute-start | bytes 786440 | tf_op jit(solution)/shard_map/ppermute | solution.py:61
  257.6 9.2 %collective-permute-start.62 = (bf16[128,1024]{1,0:T(8,128)(2,1)S(1)}, bf16[128,1024]{1,0:T(8,128)(2,1)S(1)}, u32[]{:S(2)}, u32[]{:S(2)}) collective-permute-start(bf16[128,1024]{1,0:T(8,128)(2,1)S(1)} %fold.9), channel_id=1, source_target_pairs={{0,2},{1,3},{2,0},{3,1},{4,6},{5,7},{6,4},{7,5},{8,10},{9,11},{10,... | collective-permute-start | bytes 786440 | tf_op jit(solution)/shard_map/ppermute | solution.py:61
  265.0 14.4 %collective-permute-start.65 = (bf16[4,128,512]{2,1,0:T(8,128)(2,1)S(1)}, bf16[4,128,512]{2,1,0:T(8,128)(2,1)S(1)}, u32[]{:S(2)}, u32[]{:S(2)}) collective-permute-start(bf16[4,128,512]{2,1,0:T(8,128)(2,1)S(1)} %get-tuple-element.603), channel_id=1, source_target_pairs={{0,4},{4,0},{8,12},{12,8},{16,20},{20,16},{24,28},{28,24},{1,5},{5... | collective-permute-start | bytes 1572872 | tf_op jit(solution)/shard_map/ppermute | solution.py:61
  267.0 7.9 %collective-permute-start.63 = (bf16[128,1024]{1,0:T(8,128)(2,1)S(1)}, bf16[128,1024]{1,0:T(8,128)(2,1)S(1)}, u32[]{:S(2)}, u32[]{:S(2)}) collective-permute-start(bf16[128,1024]{1,0:T(8,128)(2,1)S(1)} %close.1.refs_0_), channel_id=1, source_target_pairs={{0,2},{1,3},{2,0},{3,1},{4,6},{5,7},{6,4},{7,5},{8,10},{9,11},{10,... | collective-permute-start | bytes 786440 | tf_op jit(solution)/shard_map/ppermute | solution.py:61
  267.6 12.1 %collective-permute-start.66 = (bf16[128,1024]{1,0:T(8,128)(2,1)S(1)}, bf16[128,1024]{1,0:T(8,128)(2,1)S(1)}, u32[]{:S(2)}, u32[]{:S(2)}) collective-permute-start(bf16[128,1024]{1,0:T(8,128)(2,1)S(1)} %close.1.refs_0_), channel_id=1, source_target_pairs={{0,1},{1,0},{2,3},{3,2},{4,5},{5,4},{6,7},{7,6},{8,9},{9,8},{10,11... | collective-permute-start | bytes 786440 | tf_op jit(solution)/shard_map/ppermute | solution.py:61
  267.6 24.0 %collective-permute-start.72 = (bf16[1,128,1280]{2,1,0:T(8,128)(2,1)}, bf16[1,128,1280]{2,1,0:T(8,128)(2,1)S(1)}, u32[]{:S(2)}, u32[]{:S(2)}) collective-permute-start(bf16[1,128,1280]{2,1,0:T(8,128)(2,1)} %get-tuple-element.621), channel_id=1, source_target_pairs={{0,16},{4,20},{8,24},{12,28},{16,0},{20,4},{24,8},{28,12},{1,17},{... | collective-permute-start | bytes 983048 | tf_op jit(solution)/shard_map/ppermute | solution.py:61
  275.7 8.9 %collective-permute-start.64 = (bf16[2,528,128]{2,1,0:T(8,128)(2,1)}, bf16[2,528,128]{2,1,0:T(8,128)(2,1)S(1)}, u32[]{:S(2)}, u32[]{:S(2)}) collective-permute-start(bf16[2,528,128]{2,1,0:T(8,128)(2,1)} %get-tuple-element.601), channel_id=1, source_target_pairs={{0,4},{4,0},{8,12},{12,8},{16,20},{20,16},{24,28},{28,24},{1,5},{5... | collective-permute-start | bytes 811016 | tf_op jit(solution)/shard_map/ppermute | solution.py:61
  279.6 11.9 %collective-permute-start.69 = (bf16[2,128,512]{2,1,0:T(8,128)(2,1)S(1)}, bf16[2,128,512]{2,1,0:T(8,128)(2,1)S(1)}, u32[]{:S(2)}, u32[]{:S(2)}) collective-permute-start(bf16[2,128,512]{2,1,0:T(8,128)(2,1)S(1)} %get-tuple-element.614), channel_id=1, source_target_pairs={{0,8},{4,12},{8,0},{12,4},{16,24},{20,28},{24,16},{28,20},{1,9},{5... | collective-permute-start | bytes 786440 | tf_op jit(solution)/shard_map/ppermute | solution.py:61
  279.7 17.5 %collective-permute-start.71 = (bf16[1,1024,128]{2,1,0:T(8,128)(2,1)}, bf16[1,1024,128]{2,1,0:T(8,128)(2,1)}, u32[]{:S(2)}, u32[]{:S(2)}) collective-permute-start(bf16[1,1024,128]{2,1,0:T(8,128)(2,1)} %get-tuple-element.620), channel_id=1, source_target_pairs={{0,8},{4,12},{8,0},{12,4},{16,24},{20,28},{24,16},{28,20},{1,9},{5... | collective-permute-start | bytes 786440 | tf_op jit(solution)/shard_map/ppermute | solution.py:61
  297.2 11.7 %collective-permute-start.70 = (bf16[1,128,512]{2,1,0:T(8,128)(2,1)S(1)}, bf16[1,128,512]{2,1,0:T(8,128)(2,1)S(1)}, u32[]{:S(2)}, u32[]{:S(2)}) collective-permute-start(bf16[1,128,512]{2,1,0:T(8,128)(2,1)S(1)} %get-tuple-element.619), channel_id=1, source_target_pairs={{0,16},{4,20},{8,24},{12,28},{16,0},{20,4},{24,8},{28,12},{1,17},{... | collective-permute-start | bytes 393224 | tf_op jit(solution)/shard_map/ppermute | solution.py:61
  297.4 14.2 %collective-permute-start.68 = (bf16[1,528,128]{2,1,0:T(8,128)(2,1)S(1)}, bf16[1,528,128]{2,1,0:T(8,128)(2,1)S(1)}, u32[]{:S(2)}, u32[]{:S(2)}) collective-permute-start(bf16[1,528,128]{2,1,0:T(8,128)(2,1)S(1)} %get-tuple-element.612), channel_id=1, source_target_pairs={{0,16},{4,20},{8,24},{12,28},{16,0},{20,4},{24,8},{28,12},{1,17},{... | collective-permute-start | bytes 405512 | tf_op jit(solution)/shard_map/ppermute | solution.py:61
  (60 other events, 342.7 us)

commit v3 on v2

--- a/solution.py
+++ b/solution.py
@@ -24,8 +24,12 @@
     return pltpu.CompilerParams(vmem_limit_bytes=mebibytes * 1024 * 1024)
 
 
+def rows_for_keys(keys):
+    return 256 if keys <= 2048 else LANES
+
+
 def room_for_keys(keys):
-    return room(min(56, 4 + keys // 128))
+    return room(min(56, 4 + keys * rows_for_keys(keys) // 16384))
 
 
 brief = pl.CostEstimate(flops=1, bytes_accessed=1, transcendentals=0)
@@ -233,9 +237,9 @@
 
 def attend_forward_kernel(q_ref, k_ref, v_ref, segq_ref, segk_ref, o_ref, stat_ref):
     tile, width = q_ref.shape
-    bias = jnp.where(segq_ref[...] == segk_ref[...], 0.0, neg_big)
+    stat = jnp.broadcast_to(segq_ref[...], (LANES, tile)).T
+    bias = jnp.where(stat[:, 0:1] == segk_ref[...], 0.0, neg_big)
     out = jnp.zeros((tile, width), full_type)
-    stat = jnp.zeros((tile, LANES), full_type)
     lane = lax.broadcasted_iota(jnp.int32, (1, LANES), 1)
     queries = q_ref[...] * jnp.asarray(0.125, low_type)
     for head in range(width // HEAD_DIM):
@@ -251,9 +255,9 @@
 
 
 def attend_forward(query_key, value_rows, seg_rows, seg_keys):
-    rows = seg_rows.shape[0]
+    rows = seg_rows.shape[1]
     keys, width = value_rows.shape
-    tile = LANES
+    tile = rows_for_keys(keys)
     return pl.pallas_call(
         attend_forward_kernel,
         grid=(rows // tile,),
@@ -261,7 +265,7 @@
             pl.BlockSpec((tile, width), lambda i: (i, 0)),
             pl.BlockSpec((keys, width), lambda i: (0, 1)),
             pl.BlockSpec((keys, width), lambda i: (0, 0)),
-            pl.BlockSpec((tile, 1), lambda i: (i, 0)),
+            pl.BlockSpec((1, tile), lambda i: (0, i)),
             pl.BlockSpec((1, keys), lambda i: (0, 0)),
         ],
         out_specs=[
@@ -275,11 +279,12 @@
     )(query_key, query_key, value_rows, seg_rows, seg_keys)
 
 
-def attend_terms(q_ref, k_ref, v_ref, do_ref, o_ref, segq_ref, segk_ref, lse_ref):
+def attend_terms(q_ref, k_ref, v_ref, do_ref, o_ref, segk_ref, lse_ref):
     tile, width = q_ref.shape
-    bias = jnp.where(segq_ref[...] == segk_ref[...], 0.0, neg_big)
     pad = jnp.zeros((LANES - lse_ref.shape[0], tile), full_type)
     lse = jnp.concatenate([lse_ref[...], pad], 0).T
+    heads = width // HEAD_DIM
+    bias = jnp.where(lse[:, heads : heads + 1] == segk_ref[...], 0.0, neg_big)
     queries = q_ref[...] * jnp.asarray(0.125, low_type)
     grads = do_ref[...]
     both = grads.astype(full_type) * o_ref[...].astype(full_type)
@@ -295,10 +300,10 @@
 
 
 def attend_back(rows_of_q, part, keys, masks, sums, wants_dq, dq_parts=()):
-    query_key, first_row, grads, attended, lse, seg_rows = rows_of_q
+    query_key, first_row, grads, attended, lse = rows_of_q
     value_rows, seg_keys, own = masks
     width = value_rows.shape[1]
-    tile = LANES
+    tile = rows_for_keys(keys)
     parts_of = 1 if part is None else 2
     steps = grads.shape[0] // tile // parts_of
     shift = steps if part == 1 else 0
@@ -306,7 +311,7 @@
     closing = len(dq_parts) > 0
 
     def kernel(*refs):
-        base, refs = refs[:8], refs[8:]
+        base, refs = refs[:7], refs[7:]
         q_ref, k_ref = base[:2]
         before, refs = (refs[:2], refs[2:]) if sums else (None, refs)
         parts, refs = refs[: len(dq_parts)], refs[len(dq_parts) :]
@@ -347,11 +352,10 @@
         pl.BlockSpec((keys, width), lambda i: (0, 0)),
         tile_rows,
         tile_rows,
-        pl.BlockSpec((tile, 1), lambda i: (shift + i, 0)),
         pl.BlockSpec((1, keys), lambda i: (0, 0)),
         pl.BlockSpec((8, tile), lambda i: (0, shift + i)),
     ]
-    args = [query_key, query_key, value_rows, grads, attended, seg_rows, seg_keys, lse]
+    args = [query_key, query_key, value_rows, grads, attended, seg_keys, lse]
     if sums:
         in_specs, args = in_specs + [held, held], args + list(sums)
     in_specs = in_specs + [whole_block(each.shape) for each in dq_parts]
@@ -387,11 +391,22 @@
     return jnp.concatenate([ref[...] for ref in refs], axis=0)
 
 
+def gather_blocks(block_refs, rows):
+    @pl.when(pl.program_id(0) == 0)
+    def _():
+        span = block_refs[0].shape[0]
+        for at, ref in enumerate(block_refs):
+            rows[at * span : (at + 1) * span, :] = ref[...]
+
+
 def feed_up_kernel(*refs):
-    *row_refs, up_ref, g_ref, slope_ref = refs
-    for at, ref in enumerate(row_refs):
-        place = pl.ds(at * ref.shape[0], ref.shape[0])
-        inner = low_dot(ref[...], up_ref[...])
+    *row_refs, up_ref, g_ref, slope_ref, rows = refs
+    gather_blocks(row_refs, rows)
+    whole = low_dot(rows[...], up_ref[...])
+    span = row_refs[0].shape[0]
+    for at in range(len(row_refs)):
+        place = pl.ds(at * span, span)
+        inner = whole[at * span : (at + 1) * span]
         normal = 0.5 * (1.0 + lax.erf(inner * 0.7071067811865476))
         g_ref[place, :] = (inner * normal).astype(low_type)
         slope = normal + inner * jnp.exp(-0.5 * inner * inner) * 0.3989422804014327
@@ -409,6 +424,7 @@
         + [pl.BlockSpec((width, tile), lambda i: (0, i))],
         out_specs=[pl.BlockSpec((rows, tile), lambda i: (0, i))] * 2,
         out_shape=[shape_of((rows, units))] * 2,
+        scratch_shapes=[pltpu.VMEM((rows, width), low_type)],
         compiler_params=room(10),
         cost_estimate=brief,
         name="feed_up",
@@ -454,12 +470,10 @@
 
 
 def feed_inner_kernel(*refs):
-    *row_refs, down_ref, slope_ref, dz_ref = refs
-    weight = lanes_of(down_ref)
-    for at, ref in enumerate(row_refs):
-        place = pl.ds(at * ref.shape[0], ref.shape[0])
-        dactive = low_dot(ref[...], weight, contract_cols)
-        dz_ref[place, :] = (dactive * slope_ref[place, :].astype(full_type)).astype(low_type)
+    *row_refs, down_ref, slope_ref, dz_ref, rows = refs
+    gather_blocks(row_refs, rows)
+    dactive = low_dot(rows[...], lanes_of(down_ref), contract_cols)
+    dz_ref[...] = (dactive * slope_ref[...].astype(full_type)).astype(low_type)
 
 
 def feed_inner(blocks, w_down, slope):
@@ -477,6 +491,7 @@
         ],
         out_specs=pl.BlockSpec((rows, tile), lambda i: (0, i)),
         out_shape=shape_of((rows, units)),
+        scratch_shapes=[pltpu.VMEM((rows, width), low_type)],
         compiler_params=room(10),
         cost_estimate=brief,
         name="feed_inner",
@@ -510,13 +525,15 @@
 
 
 def late_forward_kernel(*refs):
-    *e_refs, q_ref, live_ref, sharp_ref, soft_ref = refs
+    *e_refs, q_ref, live_ref, sharp_ref, soft_ref, e_rows = refs
+    gather_blocks(e_refs, e_rows)
     blocks = soft_ref.shape[0]
     per = blocks // len(e_refs)
-    for at, e_ref in enumerate(e_refs):
-        rows = e_ref.shape[0]
+    whole = low_dot(e_rows[...], q_ref[...], contract_cols)
+    rows = e_refs[0].shape[0]
+    for at in range(len(e_refs)):
         place = pl.ds(at * rows, rows)
-        sharp = low_dot(e_ref[...], q_ref[...], contract_cols) * 2.0 + live_ref[place, :]
+        sharp = whole[at * rows : (at + 1) * rows] * 2.0 + live_ref[place, :]
         sharp_ref[place, :] = sharp
         cube = sharp.reshape(per, rows // per, sharp.shape[1])
         top = jnp.max(cube, axis=1)
@@ -543,6 +560,7 @@
             pl.BlockSpec((blocks, tile), lambda i: (0, i)),
         ],
         out_shape=[shape_of((rows, count), full_type), shape_of((blocks, count), full_type)],
+        scratch_shapes=[pltpu.VMEM((rows, width), low_type)],
         compiler_params=room(14),
         cost_estimate=brief,
         name="late_forward",
@@ -604,7 +622,7 @@
     rows, count = sharp.shape
     width = queries.shape[1]
     blocks = soft.shape[0]
-    tile = 512
+    tile = min(1024, count)
     outs = blocks_of(rows, width)
     return pl.pallas_call(
         late_backward_kernel,
@@ -622,7 +640,7 @@
         + [pl.BlockSpec((tile // QLEN, NPASS), lambda i: (i, 0))],
         out_shape=outs + [shape_of((count // QLEN, NPASS), full_type)],
         scratch_shapes=[pltpu.VMEM((rows, width), full_type)],
-        compiler_params=room(16),
+        compiler_params=room(24),
         cost_estimate=brief,
         name="late_backward",
     )(sharp, soft, far, same, place, weight, queries)
@@ -752,9 +770,9 @@
     weight = jnp.concatenate([out_ref[at, 0:rows, :] for at in range(out_ref.shape[0])], axis=1)
     own = packs[0].shape[0] - SPARE
     sums = jnp.zeros((8, weight.shape[1]), full_type)
-    for at, ref in enumerate(packs):
-        do = low_dot(ref[0:own, :], weight, contract_cols)
-        do_ref[at * own : (at + 1) * own, :] = do.astype(low_type)
+    mixed = jnp.concatenate([ref[0:own, :] for ref in packs], axis=0)
+    do_ref[...] = low_dot(mixed, weight, contract_cols).astype(low_type)
+    for ref in packs:
         sums = sums + ref[own : own + SPARE, :].astype(full_type)[:8]
     sums_ref[...] = split_sums(sums[:4] + sums[4:])
 
@@ -1038,9 +1056,21 @@
     return whole_call(unproject_kernel, outs, "unproject", dqk, dvalue, w_qk, w_v)
 
 
+def fold_pair_kernel(keep_ref, got_ref, *low_refs):
+    total = keep_ref[...] + got_ref[...].astype(full_type)
+    rows = low_refs[0].shape[0]
+    for at, ref in enumerate(low_refs):
+        ref[...] = total[at * rows : (at + 1) * rows].astype(low_type)
+
+
 def close_kernel(*refs):
-    *terms, out_ref = refs
-    out_ref[...] = add_up(terms).astype(low_type)
+    *terms, low_far, high_far, out_ref = refs
+    total = add_up(terms)
+    half = low_far.shape[0]
+    for at, ref in enumerate((low_far, high_far)):
+        place = pl.ds(at * half, half)
+        part = total[at * half : (at + 1) * half] + ref[...].astype(full_type)
+        out_ref[place, :] = part.astype(low_type)
 
 
 def pack_kernel(order_ref, *refs):
@@ -1164,7 +1194,8 @@
     live_others = jnp.concatenate([ordered(live, device ^ at) for at in range(1, group_size)])
     slot_own = jnp.where(live_own == 1, seg_own, -1)
     slot_keys = jnp.concatenate([slot_own, jnp.where(live_others == 1, seg_others, -1)])
-    seg_column, seg_far, slot_row = seg_own[:, None], seg_others[:, None], slot_keys[None, :]
+    seg_row = seg_own.astype(full_type)[None, :]
+    slot_row = slot_keys.astype(full_type)[None, :]
     blocks = 2 ** (NBUCKET - 1)
     seg_block = seg_own.reshape(blocks, -1)[:, 0]
     live_bias = jnp.where(live_own == 1, 0.0, neg_big)[:, None]
@@ -1175,10 +1206,10 @@
     weight = jnp.repeat(grad_block / QLEN, QLEN, axis=1)
     same = same.astype(full_type)
     place = place / jnp.sum(same, axis=1, keepdims=True)
-    slot_own = slot_own[None, :]
-    early = (seg_column, seg_far, slot_own, slot_row, live_bias, weight, same, place)
+    slot_own = slot_own.astype(full_type)[None, :]
+    early = (seg_row, slot_own, slot_row, live_bias, weight, same, place)
     early, main = tie(early, main)
-    seg_column, seg_far, slot_own, slot_row, live_bias, weight, same, place = early
+    seg_row, slot_own, slot_row, live_bias, weight, same, place = early
     main = pack_a.step(main)
     main = pack_b.step(main)
     others, main = tie(others, main)
@@ -1213,15 +1244,11 @@
     value_rows = low_dot(hidden_all, full_b).astype(low_type)
     norm_rows = jnp.swapaxes(full_out[:, head_width : head_width + 4], 0, 1).reshape(4, width)
     norm_rows = norm_rows.astype(full_type)
-    attended, lse = attend_forward(query_key, value_rows, seg_column, slot_row)
+    attended, lse = attend_forward(query_key, value_rows, seg_row, slot_row)
     norm_rows, attended = tie(norm_rows, attended)
     parts = whole_call(mix_kernel, blocks_of(tok_rows, width), "mix", attended, full_out)
     terms = rows_scatter(parts)
-    terms = pack_u.drain(terms)
-    full_up = pack_u.value().reshape(width, -1)
     units = w_up.shape[1]
-    col_own = full_up[:, units:]
-    col_own, terms = tie(col_own, terms)
     square = shape_of((own_rows, width), full_type)
     low_square = shape_of((own_rows, width))
     narrow = shape_of((own_rows, 1), full_type)
@@ -1235,18 +1262,18 @@
     )
 
     rows_one = [normed_low, swap(normed_low, "mp", 2)]
-    rows_one = pack_d.drain(rows_one)
+    rows_one = pack_u.drain(rows_one)
+    full_up = pack_u.value().reshape(width, -1)
+    col_own = full_up[:, units:]
+    (full_up, col_own), rows_one = tie((full_up, col_own), rows_one)
     rows_one = rows_one + [swap(each, "mp", 1) for each in rows_one]
-    full_down = to_lanes(pack_d.value())
     far_col = swap(col_own, "mp", 2)
     active, slope = feed_up(rows_one, full_up, units)
+    active = pack_d.drain(active)
+    full_down = to_lanes(pack_d.value())
     parts = feed_down(active, full_down)
-    (far, far_lse), parts = tie((attended, lse), parts)
-    far = group_gather(far[None])[1:]
-    far_lse = group_gather(far_lse[None])[1:]
     far_col, parts = tie(far_col, parts)
     terms = rows_scatter(parts)
-    (far, far_lse), terms = tie((far, far_lse), terms)
     col_blocks = [col_own, far_col]
     col_blocks = col_blocks + [swap(each, "mp", 1) for each in col_blocks]
     normed_two_low, unit_two, scale_two, embedded, embed_low, inv_length = ordered_call(
@@ -1261,10 +1288,14 @@
         *col_blocks,
     )
 
+    (far, far_lse), embed_low = tie((attended, lse), embed_low)
+    far = group_gather(far[None])[1:]
+    far_lse = group_gather(far_lse[None])[1:]
     e_blocks = rows_gather(embed_low)
     two_low, e_blocks = tie(normed_two_low, e_blocks)
     far_two = swap(two_low, "mp", 2)
     sharp, soft_block = late_forward(e_blocks, queries, live_bias, blocks)
+    (far, far_lse), soft_block = tie((far, far_lse), soft_block)
     soft_far = group_gather(soft_block[None])[1:]
     *parts, scores = late_backward(
         sharp, soft_block, soft_far, same, place, weight, queries
@@ -1314,9 +1345,9 @@
     du_blocks = [du_own, du_far]
     du_blocks = du_blocks + [swap(each, "mp", 1) for each in du_blocks]
     low = rows_fold([parts[1], got_far])
-    (active, dinner), low = tie((active, dinner), low)
+    (active, dinner, got), low = tie((active, dinner, got), low)
     far_low = swap(low, "mp", 2)
-    grad_d = Scatter(*grad_down(active, dresid_blocks, turned), "dp", turned)
+    grad_d = Scatter(*grad_down(active, dresid_blocks, dp_up), "dp", dp_up)
     dinner = grad_d.start(dinner)
     grad_u = Scatter(
         *grad_up(dinner, rows_one, two_blocks, du_blocks, w_colbert.shape[1], across_back),
@@ -1347,22 +1378,26 @@
         full_out,
     )
     far_grads = group_gather(dattended[None])[1:].reshape(-1, head_width)
-    own_q = (query_key, 0, dattended, attended, lse, seg_column)
+    own_q = (query_key, 0, dattended, attended, lse)
     all_keys = (value_rows, slot_row, tok_rows)
     keys = value_rows.shape[0]
     *sums, dquery = attend_back(own_q, None, keys, all_keys, None, True)
-    dquery = grad_d.step(dquery)
     far_grads, dquery = tie(far_grads, dquery)
-    far_q = (query_key, tok_rows, far_grads, far_attended, far_lse, seg_far)
+    dquery = grad_d.step(grad_u.step(dquery))
+    far_q = (query_key, tok_rows, far_grads, far_attended, far_lse)
     own_keys = (value_rows, slot_own, tok_rows)
-    sums = attend_back(far_q, 0, tok_rows, own_keys, sums, False)
-    sums = grad_u.step(sums)
-    dqk, dvalue_low = attend_back(far_q, 1, tok_rows, own_keys, sums, False, (dquery,))
+    dqk, dvalue_low = attend_back(far_q, None, tok_rows, own_keys, sums, False, (dquery,))
     parts = unproject(dqk, dvalue_low, full_a, full_b)
     got_far, got = swap(parts[3], "mp", 1), swap(parts[2], "mp", 1)
-    low = rows_fold([parts[1], got_far])
+    low = whole_call(
+        fold_pair_kernel,
+        [shape_of((own_rows // 2, width))] * 2,
+        "fold_pair",
+        parts[1],
+        got_far,
+    )
     (dqk, dvalue_low), low = tie((dqk, dvalue_low), low)
-    far_low = swap(low, "mp", 2)
+    far_low = [swap(each, "mp", 2) for each in low]
     grad_b = Scatter(
         *grad_vo(hidden_own, dvalue_low, attended, packs, norm_sums, across_back),
         "dp",
@@ -1372,15 +1407,15 @@
     dqk = grad_d.step(dqk)
     grad_a = Scatter(*grad_qk(hidden_own, dqk, dp_up), "dp", dp_up)
     last = grad_a.start(parts[0])
-    last = grad_u.step(last)
-    terms = [dresid_one, last, got, far_low]
+    far_low = grad_u.step(far_low)
+    terms = [dresid_one, last, got, *far_low]
     input_own = whole_call(close_kernel, [low_square], "close", *terms)[0]
     far_own = swap(input_own, "mp", 2)
     far_own = grad_a.step(grad_b.step(far_own))
     input_blocks = [input_own, far_own]
     input_blocks = input_blocks + [swap(each, "mp", 1) for each in input_blocks]
     input_grad = place_rows(col_order, input_blocks)
-    input_grad = grad_a.step(grad_b.step(input_grad))
+    input_grad = grad_b.step(grad_a.step(input_grad))
     input_grad = grad_d.finish(grad_u.finish(input_grad))
     down_grad = grad_d.value()
     up_grad, colbert_grad = finish_pair(grad_u, units)

time: 313 us -> 294 us (0.939)
  Pallas kernels: 80.6 us -> 57.4 us
  starting transfers between devices: 58 us -> 71.4 us
  other arithmetic: 16.3 us -> 8.41 us
  local copies, waits for them, and re-layouts: 8.26 us -> 2.88 us
  waiting for transfers between devices: 146 us -> 151 us
    ppermute x73 -> x74, starting transfers between devices: 58 us -> 71.4 us  [swap(): return lax.ppermute(value, axis, pairs)]
    pallas_call x3 -> x2, Pallas kernels: 20.9 us -> 11.2 us  [attend_back(): pl.pallas_call(kernel, grid=(steps,), in_specs=in_specs, out_specs=out_sp...]
    select_n x12, other arithmetic: 10.3 us -> 3.69 us  [finish(): jnp.where(has_bit(self.axis, mask), jnp.concatenate([other, self.whole],...]
    unnamed x71 -> x17, local copies, waits for them, and re-layouts: 5.8 us -> 0.72 us
    ppermute x73 -> x74, waiting for transfers between devices: 146 us -> 151 us  [swap(): return lax.ppermute(value, axis, pairs)]
    pallas_call x1, Pallas kernels: 8.01 us -> 4.8 us  [attend_forward(): pl.pallas_call(attend_forward_kernel, grid=(rows // tile,), in_specs=[pl....]
  transfers between devices with their start and end apart: 73 -> 74, of which waited for: 43 -> 42; matrix products, arithmetic and copies ran while one was open for 6% -> 4% of each run, Pallas kernels for 23% -> 16%
where the time goes in v3:
time: 294 us
  waiting for transfers between devices  151 us (51%)
  starting transfers between devices  71.4 us (24%)
  Pallas kernels  57.4 us (20%)
  other arithmetic  8.41 us (3%)
    ppermute x74, waiting for transfers between devices, swap(): return lax.ppermute(value, axis, pairs)  151 us
    ppermute x74, starting transfers between devices, swap(): return lax.ppermute(value, axis, pairs)  71.4 us
    pallas_call x8, Pallas kernels, ordered_call(): pl.pallas_call(kernel, grid=(1,), in_specs=[pl.BlockSpec(memory_space=plt...  15.3 us
    pallas_call x2, Pallas kernels, attend_back(): pl.pallas_call(kernel, grid=(steps,), in_specs=in_specs, out_specs=out_sp...  11.2 us
  transfers between devices with their start and end apart: 74, of which 42 were waited for; matrix products, arithmetic and copies ran while one was open for 4% of the time, Pallas kernels for 16%

profile of v3, /device:TPU:0, one launch (start us, length us, event | category | flops | bytes accessed | tf_op | source)
XLA Modules:
  0.0 294.0 jit_solution(12238892788711388069)
XLA Ops:
  1.8 2.7 pack.1
  4.5 4.1 %collective-permute-start = (bf16[1,1,1,128,512]{4,3,2,1,0:T(8,128)(2,1)}, bf16[1,1,1,128,512]{4,3,2,1,0:T(8,128)(2,1)S(1)}, u32[]{:S(2)}, u32[]{:S(2)}) collective-permute-start(bf16[1,1,1,128,512]{4,3,2,1,0:T(8,128)(2,1)} %bitcast.93), channel_id=1, source_target_pairs={{0,16},{4,20},{8,24},{12,28},{16,0},{20,4},{24,8},{28,12},{1,17},{... | collective-permute-start | bytes 393224 | tf_op jit(solution)/shard_map/ppermute | solution.py:65
  10.7 2.8 collective-permute-start.5
  17.1 8.8 %collective-permute-done = bf16[1,1,1,128,512]{4,3,2,1,0:T(8,128)(2,1)S(1)} collective-permute-done((bf16[1,1,1,128,512]{4,3,2,1,0:T(8,128)(2,1)}, bf16[1,1,1,128,512]{4,3,2,1,0:T(8,128)(2,1)S(1)}, u32[]{:S(2)}, u32[]{:S(2)}) %collective-permute-start) | collective-permute-done | bytes 131104 | tf_op jit(solution)/shard_map/ppermute | solution.py:65
  27.1 1.8 collective-permute-done.4
  30.1 1.8 collective-permute-start.8
  31.9 3.1 %collective-permute-done.5 = bf16[1,1,1,128,1280]{4,3,2,1,0:T(8,128)(2,1)S(1)} collective-permute-done((bf16[1,1,1,128,1280]{4,3,2,1,0:T(8,128)(2,1)}, bf16[1,1,1,128,1280]{4,3,2,1,0:T(8,128)(2,1)S(1)}, u32[]{:S(2)}, u32[]{:S(2)}) %collective-permute-start.5) | collective-permute-done | bytes 327712 | tf_op jit(solution)/shard_map/ppermute | solution.py:65
  36.1 4.6 %collective-permute-done.1 = bf16[2,1,1,128,512]{4,3,2,1,0:T(8,128)(2,1)S(1)} collective-permute-done((bf16[2,1,1,128,512]{4,3,2,1,0:T(8,128)(2,1)S(1)}, bf16[2,1,1,128,512]{4,3,2,1,0:T(8,128)(2,1)S(1)}, u32[]{:S(2)}, u32[]{:S(2)}) %collective-permute-start.1) | collective-permute-done | bytes 262176 | tf_op jit(solution)/shard_map/ppermute | solution.py:65
  40.7 5.7 %collective-permute-done.9 = bf16[2,1,1,528,128]{4,3,2,1,0:T(8,128)(2,1)S(1)} collective-permute-done((bf16[2,1,1,528,128]{4,3,2,1,0:T(8,128)(2,1)S(1)}, bf16[2,1,1,528,128]{4,3,2,1,0:T(8,128)(2,1)S(1)}, u32[]{:S(2)}, u32[]{:S(2)}) %collective-permute-start.9) | collective-permute-done | bytes 270368 | tf_op jit(solution)/shard_map/ppermute | solution.py:65
  50.5 15.4 %collective-permute-done.7 = bf16[2,1,1,128,1280]{4,3,2,1,0:T(8,128)(2,1)S(1)} collective-permute-done((bf16[2,1,1,128,1280]{4,3,2,1,0:T(8,128)(2,1)S(1)}, bf16[2,1,1,128,1280]{4,3,2,1,0:T(8,128)(2,1)S(1)}, u32[]{:S(2)}, u32[]{:S(2)}) %collective-permute-start.7) | collective-permute-done | bytes 655392 | tf_op jit(solution)/shard_map/ppermute | solution.py:65
  67.6 6.3 %collective-permute-done.12 = bf16[2,2,1,528,128]{4,3,2,1,0:T(8,128)(2,1)S(1)} collective-permute-done((bf16[2,2,1,528,128]{4,3,2,1,0:T(8,128)(2,1)S(1)}, bf16[2,2,1,528,128]{4,3,2,1,0:T(8,128)(2,1)S(1)}, u32[]{:S(2)}, u32[]{:S(2)}) %collective-permute-start.12) | collective-permute-done | bytes 540704 | tf_op jit(solution)/shard_map/ppermute | solution.py:65
  76.7 4.8 %attend_forward.1 = (bf16[512,256]{1,0:T(8,128)(2,1)S(1)}, f32[8,512]{1,0:T(8,128)S(1)}) custom-call(bf16[1024,512]{1,0:T(8,128)(2,1)S(1)} %convolution_convert_fusion.q_ref.k_ref.refs_0_.refs_1_, bf16[1024,512]{1,0:T(8,128)(2,1)S(1)} %convolution_convert_fusion.q_ref.k_ref.refs_0_.refs_1_, bf16[1024,256]{1,0:T(8,128)(2,1)S(1)} %convolution_convert_fusion.1.v_ref.refs_2_, ...), custom_call_target="tpu_custom_call" | custom-call | flops 1 | bytes 1 | tf_op jit(solution)/shard_map/attend_forward/pallas_call | solution.py:261
  85.2 2.5 collective-permute-start.20
  87.6 4.4 %collective-permute-done.16.refs_3_ = bf16[128,1024]{1,0:T(8,128)(2,1)S(1)} collective-permute-done((bf16[128,1024]{1,0:T(8,128)(2,1)S(1)}, bf16[128,1024]{1,0:T(8,128)(2,1)S(1)}, u32[]{:S(2)}, u32[]{:S(2)}) %collective-permute-start.16) | collective-permute-done | bytes 262176 | tf_op jit(solution)/shard_map/ppermute | solution.py:65
  93.9 6.0 %collective-permute-done.18.refs_1_ = bf16[128,1024]{1,0:T(8,128)(2,1)S(1)} collective-permute-done((bf16[128,1024]{1,0:T(8,128)(2,1)S(1)}, bf16[128,1024]{1,0:T(8,128)(2,1)S(1)}, u32[]{:S(2)}, u32[]{:S(2)}) %collective-permute-start.18) | collective-permute-done | bytes 262176 | tf_op jit(solution)/shard_map/ppermute | solution.py:65
  99.9 4.5 %collective-permute-done.17 = bf16[2,2,1,128,1280]{4,3,2,1,0:T(8,128)(2,1)S(1)} collective-permute-done((bf16[2,2,1,128,1280]{4,3,2,1,0:T(8,128)(2,1)S(1)}, bf16[2,2,1,128,1280]{4,3,2,1,0:T(8,128)(2,1)S(1)}, u32[]{:S(2)}, u32[]{:S(2)}) %collective-permute-start.17) | collective-permute-done | bytes 1310752 | tf_op jit(solution)/shard_map/ppermute | solution.py:65
  108.4 2.7 feed_up.1
  111.5 1.9 feed_down.1
  113.4 3.8 %collective-permute-done.19.refs_6_.refs_9_ = bf16[1024,256]{1,0:T(8,128)(2,1)S(1)} collective-permute-done((bf16[1024,256]{1,0:T(8,128)(2,1)S(1)}, bf16[1024,256]{1,0:T(8,128)(2,1)S(1)}, u32[]{:S(2)}, u32[]{:S(2)}) %collective-permute-start.19) | collective-permute-done | bytes 524320 | tf_op jit(solution)/shard_map/ppermute | solution.py:65
  120.7 6.6 %collective-permute-done.25.refs_3_ = bf16[128,1024]{1,0:T(8,128)(2,1)S(1)} collective-permute-done((bf16[128,1024]{1,0:T(8,128)(2,1)S(1)}, bf16[128,1024]{1,0:T(8,128)(2,1)S(1)}, u32[]{:S(2)}, u32[]{:S(2)}) %collective-permute-start.25) | collective-permute-done | bytes 262176 | tf_op jit(solution)/shard_map/ppermute | solution.py:65
  130.1 6.0 %collective-permute-done.28.refs_1_ = bf16[128,1024]{1,0:T(8,128)(2,1)S(1)} collective-permute-done((bf16[128,1024]{1,0:T(8,128)(2,1)S(1)}, bf16[128,1024]{1,0:T(8,128)(2,1)S(1)}, u32[]{:S(2)}, u32[]{:S(2)}) %collective-permute-start.28) | collective-permute-done | bytes 262176 | tf_op jit(solution)/shard_map/ppermute | solution.py:65
  140.7 4.2 %late_forward.1 = (f32[512,2048]{1,0:T(8,128)S(1)}, f32[8,2048]{1,0:T(8,128)S(1)}) custom-call(bf16[128,1024]{1,0:T(8,128)(2,1)S(1)} %get-tuple-element.448.refs_0_, bf16[128,1024]{1,0:T(8,128)(2,1)S(1)} %collective-permute-done.28.refs_1_, bf16[128,1024]{1,0:T(8,128)(2,1)S(1)} %collective-permute-done.29.refs_2_, ...), custom_call_target="tpu_custom_call" | custom-call | flops 1 | bytes 1 | tf_op jit(solution)/shard_map/late_forward/pallas_call | solution.py:550
  146.8 2.7 collective-permute-done.33.far_ref
  149.5 4.1 %late_backward.1 = (f32[128,1024]{1,0:T(8,128)S(1)}, f32[128,1024]{1,0:T(8,128)S(1)}, bf16[128,1024]{1,0:T(8,128)(2,1)S(1)}, bf16[128,1024]{1,0:T(8,128)(2,1)S(1)}, f32[64,15]{1,0:T(8,128)S(1)}) custom-call(f32[512,2048]{1,0:T(8,128)S(1)} %get-tuple-element.453.sharp_ref, f32[8,2048]{1,0:T(8,128)S(1)} %get-tuple-element.457.soft_ref, ...), custom_call_target="tpu_custom_call" | custom-call | flops 1 | bytes 1 | tf_op jit(solution)/shard_map/late_backward/pallas_call | solution.py:627
  156.9 2.5 collective-permute-start.35
  159.3 1.9 collective-permute-done.35
  161.2 2.5 collective-permute-done.38.refs_2_
  168.9 3.3 %collective-permute-done.39 = f32[64,15]{1,0:T(8,128)S(1)} collective-permute-done((f32[64,15]{1,0:T(8,128)S(1)}, f32[64,15]{1,0:T(8,128)S(1)}, u32[]{:S(2)}, u32[]{:S(2)}) %collective-permute-start.39) | collective-permute-done | bytes 3872 | tf_op jit(solution)/shard_map/ppermute | solution.py:65
  176.4 2.4 feed_inner.1.dz_ref.dinner_ref
  180.5 2.2 feed_back.1
  186.2 2.4 grad_down.1
  188.7 2.3 grad_up.1
  191.0 2.0 collective-permute-done.50.refs_3_
  193.0 2.5 collective-permute-start.56
  199.0 6.2 %collective-permute-done.51.refs_1_ = bf16[144,1024]{1,0:T(8,128)(2,1)S(1)} collective-permute-done((bf16[144,1024]{1,0:T(8,128)(2,1)S(1)}, bf16[144,1024]{1,0:T(8,128)(2,1)S(1)}, u32[]{:S(2)}, u32[]{:S(2)}) %collective-permute-start.51) | collective-permute-done | bytes 294944 | tf_op jit(solution)/shard_map/ppermute | solution.py:65
  207.8 6.3 %attend_back.2 = (f32[512,256]{1,0:T(8,128)S(1)}, f32[512,256]{1,0:T(8,128)S(1)}, bf16[512,256]{1,0:T(8,128)(2,1)S(1)}) custom-call(bf16[1024,512]{1,0:T(8,128)(2,1)S(1)} %convolution_convert_fusion.q_ref.k_ref.refs_0_.refs_1_, bf16[1024,512]{1,0:T(8,128)(2,1)S(1)} %convolution_convert_fusion.q_ref.k_ref.refs_0_.refs_1_, ...), custom_call_target="tpu_custom_call" | custom-call | flops 1 | bytes 1 | tf_op jit(solution)/shard_map/attend_back/pallas_call | solution.py:373
  214.1 11.1 %collective-permute-done.54 = bf16[1,512,256]{2,1,0:T(8,128)(2,1)S(1)} collective-permute-done((bf16[1,512,256]{2,1,0:T(8,128)(2,1)S(1)}, bf16[1,512,256]{2,1,0:T(8,128)(2,1)S(1)}, u32[]{:S(2)}, u32[]{:S(2)}) %collective-permute-start.54) | collective-permute-done | bytes 262176 | tf_op jit(solution)/shard_map/ppermute | solution.py:65
  227.8 4.9 %attend_back.3 = (bf16[512,512]{1,0:T(8,128)(2,1)S(1)}, bf16[512,256]{1,0:T(8,128)(2,1)S(1)}) custom-call(bf16[1024,512]{1,0:T(8,128)(2,1)S(1)} %convolution_convert_fusion.q_ref.k_ref.refs_0_.refs_1_, bf16[1024,512]{1,0:T(8,128)(2,1)S(1)} %convolution_convert_fusion.q_ref.k_ref.refs_0_.refs_1_, ...), custom_call_target="tpu_custom_call" | custom-call | flops 1 | bytes 1 | tf_op jit(solution)/shard_map/attend_back/pallas_call | solution.py:373
  236.9 1.8 collective-permute-start.58
  245.4 3.5 %collective-permute-done.63.refs_4_ = bf16[64,1024]{1,0:T(8,128)(2,1)S(1)} collective-permute-done((bf16[64,1024]{1,0:T(8,128)(2,1)S(1)}, bf16[64,1024]{1,0:T(8,128)(2,1)S(1)}, u32[]{:S(2)}, u32[]{:S(2)}) %collective-permute-start.63) | collective-permute-done | bytes 131104 | tf_op jit(solution)/shard_map/ppermute | solution.py:65
  252.1 3.8 %collective-permute-done.64.refs_1_ = bf16[128,1024]{1,0:T(8,128)(2,1)S(1)} collective-permute-done((bf16[128,1024]{1,0:T(8,128)(2,1)S(1)}, bf16[128,1024]{1,0:T(8,128)(2,1)S(1)}, u32[]{:S(2)}, u32[]{:S(2)}) %collective-permute-start.64) | collective-permute-done | bytes 262176 | tf_op jit(solution)/shard_map/ppermute | solution.py:65
  256.6 2.2 collective-permute-start.65
  261.8 2.0 place_rows.1
  263.8 11.1 %collective-permute-done.67.other_low.other_high = bf16[2,128,512]{2,1,0:T(8,128)(2,1)S(1)} collective-permute-done((bf16[2,128,512]{2,1,0:T(8,128)(2,1)}, bf16[2,128,512]{2,1,0:T(8,128)(2,1)S(1)}, u32[]{:S(2)}, u32[]{:S(2)}) %collective-permute-start.67) | collective-permute-done | bytes 262176 | tf_op jit(solution)/shard_map/ppermute | solution.py:65
  275.1 5.0 %collective-permute-done.72 = bf16[1,1024,128]{2,1,0:T(8,128)(2,1)} collective-permute-done((bf16[1,1024,128]{2,1,0:T(8,128)(2,1)}, bf16[1,1024,128]{2,1,0:T(8,128)(2,1)}, u32[]{:S(2)}, u32[]{:S(2)}) %collective-permute-start.72) | collective-permute-done | bytes 262176 | tf_op jit(solution)/shard_map/ppermute | solution.py:65
  280.0 2.9 collective-permute-start.70
  285.6 4.8 %collective-permute-done.71 = bf16[1,128,512]{2,1,0:T(8,128)(2,1)S(1)} collective-permute-done((bf16[1,128,512]{2,1,0:T(8,128)(2,1)S(1)}, bf16[1,128,512]{2,1,0:T(8,128)(2,1)S(1)}, u32[]{:S(2)}, u32[]{:S(2)}) %collective-permute-start.71) | collective-permute-done | bytes 131104 | tf_op jit(solution)/shard_map/ppermute | solution.py:65
  291.2 2.1 collective-permute-done.70
  (208 shorter events, 89.6 us)
Async XLA Ops:
  4.5 21.4 %collective-permute-start = (bf16[1,1,1,128,512]{4,3,2,1,0:T(8,128)(2,1)}, bf16[1,1,1,128,512]{4,3,2,1,0:T(8,128)(2,1)S(1)}, u32[]{:S(2)}, u32[]{:S(2)}) collective-permute-start(bf16[1,1,1,128,512]{4,3,2,1,0:T(8,128)(2,1)} %bitcast.93), channel_id=1, source_target_pairs={{0,16},{4,20},{8,24},{12,28},{16,0},{20,4},{24,8},{28,12},{1,17},{... | collective-permute-start | bytes 393224 | tf_op jit(solution)/shard_map/ppermute | solution.py:65
  8.6 20.2 %collective-permute-start.4 = (bf16[1,1,1,528,128]{4,3,2,1,0:T(8,128)(2,1)}, bf16[1,1,1,528,128]{4,3,2,1,0:T(8,128)(2,1)S(1)}, u32[]{:S(2)}, u32[]{:S(2)}) collective-permute-start(bf16[1,1,1,528,128]{4,3,2,1,0:T(8,128)(2,1)} %bitcast.91), channel_id=1, source_target_pairs={{0,16},{4,20},{8,24},{12,28},{16,0},{20,4},{24,8},{28,12},{1,17},{... | collective-permute-start | bytes 405512 | tf_op jit(solution)/shard_map/ppermute | solution.py:65
  8.7 21.4 %collective-permute-start.3 = (bf16[1,128,1024]{2,1,0:T(8,128)(2,1)}, bf16[1,128,1024]{2,1,0:T(8,128)(2,1)S(1)}, u32[]{:S(2)}, u32[]{:S(2)}) collective-permute-start(bf16[1,128,1024]{2,1,0:T(8,128)(2,1)} %bitcast.72), channel_id=1, source_target_pairs={{0,4},{4,0},{8,12},{12,8},{16,20},{20,16},{24,28},{28,24},{1,5},{5... | collective-permute-start | bytes 786440 | tf_op jit(solution)/shard_map/ppermute | solution.py:65
  10.5 21.5 %collective-permute-start.2 = (bf16[1,1,1,1024,128]{4,3,2,1,0:T(8,128)(2,1)}, bf16[1,1,1,1024,128]{4,3,2,1,0:T(8,128)(2,1)S(1)}, u32[]{:S(2)}, u32[]{:S(2)}) collective-permute-start(bf16[1,1,1,1024,128]{4,3,2,1,0:T(8,128)(2,1)} %bitcast.85), channel_id=1, source_target_pairs={{0,4},{4,0},{8,12},{12,8},{16,20},{20,16},{24,28},{28,24},{1,5},{5... | collective-permute-start | bytes 786440 | tf_op jit(solution)/shard_map/ppermute | solution.py:65
  10.7 24.4 %collective-permute-start.5 = (bf16[1,1,1,128,1280]{4,3,2,1,0:T(8,128)(2,1)}, bf16[1,1,1,128,1280]{4,3,2,1,0:T(8,128)(2,1)S(1)}, u32[]{:S(2)}, u32[]{:S(2)}) collective-permute-start(bf16[1,1,1,128,1280]{4,3,2,1,0:T(8,128)(2,1)} %bitcast.83), channel_id=1, source_target_pairs={{0,16},{4,20},{8,24},{12,28},{16,0},{20,4},{24,8},{28,12},{1,17},{... | collective-permute-start | bytes 983048 | tf_op jit(solution)/shard_map/ppermute | solution.py:65
  26.9 13.8 %collective-permute-start.1 = (bf16[2,1,1,128,512]{4,3,2,1,0:T(8,128)(2,1)S(1)}, bf16[2,1,1,128,512]{4,3,2,1,0:T(8,128)(2,1)S(1)}, u32[]{:S(2)}, u32[]{:S(2)}) collective-permute-start(bf16[2,1,1,128,512]{4,3,2,1,0:T(8,128)(2,1)S(1)} %maximum_select_fusion.11), channel_id=1, source_target_pairs={{0,8},{4,12},{8,0},{12,4},{16,24},{20,28},{24,16},{28,20},{1,9},{5... | collective-permute-start | bytes 786440 | tf_op jit(solution)/shard_map/ppermute | solution.py:65
  29.9 16.6 %collective-permute-start.9 = (bf16[2,1,1,528,128]{4,3,2,1,0:T(8,128)(2,1)S(1)}, bf16[2,1,1,528,128]{4,3,2,1,0:T(8,128)(2,1)S(1)}, u32[]{:S(2)}, u32[]{:S(2)}) collective-permute-start(bf16[2,1,1,528,128]{4,3,2,1,0:T(8,128)(2,1)S(1)} %maximum_select_fusion.10), channel_id=1, source_target_pairs={{0,8},{4,12},{8,0},{12,4},{16,24},{20,28},{24,16},{28,20},{1,9},{5... | collective-permute-start | bytes 811016 | tf_op jit(solution)/shard_map/ppermute | solution.py:65
  30.1 16.4 %collective-permute-start.8 = (bf16[1,128,1024]{2,1,0:T(8,128)(2,1)S(1)}, bf16[1,128,1024]{2,1,0:T(8,128)(2,1)S(1)}, u32[]{:S(2)}, u32[]{:S(2)}) collective-permute-start(bf16[1,128,1024]{2,1,0:T(8,128)(2,1)S(1)} %collective-permute-done.3), channel_id=1, source_target_pairs={{0,2},{1,3},{2,0},{3,1},{4,6},{5,7},{6,4},{7,5},{8,10},{9,11},{10,... | collective-permute-start | bytes 786440 | tf_op jit(solution)/shard_map/ppermute | solution.py:65
  31.9 17.9 %collective-permute-start.10 = (bf16[1,128,1024]{2,1,0:T(8,128)(2,1)S(1)}, bf16[1,128,1024]{2,1,0:T(8,128)(2,1)S(1)}, u32[]{:S(2)}, u32[]{:S(2)}) collective-permute-start(bf16[1,128,1024]{2,1,0:T(8,128)(2,1)S(1)} %collective-permute-done.3), channel_id=1, source_target_pairs={{0,1},{1,0},{2,3},{3,2},{4,5},{5,4},{6,7},{7,6},{8,9},{9,8},{10,11... | collective-permute-start | bytes 786440 | tf_op jit(solution)/shard_map/ppermute | solution.py:65
  35.2 30.7 %collective-permute-start.7 = (bf16[2,1,1,128,1280]{4,3,2,1,0:T(8,128)(2,1)S(1)}, bf16[2,1,1,128,1280]{4,3,2,1,0:T(8,128)(2,1)S(1)}, u32[]{:S(2)}, u32[]{:S(2)}) collective-permute-start(bf16[2,1,1,128,1280]{4,3,2,1,0:T(8,128)(2,1)S(1)} %maximum_select_fusion.6), channel_id=1, source_target_pairs={{0,8},{4,12},{8,0},{12,4},{16,24},{20,28},{24,16},{28,20},{1,9},{5... | collective-permute-start | bytes 1966088 | tf_op jit(solution)/shard_map/ppermute | solution.py:65
  46.6 27.5 %collective-permute-start.13 = (bf16[1,1,2,1024,128]{4,3,2,1,0:T(8,128)(2,1)S(1)}, bf16[1,1,2,1024,128]{4,3,2,1,0:T(8,128)(2,1)S(1)}, u32[]{:S(2)}, u32[]{:S(2)}) collective-permute-start(bf16[1,1,2,1024,128]{4,3,2,1,0:T(8,128)(2,1)S(1)} %maximum_select_fusion.8), channel_id=1, source_target_pairs={{0,16},{4,20},{8,24},{12,28},{16,0},{20,4},{24,8},{28,12},{1,17},{... | collective-permute-start | bytes 1572872 | tf_op jit(solution)/shard_map/ppermute | solution.py:65
  48.3 17.9 %collective-permute-start.6 = (bf16[2,2,1,128,512]{4,3,2,1,0:T(8,128)(2,1)S(1)}, bf16[2,2,1,128,512]{4,3,2,1,0:T(8,128)(2,1)S(1)}, u32[]{:S(2)}, u32[]{:S(2)}) collective-permute-start(bf16[2,2,1,128,512]{4,3,2,1,0:T(8,128)(2,1)S(1)} %maximum_select_fusion.9), channel_id=1, source_target_pairs={{0,4},{4,0},{8,12},{12,8},{16,20},{20,16},{24,28},{28,24},{1,5},{5... | collective-permute-start | bytes 1572872 | tf_op jit(solution)/shard_map/ppermute | solution.py:65
  49.8 24.1 %collective-permute-start.12 = (bf16[2,2,1,528,128]{4,3,2,1,0:T(8,128)(2,1)S(1)}, bf16[2,2,1,528,128]{4,3,2,1,0:T(8,128)(2,1)S(1)}, u32[]{:S(2)}, u32[]{:S(2)}) collective-permute-start(bf16[2,2,1,528,128]{4,3,2,1,0:T(8,128)(2,1)S(1)} %maximum_select_fusion.7), channel_id=1, source_target_pairs={{0,4},{4,0},{8,12},{12,8},{16,20},{20,16},{24,28},{28,24},{1,5},{5... | collective-permute-start | bytes 1622024 | tf_op jit(solution)/shard_map/ppermute | solution.py:65
  74.4 30.1 %collective-permute-start.17 = (bf16[2,2,1,128,1280]{4,3,2,1,0:T(8,128)(2,1)S(1)}, bf16[2,2,1,128,1280]{4,3,2,1,0:T(8,128)(2,1)S(1)}, u32[]{:S(2)}, u32[]{:S(2)}) collective-permute-start(bf16[2,2,1,128,1280]{4,3,2,1,0:T(8,128)(2,1)S(1)} %maximum_select_fusion.2), channel_id=1, source_target_pairs={{0,4},{4,0},{8,12},{12,8},{16,20},{20,16},{24,28},{28,24},{1,5},{5... | collective-permute-start | bytes 3932168 | tf_op jit(solution)/shard_map/ppermute | solution.py:65
  82.0 5.6 %collective-permute-start.14 = (bf16[128,1024]{1,0:T(8,128)(2,1)S(1)}, bf16[128,1024]{1,0:T(8,128)(2,1)S(1)}, u32[]{:S(2)}, u32[]{:S(2)}) collective-permute-start(bf16[128,1024]{1,0:T(8,128)(2,1)S(1)} %get-tuple-element.417), channel_id=1, source_target_pairs={{0,1},{1,0},{2,3},{3,2},{4,5},{5,4},{6,7},{7,6},{8,9},{9,8},{10,11... | collective-permute-start | bytes 786440 | tf_op jit(solution)/shard_map/ppermute | solution.py:65
  83.6 8.4 %collective-permute-start.16 = (bf16[128,1024]{1,0:T(8,128)(2,1)S(1)}, bf16[128,1024]{1,0:T(8,128)(2,1)S(1)}, u32[]{:S(2)}, u32[]{:S(2)}) collective-permute-start(bf16[128,1024]{1,0:T(8,128)(2,1)S(1)} %fold.4), channel_id=1, source_target_pairs={{0,2},{1,3},{2,0},{3,1},{4,6},{5,7},{6,4},{7,5},{8,10},{9,11},{10,... | collective-permute-start | bytes 786440 | tf_op jit(solution)/shard_map/ppermute | solution.py:65
  85.2 25.9 %collective-permute-start.20 = (bf16[2,1,2,1024,128]{4,3,2,1,0:T(8,128)(2,1)S(1)}, bf16[2,1,2,1024,128]{4,3,2,1,0:T(8,128)(2,1)S(1)}, u32[]{:S(2)}, u32[]{:S(2)}) collective-permute-start(bf16[2,1,2,1024,128]{4,3,2,1,0:T(8,128)(2,1)S(1)} %maximum_select_fusion.5), channel_id=1, source_target_pairs={{0,8},{4,12},{8,0},{12,4},{16,24},{20,28},{24,16},{28,20},{1,9},{5... | collective-permute-start | bytes 3145736 | tf_op jit(solution)/shard_map/ppermute | solution.py:65
  92.3 7.6 %collective-permute-start.18 = (bf16[128,1024]{1,0:T(8,128)(2,1)S(1)}, bf16[128,1024]{1,0:T(8,128)(2,1)S(1)}, u32[]{:S(2)}, u32[]{:S(2)}) collective-permute-start(bf16[128,1024]{1,0:T(8,128)(2,1)S(1)} %get-tuple-element.429.refs_0_), channel_id=1, source_target_pairs={{0,2},{1,3},{2,0},{3,1},{4,6},{5,7},{6,4},{7,5},{8,10},{9,11},{10,... | collective-permute-start | bytes 786440 | tf_op jit(solution)/shard_map/ppermute | solution.py:65
  104.9 12.3 %collective-permute-start.19 = (bf16[1024,256]{1,0:T(8,128)(2,1)S(1)}, bf16[1024,256]{1,0:T(8,128)(2,1)S(1)}, u32[]{:S(2)}, u32[]{:S(2)}) collective-permute-start(bf16[1024,256]{1,0:T(8,128)(2,1)S(1)} %slice.27.refs_5_.refs_8_), channel_id=1, source_target_pairs={{0,2},{1,3},{2,0},{3,1},{4,6},{5,7},{6,4},{7,5},{8,10},{9,11},{10,... | collective-permute-start | bytes 1572872 | tf_op jit(solution)/shard_map/ppermute | solution.py:65
  117.8 9.5 %collective-permute-start.27 = (bf16[1024,256]{1,0:T(8,128)(2,1)S(1)}, bf16[1024,256]{1,0:T(8,128)(2,1)S(1)}, u32[]{:S(2)}, u32[]{:S(2)}) collective-permute-start(bf16[1024,256]{1,0:T(8,128)(2,1)S(1)} %collective-permute-done.19.refs_6_.refs_9_), channel_id=1, source_target_pairs={{0,1},{1,0},{2,3},{3,2},{4,5},{5,4},{6,7},{7,6},{8,9},{9,8},{10,11... | collective-permute-start | bytes 1572872 | tf_op jit(solution)/shard_map/ppermute | solution.py:65
  118.8 8.4 %collective-permute-start.25 = (bf16[128,1024]{1,0:T(8,128)(2,1)S(1)}, bf16[128,1024]{1,0:T(8,128)(2,1)S(1)}, u32[]{:S(2)}, u32[]{:S(2)}) collective-permute-start(bf16[128,1024]{1,0:T(8,128)(2,1)S(1)} %fold.5), channel_id=1, source_target_pairs={{0,2},{1,3},{2,0},{3,1},{4,6},{5,7},{6,4},{7,5},{8,10},{9,11},{10,... | collective-permute-start | bytes 786440 | tf_op jit(solution)/shard_map/ppermute | solution.py:65
  128.6 7.6 %collective-permute-start.28 = (bf16[128,1024]{1,0:T(8,128)(2,1)S(1)}, bf16[128,1024]{1,0:T(8,128)(2,1)S(1)}, u32[]{:S(2)}, u32[]{:S(2)}) collective-permute-start(bf16[128,1024]{1,0:T(8,128)(2,1)S(1)} %get-tuple-element.448.refs_0_), channel_id=1, source_target_pairs={{0,2},{1,3},{2,0},{3,1},{4,6},{5,7},{6,4},{7,5},{8,10},{9,11},{10,... | collective-permute-start | bytes 786440 | tf_op jit(solution)/shard_map/ppermute | solution.py:65
  130.1 7.6 %collective-permute-start.29 = (bf16[128,1024]{1,0:T(8,128)(2,1)S(1)}, bf16[128,1024]{1,0:T(8,128)(2,1)S(1)}, u32[]{:S(2)}, u32[]{:S(2)}) collective-permute-start(bf16[128,1024]{1,0:T(8,128)(2,1)S(1)} %get-tuple-element.448.refs_0_), channel_id=1, source_target_pairs={{0,1},{1,0},{2,3},{3,2},{4,5},{5,4},{6,7},{7,6},{8,9},{9,8},{10,11... | collective-permute-start | bytes 786440 | tf_op jit(solution)/shard_map/ppermute | solution.py:65
  136.2 9.1 %collective-permute-start.31 = (bf16[1,512,256]{2,1,0:T(8,128)(2,1)S(1)}, bf16[1,512,256]{2,1,0:T(8,128)(2,1)S(1)}, u32[]{:S(2)}, u32[]{:S(2)}) collective-permute-start(bf16[1,512,256]{2,1,0:T(8,128)(2,1)S(1)} %bitcast.64), channel_id=1, source_target_pairs={{0,4},{4,0},{8,12},{12,8},{16,20},{20,16},{24,28},{28,24},{1,5},{5... | collective-permute-start | bytes 786440 | tf_op jit(solution)/shard_map/ppermute | solution.py:65
  137.7 15.9 %collective-permute-start.34 = (bf16[128,1024]{1,0:T(8,128)(2,1)S(1)}, bf16[128,1024]{1,0:T(8,128)(2,1)S(1)}, u32[]{:S(2)}, u32[]{:S(2)}) collective-permute-start(bf16[128,1024]{1,0:T(8,128)(2,1)S(1)} %get-tuple-element.517.refs_4_), channel_id=1, source_target_pairs={{0,2},{1,3},{2,0},{3,1},{4,6},{5,7},{6,4},{7,5},{8,10},{9,11},{10,... | collective-permute-start | bytes 786440 | tf_op jit(solution)/shard_map/ppermute | solution.py:65
  139.2 6.0 %collective-permute-start.32 = (f32[1,8,512]{2,1,0:T(8,128)S(1)}, f32[1,8,512]{2,1,0:T(8,128)S(1)}, u32[]{:S(2)}, u32[]{:S(2)}) collective-permute-start(f32[1,8,512]{2,1,0:T(8,128)S(1)} %bitcast.78), channel_id=1, source_target_pairs={{0,4},{4,0},{8,12},{12,8},{16,20},{20,16},{24,28},{28,24},{1,5},{5... | collective-permute-start | bytes 49160 | tf_op jit(solution)/shard_map/ppermute | solution.py:65
  153.7 7.5 %collective-permute-start.36 = (bf16[128,1024]{1,0:T(8,128)(2,1)S(1)}, bf16[128,1024]{1,0:T(8,128)(2,1)S(1)}, u32[]{:S(2)}, u32[]{:S(2)}) collective-permute-start(bf16[128,1024]{1,0:T(8,128)(2,1)S(1)} %get-tuple-element.473), channel_id=1, source_target_pairs={{0,1},{1,0},{2,3},{3,2},{4,5},{5,4},{6,7},{7,6},{8,9},{9,8},{10,11... | collective-permute-start | bytes 786440 | tf_op jit(solution)/shard_map/ppermute | solution.py:65
  155.3 8.4 %collective-permute-start.38 = (bf16[128,1024]{1,0:T(8,128)(2,1)S(1)}, bf16[128,1024]{1,0:T(8,128)(2,1)S(1)}, u32[]{:S(2)}, u32[]{:S(2)}) collective-permute-start(bf16[128,1024]{1,0:T(8,128)(2,1)S(1)} %fold.6), channel_id=1, source_target_pairs={{0,2},{1,3},{2,0},{3,1},{4,6},{5,7},{6,4},{7,5},{8,10},{9,11},{10,... | collective-permute-start | bytes 786440 | tf_op jit(solution)/shard_map/ppermute | solution.py:65
  165.4 7.6 %collective-permute-start.40 = (bf16[128,1024]{1,0:T(8,128)(2,1)S(1)}, bf16[128,1024]{1,0:T(8,128)(2,1)S(1)}, u32[]{:S(2)}, u32[]{:S(2)}) collective-permute-start(bf16[128,1024]{1,0:T(8,128)(2,1)S(1)} %get-tuple-element.502.refs_0_), channel_id=1, source_target_pairs={{0,2},{1,3},{2,0},{3,1},{4,6},{5,7},{6,4},{7,5},{8,10},{9,11},{10,... | collective-permute-start | bytes 786440 | tf_op jit(solution)/shard_map/ppermute | solution.py:65
  184.6 8.3 %collective-permute-start.50 = (bf16[128,1024]{1,0:T(8,128)(2,1)S(1)}, bf16[128,1024]{1,0:T(8,128)(2,1)S(1)}, u32[]{:S(2)}, u32[]{:S(2)}) collective-permute-start(bf16[128,1024]{1,0:T(8,128)(2,1)S(1)} %fold.7), channel_id=1, source_target_pairs={{0,2},{1,3},{2,0},{3,1},{4,6},{5,7},{6,4},{7,5},{8,10},{9,11},{10,... | collective-permute-start | bytes 786440 | tf_op jit(solution)/shard_map/ppermute | solution.py:65
  193.0 32.2 %collective-permute-start.56 = (bf16[4,128,1280]{2,1,0:T(8,128)(2,1)S(1)}, bf16[4,128,1280]{2,1,0:T(8,128)(2,1)S(1)}, u32[]{:S(2)}, u32[]{:S(2)}) collective-permute-start(bf16[4,128,1280]{2,1,0:T(8,128)(2,1)S(1)} %get-tuple-element.541), channel_id=1, source_target_pairs={{0,8},{4,12},{8,0},{12,4},{16,24},{20,28},{24,16},{28,20},{1,9},{5... | collective-permute-start | bytes 3932168 | tf_op jit(solution)/shard_map/ppermute | solution.py:65
  195.5 30.1 %collective-permute-start.55 = (bf16[4,1024,128]{2,1,0:T(8,128)(2,1)S(1)}, bf16[4,1024,128]{2,1,0:T(8,128)(2,1)S(1)}, u32[]{:S(2)}, u32[]{:S(2)}) collective-permute-start(bf16[4,1024,128]{2,1,0:T(8,128)(2,1)S(1)} %get-tuple-element.539), channel_id=1, source_target_pairs={{0,4},{4,0},{8,12},{12,8},{16,20},{20,16},{24,28},{28,24},{1,5},{5... | collective-permute-start | bytes 3145736 | tf_op jit(solution)/shard_map/ppermute | solution.py:65
  197.4 7.7 %collective-permute-start.51 = (bf16[144,1024]{1,0:T(8,128)(2,1)S(1)}, bf16[144,1024]{1,0:T(8,128)(2,1)S(1)}, u32[]{:S(2)}, u32[]{:S(2)}) collective-permute-start(bf16[144,1024]{1,0:T(8,128)(2,1)S(1)} %get-tuple-element.529.refs_0_), channel_id=1, source_target_pairs={{0,2},{1,3},{2,0},{3,1},{4,6},{5,7},{6,4},{7,5},{8,10},{9,11},{10,... | collective-permute-start | bytes 884744 | tf_op jit(solution)/shard_map/ppermute | solution.py:65
  199.0 6.2 %collective-permute-start.52 = (bf16[144,1024]{1,0:T(8,128)(2,1)S(1)}, bf16[144,1024]{1,0:T(8,128)(2,1)S(1)}, u32[]{:S(2)}, u32[]{:S(2)}) collective-permute-start(bf16[144,1024]{1,0:T(8,128)(2,1)S(1)} %get-tuple-element.529.refs_0_), channel_id=1, source_target_pairs={{0,1},{1,0},{2,3},{3,2},{4,5},{5,4},{6,7},{7,6},{8,9},{9,8},{10,11... | collective-permute-start | bytes 884744 | tf_op jit(solution)/shard_map/ppermute | solution.py:65
  207.2 18.0 %collective-permute-start.54 = (bf16[1,512,256]{2,1,0:T(8,128)(2,1)S(1)}, bf16[1,512,256]{2,1,0:T(8,128)(2,1)S(1)}, u32[]{:S(2)}, u32[]{:S(2)}) collective-permute-start(bf16[1,512,256]{2,1,0:T(8,128)(2,1)S(1)} %bitcast.71), channel_id=1, source_target_pairs={{0,4},{4,0},{8,12},{12,8},{16,20},{20,16},{24,28},{28,24},{1,5},{5... | collective-permute-start | bytes 786440 | tf_op jit(solution)/shard_map/ppermute | solution.py:65
  225.9 14.3 %collective-permute-start.59 = (bf16[2,1024,128]{2,1,0:T(8,128)(2,1)S(1)}, bf16[2,1024,128]{2,1,0:T(8,128)(2,1)S(1)}, u32[]{:S(2)}, u32[]{:S(2)}) collective-permute-start(bf16[2,1024,128]{2,1,0:T(8,128)(2,1)S(1)} %get-tuple-element.565), channel_id=1, source_target_pairs={{0,8},{4,12},{8,0},{12,4},{16,24},{20,28},{24,16},{28,20},{1,9},{5... | collective-permute-start | bytes 1572872 | tf_op jit(solution)/shard_map/ppermute | solution.py:65
  226.2 22.7 %collective-permute-start.61 = (bf16[2,128,1280]{2,1,0:T(8,128)(2,1)S(1)}, bf16[2,128,1280]{2,1,0:T(8,128)(2,1)S(1)}, u32[]{:S(2)}, u32[]{:S(2)}) collective-permute-start(bf16[2,128,1280]{2,1,0:T(8,128)(2,1)S(1)} %get-tuple-element.576), channel_id=1, source_target_pairs={{0,4},{4,0},{8,12},{12,8},{16,20},{20,16},{24,28},{28,24},{1,5},{5... | collective-permute-start | bytes 1966088 | tf_op jit(solution)/shard_map/ppermute | solution.py:65
  236.9 15.2 %collective-permute-start.58 = (bf16[4,528,128]{2,1,0:T(8,128)(2,1)S(1)}, bf16[4,528,128]{2,1,0:T(8,128)(2,1)S(1)}, u32[]{:S(2)}, u32[]{:S(2)}) collective-permute-start(bf16[4,528,128]{2,1,0:T(8,128)(2,1)S(1)} %get-tuple-element.562), channel_id=1, source_target_pairs={{0,8},{4,12},{8,0},{12,4},{16,24},{20,28},{24,16},{28,20},{1,9},{5... | collective-permute-start | bytes 1622024 | tf_op jit(solution)/shard_map/ppermute | solution.py:65
  240.2 8.9 %collective-permute-start.60 = (bf16[128,1024]{1,0:T(8,128)(2,1)S(1)}, bf16[128,1024]{1,0:T(8,128)(2,1)S(1)}, u32[]{:S(2)}, u32[]{:S(2)}) collective-permute-start(bf16[128,1024]{1,0:T(8,128)(2,1)S(1)} %get-tuple-element.574), channel_id=1, source_target_pairs={{0,1},{1,0},{2,3},{3,2},{4,5},{5,4},{6,7},{7,6},{8,9},{9,8},{10,11... | collective-permute-start | bytes 786440 | tf_op jit(solution)/shard_map/ppermute | solution.py:65
  242.3 16.5 %collective-permute-start.66 = (bf16[4,128,512]{2,1,0:T(8,128)(2,1)S(1)}, bf16[4,128,512]{2,1,0:T(8,128)(2,1)S(1)}, u32[]{:S(2)}, u32[]{:S(2)}) collective-permute-start(bf16[4,128,512]{2,1,0:T(8,128)(2,1)S(1)} %get-tuple-element.591), channel_id=1, source_target_pairs={{0,4},{4,0},{8,12},{12,8},{16,20},{20,16},{24,28},{28,24},{1,5},{5... | collective-permute-start | bytes 1572872 | tf_op jit(solution)/shard_map/ppermute | solution.py:65
  249.2 6.6 %collective-permute-start.64 = (bf16[128,1024]{1,0:T(8,128)(2,1)S(1)}, bf16[128,1024]{1,0:T(8,128)(2,1)S(1)}, u32[]{:S(2)}, u32[]{:S(2)}) collective-permute-start(bf16[128,1024]{1,0:T(8,128)(2,1)S(1)} %close.1.refs_0_), channel_id=1, source_target_pairs={{0,2},{1,3},{2,0},{3,1},{4,6},{5,7},{6,4},{7,5},{8,10},{9,11},{10,... | collective-permute-start | bytes 786440 | tf_op jit(solution)/shard_map/ppermute | solution.py:65
  250.8 9.0 %collective-permute-start.68 = (bf16[128,1024]{1,0:T(8,128)(2,1)S(1)}, bf16[128,1024]{1,0:T(8,128)(2,1)S(1)}, u32[]{:S(2)}, u32[]{:S(2)}) collective-permute-start(bf16[128,1024]{1,0:T(8,128)(2,1)S(1)} %close.1.refs_0_), channel_id=1, source_target_pairs={{0,1},{1,0},{2,3},{3,2},{4,5},{5,4},{6,7},{7,6},{8,9},{9,8},{10,11... | collective-permute-start | bytes 786440 | tf_op jit(solution)/shard_map/ppermute | solution.py:65
  250.8 24.3 %collective-permute-start.73 = (bf16[1,128,1280]{2,1,0:T(8,128)(2,1)S(1)}, bf16[1,128,1280]{2,1,0:T(8,128)(2,1)S(1)}, u32[]{:S(2)}, u32[]{:S(2)}) collective-permute-start(bf16[1,128,1280]{2,1,0:T(8,128)(2,1)S(1)} %get-tuple-element.609), channel_id=1, source_target_pairs={{0,16},{4,20},{8,24},{12,28},{16,0},{20,4},{24,8},{28,12},{1,17},{... | collective-permute-start | bytes 983048 | tf_op jit(solution)/shard_map/ppermute | solution.py:65
  256.6 18.4 %collective-permute-start.65 = (bf16[2,528,128]{2,1,0:T(8,128)(2,1)}, bf16[2,528,128]{2,1,0:T(8,128)(2,1)S(1)}, u32[]{:S(2)}, u32[]{:S(2)}) collective-permute-start(bf16[2,528,128]{2,1,0:T(8,128)(2,1)} %get-tuple-element.589), channel_id=1, source_target_pairs={{0,4},{4,0},{8,12},{12,8},{16,20},{20,16},{24,28},{28,24},{1,5},{5... | collective-permute-start | bytes 811016 | tf_op jit(solution)/shard_map/ppermute | solution.py:65
  259.6 15.3 %collective-permute-start.67 = (bf16[2,128,512]{2,1,0:T(8,128)(2,1)}, bf16[2,128,512]{2,1,0:T(8,128)(2,1)S(1)}, u32[]{:S(2)}, u32[]{:S(2)}) collective-permute-start(bf16[2,128,512]{2,1,0:T(8,128)(2,1)} %get-tuple-element.597), channel_id=1, source_target_pairs={{0,8},{4,12},{8,0},{12,4},{16,24},{20,28},{24,16},{28,20},{1,9},{5... | collective-permute-start | bytes 786440 | tf_op jit(solution)/shard_map/ppermute | solution.py:65
  259.8 20.2 %collective-permute-start.72 = (bf16[1,1024,128]{2,1,0:T(8,128)(2,1)}, bf16[1,1024,128]{2,1,0:T(8,128)(2,1)}, u32[]{:S(2)}, u32[]{:S(2)}) collective-permute-start(bf16[1,1024,128]{2,1,0:T(8,128)(2,1)} %get-tuple-element.608), channel_id=1, source_target_pairs={{0,16},{4,20},{8,24},{12,28},{16,0},{20,4},{24,8},{28,12},{1,17},{... | collective-permute-start | bytes 786440 | tf_op jit(solution)/shard_map/ppermute | solution.py:65
  280.0 10.4 %collective-permute-start.71 = (bf16[1,128,512]{2,1,0:T(8,128)(2,1)S(1)}, bf16[1,128,512]{2,1,0:T(8,128)(2,1)S(1)}, u32[]{:S(2)}, u32[]{:S(2)}) collective-permute-start(bf16[1,128,512]{2,1,0:T(8,128)(2,1)S(1)} %get-tuple-element.607), channel_id=1, source_target_pairs={{0,16},{4,20},{8,24},{12,28},{16,0},{20,4},{24,8},{28,12},{1,17},{... | collective-permute-start | bytes 393224 | tf_op jit(solution)/shard_map/ppermute | solution.py:65
  280.0 13.3 %collective-permute-start.70 = (bf16[1,528,128]{2,1,0:T(8,128)(2,1)S(1)}, bf16[1,528,128]{2,1,0:T(8,128)(2,1)S(1)}, u32[]{:S(2)}, u32[]{:S(2)}) collective-permute-start(bf16[1,528,128]{2,1,0:T(8,128)(2,1)S(1)} %get-tuple-element.606), channel_id=1, source_target_pairs={{0,16},{4,20},{8,24},{12,28},{16,0},{20,4},{24,8},{28,12},{1,17},{... | collective-permute-start | bytes 405512 | tf_op jit(solution)/shard_map/ppermute | solution.py:65
  (34 other events, 225.1 us)

commit v4 on v3

--- a/solution.py
+++ b/solution.py
@@ -1291,11 +1291,13 @@
     (far, far_lse), embed_low = tie((attended, lse), embed_low)
     far = group_gather(far[None])[1:]
     far_lse = group_gather(far_lse[None])[1:]
-    e_blocks = rows_gather(embed_low)
-    two_low, e_blocks = tie(normed_two_low, e_blocks)
+    far_e = swap(embed_low, "mp", 2)
+    (far, far_lse), far_e = tie((far, far_lse), far_e)
+    e_blocks = [embed_low, far_e]
+    e_blocks = e_blocks + [swap(each, "mp", 1) for each in e_blocks]
+    sharp, soft_block = late_forward(e_blocks, queries, live_bias, blocks)
+    two_low, soft_block = tie(normed_two_low, soft_block)
     far_two = swap(two_low, "mp", 2)
-    sharp, soft_block = late_forward(e_blocks, queries, live_bias, blocks)
-    (far, far_lse), soft_block = tie((far, far_lse), soft_block)
     soft_far = group_gather(soft_block[None])[1:]
     *parts, scores = late_backward(
         sharp, soft_block, soft_far, same, place, weight, queries

time: 294 us -> 292 us (level)
  starting transfers between devices: 71.4 us -> 61.5 us
  waiting for transfers between devices: 151 us -> 159 us
    ppermute x74, starting transfers between devices: 71.4 us -> 61.5 us  [swap(): return lax.ppermute(value, axis, pairs)]
    ppermute x74, waiting for transfers between devices: 151 us -> 159 us  [swap(): return lax.ppermute(value, axis, pairs)]
  transfers between devices with their start and end apart: 74 -> 74, of which waited for: 42 -> 43; matrix products, arithmetic and copies ran while one was open for 4% -> 4% of each run, Pallas kernels for 16% -> 15%
where the time goes in v4:
time: 292 us
  waiting for transfers between devices  159 us (54%)
  starting transfers between devices  61.5 us (21%)
  Pallas kernels  57.4 us (20%)
  other arithmetic  8.41 us (3%)
    ppermute x74, waiting for transfers between devices, swap(): return lax.ppermute(value, axis, pairs)  159 us
    ppermute x74, starting transfers between devices, swap(): return lax.ppermute(value, axis, pairs)  61.5 us
    pallas_call x8, Pallas kernels, ordered_call(): pl.pallas_call(kernel, grid=(1,), in_specs=[pl.BlockSpec(memory_space=plt...  15.3 us
    pallas_call x2, Pallas kernels, attend_back(): pl.pallas_call(kernel, grid=(steps,), in_specs=in_specs, out_specs=out_sp...  11.2 us
  transfers between devices with their start and end apart: 74, of which 43 were waited for; matrix products, arithmetic and copies ran while one was open for 4% of the time, Pallas kernels for 15%

profile of v4, /device:TPU:0, one launch (start us, length us, event | category | flops | bytes accessed | tf_op | source)
XLA Modules:
  0.0 292.0 jit_solution(3940842976954059659)
XLA Ops:
  1.8 2.7 pack.1
  4.5 4.1 %collective-permute-start.1 = (bf16[1,1,1,128,512]{4,3,2,1,0:T(8,128)(2,1)}, bf16[1,1,1,128,512]{4,3,2,1,0:T(8,128)(2,1)S(1)}, u32[]{:S(2)}, u32[]{:S(2)}) collective-permute-start(bf16[1,1,1,128,512]{4,3,2,1,0:T(8,128)(2,1)} %bitcast.93), channel_id=1, source_target_pairs={{0,16},{4,20},{8,24},{12,28},{16,0},{20,4},{24,8},{28,12},{1,17},{... | collective-permute-start | bytes 393224 | tf_op jit(solution)/shard_map/ppermute | solution.py:65
  10.7 2.8 collective-permute-start.6
  17.1 8.8 %collective-permute-done.1 = bf16[1,1,1,128,512]{4,3,2,1,0:T(8,128)(2,1)S(1)} collective-permute-done((bf16[1,1,1,128,512]{4,3,2,1,0:T(8,128)(2,1)}, bf16[1,1,1,128,512]{4,3,2,1,0:T(8,128)(2,1)S(1)}, u32[]{:S(2)}, u32[]{:S(2)}) %collective-permute-start.1) | collective-permute-done | bytes 131104 | tf_op jit(solution)/shard_map/ppermute | solution.py:65
  30.1 1.8 collective-permute-start.10
  31.9 3.1 %collective-permute-done.6 = bf16[1,1,1,128,1280]{4,3,2,1,0:T(8,128)(2,1)S(1)} collective-permute-done((bf16[1,1,1,128,1280]{4,3,2,1,0:T(8,128)(2,1)}, bf16[1,1,1,128,1280]{4,3,2,1,0:T(8,128)(2,1)S(1)}, u32[]{:S(2)}, u32[]{:S(2)}) %collective-permute-start.6) | collective-permute-done | bytes 327712 | tf_op jit(solution)/shard_map/ppermute | solution.py:65
  36.1 4.6 %collective-permute-done.3 = bf16[2,1,1,128,512]{4,3,2,1,0:T(8,128)(2,1)S(1)} collective-permute-done((bf16[2,1,1,128,512]{4,3,2,1,0:T(8,128)(2,1)S(1)}, bf16[2,1,1,128,512]{4,3,2,1,0:T(8,128)(2,1)S(1)}, u32[]{:S(2)}, u32[]{:S(2)}) %collective-permute-start.3) | collective-permute-done | bytes 262176 | tf_op jit(solution)/shard_map/ppermute | solution.py:65
  40.7 5.7 %collective-permute-done.2 = bf16[2,1,1,528,128]{4,3,2,1,0:T(8,128)(2,1)S(1)} collective-permute-done((bf16[2,1,1,528,128]{4,3,2,1,0:T(8,128)(2,1)S(1)}, bf16[2,1,1,528,128]{4,3,2,1,0:T(8,128)(2,1)S(1)}, u32[]{:S(2)}, u32[]{:S(2)}) %collective-permute-start.2) | collective-permute-done | bytes 270368 | tf_op jit(solution)/shard_map/ppermute | solution.py:65
  50.5 15.4 %collective-permute-done.9 = bf16[2,1,1,128,1280]{4,3,2,1,0:T(8,128)(2,1)S(1)} collective-permute-done((bf16[2,1,1,128,1280]{4,3,2,1,0:T(8,128)(2,1)S(1)}, bf16[2,1,1,128,1280]{4,3,2,1,0:T(8,128)(2,1)S(1)}, u32[]{:S(2)}, u32[]{:S(2)}) %collective-permute-start.9) | collective-permute-done | bytes 655392 | tf_op jit(solution)/shard_map/ppermute | solution.py:65
  67.6 6.3 %collective-permute-done.7 = bf16[2,2,1,528,128]{4,3,2,1,0:T(8,128)(2,1)S(1)} collective-permute-done((bf16[2,2,1,528,128]{4,3,2,1,0:T(8,128)(2,1)S(1)}, bf16[2,2,1,528,128]{4,3,2,1,0:T(8,128)(2,1)S(1)}, u32[]{:S(2)}, u32[]{:S(2)}) %collective-permute-start.7) | collective-permute-done | bytes 540704 | tf_op jit(solution)/shard_map/ppermute | solution.py:65
  76.7 4.8 %attend_forward.1 = (bf16[512,256]{1,0:T(8,128)(2,1)S(1)}, f32[8,512]{1,0:T(8,128)S(1)}) custom-call(bf16[1024,512]{1,0:T(8,128)(2,1)S(1)} %convolution_convert_fusion.q_ref.k_ref.refs_0_.refs_1_, bf16[1024,512]{1,0:T(8,128)(2,1)S(1)} %convolution_convert_fusion.q_ref.k_ref.refs_0_.refs_1_, bf16[1024,256]{1,0:T(8,128)(2,1)S(1)} %convolution_convert_fusion.1.v_ref.refs_2_, ...), custom_call_target="tpu_custom_call" | custom-call | flops 1 | bytes 1 | tf_op jit(solution)/shard_map/attend_forward/pallas_call | solution.py:261
  85.2 2.5 collective-permute-start.20
  87.6 4.4 %collective-permute-done.16.refs_3_ = bf16[128,1024]{1,0:T(8,128)(2,1)S(1)} collective-permute-done((bf16[128,1024]{1,0:T(8,128)(2,1)S(1)}, bf16[128,1024]{1,0:T(8,128)(2,1)S(1)}, u32[]{:S(2)}, u32[]{:S(2)}) %collective-permute-start.16) | collective-permute-done | bytes 262176 | tf_op jit(solution)/shard_map/ppermute | solution.py:65
  93.9 6.0 %collective-permute-done.18.refs_1_ = bf16[128,1024]{1,0:T(8,128)(2,1)S(1)} collective-permute-done((bf16[128,1024]{1,0:T(8,128)(2,1)S(1)}, bf16[128,1024]{1,0:T(8,128)(2,1)S(1)}, u32[]{:S(2)}, u32[]{:S(2)}) %collective-permute-start.18) | collective-permute-done | bytes 262176 | tf_op jit(solution)/shard_map/ppermute | solution.py:65
  99.9 4.5 %collective-permute-done.17 = bf16[2,2,1,128,1280]{4,3,2,1,0:T(8,128)(2,1)S(1)} collective-permute-done((bf16[2,2,1,128,1280]{4,3,2,1,0:T(8,128)(2,1)S(1)}, bf16[2,2,1,128,1280]{4,3,2,1,0:T(8,128)(2,1)S(1)}, u32[]{:S(2)}, u32[]{:S(2)}) %collective-permute-start.17) | collective-permute-done | bytes 1310752 | tf_op jit(solution)/shard_map/ppermute | solution.py:65
  108.4 2.7 feed_up.1
  111.5 1.9 feed_down.1
  113.4 3.8 %collective-permute-done.19.refs_6_.refs_9_ = bf16[1024,256]{1,0:T(8,128)(2,1)S(1)} collective-permute-done((bf16[1024,256]{1,0:T(8,128)(2,1)S(1)}, bf16[1024,256]{1,0:T(8,128)(2,1)S(1)}, u32[]{:S(2)}, u32[]{:S(2)}) %collective-permute-start.19) | collective-permute-done | bytes 524320 | tf_op jit(solution)/shard_map/ppermute | solution.py:65
  120.7 6.6 %collective-permute-done.25.refs_3_ = bf16[128,1024]{1,0:T(8,128)(2,1)S(1)} collective-permute-done((bf16[128,1024]{1,0:T(8,128)(2,1)S(1)}, bf16[128,1024]{1,0:T(8,128)(2,1)S(1)}, u32[]{:S(2)}, u32[]{:S(2)}) %collective-permute-start.25) | collective-permute-done | bytes 262176 | tf_op jit(solution)/shard_map/ppermute | solution.py:65
  132.2 4.4 %collective-permute-done.29 = f32[1,8,512]{2,1,0:T(8,128)S(1)} collective-permute-done((f32[1,8,512]{2,1,0:T(8,128)S(1)}, f32[1,8,512]{2,1,0:T(8,128)S(1)}, u32[]{:S(2)}, u32[]{:S(2)}) %collective-permute-start.29) | collective-permute-done | bytes 16416 | tf_op jit(solution)/shard_map/ppermute | solution.py:65
  139.0 4.2 %late_forward.1 = (f32[512,2048]{1,0:T(8,128)S(1)}, f32[8,2048]{1,0:T(8,128)S(1)}) custom-call(bf16[128,1024]{1,0:T(8,128)(2,1)S(1)} %get-tuple-element.443.refs_0_, bf16[128,1024]{1,0:T(8,128)(2,1)S(1)} %collective-permute-done.30.refs_1_, bf16[128,1024]{1,0:T(8,128)(2,1)S(1)} %collective-permute-done.31.refs_2_, ...), custom_call_target="tpu_custom_call" | custom-call | flops 1 | bytes 1 | tf_op jit(solution)/shard_map/late_forward/pallas_call | solution.py:550
  145.3 3.6 %collective-permute-done.33.far_ref = f32[1,8,2048]{2,1,0:T(8,128)S(1)} collective-permute-done((f32[1,8,2048]{2,1,0:T(8,128)S(1)}, f32[1,8,2048]{2,1,0:T(8,128)S(1)}, u32[]{:S(2)}, u32[]{:S(2)}) %collective-permute-start.33) | collective-permute-done | bytes 65568 | tf_op jit(solution)/shard_map/ppermute | solution.py:65
  148.9 4.1 %late_backward.1 = (f32[128,1024]{1,0:T(8,128)S(1)}, f32[128,1024]{1,0:T(8,128)S(1)}, bf16[128,1024]{1,0:T(8,128)(2,1)S(1)}, bf16[128,1024]{1,0:T(8,128)(2,1)S(1)}, f32[64,15]{1,0:T(8,128)S(1)}) custom-call(f32[512,2048]{1,0:T(8,128)S(1)} %get-tuple-element.448.sharp_ref, f32[8,2048]{1,0:T(8,128)S(1)} %get-tuple-element.451.soft_ref, ...), custom_call_target="tpu_custom_call" | custom-call | flops 1 | bytes 1 | tf_op jit(solution)/shard_map/late_backward/pallas_call | solution.py:627
  155.3 2.5 collective-permute-start.35
  157.8 1.9 collective-permute-done.35
  159.7 3.4 %collective-permute-done.38.refs_2_ = bf16[128,1024]{1,0:T(8,128)(2,1)S(1)} collective-permute-done((bf16[128,1024]{1,0:T(8,128)(2,1)S(1)}, bf16[128,1024]{1,0:T(8,128)(2,1)S(1)}, u32[]{:S(2)}, u32[]{:S(2)}) %collective-permute-start.38) | collective-permute-done | bytes 262176 | tf_op jit(solution)/shard_map/ppermute | solution.py:65
  167.3 3.3 %collective-permute-done.39 = f32[64,15]{1,0:T(8,128)S(1)} collective-permute-done((f32[64,15]{1,0:T(8,128)S(1)}, f32[64,15]{1,0:T(8,128)S(1)}, u32[]{:S(2)}, u32[]{:S(2)}) %collective-permute-start.39) | collective-permute-done | bytes 3872 | tf_op jit(solution)/shard_map/ppermute | solution.py:65
  170.6 1.8 collective-permute-done.40.refs_1_
  174.9 2.4 feed_inner.1.dz_ref.dinner_ref
  177.3 2.6 collective-permute-done.45.refs_9_
  179.9 2.2 feed_back.1
  184.7 2.4 grad_down.1
  187.1 2.3 grad_up.1
  189.5 3.0 %collective-permute-done.50.refs_3_ = bf16[128,1024]{1,0:T(8,128)(2,1)S(1)} collective-permute-done((bf16[128,1024]{1,0:T(8,128)(2,1)S(1)}, bf16[128,1024]{1,0:T(8,128)(2,1)S(1)}, u32[]{:S(2)}, u32[]{:S(2)}) %collective-permute-start.50) | collective-permute-done | bytes 262176 | tf_op jit(solution)/shard_map/ppermute | solution.py:65
  192.4 2.5 collective-permute-start.56
  196.6 7.1 %collective-permute-done.51.refs_1_ = bf16[144,1024]{1,0:T(8,128)(2,1)S(1)} collective-permute-done((bf16[144,1024]{1,0:T(8,128)(2,1)S(1)}, bf16[144,1024]{1,0:T(8,128)(2,1)S(1)}, u32[]{:S(2)}, u32[]{:S(2)}) %collective-permute-start.51) | collective-permute-done | bytes 294944 | tf_op jit(solution)/shard_map/ppermute | solution.py:65
  207.2 6.3 %attend_back.2 = (f32[512,256]{1,0:T(8,128)S(1)}, f32[512,256]{1,0:T(8,128)S(1)}, bf16[512,256]{1,0:T(8,128)(2,1)S(1)}) custom-call(bf16[1024,512]{1,0:T(8,128)(2,1)S(1)} %convolution_convert_fusion.q_ref.k_ref.refs_0_.refs_1_, bf16[1024,512]{1,0:T(8,128)(2,1)S(1)} %convolution_convert_fusion.q_ref.k_ref.refs_0_.refs_1_, ...), custom_call_target="tpu_custom_call" | custom-call | flops 1 | bytes 1 | tf_op jit(solution)/shard_map/attend_back/pallas_call | solution.py:373
  213.5 11.2 %collective-permute-done.54 = bf16[1,512,256]{2,1,0:T(8,128)(2,1)S(1)} collective-permute-done((bf16[1,512,256]{2,1,0:T(8,128)(2,1)S(1)}, bf16[1,512,256]{2,1,0:T(8,128)(2,1)S(1)}, u32[]{:S(2)}, u32[]{:S(2)}) %collective-permute-start.54) | collective-permute-done | bytes 262176 | tf_op jit(solution)/shard_map/ppermute | solution.py:65
  226.3 4.9 %attend_back.3 = (bf16[512,512]{1,0:T(8,128)(2,1)S(1)}, bf16[512,256]{1,0:T(8,128)(2,1)S(1)}) custom-call(bf16[1024,512]{1,0:T(8,128)(2,1)S(1)} %convolution_convert_fusion.q_ref.k_ref.refs_0_.refs_1_, bf16[1024,512]{1,0:T(8,128)(2,1)S(1)} %convolution_convert_fusion.q_ref.k_ref.refs_0_.refs_1_, ...), custom_call_target="tpu_custom_call" | custom-call | flops 1 | bytes 1 | tf_op jit(solution)/shard_map/attend_back/pallas_call | solution.py:373
  235.4 1.8 collective-permute-start.58
  243.0 4.4 %collective-permute-done.63.refs_4_ = bf16[64,1024]{1,0:T(8,128)(2,1)S(1)} collective-permute-done((bf16[64,1024]{1,0:T(8,128)(2,1)S(1)}, bf16[64,1024]{1,0:T(8,128)(2,1)S(1)}, u32[]{:S(2)}, u32[]{:S(2)}) %collective-permute-start.63) | collective-permute-done | bytes 131104 | tf_op jit(solution)/shard_map/ppermute | solution.py:65
  250.2 4.4 %collective-permute-done.64.refs_1_ = bf16[128,1024]{1,0:T(8,128)(2,1)S(1)} collective-permute-done((bf16[128,1024]{1,0:T(8,128)(2,1)S(1)}, bf16[128,1024]{1,0:T(8,128)(2,1)S(1)}, u32[]{:S(2)}, u32[]{:S(2)}) %collective-permute-start.64) | collective-permute-done | bytes 262176 | tf_op jit(solution)/shard_map/ppermute | solution.py:65
  259.5 2.0 place_rows.1
  261.5 10.9 %collective-permute-done.67.other_low.other_high = bf16[2,128,512]{2,1,0:T(8,128)(2,1)S(1)} collective-permute-done((bf16[2,128,512]{2,1,0:T(8,128)(2,1)}, bf16[2,128,512]{2,1,0:T(8,128)(2,1)S(1)}, u32[]{:S(2)}, u32[]{:S(2)}) %collective-permute-start.67) | collective-permute-done | bytes 262176 | tf_op jit(solution)/shard_map/ppermute | solution.py:65
  272.6 5.4 %collective-permute-done.72 = bf16[1,1024,128]{2,1,0:T(8,128)(2,1)} collective-permute-done((bf16[1,1024,128]{2,1,0:T(8,128)(2,1)}, bf16[1,1024,128]{2,1,0:T(8,128)(2,1)}, u32[]{:S(2)}, u32[]{:S(2)}) %collective-permute-start.72) | collective-permute-done | bytes 262176 | tf_op jit(solution)/shard_map/ppermute | solution.py:65
  278.0 2.9 %collective-permute-start.70 = (bf16[1,528,128]{2,1,0:T(8,128)(2,1)S(1)}, bf16[1,528,128]{2,1,0:T(8,128)(2,1)S(1)}, u32[]{:S(2)}, u32[]{:S(2)}) collective-permute-start(bf16[1,528,128]{2,1,0:T(8,128)(2,1)S(1)} %get-tuple-element.600), channel_id=1, source_target_pairs={{0,16},{4,20},{8,24},{12,28},{16,0},{20,4},{24,8},{28,12},{1,17},{... | collective-permute-start | bytes 405512 | tf_op jit(solution)/shard_map/ppermute | solution.py:65
  283.6 4.8 %collective-permute-done.71 = bf16[1,128,512]{2,1,0:T(8,128)(2,1)S(1)} collective-permute-done((bf16[1,128,512]{2,1,0:T(8,128)(2,1)S(1)}, bf16[1,128,512]{2,1,0:T(8,128)(2,1)S(1)}, u32[]{:S(2)}, u32[]{:S(2)}) %collective-permute-start.71) | collective-permute-done | bytes 131104 | tf_op jit(solution)/shard_map/ppermute | solution.py:65
  289.2 2.1 collective-permute-done.70
  (208 shorter events, 83.3 us)
Async XLA Ops:
  4.5 21.4 %collective-permute-start.1 = (bf16[1,1,1,128,512]{4,3,2,1,0:T(8,128)(2,1)}, bf16[1,1,1,128,512]{4,3,2,1,0:T(8,128)(2,1)S(1)}, u32[]{:S(2)}, u32[]{:S(2)}) collective-permute-start(bf16[1,1,1,128,512]{4,3,2,1,0:T(8,128)(2,1)} %bitcast.93), channel_id=1, source_target_pairs={{0,16},{4,20},{8,24},{12,28},{16,0},{20,4},{24,8},{28,12},{1,17},{... | collective-permute-start | bytes 393224 | tf_op jit(solution)/shard_map/ppermute | solution.py:65
  8.6 20.2 %collective-permute-start = (bf16[1,1,1,528,128]{4,3,2,1,0:T(8,128)(2,1)}, bf16[1,1,1,528,128]{4,3,2,1,0:T(8,128)(2,1)S(1)}, u32[]{:S(2)}, u32[]{:S(2)}) collective-permute-start(bf16[1,1,1,528,128]{4,3,2,1,0:T(8,128)(2,1)} %bitcast.91), channel_id=1, source_target_pairs={{0,16},{4,20},{8,24},{12,28},{16,0},{20,4},{24,8},{28,12},{1,17},{... | collective-permute-start | bytes 405512 | tf_op jit(solution)/shard_map/ppermute | solution.py:65
  8.7 21.4 %collective-permute-start.5 = (bf16[1,128,1024]{2,1,0:T(8,128)(2,1)}, bf16[1,128,1024]{2,1,0:T(8,128)(2,1)S(1)}, u32[]{:S(2)}, u32[]{:S(2)}) collective-permute-start(bf16[1,128,1024]{2,1,0:T(8,128)(2,1)} %bitcast.72), channel_id=1, source_target_pairs={{0,4},{4,0},{8,12},{12,8},{16,20},{20,16},{24,28},{28,24},{1,5},{5... | collective-permute-start | bytes 786440 | tf_op jit(solution)/shard_map/ppermute | solution.py:65
  10.5 21.5 %collective-permute-start.4 = (bf16[1,1,1,1024,128]{4,3,2,1,0:T(8,128)(2,1)}, bf16[1,1,1,1024,128]{4,3,2,1,0:T(8,128)(2,1)S(1)}, u32[]{:S(2)}, u32[]{:S(2)}) collective-permute-start(bf16[1,1,1,1024,128]{4,3,2,1,0:T(8,128)(2,1)} %bitcast.85), channel_id=1, source_target_pairs={{0,4},{4,0},{8,12},{12,8},{16,20},{20,16},{24,28},{28,24},{1,5},{5... | collective-permute-start | bytes 786440 | tf_op jit(solution)/shard_map/ppermute | solution.py:65
  10.7 24.4 %collective-permute-start.6 = (bf16[1,1,1,128,1280]{4,3,2,1,0:T(8,128)(2,1)}, bf16[1,1,1,128,1280]{4,3,2,1,0:T(8,128)(2,1)S(1)}, u32[]{:S(2)}, u32[]{:S(2)}) collective-permute-start(bf16[1,1,1,128,1280]{4,3,2,1,0:T(8,128)(2,1)} %bitcast.83), channel_id=1, source_target_pairs={{0,16},{4,20},{8,24},{12,28},{16,0},{20,4},{24,8},{28,12},{1,17},{... | collective-permute-start | bytes 983048 | tf_op jit(solution)/shard_map/ppermute | solution.py:65
  26.9 13.8 %collective-permute-start.3 = (bf16[2,1,1,128,512]{4,3,2,1,0:T(8,128)(2,1)S(1)}, bf16[2,1,1,128,512]{4,3,2,1,0:T(8,128)(2,1)S(1)}, u32[]{:S(2)}, u32[]{:S(2)}) collective-permute-start(bf16[2,1,1,128,512]{4,3,2,1,0:T(8,128)(2,1)S(1)} %maximum_select_fusion.11), channel_id=1, source_target_pairs={{0,8},{4,12},{8,0},{12,4},{16,24},{20,28},{24,16},{28,20},{1,9},{5... | collective-permute-start | bytes 786440 | tf_op jit(solution)/shard_map/ppermute | solution.py:65
  29.9 16.6 %collective-permute-start.2 = (bf16[2,1,1,528,128]{4,3,2,1,0:T(8,128)(2,1)S(1)}, bf16[2,1,1,528,128]{4,3,2,1,0:T(8,128)(2,1)S(1)}, u32[]{:S(2)}, u32[]{:S(2)}) collective-permute-start(bf16[2,1,1,528,128]{4,3,2,1,0:T(8,128)(2,1)S(1)} %maximum_select_fusion.10), channel_id=1, source_target_pairs={{0,8},{4,12},{8,0},{12,4},{16,24},{20,28},{24,16},{28,20},{1,9},{5... | collective-permute-start | bytes 811016 | tf_op jit(solution)/shard_map/ppermute | solution.py:65
  30.1 16.4 %collective-permute-start.10 = (bf16[1,128,1024]{2,1,0:T(8,128)(2,1)S(1)}, bf16[1,128,1024]{2,1,0:T(8,128)(2,1)S(1)}, u32[]{:S(2)}, u32[]{:S(2)}) collective-permute-start(bf16[1,128,1024]{2,1,0:T(8,128)(2,1)S(1)} %collective-permute-done.5), channel_id=1, source_target_pairs={{0,2},{1,3},{2,0},{3,1},{4,6},{5,7},{6,4},{7,5},{8,10},{9,11},{10,... | collective-permute-start | bytes 786440 | tf_op jit(solution)/shard_map/ppermute | solution.py:65
  31.9 17.9 %collective-permute-start.11 = (bf16[1,128,1024]{2,1,0:T(8,128)(2,1)S(1)}, bf16[1,128,1024]{2,1,0:T(8,128)(2,1)S(1)}, u32[]{:S(2)}, u32[]{:S(2)}) collective-permute-start(bf16[1,128,1024]{2,1,0:T(8,128)(2,1)S(1)} %collective-permute-done.5), channel_id=1, source_target_pairs={{0,1},{1,0},{2,3},{3,2},{4,5},{5,4},{6,7},{7,6},{8,9},{9,8},{10,11... | collective-permute-start | bytes 786440 | tf_op jit(solution)/shard_map/ppermute | solution.py:65
  35.2 30.7 %collective-permute-start.9 = (bf16[2,1,1,128,1280]{4,3,2,1,0:T(8,128)(2,1)S(1)}, bf16[2,1,1,128,1280]{4,3,2,1,0:T(8,128)(2,1)S(1)}, u32[]{:S(2)}, u32[]{:S(2)}) collective-permute-start(bf16[2,1,1,128,1280]{4,3,2,1,0:T(8,128)(2,1)S(1)} %maximum_select_fusion.6), channel_id=1, source_target_pairs={{0,8},{4,12},{8,0},{12,4},{16,24},{20,28},{24,16},{28,20},{1,9},{5... | collective-permute-start | bytes 1966088 | tf_op jit(solution)/shard_map/ppermute | solution.py:65
  46.6 27.5 %collective-permute-start.13 = (bf16[1,1,2,1024,128]{4,3,2,1,0:T(8,128)(2,1)S(1)}, bf16[1,1,2,1024,128]{4,3,2,1,0:T(8,128)(2,1)S(1)}, u32[]{:S(2)}, u32[]{:S(2)}) collective-permute-start(bf16[1,1,2,1024,128]{4,3,2,1,0:T(8,128)(2,1)S(1)} %maximum_select_fusion.8), channel_id=1, source_target_pairs={{0,16},{4,20},{8,24},{12,28},{16,0},{20,4},{24,8},{28,12},{1,17},{... | collective-permute-start | bytes 1572872 | tf_op jit(solution)/shard_map/ppermute | solution.py:65
  48.3 17.9 %collective-permute-start.8 = (bf16[2,2,1,128,512]{4,3,2,1,0:T(8,128)(2,1)S(1)}, bf16[2,2,1,128,512]{4,3,2,1,0:T(8,128)(2,1)S(1)}, u32[]{:S(2)}, u32[]{:S(2)}) collective-permute-start(bf16[2,2,1,128,512]{4,3,2,1,0:T(8,128)(2,1)S(1)} %maximum_select_fusion.9), channel_id=1, source_target_pairs={{0,4},{4,0},{8,12},{12,8},{16,20},{20,16},{24,28},{28,24},{1,5},{5... | collective-permute-start | bytes 1572872 | tf_op jit(solution)/shard_map/ppermute | solution.py:65
  49.8 24.1 %collective-permute-start.7 = (bf16[2,2,1,528,128]{4,3,2,1,0:T(8,128)(2,1)S(1)}, bf16[2,2,1,528,128]{4,3,2,1,0:T(8,128)(2,1)S(1)}, u32[]{:S(2)}, u32[]{:S(2)}) collective-permute-start(bf16[2,2,1,528,128]{4,3,2,1,0:T(8,128)(2,1)S(1)} %maximum_select_fusion.7), channel_id=1, source_target_pairs={{0,4},{4,0},{8,12},{12,8},{16,20},{20,16},{24,28},{28,24},{1,5},{5... | collective-permute-start | bytes 1622024 | tf_op jit(solution)/shard_map/ppermute | solution.py:65
  74.4 30.1 %collective-permute-start.17 = (bf16[2,2,1,128,1280]{4,3,2,1,0:T(8,128)(2,1)S(1)}, bf16[2,2,1,128,1280]{4,3,2,1,0:T(8,128)(2,1)S(1)}, u32[]{:S(2)}, u32[]{:S(2)}) collective-permute-start(bf16[2,2,1,128,1280]{4,3,2,1,0:T(8,128)(2,1)S(1)} %maximum_select_fusion.2), channel_id=1, source_target_pairs={{0,4},{4,0},{8,12},{12,8},{16,20},{20,16},{24,28},{28,24},{1,5},{5... | collective-permute-start | bytes 3932168 | tf_op jit(solution)/shard_map/ppermute | solution.py:65
  82.0 5.6 %collective-permute-start.14 = (bf16[128,1024]{1,0:T(8,128)(2,1)S(1)}, bf16[128,1024]{1,0:T(8,128)(2,1)S(1)}, u32[]{:S(2)}, u32[]{:S(2)}) collective-permute-start(bf16[128,1024]{1,0:T(8,128)(2,1)S(1)} %get-tuple-element.415), channel_id=1, source_target_pairs={{0,1},{1,0},{2,3},{3,2},{4,5},{5,4},{6,7},{7,6},{8,9},{9,8},{10,11... | collective-permute-start | bytes 786440 | tf_op jit(solution)/shard_map/ppermute | solution.py:65
  83.6 8.4 %collective-permute-start.16 = (bf16[128,1024]{1,0:T(8,128)(2,1)S(1)}, bf16[128,1024]{1,0:T(8,128)(2,1)S(1)}, u32[]{:S(2)}, u32[]{:S(2)}) collective-permute-start(bf16[128,1024]{1,0:T(8,128)(2,1)S(1)} %fold.4), channel_id=1, source_target_pairs={{0,2},{1,3},{2,0},{3,1},{4,6},{5,7},{6,4},{7,5},{8,10},{9,11},{10,... | collective-permute-start | bytes 786440 | tf_op jit(solution)/shard_map/ppermute | solution.py:65
  85.2 25.9 %collective-permute-start.20 = (bf16[2,1,2,1024,128]{4,3,2,1,0:T(8,128)(2,1)S(1)}, bf16[2,1,2,1024,128]{4,3,2,1,0:T(8,128)(2,1)S(1)}, u32[]{:S(2)}, u32[]{:S(2)}) collective-permute-start(bf16[2,1,2,1024,128]{4,3,2,1,0:T(8,128)(2,1)S(1)} %maximum_select_fusion.5), channel_id=1, source_target_pairs={{0,8},{4,12},{8,0},{12,4},{16,24},{20,28},{24,16},{28,20},{1,9},{5... | collective-permute-start | bytes 3145736 | tf_op jit(solution)/shard_map/ppermute | solution.py:65
  92.3 7.6 %collective-permute-start.18 = (bf16[128,1024]{1,0:T(8,128)(2,1)S(1)}, bf16[128,1024]{1,0:T(8,128)(2,1)S(1)}, u32[]{:S(2)}, u32[]{:S(2)}) collective-permute-start(bf16[128,1024]{1,0:T(8,128)(2,1)S(1)} %get-tuple-element.427.refs_0_), channel_id=1, source_target_pairs={{0,2},{1,3},{2,0},{3,1},{4,6},{5,7},{6,4},{7,5},{8,10},{9,11},{10,... | collective-permute-start | bytes 786440 | tf_op jit(solution)/shard_map/ppermute | solution.py:65
  104.9 12.3 %collective-permute-start.19 = (bf16[1024,256]{1,0:T(8,128)(2,1)S(1)}, bf16[1024,256]{1,0:T(8,128)(2,1)S(1)}, u32[]{:S(2)}, u32[]{:S(2)}) collective-permute-start(bf16[1024,256]{1,0:T(8,128)(2,1)S(1)} %slice.27.refs_5_.refs_8_), channel_id=1, source_target_pairs={{0,2},{1,3},{2,0},{3,1},{4,6},{5,7},{6,4},{7,5},{8,10},{9,11},{10,... | collective-permute-start | bytes 1572872 | tf_op jit(solution)/shard_map/ppermute | solution.py:65
  117.8 9.5 %collective-permute-start.27 = (bf16[1024,256]{1,0:T(8,128)(2,1)S(1)}, bf16[1024,256]{1,0:T(8,128)(2,1)S(1)}, u32[]{:S(2)}, u32[]{:S(2)}) collective-permute-start(bf16[1024,256]{1,0:T(8,128)(2,1)S(1)} %collective-permute-done.19.refs_6_.refs_9_), channel_id=1, source_target_pairs={{0,1},{1,0},{2,3},{3,2},{4,5},{5,4},{6,7},{7,6},{8,9},{9,8},{10,11... | collective-permute-start | bytes 1572872 | tf_op jit(solution)/shard_map/ppermute | solution.py:65
  118.8 8.4 %collective-permute-start.25 = (bf16[128,1024]{1,0:T(8,128)(2,1)S(1)}, bf16[128,1024]{1,0:T(8,128)(2,1)S(1)}, u32[]{:S(2)}, u32[]{:S(2)}) collective-permute-start(bf16[128,1024]{1,0:T(8,128)(2,1)S(1)} %fold.5), channel_id=1, source_target_pairs={{0,2},{1,3},{2,0},{3,1},{4,6},{5,7},{6,4},{7,5},{8,10},{9,11},{10,... | collective-permute-start | bytes 786440 | tf_op jit(solution)/shard_map/ppermute | solution.py:65
  128.6 7.9 %collective-permute-start.28 = (bf16[1,512,256]{2,1,0:T(8,128)(2,1)S(1)}, bf16[1,512,256]{2,1,0:T(8,128)(2,1)S(1)}, u32[]{:S(2)}, u32[]{:S(2)}) collective-permute-start(bf16[1,512,256]{2,1,0:T(8,128)(2,1)S(1)} %bitcast.64), channel_id=1, source_target_pairs={{0,4},{4,0},{8,12},{12,8},{16,20},{20,16},{24,28},{28,24},{1,5},{5... | collective-permute-start | bytes 786440 | tf_op jit(solution)/shard_map/ppermute | solution.py:65
  130.2 7.2 %collective-permute-start.30 = (bf16[128,1024]{1,0:T(8,128)(2,1)S(1)}, bf16[128,1024]{1,0:T(8,128)(2,1)S(1)}, u32[]{:S(2)}, u32[]{:S(2)}) collective-permute-start(bf16[128,1024]{1,0:T(8,128)(2,1)S(1)} %get-tuple-element.443.refs_0_), channel_id=1, source_target_pairs={{0,2},{1,3},{2,0},{3,1},{4,6},{5,7},{6,4},{7,5},{8,10},{9,11},{10,... | collective-permute-start | bytes 786440 | tf_op jit(solution)/shard_map/ppermute | solution.py:65
  143.1 9.9 %collective-permute-start.34 = (bf16[128,1024]{1,0:T(8,128)(2,1)S(1)}, bf16[128,1024]{1,0:T(8,128)(2,1)S(1)}, u32[]{:S(2)}, u32[]{:S(2)}) collective-permute-start(bf16[128,1024]{1,0:T(8,128)(2,1)S(1)} %get-tuple-element.511.refs_4_), channel_id=1, source_target_pairs={{0,2},{1,3},{2,0},{3,1},{4,6},{5,7},{6,4},{7,5},{8,10},{9,11},{10,... | collective-permute-start | bytes 786440 | tf_op jit(solution)/shard_map/ppermute | solution.py:65
  153.1 6.6 %collective-permute-start.36 = (bf16[128,1024]{1,0:T(8,128)(2,1)S(1)}, bf16[128,1024]{1,0:T(8,128)(2,1)S(1)}, u32[]{:S(2)}, u32[]{:S(2)}) collective-permute-start(bf16[128,1024]{1,0:T(8,128)(2,1)S(1)} %get-tuple-element.467), channel_id=1, source_target_pairs={{0,1},{1,0},{2,3},{3,2},{4,5},{5,4},{6,7},{7,6},{8,9},{9,8},{10,11... | collective-permute-start | bytes 786440 | tf_op jit(solution)/shard_map/ppermute | solution.py:65
  154.7 8.4 %collective-permute-start.38 = (bf16[128,1024]{1,0:T(8,128)(2,1)S(1)}, bf16[128,1024]{1,0:T(8,128)(2,1)S(1)}, u32[]{:S(2)}, u32[]{:S(2)}) collective-permute-start(bf16[128,1024]{1,0:T(8,128)(2,1)S(1)} %fold.6), channel_id=1, source_target_pairs={{0,2},{1,3},{2,0},{3,1},{4,6},{5,7},{6,4},{7,5},{8,10},{9,11},{10,... | collective-permute-start | bytes 786440 | tf_op jit(solution)/shard_map/ppermute | solution.py:65
  164.9 7.6 %collective-permute-start.40 = (bf16[128,1024]{1,0:T(8,128)(2,1)S(1)}, bf16[128,1024]{1,0:T(8,128)(2,1)S(1)}, u32[]{:S(2)}, u32[]{:S(2)}) collective-permute-start(bf16[128,1024]{1,0:T(8,128)(2,1)S(1)} %get-tuple-element.496.refs_0_), channel_id=1, source_target_pairs={{0,2},{1,3},{2,0},{3,1},{4,6},{5,7},{6,4},{7,5},{8,10},{9,11},{10,... | collective-permute-start | bytes 786440 | tf_op jit(solution)/shard_map/ppermute | solution.py:65
  166.8 6.1 %collective-permute-start.41 = (bf16[128,1024]{1,0:T(8,128)(2,1)S(1)}, bf16[128,1024]{1,0:T(8,128)(2,1)S(1)}, u32[]{:S(2)}, u32[]{:S(2)}) collective-permute-start(bf16[128,1024]{1,0:T(8,128)(2,1)S(1)} %get-tuple-element.511.refs_4_), channel_id=1, source_target_pairs={{0,1},{1,0},{2,3},{3,2},{4,5},{5,4},{6,7},{7,6},{8,9},{9,8},{10,11... | collective-permute-start | bytes 786440 | tf_op jit(solution)/shard_map/ppermute | solution.py:65
  166.8 6.1 %collective-permute-start.42 = (bf16[128,1024]{1,0:T(8,128)(2,1)S(1)}, bf16[128,1024]{1,0:T(8,128)(2,1)S(1)}, u32[]{:S(2)}, u32[]{:S(2)}) collective-permute-start(bf16[128,1024]{1,0:T(8,128)(2,1)S(1)} %collective-permute-done.34.refs_5_), channel_id=1, source_target_pairs={{0,1},{1,0},{2,3},{3,2},{4,5},{5,4},{6,7},{7,6},{8,9},{9,8},{10,11... | collective-permute-start | bytes 786440 | tf_op jit(solution)/shard_map/ppermute | solution.py:65
  184.1 8.3 %collective-permute-start.50 = (bf16[128,1024]{1,0:T(8,128)(2,1)S(1)}, bf16[128,1024]{1,0:T(8,128)(2,1)S(1)}, u32[]{:S(2)}, u32[]{:S(2)}) collective-permute-start(bf16[128,1024]{1,0:T(8,128)(2,1)S(1)} %fold.7), channel_id=1, source_target_pairs={{0,2},{1,3},{2,0},{3,1},{4,6},{5,7},{6,4},{7,5},{8,10},{9,11},{10,... | collective-permute-start | bytes 786440 | tf_op jit(solution)/shard_map/ppermute | solution.py:65
  192.4 32.2 %collective-permute-start.56 = (bf16[4,128,1280]{2,1,0:T(8,128)(2,1)S(1)}, bf16[4,128,1280]{2,1,0:T(8,128)(2,1)S(1)}, u32[]{:S(2)}, u32[]{:S(2)}) collective-permute-start(bf16[4,128,1280]{2,1,0:T(8,128)(2,1)S(1)} %get-tuple-element.535), channel_id=1, source_target_pairs={{0,8},{4,12},{8,0},{12,4},{16,24},{20,28},{24,16},{28,20},{1,9},{5... | collective-permute-start | bytes 3932168 | tf_op jit(solution)/shard_map/ppermute | solution.py:65
  194.9 30.1 %collective-permute-start.55 = (bf16[4,1024,128]{2,1,0:T(8,128)(2,1)S(1)}, bf16[4,1024,128]{2,1,0:T(8,128)(2,1)S(1)}, u32[]{:S(2)}, u32[]{:S(2)}) collective-permute-start(bf16[4,1024,128]{2,1,0:T(8,128)(2,1)S(1)} %get-tuple-element.533), channel_id=1, source_target_pairs={{0,4},{4,0},{8,12},{12,8},{16,20},{20,16},{24,28},{28,24},{1,5},{5... | collective-permute-start | bytes 3145736 | tf_op jit(solution)/shard_map/ppermute | solution.py:65
  195.9 7.7 %collective-permute-start.51 = (bf16[144,1024]{1,0:T(8,128)(2,1)S(1)}, bf16[144,1024]{1,0:T(8,128)(2,1)S(1)}, u32[]{:S(2)}, u32[]{:S(2)}) collective-permute-start(bf16[144,1024]{1,0:T(8,128)(2,1)S(1)} %get-tuple-element.523.refs_0_), channel_id=1, source_target_pairs={{0,2},{1,3},{2,0},{3,1},{4,6},{5,7},{6,4},{7,5},{8,10},{9,11},{10,... | collective-permute-start | bytes 884744 | tf_op jit(solution)/shard_map/ppermute | solution.py:65
  196.6 7.1 %collective-permute-start.52 = (bf16[144,1024]{1,0:T(8,128)(2,1)S(1)}, bf16[144,1024]{1,0:T(8,128)(2,1)S(1)}, u32[]{:S(2)}, u32[]{:S(2)}) collective-permute-start(bf16[144,1024]{1,0:T(8,128)(2,1)S(1)} %get-tuple-element.523.refs_0_), channel_id=1, source_target_pairs={{0,1},{1,0},{2,3},{3,2},{4,5},{5,4},{6,7},{7,6},{8,9},{9,8},{10,11... | collective-permute-start | bytes 884744 | tf_op jit(solution)/shard_map/ppermute | solution.py:65
  205.7 18.9 %collective-permute-start.54 = (bf16[1,512,256]{2,1,0:T(8,128)(2,1)S(1)}, bf16[1,512,256]{2,1,0:T(8,128)(2,1)S(1)}, u32[]{:S(2)}, u32[]{:S(2)}) collective-permute-start(bf16[1,512,256]{2,1,0:T(8,128)(2,1)S(1)} %bitcast.71), channel_id=1, source_target_pairs={{0,4},{4,0},{8,12},{12,8},{16,20},{20,16},{24,28},{28,24},{1,5},{5... | collective-permute-start | bytes 786440 | tf_op jit(solution)/shard_map/ppermute | solution.py:65
  225.3 12.5 %collective-permute-start.59 = (bf16[2,1024,128]{2,1,0:T(8,128)(2,1)S(1)}, bf16[2,1024,128]{2,1,0:T(8,128)(2,1)S(1)}, u32[]{:S(2)}, u32[]{:S(2)}) collective-permute-start(bf16[2,1024,128]{2,1,0:T(8,128)(2,1)S(1)} %get-tuple-element.559), channel_id=1, source_target_pairs={{0,8},{4,12},{8,0},{12,4},{16,24},{20,28},{24,16},{28,20},{1,9},{5... | collective-permute-start | bytes 1572872 | tf_op jit(solution)/shard_map/ppermute | solution.py:65
  225.7 21.8 %collective-permute-start.61 = (bf16[2,128,1280]{2,1,0:T(8,128)(2,1)S(1)}, bf16[2,128,1280]{2,1,0:T(8,128)(2,1)S(1)}, u32[]{:S(2)}, u32[]{:S(2)}) collective-permute-start(bf16[2,128,1280]{2,1,0:T(8,128)(2,1)S(1)} %get-tuple-element.570), channel_id=1, source_target_pairs={{0,4},{4,0},{8,12},{12,8},{16,20},{20,16},{24,28},{28,24},{1,5},{5... | collective-permute-start | bytes 1966088 | tf_op jit(solution)/shard_map/ppermute | solution.py:65
  235.4 14.7 %collective-permute-start.58 = (bf16[4,528,128]{2,1,0:T(8,128)(2,1)S(1)}, bf16[4,528,128]{2,1,0:T(8,128)(2,1)S(1)}, u32[]{:S(2)}, u32[]{:S(2)}) collective-permute-start(bf16[4,528,128]{2,1,0:T(8,128)(2,1)S(1)} %get-tuple-element.556), channel_id=1, source_target_pairs={{0,8},{4,12},{8,0},{12,4},{16,24},{20,28},{24,16},{28,20},{1,9},{5... | collective-permute-start | bytes 1622024 | tf_op jit(solution)/shard_map/ppermute | solution.py:65
  237.8 9.8 %collective-permute-start.60 = (bf16[128,1024]{1,0:T(8,128)(2,1)S(1)}, bf16[128,1024]{1,0:T(8,128)(2,1)S(1)}, u32[]{:S(2)}, u32[]{:S(2)}) collective-permute-start(bf16[128,1024]{1,0:T(8,128)(2,1)S(1)} %get-tuple-element.568), channel_id=1, source_target_pairs={{0,1},{1,0},{2,3},{3,2},{4,5},{5,4},{6,7},{7,6},{8,9},{9,8},{10,11... | collective-permute-start | bytes 786440 | tf_op jit(solution)/shard_map/ppermute | solution.py:65
  239.9 16.4 %collective-permute-start.66 = (bf16[4,128,512]{2,1,0:T(8,128)(2,1)S(1)}, bf16[4,128,512]{2,1,0:T(8,128)(2,1)S(1)}, u32[]{:S(2)}, u32[]{:S(2)}) collective-permute-start(bf16[4,128,512]{2,1,0:T(8,128)(2,1)S(1)} %get-tuple-element.585), channel_id=1, source_target_pairs={{0,4},{4,0},{8,12},{12,8},{16,20},{20,16},{24,28},{28,24},{1,5},{5... | collective-permute-start | bytes 1572872 | tf_op jit(solution)/shard_map/ppermute | solution.py:65
  247.8 6.8 %collective-permute-start.64 = (bf16[128,1024]{1,0:T(8,128)(2,1)S(1)}, bf16[128,1024]{1,0:T(8,128)(2,1)S(1)}, u32[]{:S(2)}, u32[]{:S(2)}) collective-permute-start(bf16[128,1024]{1,0:T(8,128)(2,1)S(1)} %close.1.refs_0_), channel_id=1, source_target_pairs={{0,2},{1,3},{2,0},{3,1},{4,6},{5,7},{6,4},{7,5},{8,10},{9,11},{10,... | collective-permute-start | bytes 786440 | tf_op jit(solution)/shard_map/ppermute | solution.py:65
  248.9 8.7 %collective-permute-start.68 = (bf16[128,1024]{1,0:T(8,128)(2,1)S(1)}, bf16[128,1024]{1,0:T(8,128)(2,1)S(1)}, u32[]{:S(2)}, u32[]{:S(2)}) collective-permute-start(bf16[128,1024]{1,0:T(8,128)(2,1)S(1)} %close.1.refs_0_), channel_id=1, source_target_pairs={{0,1},{1,0},{2,3},{3,2},{4,5},{5,4},{6,7},{7,6},{8,9},{9,8},{10,11... | collective-permute-start | bytes 786440 | tf_op jit(solution)/shard_map/ppermute | solution.py:65
  248.9 23.7 %collective-permute-start.73 = (bf16[1,128,1280]{2,1,0:T(8,128)(2,1)S(1)}, bf16[1,128,1280]{2,1,0:T(8,128)(2,1)S(1)}, u32[]{:S(2)}, u32[]{:S(2)}) collective-permute-start(bf16[1,128,1280]{2,1,0:T(8,128)(2,1)S(1)} %get-tuple-element.603), channel_id=1, source_target_pairs={{0,16},{4,20},{8,24},{12,28},{16,0},{20,4},{24,8},{28,12},{1,17},{... | collective-permute-start | bytes 983048 | tf_op jit(solution)/shard_map/ppermute | solution.py:65
  255.3 17.2 %collective-permute-start.65 = (bf16[2,528,128]{2,1,0:T(8,128)(2,1)}, bf16[2,528,128]{2,1,0:T(8,128)(2,1)S(1)}, u32[]{:S(2)}, u32[]{:S(2)}) collective-permute-start(bf16[2,528,128]{2,1,0:T(8,128)(2,1)} %get-tuple-element.583), channel_id=1, source_target_pairs={{0,4},{4,0},{8,12},{12,8},{16,20},{20,16},{24,28},{28,24},{1,5},{5... | collective-permute-start | bytes 811016 | tf_op jit(solution)/shard_map/ppermute | solution.py:65
  257.1 15.3 %collective-permute-start.67 = (bf16[2,128,512]{2,1,0:T(8,128)(2,1)}, bf16[2,128,512]{2,1,0:T(8,128)(2,1)S(1)}, u32[]{:S(2)}, u32[]{:S(2)}) collective-permute-start(bf16[2,128,512]{2,1,0:T(8,128)(2,1)} %get-tuple-element.591), channel_id=1, source_target_pairs={{0,8},{4,12},{8,0},{12,4},{16,24},{20,28},{24,16},{28,20},{1,9},{5... | collective-permute-start | bytes 786440 | tf_op jit(solution)/shard_map/ppermute | solution.py:65
  257.6 20.5 %collective-permute-start.72 = (bf16[1,1024,128]{2,1,0:T(8,128)(2,1)}, bf16[1,1024,128]{2,1,0:T(8,128)(2,1)}, u32[]{:S(2)}, u32[]{:S(2)}) collective-permute-start(bf16[1,1024,128]{2,1,0:T(8,128)(2,1)} %get-tuple-element.602), channel_id=1, source_target_pairs={{0,16},{4,20},{8,24},{12,28},{16,0},{20,4},{24,8},{28,12},{1,17},{... | collective-permute-start | bytes 786440 | tf_op jit(solution)/shard_map/ppermute | solution.py:65
  278.0 10.5 %collective-permute-start.71 = (bf16[1,128,512]{2,1,0:T(8,128)(2,1)S(1)}, bf16[1,128,512]{2,1,0:T(8,128)(2,1)S(1)}, u32[]{:S(2)}, u32[]{:S(2)}) collective-permute-start(bf16[1,128,512]{2,1,0:T(8,128)(2,1)S(1)} %get-tuple-element.601), channel_id=1, source_target_pairs={{0,16},{4,20},{8,24},{12,28},{16,0},{20,4},{24,8},{28,12},{1,17},{... | collective-permute-start | bytes 393224 | tf_op jit(solution)/shard_map/ppermute | solution.py:65
  278.0 13.3 %collective-permute-start.70 = (bf16[1,528,128]{2,1,0:T(8,128)(2,1)S(1)}, bf16[1,528,128]{2,1,0:T(8,128)(2,1)S(1)}, u32[]{:S(2)}, u32[]{:S(2)}) collective-permute-start(bf16[1,528,128]{2,1,0:T(8,128)(2,1)S(1)} %get-tuple-element.600), channel_id=1, source_target_pairs={{0,16},{4,20},{8,24},{12,28},{16,0},{20,4},{24,8},{28,12},{1,17},{... | collective-permute-start | bytes 405512 | tf_op jit(solution)/shard_map/ppermute | solution.py:65
  (34 other events, 222.4 us)

commit v5 on v4

--- a/solution.py
+++ b/solution.py
@@ -1185,7 +1185,6 @@
     main = (hidden_own, own_hidden)
     main = pack_a.start(main)
     main = pack_b.start(main)
-    main = pack_u.start(main)
     main = pack_d.start(main)
     others = group_gather(main[1][None])[1:]
     seg_own = ordered(passage, device)
@@ -1212,13 +1211,14 @@
     seg_row, slot_own, slot_row, live_bias, weight, same, place = early
     main = pack_a.step(main)
     main = pack_b.step(main)
+    main = pack_u.start(main)
     others, main = tie(others, main)
     far_others = swap(others, "mp", 2)
     main = pack_d.finish(main)
+    main = pack_a.step(main)
+    main = pack_b.step(main)
     main = pack_u.step(main)
     main = pack_d.start(main)
-    main = pack_a.step(main)
-    main = pack_b.step(main)
     far_others, main = tie(far_others, main)
     main = pack_u.step(main)
     others = [others, far_others]

time: 292 us -> 287 us (0.983)
  waiting for transfers between devices: 159 us -> 155 us
    ppermute x74, waiting for transfers between devices: 159 us -> 155 us  [swap(): return lax.ppermute(value, axis, pairs)]
  transfers between devices with their start and end apart: 74 -> 74, of which waited for: 43 -> 45; matrix products, arithmetic and copies ran while one was open for 4% -> 5% of each run, Pallas kernels for 15% -> 15%
where the time goes in v5:
time: 287 us
  waiting for transfers between devices  155 us (54%)
  starting transfers between devices  58.7 us (20%)
  Pallas kernels  57.4 us (20%)
  other arithmetic  9.52 us (3%)
  local copies, waits for them, and re-layouts  2.89 us (1%)
    ppermute x74, waiting for transfers between devices, swap(): return lax.ppermute(value, axis, pairs)  155 us
    ppermute x74, starting transfers between devices, swap(): return lax.ppermute(value, axis, pairs)  58.7 us
    pallas_call x8, Pallas kernels, ordered_call(): pl.pallas_call(kernel, grid=(1,), in_specs=[pl.BlockSpec(memory_space=plt...  15.3 us
    pallas_call x2, Pallas kernels, attend_back(): pl.pallas_call(kernel, grid=(steps,), in_specs=in_specs, out_specs=out_sp...  11.2 us
  transfers between devices with their start and end apart: 74, of which 45 were waited for; matrix products, arithmetic and copies ran while one was open for 5% of the time, Pallas kernels for 15%

profile of v5, /device:TPU:0, one launch (start us, length us, event | category | flops | bytes accessed | tf_op | source)
XLA Modules:
  0.0 286.6 jit_solution(14524476684653398985)
XLA Ops:
  1.8 2.7 pack.1
  4.5 4.1 %collective-permute-start.1 = (bf16[1,1,1,128,512]{4,3,2,1,0:T(8,128)(2,1)}, bf16[1,1,1,128,512]{4,3,2,1,0:T(8,128)(2,1)S(1)}, u32[]{:S(2)}, u32[]{:S(2)}) collective-permute-start(bf16[1,1,1,128,512]{4,3,2,1,0:T(8,128)(2,1)} %bitcast.91), channel_id=1, source_target_pairs={{0,16},{4,20},{8,24},{12,28},{16,0},{20,4},{24,8},{28,12},{1,17},{... | collective-permute-start | bytes 393224 | tf_op jit(solution)/shard_map/ppermute | solution.py:65
  8.7 1.8 collective-permute-start.5
  14.2 4.7 %collective-permute-done.1 = bf16[1,1,1,128,512]{4,3,2,1,0:T(8,128)(2,1)S(1)} collective-permute-done((bf16[1,1,1,128,512]{4,3,2,1,0:T(8,128)(2,1)}, bf16[1,1,1,128,512]{4,3,2,1,0:T(8,128)(2,1)S(1)}, u32[]{:S(2)}, u32[]{:S(2)}) %collective-permute-start.1) | collective-permute-done | bytes 131104 | tf_op jit(solution)/shard_map/ppermute | solution.py:65
  23.0 3.0 %collective-permute-start.8 = (bf16[1,1,1,128,1280]{4,3,2,1,0:T(8,128)(2,1)S(1)}, bf16[1,1,1,128,1280]{4,3,2,1,0:T(8,128)(2,1)S(1)}, u32[]{:S(2)}, u32[]{:S(2)}) collective-permute-start(bf16[1,1,1,128,1280]{4,3,2,1,0:T(8,128)(2,1)S(1)} %bitcast.83), channel_id=1, source_target_pairs={{0,16},{4,20},{8,24},{12,28},{16,0},{20,4},{24,8},{28,12},{1,17},{... | collective-permute-start | bytes 983048 | tf_op jit(solution)/shard_map/ppermute | solution.py:65
  27.6 8.6 %collective-permute-done.3 = bf16[2,1,1,128,512]{4,3,2,1,0:T(8,128)(2,1)S(1)} collective-permute-done((bf16[2,1,1,128,512]{4,3,2,1,0:T(8,128)(2,1)S(1)}, bf16[2,1,1,128,512]{4,3,2,1,0:T(8,128)(2,1)S(1)}, u32[]{:S(2)}, u32[]{:S(2)}) %collective-permute-start.3) | collective-permute-done | bytes 262176 | tf_op jit(solution)/shard_map/ppermute | solution.py:65
  36.2 3.2 %collective-permute-done.2 = bf16[2,1,1,528,128]{4,3,2,1,0:T(8,128)(2,1)S(1)} collective-permute-done((bf16[2,1,1,528,128]{4,3,2,1,0:T(8,128)(2,1)S(1)}, bf16[2,1,1,528,128]{4,3,2,1,0:T(8,128)(2,1)S(1)}, u32[]{:S(2)}, u32[]{:S(2)}) %collective-permute-start.2) | collective-permute-done | bytes 270368 | tf_op jit(solution)/shard_map/ppermute | solution.py:65
  39.6 3.1 %collective-permute-start.9 = (bf16[2,1,1,128,1280]{4,3,2,1,0:T(8,128)(2,1)S(1)}, bf16[2,1,1,128,1280]{4,3,2,1,0:T(8,128)(2,1)S(1)}, u32[]{:S(2)}, u32[]{:S(2)}) collective-permute-start(bf16[2,1,1,128,1280]{4,3,2,1,0:T(8,128)(2,1)S(1)} %maximum_select_fusion.6), channel_id=1, source_target_pairs={{0,8},{4,12},{8,0},{12,4},{16,24},{20,28},{24,16},{28,20},{1,9},{5... | collective-permute-start | bytes 1966088 | tf_op jit(solution)/shard_map/ppermute | solution.py:65
  45.4 1.8 collective-permute-start.13
  48.4 17.7 %collective-permute-done.9 = bf16[2,1,1,128,1280]{4,3,2,1,0:T(8,128)(2,1)S(1)} collective-permute-done((bf16[2,1,1,128,1280]{4,3,2,1,0:T(8,128)(2,1)S(1)}, bf16[2,1,1,128,1280]{4,3,2,1,0:T(8,128)(2,1)S(1)}, u32[]{:S(2)}, u32[]{:S(2)}) %collective-permute-start.9) | collective-permute-done | bytes 655392 | tf_op jit(solution)/shard_map/ppermute | solution.py:65
  69.1 1.8 collective-permute-done.13
  73.4 4.8 %attend_forward.1 = (bf16[512,256]{1,0:T(8,128)(2,1)S(1)}, f32[8,512]{1,0:T(8,128)S(1)}) custom-call(bf16[1024,512]{1,0:T(8,128)(2,1)S(1)} %convolution_convert_fusion.q_ref.k_ref.refs_0_.refs_1_, bf16[1024,512]{1,0:T(8,128)(2,1)S(1)} %convolution_convert_fusion.q_ref.k_ref.refs_0_.refs_1_, bf16[1024,256]{1,0:T(8,128)(2,1)S(1)} %convolution_convert_fusion.1.v_ref.refs_2_, ...), custom_call_target="tpu_custom_call" | custom-call | flops 1 | bytes 1 | tf_op jit(solution)/shard_map/attend_forward/pallas_call | solution.py:261
  81.9 6.8 %collective-permute-done.16.refs_3_ = bf16[128,1024]{1,0:T(8,128)(2,1)S(1)} collective-permute-done((bf16[128,1024]{1,0:T(8,128)(2,1)S(1)}, bf16[128,1024]{1,0:T(8,128)(2,1)S(1)}, u32[]{:S(2)}, u32[]{:S(2)}) %collective-permute-start.16) | collective-permute-done | bytes 262176 | tf_op jit(solution)/shard_map/ppermute | solution.py:65
  90.6 6.0 %collective-permute-done.18.refs_1_ = bf16[128,1024]{1,0:T(8,128)(2,1)S(1)} collective-permute-done((bf16[128,1024]{1,0:T(8,128)(2,1)S(1)}, bf16[128,1024]{1,0:T(8,128)(2,1)S(1)}, u32[]{:S(2)}, u32[]{:S(2)}) %collective-permute-start.18) | collective-permute-done | bytes 262176 | tf_op jit(solution)/shard_map/ppermute | solution.py:65
  96.6 3.9 %collective-permute-done.17 = bf16[2,2,1,128,1280]{4,3,2,1,0:T(8,128)(2,1)S(1)} collective-permute-done((bf16[2,2,1,128,1280]{4,3,2,1,0:T(8,128)(2,1)S(1)}, bf16[2,2,1,128,1280]{4,3,2,1,0:T(8,128)(2,1)S(1)}, u32[]{:S(2)}, u32[]{:S(2)}) %collective-permute-start.17) | collective-permute-done | bytes 1310752 | tf_op jit(solution)/shard_map/ppermute | solution.py:65
  104.4 2.7 feed_up.1
  107.5 1.9 feed_down.1
  109.4 3.2 %collective-permute-done.19.refs_6_.refs_9_ = bf16[1024,256]{1,0:T(8,128)(2,1)S(1)} collective-permute-done((bf16[1024,256]{1,0:T(8,128)(2,1)S(1)}, bf16[1024,256]{1,0:T(8,128)(2,1)S(1)}, u32[]{:S(2)}, u32[]{:S(2)}) %collective-permute-start.19) | collective-permute-done | bytes 524320 | tf_op jit(solution)/shard_map/ppermute | solution.py:65
  116.0 6.6 %collective-permute-done.25.refs_3_ = bf16[128,1024]{1,0:T(8,128)(2,1)S(1)} collective-permute-done((bf16[128,1024]{1,0:T(8,128)(2,1)S(1)}, bf16[128,1024]{1,0:T(8,128)(2,1)S(1)}, u32[]{:S(2)}, u32[]{:S(2)}) %collective-permute-start.25) | collective-permute-done | bytes 262176 | tf_op jit(solution)/shard_map/ppermute | solution.py:65
  127.5 4.3 %collective-permute-done.29 = f32[1,8,512]{2,1,0:T(8,128)S(1)} collective-permute-done((f32[1,8,512]{2,1,0:T(8,128)S(1)}, f32[1,8,512]{2,1,0:T(8,128)S(1)}, u32[]{:S(2)}, u32[]{:S(2)}) %collective-permute-start.29) | collective-permute-done | bytes 16416 | tf_op jit(solution)/shard_map/ppermute | solution.py:65
  134.3 4.2 %late_forward.1 = (f32[512,2048]{1,0:T(8,128)S(1)}, f32[8,2048]{1,0:T(8,128)S(1)}) custom-call(bf16[128,1024]{1,0:T(8,128)(2,1)S(1)} %get-tuple-element.443.refs_0_, bf16[128,1024]{1,0:T(8,128)(2,1)S(1)} %collective-permute-done.30.refs_1_, bf16[128,1024]{1,0:T(8,128)(2,1)S(1)} %collective-permute-done.31.refs_2_, ...), custom_call_target="tpu_custom_call" | custom-call | flops 1 | bytes 1 | tf_op jit(solution)/shard_map/late_forward/pallas_call | solution.py:550
  140.6 3.6 %collective-permute-done.33.far_ref = f32[1,8,2048]{2,1,0:T(8,128)S(1)} collective-permute-done((f32[1,8,2048]{2,1,0:T(8,128)S(1)}, f32[1,8,2048]{2,1,0:T(8,128)S(1)}, u32[]{:S(2)}, u32[]{:S(2)}) %collective-permute-start.33) | collective-permute-done | bytes 65568 | tf_op jit(solution)/shard_map/ppermute | solution.py:65
  144.3 4.1 %late_backward.1 = (f32[128,1024]{1,0:T(8,128)S(1)}, f32[128,1024]{1,0:T(8,128)S(1)}, bf16[128,1024]{1,0:T(8,128)(2,1)S(1)}, bf16[128,1024]{1,0:T(8,128)(2,1)S(1)}, f32[64,15]{1,0:T(8,128)S(1)}) custom-call(f32[512,2048]{1,0:T(8,128)S(1)} %get-tuple-element.448.sharp_ref, f32[8,2048]{1,0:T(8,128)S(1)} %get-tuple-element.451.soft_ref, ...), custom_call_target="tpu_custom_call" | custom-call | flops 1 | bytes 1 | tf_op jit(solution)/shard_map/late_backward/pallas_call | solution.py:627
  150.7 3.9 %collective-permute-done.35 = f32[64,15]{1,0:T(8,128)S(1)} collective-permute-done((f32[64,15]{1,0:T(8,128)S(1)}, f32[64,15]{1,0:T(8,128)S(1)}, u32[]{:S(2)}, u32[]{:S(2)}) %collective-permute-start.35) | collective-permute-done | bytes 3872 | tf_op jit(solution)/shard_map/ppermute | solution.py:65
  154.6 3.9 %collective-permute-done.38.refs_2_ = bf16[128,1024]{1,0:T(8,128)(2,1)S(1)} collective-permute-done((bf16[128,1024]{1,0:T(8,128)(2,1)S(1)}, bf16[128,1024]{1,0:T(8,128)(2,1)S(1)}, u32[]{:S(2)}, u32[]{:S(2)}) %collective-permute-start.38) | collective-permute-done | bytes 262176 | tf_op jit(solution)/shard_map/ppermute | solution.py:65
  158.5 1.7 norm_two_back.1
  162.5 3.1 %collective-permute-done.39 = f32[64,15]{1,0:T(8,128)S(1)} collective-permute-done((f32[64,15]{1,0:T(8,128)S(1)}, f32[64,15]{1,0:T(8,128)S(1)}, u32[]{:S(2)}, u32[]{:S(2)}) %collective-permute-start.39) | collective-permute-done | bytes 3872 | tf_op jit(solution)/shard_map/ppermute | solution.py:65
  165.6 2.2 collective-permute-done.40.refs_1_
  170.2 2.4 feed_inner.1.dz_ref.dinner_ref
  172.7 2.6 collective-permute-done.45.refs_9_
  175.2 2.2 feed_back.1
  180.0 2.4 grad_down.1
  182.4 2.3 grad_up.1
  184.8 3.0 %collective-permute-done.50.refs_3_ = bf16[128,1024]{1,0:T(8,128)(2,1)S(1)} collective-permute-done((bf16[128,1024]{1,0:T(8,128)(2,1)S(1)}, bf16[128,1024]{1,0:T(8,128)(2,1)S(1)}, u32[]{:S(2)}, u32[]{:S(2)}) %collective-permute-start.50) | collective-permute-done | bytes 262176 | tf_op jit(solution)/shard_map/ppermute | solution.py:65
  189.4 7.4 %collective-permute-done.51.refs_1_ = bf16[144,1024]{1,0:T(8,128)(2,1)S(1)} collective-permute-done((bf16[144,1024]{1,0:T(8,128)(2,1)S(1)}, bf16[144,1024]{1,0:T(8,128)(2,1)S(1)}, u32[]{:S(2)}, u32[]{:S(2)}) %collective-permute-start.51) | collective-permute-done | bytes 294944 | tf_op jit(solution)/shard_map/ppermute | solution.py:65
  200.3 6.3 %attend_back.2 = (f32[512,256]{1,0:T(8,128)S(1)}, f32[512,256]{1,0:T(8,128)S(1)}, bf16[512,256]{1,0:T(8,128)(2,1)S(1)}) custom-call(bf16[1024,512]{1,0:T(8,128)(2,1)S(1)} %convolution_convert_fusion.q_ref.k_ref.refs_0_.refs_1_, bf16[1024,512]{1,0:T(8,128)(2,1)S(1)} %convolution_convert_fusion.q_ref.k_ref.refs_0_.refs_1_, ...), custom_call_target="tpu_custom_call" | custom-call | flops 1 | bytes 1 | tf_op jit(solution)/shard_map/attend_back/pallas_call | solution.py:373
  206.6 11.1 %collective-permute-done.54 = bf16[1,512,256]{2,1,0:T(8,128)(2,1)S(1)} collective-permute-done((bf16[1,512,256]{2,1,0:T(8,128)(2,1)S(1)}, bf16[1,512,256]{2,1,0:T(8,128)(2,1)S(1)}, u32[]{:S(2)}, u32[]{:S(2)}) %collective-permute-start.54) | collective-permute-done | bytes 262176 | tf_op jit(solution)/shard_map/ppermute | solution.py:65
  218.4 1.8 collective-permute-start.59
  220.9 4.9 %attend_back.3 = (bf16[512,512]{1,0:T(8,128)(2,1)S(1)}, bf16[512,256]{1,0:T(8,128)(2,1)S(1)}) custom-call(bf16[1024,512]{1,0:T(8,128)(2,1)S(1)} %convolution_convert_fusion.q_ref.k_ref.refs_0_.refs_1_, bf16[1024,512]{1,0:T(8,128)(2,1)S(1)} %convolution_convert_fusion.q_ref.k_ref.refs_0_.refs_1_, ...), custom_call_target="tpu_custom_call" | custom-call | flops 1 | bytes 1 | tf_op jit(solution)/shard_map/attend_back/pallas_call | solution.py:373
  236.2 4.4 %collective-permute-done.63.refs_4_ = bf16[64,1024]{1,0:T(8,128)(2,1)S(1)} collective-permute-done((bf16[64,1024]{1,0:T(8,128)(2,1)S(1)}, bf16[64,1024]{1,0:T(8,128)(2,1)S(1)}, u32[]{:S(2)}, u32[]{:S(2)}) %collective-permute-start.63) | collective-permute-done | bytes 131104 | tf_op jit(solution)/shard_map/ppermute | solution.py:65
  244.4 3.2 %collective-permute-done.64.refs_1_ = bf16[128,1024]{1,0:T(8,128)(2,1)S(1)} collective-permute-done((bf16[128,1024]{1,0:T(8,128)(2,1)S(1)}, bf16[128,1024]{1,0:T(8,128)(2,1)S(1)}, u32[]{:S(2)}, u32[]{:S(2)}) %collective-permute-start.64) | collective-permute-done | bytes 262176 | tf_op jit(solution)/shard_map/ppermute | solution.py:65
  253.9 2.0 place_rows.1
  255.9 9.1 %collective-permute-done.67.other_low.other_high = bf16[2,128,512]{2,1,0:T(8,128)(2,1)S(1)} collective-permute-done((bf16[2,128,512]{2,1,0:T(8,128)(2,1)}, bf16[2,128,512]{2,1,0:T(8,128)(2,1)S(1)}, u32[]{:S(2)}, u32[]{:S(2)}) %collective-permute-start.67) | collective-permute-done | bytes 262176 | tf_op jit(solution)/shard_map/ppermute | solution.py:65
  266.1 5.3 %collective-permute-done.72 = bf16[1,1024,128]{2,1,0:T(8,128)(2,1)} collective-permute-done((bf16[1,1024,128]{2,1,0:T(8,128)(2,1)}, bf16[1,1024,128]{2,1,0:T(8,128)(2,1)}, u32[]{:S(2)}, u32[]{:S(2)}) %collective-permute-start.72) | collective-permute-done | bytes 262176 | tf_op jit(solution)/shard_map/ppermute | solution.py:65
  271.4 2.9 %collective-permute-start.70 = (bf16[1,528,128]{2,1,0:T(8,128)(2,1)S(1)}, bf16[1,528,128]{2,1,0:T(8,128)(2,1)S(1)}, u32[]{:S(2)}, u32[]{:S(2)}) collective-permute-start(bf16[1,528,128]{2,1,0:T(8,128)(2,1)S(1)} %get-tuple-element.600), channel_id=1, source_target_pairs={{0,16},{4,20},{8,24},{12,28},{16,0},{20,4},{24,8},{28,12},{1,17},{... | collective-permute-start | bytes 405512 | tf_op jit(solution)/shard_map/ppermute | solution.py:65
  275.2 1.8 add_bitcast_fusion
  277.0 6.0 %collective-permute-done.71 = bf16[1,128,512]{2,1,0:T(8,128)(2,1)S(1)} collective-permute-done((bf16[1,128,512]{2,1,0:T(8,128)(2,1)S(1)}, bf16[1,128,512]{2,1,0:T(8,128)(2,1)S(1)}, u32[]{:S(2)}, u32[]{:S(2)}) %collective-permute-start.71) | collective-permute-done | bytes 131104 | tf_op jit(solution)/shard_map/ppermute | solution.py:65
  283.8 2.1 collective-permute-done.70
  (208 shorter events, 82.7 us)
Async XLA Ops:
  4.5 14.3 %collective-permute-start.1 = (bf16[1,1,1,128,512]{4,3,2,1,0:T(8,128)(2,1)}, bf16[1,1,1,128,512]{4,3,2,1,0:T(8,128)(2,1)S(1)}, u32[]{:S(2)}, u32[]{:S(2)}) collective-permute-start(bf16[1,1,1,128,512]{4,3,2,1,0:T(8,128)(2,1)} %bitcast.91), channel_id=1, source_target_pairs={{0,16},{4,20},{8,24},{12,28},{16,0},{20,4},{24,8},{28,12},{1,17},{... | collective-permute-start | bytes 393224 | tf_op jit(solution)/shard_map/ppermute | solution.py:65
  8.6 12.3 %collective-permute-start = (bf16[1,1,1,528,128]{4,3,2,1,0:T(8,128)(2,1)}, bf16[1,1,1,528,128]{4,3,2,1,0:T(8,128)(2,1)S(1)}, u32[]{:S(2)}, u32[]{:S(2)}) collective-permute-start(bf16[1,1,1,528,128]{4,3,2,1,0:T(8,128)(2,1)} %bitcast.89), channel_id=1, source_target_pairs={{0,16},{4,20},{8,24},{12,28},{16,0},{20,4},{24,8},{28,12},{1,17},{... | collective-permute-start | bytes 405512 | tf_op jit(solution)/shard_map/ppermute | solution.py:65
  8.7 17.4 %collective-permute-start.5 = (bf16[1,128,1024]{2,1,0:T(8,128)(2,1)}, bf16[1,128,1024]{2,1,0:T(8,128)(2,1)}, u32[]{:S(2)}, u32[]{:S(2)}) collective-permute-start(bf16[1,128,1024]{2,1,0:T(8,128)(2,1)} %bitcast.72), channel_id=1, source_target_pairs={{0,4},{4,0},{8,12},{12,8},{16,20},{20,16},{24,28},{28,24},{1,5},{5... | collective-permute-start | bytes 786440 | tf_op jit(solution)/shard_map/ppermute | solution.py:65
  10.4 15.7 %collective-permute-start.4 = (bf16[1,1,1,1024,128]{4,3,2,1,0:T(8,128)(2,1)}, bf16[1,1,1,1024,128]{4,3,2,1,0:T(8,128)(2,1)S(1)}, u32[]{:S(2)}, u32[]{:S(2)}) collective-permute-start(bf16[1,1,1,1024,128]{4,3,2,1,0:T(8,128)(2,1)} %bitcast.85), channel_id=1, source_target_pairs={{0,4},{4,0},{8,12},{12,8},{16,20},{20,16},{24,28},{28,24},{1,5},{5... | collective-permute-start | bytes 786440 | tf_op jit(solution)/shard_map/ppermute | solution.py:65
  19.9 16.3 %collective-permute-start.3 = (bf16[2,1,1,128,512]{4,3,2,1,0:T(8,128)(2,1)S(1)}, bf16[2,1,1,128,512]{4,3,2,1,0:T(8,128)(2,1)S(1)}, u32[]{:S(2)}, u32[]{:S(2)}) collective-permute-start(bf16[2,1,1,128,512]{4,3,2,1,0:T(8,128)(2,1)S(1)} %maximum_select_fusion.11), channel_id=1, source_target_pairs={{0,8},{4,12},{8,0},{12,4},{16,24},{20,28},{24,16},{28,20},{1,9},{5... | collective-permute-start | bytes 786440 | tf_op jit(solution)/shard_map/ppermute | solution.py:65
  21.9 17.5 %collective-permute-start.2 = (bf16[2,1,1,528,128]{4,3,2,1,0:T(8,128)(2,1)S(1)}, bf16[2,1,1,528,128]{4,3,2,1,0:T(8,128)(2,1)S(1)}, u32[]{:S(2)}, u32[]{:S(2)}) collective-permute-start(bf16[2,1,1,528,128]{4,3,2,1,0:T(8,128)(2,1)S(1)} %maximum_select_fusion.10), channel_id=1, source_target_pairs={{0,8},{4,12},{8,0},{12,4},{16,24},{20,28},{24,16},{28,20},{1,9},{5... | collective-permute-start | bytes 811016 | tf_op jit(solution)/shard_map/ppermute | solution.py:65
  23.0 16.4 %collective-permute-start.8 = (bf16[1,1,1,128,1280]{4,3,2,1,0:T(8,128)(2,1)S(1)}, bf16[1,1,1,128,1280]{4,3,2,1,0:T(8,128)(2,1)S(1)}, u32[]{:S(2)}, u32[]{:S(2)}) collective-permute-start(bf16[1,1,1,128,1280]{4,3,2,1,0:T(8,128)(2,1)S(1)} %bitcast.83), channel_id=1, source_target_pairs={{0,16},{4,20},{8,24},{12,28},{16,0},{20,4},{24,8},{28,12},{1,17},{... | collective-permute-start | bytes 983048 | tf_op jit(solution)/shard_map/ppermute | solution.py:65
  26.1 16.7 %collective-permute-start.10 = (bf16[1,128,1024]{2,1,0:T(8,128)(2,1)}, bf16[1,128,1024]{2,1,0:T(8,128)(2,1)}, u32[]{:S(2)}, u32[]{:S(2)}) collective-permute-start(bf16[1,128,1024]{2,1,0:T(8,128)(2,1)} %collective-permute-done.5), channel_id=1, source_target_pairs={{0,2},{1,3},{2,0},{3,1},{4,6},{5,7},{6,4},{7,5},{8,10},{9,11},{10,... | collective-permute-start | bytes 786440 | tf_op jit(solution)/shard_map/ppermute | solution.py:65
  39.6 26.6 %collective-permute-start.9 = (bf16[2,1,1,128,1280]{4,3,2,1,0:T(8,128)(2,1)S(1)}, bf16[2,1,1,128,1280]{4,3,2,1,0:T(8,128)(2,1)S(1)}, u32[]{:S(2)}, u32[]{:S(2)}) collective-permute-start(bf16[2,1,1,128,1280]{4,3,2,1,0:T(8,128)(2,1)S(1)} %maximum_select_fusion.6), channel_id=1, source_target_pairs={{0,8},{4,12},{8,0},{12,4},{16,24},{20,28},{24,16},{28,20},{1,9},{5... | collective-permute-start | bytes 1966088 | tf_op jit(solution)/shard_map/ppermute | solution.py:65
  43.3 23.2 %collective-permute-start.7 = (bf16[2,2,1,128,512]{4,3,2,1,0:T(8,128)(2,1)S(1)}, bf16[2,2,1,128,512]{4,3,2,1,0:T(8,128)(2,1)S(1)}, u32[]{:S(2)}, u32[]{:S(2)}) collective-permute-start(bf16[2,2,1,128,512]{4,3,2,1,0:T(8,128)(2,1)S(1)} %maximum_select_fusion.8), channel_id=1, source_target_pairs={{0,4},{4,0},{8,12},{12,8},{16,20},{20,16},{24,28},{28,24},{1,5},{5... | collective-permute-start | bytes 1572872 | tf_op jit(solution)/shard_map/ppermute | solution.py:65
  44.9 24.0 %collective-permute-start.6 = (bf16[2,2,1,528,128]{4,3,2,1,0:T(8,128)(2,1)S(1)}, bf16[2,2,1,528,128]{4,3,2,1,0:T(8,128)(2,1)S(1)}, u32[]{:S(2)}, u32[]{:S(2)}) collective-permute-start(bf16[2,2,1,528,128]{4,3,2,1,0:T(8,128)(2,1)S(1)} %maximum_select_fusion.7), channel_id=1, source_target_pairs={{0,4},{4,0},{8,12},{12,8},{16,20},{20,16},{24,28},{28,24},{1,5},{5... | collective-permute-start | bytes 1622024 | tf_op jit(solution)/shard_map/ppermute | solution.py:65
  45.4 25.5 %collective-permute-start.13 = (bf16[1,1,2,1024,128]{4,3,2,1,0:T(8,128)(2,1)S(1)}, bf16[1,1,2,1024,128]{4,3,2,1,0:T(8,128)(2,1)S(1)}, u32[]{:S(2)}, u32[]{:S(2)}) collective-permute-start(bf16[1,1,2,1024,128]{4,3,2,1,0:T(8,128)(2,1)S(1)} %maximum_select_fusion.9), channel_id=1, source_target_pairs={{0,16},{4,20},{8,24},{12,28},{16,0},{20,4},{24,8},{28,12},{1,17},{... | collective-permute-start | bytes 1572872 | tf_op jit(solution)/shard_map/ppermute | solution.py:65
  71.1 29.4 %collective-permute-start.17 = (bf16[2,2,1,128,1280]{4,3,2,1,0:T(8,128)(2,1)S(1)}, bf16[2,2,1,128,1280]{4,3,2,1,0:T(8,128)(2,1)S(1)}, u32[]{:S(2)}, u32[]{:S(2)}) collective-permute-start(bf16[2,2,1,128,1280]{4,3,2,1,0:T(8,128)(2,1)S(1)} %maximum_select_fusion.2), channel_id=1, source_target_pairs={{0,4},{4,0},{8,12},{12,8},{16,20},{20,16},{24,28},{28,24},{1,5},{5... | collective-permute-start | bytes 3932168 | tf_op jit(solution)/shard_map/ppermute | solution.py:65
  80.3 8.4 %collective-permute-start.16 = (bf16[128,1024]{1,0:T(8,128)(2,1)S(1)}, bf16[128,1024]{1,0:T(8,128)(2,1)S(1)}, u32[]{:S(2)}, u32[]{:S(2)}) collective-permute-start(bf16[128,1024]{1,0:T(8,128)(2,1)S(1)} %fold.4), channel_id=1, source_target_pairs={{0,2},{1,3},{2,0},{3,1},{4,6},{5,7},{6,4},{7,5},{8,10},{9,11},{10,... | collective-permute-start | bytes 786440 | tf_op jit(solution)/shard_map/ppermute | solution.py:65
  81.9 25.2 %collective-permute-start.20 = (bf16[2,1,2,1024,128]{4,3,2,1,0:T(8,128)(2,1)S(1)}, bf16[2,1,2,1024,128]{4,3,2,1,0:T(8,128)(2,1)S(1)}, u32[]{:S(2)}, u32[]{:S(2)}) collective-permute-start(bf16[2,1,2,1024,128]{4,3,2,1,0:T(8,128)(2,1)S(1)} %maximum_select_fusion.5), channel_id=1, source_target_pairs={{0,8},{4,12},{8,0},{12,4},{16,24},{20,28},{24,16},{28,20},{1,9},{5... | collective-permute-start | bytes 3145736 | tf_op jit(solution)/shard_map/ppermute | solution.py:65
  89.0 7.6 %collective-permute-start.18 = (bf16[128,1024]{1,0:T(8,128)(2,1)S(1)}, bf16[128,1024]{1,0:T(8,128)(2,1)S(1)}, u32[]{:S(2)}, u32[]{:S(2)}) collective-permute-start(bf16[128,1024]{1,0:T(8,128)(2,1)S(1)} %get-tuple-element.427.refs_0_), channel_id=1, source_target_pairs={{0,2},{1,3},{2,0},{3,1},{4,6},{5,7},{6,4},{7,5},{8,10},{9,11},{10,... | collective-permute-start | bytes 786440 | tf_op jit(solution)/shard_map/ppermute | solution.py:65
  101.0 11.6 %collective-permute-start.19 = (bf16[1024,256]{1,0:T(8,128)(2,1)S(1)}, bf16[1024,256]{1,0:T(8,128)(2,1)S(1)}, u32[]{:S(2)}, u32[]{:S(2)}) collective-permute-start(bf16[1024,256]{1,0:T(8,128)(2,1)S(1)} %slice.27.refs_5_.refs_8_), channel_id=1, source_target_pairs={{0,2},{1,3},{2,0},{3,1},{4,6},{5,7},{6,4},{7,5},{8,10},{9,11},{10,... | collective-permute-start | bytes 1572872 | tf_op jit(solution)/shard_map/ppermute | solution.py:65
  113.1 9.5 %collective-permute-start.27 = (bf16[1024,256]{1,0:T(8,128)(2,1)S(1)}, bf16[1024,256]{1,0:T(8,128)(2,1)S(1)}, u32[]{:S(2)}, u32[]{:S(2)}) collective-permute-start(bf16[1024,256]{1,0:T(8,128)(2,1)S(1)} %collective-permute-done.19.refs_6_.refs_9_), channel_id=1, source_target_pairs={{0,1},{1,0},{2,3},{3,2},{4,5},{5,4},{6,7},{7,6},{8,9},{9,8},{10,11... | collective-permute-start | bytes 1572872 | tf_op jit(solution)/shard_map/ppermute | solution.py:65
  114.2 8.4 %collective-permute-start.25 = (bf16[128,1024]{1,0:T(8,128)(2,1)S(1)}, bf16[128,1024]{1,0:T(8,128)(2,1)S(1)}, u32[]{:S(2)}, u32[]{:S(2)}) collective-permute-start(bf16[128,1024]{1,0:T(8,128)(2,1)S(1)} %fold.5), channel_id=1, source_target_pairs={{0,2},{1,3},{2,0},{3,1},{4,6},{5,7},{6,4},{7,5},{8,10},{9,11},{10,... | collective-permute-start | bytes 786440 | tf_op jit(solution)/shard_map/ppermute | solution.py:65
  123.9 7.9 %collective-permute-start.28 = (bf16[1,512,256]{2,1,0:T(8,128)(2,1)S(1)}, bf16[1,512,256]{2,1,0:T(8,128)(2,1)S(1)}, u32[]{:S(2)}, u32[]{:S(2)}) collective-permute-start(bf16[1,512,256]{2,1,0:T(8,128)(2,1)S(1)} %bitcast.64), channel_id=1, source_target_pairs={{0,4},{4,0},{8,12},{12,8},{16,20},{20,16},{24,28},{28,24},{1,5},{5... | collective-permute-start | bytes 786440 | tf_op jit(solution)/shard_map/ppermute | solution.py:65
  125.5 7.2 %collective-permute-start.30 = (bf16[128,1024]{1,0:T(8,128)(2,1)S(1)}, bf16[128,1024]{1,0:T(8,128)(2,1)S(1)}, u32[]{:S(2)}, u32[]{:S(2)}) collective-permute-start(bf16[128,1024]{1,0:T(8,128)(2,1)S(1)} %get-tuple-element.443.refs_0_), channel_id=1, source_target_pairs={{0,2},{1,3},{2,0},{3,1},{4,6},{5,7},{6,4},{7,5},{8,10},{9,11},{10,... | collective-permute-start | bytes 786440 | tf_op jit(solution)/shard_map/ppermute | solution.py:65
  138.5 9.9 %collective-permute-start.34 = (bf16[128,1024]{1,0:T(8,128)(2,1)S(1)}, bf16[128,1024]{1,0:T(8,128)(2,1)S(1)}, u32[]{:S(2)}, u32[]{:S(2)}) collective-permute-start(bf16[128,1024]{1,0:T(8,128)(2,1)S(1)} %get-tuple-element.511.refs_4_), channel_id=1, source_target_pairs={{0,2},{1,3},{2,0},{3,1},{4,6},{5,7},{6,4},{7,5},{8,10},{9,11},{10,... | collective-permute-start | bytes 786440 | tf_op jit(solution)/shard_map/ppermute | solution.py:65
  148.5 6.1 %collective-permute-start.36 = (bf16[128,1024]{1,0:T(8,128)(2,1)S(1)}, bf16[128,1024]{1,0:T(8,128)(2,1)S(1)}, u32[]{:S(2)}, u32[]{:S(2)}) collective-permute-start(bf16[128,1024]{1,0:T(8,128)(2,1)S(1)} %get-tuple-element.467), channel_id=1, source_target_pairs={{0,1},{1,0},{2,3},{3,2},{4,5},{5,4},{6,7},{7,6},{8,9},{9,8},{10,11... | collective-permute-start | bytes 786440 | tf_op jit(solution)/shard_map/ppermute | solution.py:65
  150.1 8.4 %collective-permute-start.38 = (bf16[128,1024]{1,0:T(8,128)(2,1)S(1)}, bf16[128,1024]{1,0:T(8,128)(2,1)S(1)}, u32[]{:S(2)}, u32[]{:S(2)}) collective-permute-start(bf16[128,1024]{1,0:T(8,128)(2,1)S(1)} %fold.6), channel_id=1, source_target_pairs={{0,2},{1,3},{2,0},{3,1},{4,6},{5,7},{6,4},{7,5},{8,10},{9,11},{10,... | collective-permute-start | bytes 786440 | tf_op jit(solution)/shard_map/ppermute | solution.py:65
  160.2 7.6 %collective-permute-start.40 = (bf16[128,1024]{1,0:T(8,128)(2,1)S(1)}, bf16[128,1024]{1,0:T(8,128)(2,1)S(1)}, u32[]{:S(2)}, u32[]{:S(2)}) collective-permute-start(bf16[128,1024]{1,0:T(8,128)(2,1)S(1)} %get-tuple-element.496.refs_0_), channel_id=1, source_target_pairs={{0,2},{1,3},{2,0},{3,1},{4,6},{5,7},{6,4},{7,5},{8,10},{9,11},{10,... | collective-permute-start | bytes 786440 | tf_op jit(solution)/shard_map/ppermute | solution.py:65
  162.0 6.3 %collective-permute-start.41 = (bf16[128,1024]{1,0:T(8,128)(2,1)S(1)}, bf16[128,1024]{1,0:T(8,128)(2,1)S(1)}, u32[]{:S(2)}, u32[]{:S(2)}) collective-permute-start(bf16[128,1024]{1,0:T(8,128)(2,1)S(1)} %get-tuple-element.511.refs_4_), channel_id=1, source_target_pairs={{0,1},{1,0},{2,3},{3,2},{4,5},{5,4},{6,7},{7,6},{8,9},{9,8},{10,11... | collective-permute-start | bytes 786440 | tf_op jit(solution)/shard_map/ppermute | solution.py:65
  162.0 6.3 %collective-permute-start.42 = (bf16[128,1024]{1,0:T(8,128)(2,1)S(1)}, bf16[128,1024]{1,0:T(8,128)(2,1)S(1)}, u32[]{:S(2)}, u32[]{:S(2)}) collective-permute-start(bf16[128,1024]{1,0:T(8,128)(2,1)S(1)} %collective-permute-done.34.refs_5_), channel_id=1, source_target_pairs={{0,1},{1,0},{2,3},{3,2},{4,5},{5,4},{6,7},{7,6},{8,9},{9,8},{10,11... | collective-permute-start | bytes 786440 | tf_op jit(solution)/shard_map/ppermute | solution.py:65
  169.7 5.5 %collective-permute-start.45 = (bf16[128,512]{1,0:T(8,128)(2,1)S(1)}, bf16[128,512]{1,0:T(8,128)(2,1)S(1)}, u32[]{:S(2)}, u32[]{:S(2)}) collective-permute-start(bf16[128,512]{1,0:T(8,128)(2,1)S(1)} %get-tuple-element.495), channel_id=1, source_target_pairs={{0,2},{1,3},{2,0},{3,1},{4,6},{5,7},{6,4},{7,5},{8,10},{9,11},{10,... | collective-permute-start | bytes 393224 | tf_op jit(solution)/shard_map/ppermute | solution.py:65
  179.4 8.3 %collective-permute-start.50 = (bf16[128,1024]{1,0:T(8,128)(2,1)S(1)}, bf16[128,1024]{1,0:T(8,128)(2,1)S(1)}, u32[]{:S(2)}, u32[]{:S(2)}) collective-permute-start(bf16[128,1024]{1,0:T(8,128)(2,1)S(1)} %fold.7), channel_id=1, source_target_pairs={{0,2},{1,3},{2,0},{3,1},{4,6},{5,7},{6,4},{7,5},{8,10},{9,11},{10,... | collective-permute-start | bytes 786440 | tf_op jit(solution)/shard_map/ppermute | solution.py:65
  187.7 30.0 %collective-permute-start.56 = (bf16[4,128,1280]{2,1,0:T(8,128)(2,1)S(1)}, bf16[4,128,1280]{2,1,0:T(8,128)(2,1)S(1)}, u32[]{:S(2)}, u32[]{:S(2)}) collective-permute-start(bf16[4,128,1280]{2,1,0:T(8,128)(2,1)S(1)} %get-tuple-element.535), channel_id=1, source_target_pairs={{0,8},{4,12},{8,0},{12,4},{16,24},{20,28},{24,16},{28,20},{1,9},{5... | collective-permute-start | bytes 3932168 | tf_op jit(solution)/shard_map/ppermute | solution.py:65
  187.7 30.4 %collective-permute-start.55 = (bf16[4,1024,128]{2,1,0:T(8,128)(2,1)S(1)}, bf16[4,1024,128]{2,1,0:T(8,128)(2,1)S(1)}, u32[]{:S(2)}, u32[]{:S(2)}) collective-permute-start(bf16[4,1024,128]{2,1,0:T(8,128)(2,1)S(1)} %get-tuple-element.533), channel_id=1, source_target_pairs={{0,4},{4,0},{8,12},{12,8},{16,20},{20,16},{24,28},{28,24},{1,5},{5... | collective-permute-start | bytes 3145736 | tf_op jit(solution)/shard_map/ppermute | solution.py:65
  188.8 8.0 %collective-permute-start.51 = (bf16[144,1024]{1,0:T(8,128)(2,1)S(1)}, bf16[144,1024]{1,0:T(8,128)(2,1)S(1)}, u32[]{:S(2)}, u32[]{:S(2)}) collective-permute-start(bf16[144,1024]{1,0:T(8,128)(2,1)S(1)} %get-tuple-element.523.refs_0_), channel_id=1, source_target_pairs={{0,2},{1,3},{2,0},{3,1},{4,6},{5,7},{6,4},{7,5},{8,10},{9,11},{10,... | collective-permute-start | bytes 884744 | tf_op jit(solution)/shard_map/ppermute | solution.py:65
  189.4 7.4 %collective-permute-start.52 = (bf16[144,1024]{1,0:T(8,128)(2,1)S(1)}, bf16[144,1024]{1,0:T(8,128)(2,1)S(1)}, u32[]{:S(2)}, u32[]{:S(2)}) collective-permute-start(bf16[144,1024]{1,0:T(8,128)(2,1)S(1)} %get-tuple-element.523.refs_0_), channel_id=1, source_target_pairs={{0,1},{1,0},{2,3},{3,2},{4,5},{5,4},{6,7},{7,6},{8,9},{9,8},{10,11... | collective-permute-start | bytes 884744 | tf_op jit(solution)/shard_map/ppermute | solution.py:65
  198.9 18.9 %collective-permute-start.54 = (bf16[1,512,256]{2,1,0:T(8,128)(2,1)S(1)}, bf16[1,512,256]{2,1,0:T(8,128)(2,1)S(1)}, u32[]{:S(2)}, u32[]{:S(2)}) collective-permute-start(bf16[1,512,256]{2,1,0:T(8,128)(2,1)S(1)} %bitcast.71), channel_id=1, source_target_pairs={{0,4},{4,0},{8,12},{12,8},{16,20},{20,16},{24,28},{28,24},{1,5},{5... | collective-permute-start | bytes 786440 | tf_op jit(solution)/shard_map/ppermute | solution.py:65
  218.4 12.5 %collective-permute-start.59 = (bf16[2,1024,128]{2,1,0:T(8,128)(2,1)S(1)}, bf16[2,1024,128]{2,1,0:T(8,128)(2,1)S(1)}, u32[]{:S(2)}, u32[]{:S(2)}) collective-permute-start(bf16[2,1024,128]{2,1,0:T(8,128)(2,1)S(1)} %get-tuple-element.559), channel_id=1, source_target_pairs={{0,8},{4,12},{8,0},{12,4},{16,24},{20,28},{24,16},{28,20},{1,9},{5... | collective-permute-start | bytes 1572872 | tf_op jit(solution)/shard_map/ppermute | solution.py:65
  220.3 20.4 %collective-permute-start.61 = (bf16[2,128,1280]{2,1,0:T(8,128)(2,1)S(1)}, bf16[2,128,1280]{2,1,0:T(8,128)(2,1)S(1)}, u32[]{:S(2)}, u32[]{:S(2)}) collective-permute-start(bf16[2,128,1280]{2,1,0:T(8,128)(2,1)S(1)} %get-tuple-element.570), channel_id=1, source_target_pairs={{0,4},{4,0},{8,12},{12,8},{16,20},{20,16},{24,28},{28,24},{1,5},{5... | collective-permute-start | bytes 1966088 | tf_op jit(solution)/shard_map/ppermute | solution.py:65
  230.0 14.4 %collective-permute-start.58 = (bf16[4,528,128]{2,1,0:T(8,128)(2,1)S(1)}, bf16[4,528,128]{2,1,0:T(8,128)(2,1)S(1)}, u32[]{:S(2)}, u32[]{:S(2)}) collective-permute-start(bf16[4,528,128]{2,1,0:T(8,128)(2,1)S(1)} %get-tuple-element.556), channel_id=1, source_target_pairs={{0,8},{4,12},{8,0},{12,4},{16,24},{20,28},{24,16},{28,20},{1,9},{5... | collective-permute-start | bytes 1622024 | tf_op jit(solution)/shard_map/ppermute | solution.py:65
  230.4 5.3 %collective-permute-start.62 = (bf16[64,1024]{1,0:T(8,128)(2,1)S(1)}, bf16[64,1024]{1,0:T(8,128)(2,1)S(1)}, u32[]{:S(2)}, u32[]{:S(2)}) collective-permute-start(bf16[64,1024]{1,0:T(8,128)(2,1)S(1)} %get-tuple-element.571), channel_id=1, source_target_pairs={{0,2},{1,3},{2,0},{3,1},{4,6},{5,7},{6,4},{7,5},{8,10},{9,11},{10,... | collective-permute-start | bytes 393224 | tf_op jit(solution)/shard_map/ppermute | solution.py:65
  230.9 9.9 %collective-permute-start.60 = (bf16[128,1024]{1,0:T(8,128)(2,1)S(1)}, bf16[128,1024]{1,0:T(8,128)(2,1)S(1)}, u32[]{:S(2)}, u32[]{:S(2)}) collective-permute-start(bf16[128,1024]{1,0:T(8,128)(2,1)S(1)} %get-tuple-element.568), channel_id=1, source_target_pairs={{0,1},{1,0},{2,3},{3,2},{4,5},{5,4},{6,7},{7,6},{8,9},{9,8},{10,11... | collective-permute-start | bytes 786440 | tf_op jit(solution)/shard_map/ppermute | solution.py:65
  233.1 16.6 %collective-permute-start.66 = (bf16[4,128,512]{2,1,0:T(8,128)(2,1)S(1)}, bf16[4,128,512]{2,1,0:T(8,128)(2,1)S(1)}, u32[]{:S(2)}, u32[]{:S(2)}) collective-permute-start(bf16[4,128,512]{2,1,0:T(8,128)(2,1)S(1)} %get-tuple-element.585), channel_id=1, source_target_pairs={{0,4},{4,0},{8,12},{12,8},{16,20},{20,16},{24,28},{28,24},{1,5},{5... | collective-permute-start | bytes 1572872 | tf_op jit(solution)/shard_map/ppermute | solution.py:65
  241.0 6.6 %collective-permute-start.64 = (bf16[128,1024]{1,0:T(8,128)(2,1)S(1)}, bf16[128,1024]{1,0:T(8,128)(2,1)S(1)}, u32[]{:S(2)}, u32[]{:S(2)}) collective-permute-start(bf16[128,1024]{1,0:T(8,128)(2,1)S(1)} %close.1.refs_0_), channel_id=1, source_target_pairs={{0,2},{1,3},{2,0},{3,1},{4,6},{5,7},{6,4},{7,5},{8,10},{9,11},{10,... | collective-permute-start | bytes 786440 | tf_op jit(solution)/shard_map/ppermute | solution.py:65
  242.0 10.0 %collective-permute-start.68 = (bf16[128,1024]{1,0:T(8,128)(2,1)S(1)}, bf16[128,1024]{1,0:T(8,128)(2,1)S(1)}, u32[]{:S(2)}, u32[]{:S(2)}) collective-permute-start(bf16[128,1024]{1,0:T(8,128)(2,1)S(1)} %close.1.refs_0_), channel_id=1, source_target_pairs={{0,1},{1,0},{2,3},{3,2},{4,5},{5,4},{6,7},{7,6},{8,9},{9,8},{10,11... | collective-permute-start | bytes 786440 | tf_op jit(solution)/shard_map/ppermute | solution.py:65
  242.0 24.1 %collective-permute-start.73 = (bf16[1,128,1280]{2,1,0:T(8,128)(2,1)S(1)}, bf16[1,128,1280]{2,1,0:T(8,128)(2,1)S(1)}, u32[]{:S(2)}, u32[]{:S(2)}) collective-permute-start(bf16[1,128,1280]{2,1,0:T(8,128)(2,1)S(1)} %get-tuple-element.603), channel_id=1, source_target_pairs={{0,16},{4,20},{8,24},{12,28},{16,0},{20,4},{24,8},{28,12},{1,17},{... | collective-permute-start | bytes 983048 | tf_op jit(solution)/shard_map/ppermute | solution.py:65
  248.4 16.8 %collective-permute-start.65 = (bf16[2,528,128]{2,1,0:T(8,128)(2,1)}, bf16[2,528,128]{2,1,0:T(8,128)(2,1)S(1)}, u32[]{:S(2)}, u32[]{:S(2)}) collective-permute-start(bf16[2,528,128]{2,1,0:T(8,128)(2,1)} %get-tuple-element.583), channel_id=1, source_target_pairs={{0,4},{4,0},{8,12},{12,8},{16,20},{20,16},{24,28},{28,24},{1,5},{5... | collective-permute-start | bytes 811016 | tf_op jit(solution)/shard_map/ppermute | solution.py:65
  250.4 14.7 %collective-permute-start.67 = (bf16[2,128,512]{2,1,0:T(8,128)(2,1)}, bf16[2,128,512]{2,1,0:T(8,128)(2,1)S(1)}, u32[]{:S(2)}, u32[]{:S(2)}) collective-permute-start(bf16[2,128,512]{2,1,0:T(8,128)(2,1)} %get-tuple-element.591), channel_id=1, source_target_pairs={{0,8},{4,12},{8,0},{12,4},{16,24},{20,28},{24,16},{28,20},{1,9},{5... | collective-permute-start | bytes 786440 | tf_op jit(solution)/shard_map/ppermute | solution.py:65
  252.0 19.4 %collective-permute-start.72 = (bf16[1,1024,128]{2,1,0:T(8,128)(2,1)}, bf16[1,1024,128]{2,1,0:T(8,128)(2,1)}, u32[]{:S(2)}, u32[]{:S(2)}) collective-permute-start(bf16[1,1024,128]{2,1,0:T(8,128)(2,1)} %get-tuple-element.602), channel_id=1, source_target_pairs={{0,16},{4,20},{8,24},{12,28},{16,0},{20,4},{24,8},{28,12},{1,17},{... | collective-permute-start | bytes 786440 | tf_op jit(solution)/shard_map/ppermute | solution.py:65
  271.4 11.6 %collective-permute-start.71 = (bf16[1,128,512]{2,1,0:T(8,128)(2,1)S(1)}, bf16[1,128,512]{2,1,0:T(8,128)(2,1)S(1)}, u32[]{:S(2)}, u32[]{:S(2)}) collective-permute-start(bf16[1,128,512]{2,1,0:T(8,128)(2,1)S(1)} %get-tuple-element.601), channel_id=1, source_target_pairs={{0,16},{4,20},{8,24},{12,28},{16,0},{20,4},{24,8},{28,12},{1,17},{... | collective-permute-start | bytes 393224 | tf_op jit(solution)/shard_map/ppermute | solution.py:65
  271.4 14.4 %collective-permute-start.70 = (bf16[1,528,128]{2,1,0:T(8,128)(2,1)S(1)}, bf16[1,528,128]{2,1,0:T(8,128)(2,1)S(1)}, u32[]{:S(2)}, u32[]{:S(2)}) collective-permute-start(bf16[1,528,128]{2,1,0:T(8,128)(2,1)S(1)} %get-tuple-element.600), channel_id=1, source_target_pairs={{0,16},{4,20},{8,24},{12,28},{16,0},{20,4},{24,8},{28,12},{1,17},{... | collective-permute-start | bytes 405512 | tf_op jit(solution)/shard_map/ppermute | solution.py:65
  (34 other events, 200.4 us)

commit v6 on v5

--- a/solution.py
+++ b/solution.py
@@ -1056,21 +1056,9 @@
     return whole_call(unproject_kernel, outs, "unproject", dqk, dvalue, w_qk, w_v)
 
 
-def fold_pair_kernel(keep_ref, got_ref, *low_refs):
-    total = keep_ref[...] + got_ref[...].astype(full_type)
-    rows = low_refs[0].shape[0]
-    for at, ref in enumerate(low_refs):
-        ref[...] = total[at * rows : (at + 1) * rows].astype(low_type)
-
-
 def close_kernel(*refs):
-    *terms, low_far, high_far, out_ref = refs
-    total = add_up(terms)
-    half = low_far.shape[0]
-    for at, ref in enumerate((low_far, high_far)):
-        place = pl.ds(at * half, half)
-        part = total[at * half : (at + 1) * half] + ref[...].astype(full_type)
-        out_ref[place, :] = part.astype(low_type)
+    *terms, out_ref = refs
+    out_ref[...] = add_up(terms).astype(low_type)
 
 
 def pack_kernel(order_ref, *refs):
@@ -1391,26 +1379,21 @@
     dqk, dvalue_low = attend_back(far_q, None, tok_rows, own_keys, sums, False, (dquery,))
     parts = unproject(dqk, dvalue_low, full_a, full_b)
     got_far, got = swap(parts[3], "mp", 1), swap(parts[2], "mp", 1)
-    low = whole_call(
-        fold_pair_kernel,
-        [shape_of((own_rows // 2, width))] * 2,
-        "fold_pair",
-        parts[1],
-        got_far,
-    )
+    low = rows_fold([parts[1], got_far])
     (dqk, dvalue_low), low = tie((dqk, dvalue_low), low)
-    far_low = [swap(each, "mp", 2) for each in low]
+    far_low = swap(low, "mp", 2)
     grad_b = Scatter(
         *grad_vo(hidden_own, dvalue_low, attended, packs, norm_sums, across_back),
         "dp",
         across_back,
     )
     dqk = grad_b.start(dqk)
-    dqk = grad_d.step(dqk)
     grad_a = Scatter(*grad_qk(hidden_own, dqk, dp_up), "dp", dp_up)
-    last = grad_a.start(parts[0])
+    dqk = grad_a.start(dqk)
+    dqk, last = tie(dqk, parts[0])
+    last = grad_d.step(last)
     far_low = grad_u.step(far_low)
-    terms = [dresid_one, last, got, *far_low]
+    terms = [dresid_one, last, got, far_low]
     input_own = whole_call(close_kernel, [low_square], "close", *terms)[0]
     far_own = swap(input_own, "mp", 2)
     far_own = grad_a.step(grad_b.step(far_own))

time: 287 us -> 282 us (0.983)
  waiting for transfers between devices: 155 us -> 152 us
    ppermute x74 -> x73, starting transfers between devices: 58.7 us -> 55.9 us  [swap(): return lax.ppermute(value, axis, pairs)]
    ppermute x74 -> x73, waiting for transfers between devices: 155 us -> 152 us  [swap(): return lax.ppermute(value, axis, pairs)]
  transfers between devices with their start and end apart: 74 -> 73, of which waited for: 45 -> 42; matrix products, arithmetic and copies ran while one was open for 5% -> 5% of each run, Pallas kernels for 15% -> 16%
where the time goes in v6:
time: 282 us; the launch traced here: 281 us
  waiting for transfers between devices  152 us (54%)
  Pallas kernels  57.4 us (20%)
  starting transfers between devices  55.9 us (20%)
  other arithmetic  9.52 us (3%)
  local copies, waits for them, and re-layouts  2.89 us (1%)
    ppermute x73, waiting for transfers between devices, swap(): return lax.ppermute(value, axis, pairs)  152 us
    ppermute x73, starting transfers between devices, swap(): return lax.ppermute(value, axis, pairs)  55.9 us
    pallas_call x8, Pallas kernels, ordered_call(): pl.pallas_call(kernel, grid=(1,), in_specs=[pl.BlockSpec(memory_space=plt...  15.3 us
    pallas_call x2, Pallas kernels, attend_back(): pl.pallas_call(kernel, grid=(steps,), in_specs=in_specs, out_specs=out_sp...  11.2 us
  transfers between devices with their start and end apart: 73, of which 42 were waited for; matrix products, arithmetic and copies ran while one was open for 5% of the time, Pallas kernels for 16%

profile of v6, /device:TPU:0, one launch (start us, length us, event | category | flops | bytes accessed | tf_op | source)
XLA Modules:
  0.0 281.2 jit_solution(3837527075840278413)
XLA Ops:
  1.8 2.7 pack.1
  4.5 4.0 %collective-permute-start.1 = (bf16[1,1,1,128,512]{4,3,2,1,0:T(8,128)(2,1)}, bf16[1,1,1,128,512]{4,3,2,1,0:T(8,128)(2,1)S(1)}, u32[]{:S(2)}, u32[]{:S(2)}) collective-permute-start(bf16[1,1,1,128,512]{4,3,2,1,0:T(8,128)(2,1)} %bitcast.91), channel_id=1, source_target_pairs={{0,16},{4,20},{8,24},{12,28},{16,0},{20,4},{24,8},{28,12},{1,17},{... | collective-permute-start | bytes 393224 | tf_op jit(solution)/shard_map/ppermute | solution.py:65
  8.6 1.8 collective-permute-start.5
  14.1 4.7 %collective-permute-done.1 = bf16[1,1,1,128,512]{4,3,2,1,0:T(8,128)(2,1)S(1)} collective-permute-done((bf16[1,1,1,128,512]{4,3,2,1,0:T(8,128)(2,1)}, bf16[1,1,1,128,512]{4,3,2,1,0:T(8,128)(2,1)S(1)}, u32[]{:S(2)}, u32[]{:S(2)}) %collective-permute-start.1) | collective-permute-done | bytes 131104 | tf_op jit(solution)/shard_map/ppermute | solution.py:65
  23.0 3.0 %collective-permute-start.8 = (bf16[1,1,1,128,1280]{4,3,2,1,0:T(8,128)(2,1)S(1)}, bf16[1,1,1,128,1280]{4,3,2,1,0:T(8,128)(2,1)S(1)}, u32[]{:S(2)}, u32[]{:S(2)}) collective-permute-start(bf16[1,1,1,128,1280]{4,3,2,1,0:T(8,128)(2,1)S(1)} %bitcast.83), channel_id=1, source_target_pairs={{0,16},{4,20},{8,24},{12,28},{16,0},{20,4},{24,8},{28,12},{1,17},{... | collective-permute-start | bytes 983048 | tf_op jit(solution)/shard_map/ppermute | solution.py:65
  27.6 8.6 %collective-permute-done.3 = bf16[2,1,1,128,512]{4,3,2,1,0:T(8,128)(2,1)S(1)} collective-permute-done((bf16[2,1,1,128,512]{4,3,2,1,0:T(8,128)(2,1)S(1)}, bf16[2,1,1,128,512]{4,3,2,1,0:T(8,128)(2,1)S(1)}, u32[]{:S(2)}, u32[]{:S(2)}) %collective-permute-start.3) | collective-permute-done | bytes 262176 | tf_op jit(solution)/shard_map/ppermute | solution.py:65
  36.2 3.2 %collective-permute-done.2 = bf16[2,1,1,528,128]{4,3,2,1,0:T(8,128)(2,1)S(1)} collective-permute-done((bf16[2,1,1,528,128]{4,3,2,1,0:T(8,128)(2,1)S(1)}, bf16[2,1,1,528,128]{4,3,2,1,0:T(8,128)(2,1)S(1)}, u32[]{:S(2)}, u32[]{:S(2)}) %collective-permute-start.2) | collective-permute-done | bytes 270368 | tf_op jit(solution)/shard_map/ppermute | solution.py:65
  39.6 3.1 %collective-permute-start.9 = (bf16[2,1,1,128,1280]{4,3,2,1,0:T(8,128)(2,1)S(1)}, bf16[2,1,1,128,1280]{4,3,2,1,0:T(8,128)(2,1)S(1)}, u32[]{:S(2)}, u32[]{:S(2)}) collective-permute-start(bf16[2,1,1,128,1280]{4,3,2,1,0:T(8,128)(2,1)S(1)} %maximum_select_fusion.6), channel_id=1, source_target_pairs={{0,8},{4,12},{8,0},{12,4},{16,24},{20,28},{24,16},{28,20},{1,9},{5... | collective-permute-start | bytes 1966088 | tf_op jit(solution)/shard_map/ppermute | solution.py:65
  45.4 1.8 collective-permute-start.13
  48.4 17.7 %collective-permute-done.9 = bf16[2,1,1,128,1280]{4,3,2,1,0:T(8,128)(2,1)S(1)} collective-permute-done((bf16[2,1,1,128,1280]{4,3,2,1,0:T(8,128)(2,1)S(1)}, bf16[2,1,1,128,1280]{4,3,2,1,0:T(8,128)(2,1)S(1)}, u32[]{:S(2)}, u32[]{:S(2)}) %collective-permute-start.9) | collective-permute-done | bytes 655392 | tf_op jit(solution)/shard_map/ppermute | solution.py:65
  69.1 1.8 collective-permute-done.13
  71.1 1.6 collective-permute-start.17
  73.4 4.8 %attend_forward.1 = (bf16[512,256]{1,0:T(8,128)(2,1)S(1)}, f32[8,512]{1,0:T(8,128)S(1)}) custom-call(bf16[1024,512]{1,0:T(8,128)(2,1)S(1)} %convolution_convert_fusion.q_ref.k_ref.refs_0_.refs_1_, bf16[1024,512]{1,0:T(8,128)(2,1)S(1)} %convolution_convert_fusion.q_ref.k_ref.refs_0_.refs_1_, bf16[1024,256]{1,0:T(8,128)(2,1)S(1)} %convolution_convert_fusion.1.v_ref.refs_2_, ...), custom_call_target="tpu_custom_call" | custom-call | flops 1 | bytes 1 | tf_op jit(solution)/shard_map/attend_forward/pallas_call | solution.py:261
  81.9 6.9 %collective-permute-done.16.refs_3_ = bf16[128,1024]{1,0:T(8,128)(2,1)S(1)} collective-permute-done((bf16[128,1024]{1,0:T(8,128)(2,1)S(1)}, bf16[128,1024]{1,0:T(8,128)(2,1)S(1)}, u32[]{:S(2)}, u32[]{:S(2)}) %collective-permute-start.16) | collective-permute-done | bytes 262176 | tf_op jit(solution)/shard_map/ppermute | solution.py:65
  90.6 6.0 %collective-permute-done.18.refs_1_ = bf16[128,1024]{1,0:T(8,128)(2,1)S(1)} collective-permute-done((bf16[128,1024]{1,0:T(8,128)(2,1)S(1)}, bf16[128,1024]{1,0:T(8,128)(2,1)S(1)}, u32[]{:S(2)}, u32[]{:S(2)}) %collective-permute-start.18) | collective-permute-done | bytes 262176 | tf_op jit(solution)/shard_map/ppermute | solution.py:65
  96.6 3.9 %collective-permute-done.17 = bf16[2,2,1,128,1280]{4,3,2,1,0:T(8,128)(2,1)S(1)} collective-permute-done((bf16[2,2,1,128,1280]{4,3,2,1,0:T(8,128)(2,1)S(1)}, bf16[2,2,1,128,1280]{4,3,2,1,0:T(8,128)(2,1)S(1)}, u32[]{:S(2)}, u32[]{:S(2)}) %collective-permute-start.17) | collective-permute-done | bytes 1310752 | tf_op jit(solution)/shard_map/ppermute | solution.py:65
  104.4 2.7 feed_up.1
  107.5 1.9 feed_down.1
  109.4 3.2 %collective-permute-done.19.refs_6_.refs_9_ = bf16[1024,256]{1,0:T(8,128)(2,1)S(1)} collective-permute-done((bf16[1024,256]{1,0:T(8,128)(2,1)S(1)}, bf16[1024,256]{1,0:T(8,128)(2,1)S(1)}, u32[]{:S(2)}, u32[]{:S(2)}) %collective-permute-start.19) | collective-permute-done | bytes 524320 | tf_op jit(solution)/shard_map/ppermute | solution.py:65
  116.0 6.6 %collective-permute-done.25.refs_3_ = bf16[128,1024]{1,0:T(8,128)(2,1)S(1)} collective-permute-done((bf16[128,1024]{1,0:T(8,128)(2,1)S(1)}, bf16[128,1024]{1,0:T(8,128)(2,1)S(1)}, u32[]{:S(2)}, u32[]{:S(2)}) %collective-permute-start.25) | collective-permute-done | bytes 262176 | tf_op jit(solution)/shard_map/ppermute | solution.py:65
  123.9 1.6 collective-permute-start.28
  127.5 4.3 %collective-permute-done.29 = f32[1,8,512]{2,1,0:T(8,128)S(1)} collective-permute-done((f32[1,8,512]{2,1,0:T(8,128)S(1)}, f32[1,8,512]{2,1,0:T(8,128)S(1)}, u32[]{:S(2)}, u32[]{:S(2)}) %collective-permute-start.29) | collective-permute-done | bytes 16416 | tf_op jit(solution)/shard_map/ppermute | solution.py:65
  134.3 4.2 %late_forward.1 = (f32[512,2048]{1,0:T(8,128)S(1)}, f32[8,2048]{1,0:T(8,128)S(1)}) custom-call(bf16[128,1024]{1,0:T(8,128)(2,1)S(1)} %get-tuple-element.437.refs_0_, bf16[128,1024]{1,0:T(8,128)(2,1)S(1)} %collective-permute-done.30.refs_1_, bf16[128,1024]{1,0:T(8,128)(2,1)S(1)} %collective-permute-done.31.refs_2_, ...), custom_call_target="tpu_custom_call" | custom-call | flops 1 | bytes 1 | tf_op jit(solution)/shard_map/late_forward/pallas_call | solution.py:550
  140.6 3.6 %collective-permute-done.33.far_ref = f32[1,8,2048]{2,1,0:T(8,128)S(1)} collective-permute-done((f32[1,8,2048]{2,1,0:T(8,128)S(1)}, f32[1,8,2048]{2,1,0:T(8,128)S(1)}, u32[]{:S(2)}, u32[]{:S(2)}) %collective-permute-start.33) | collective-permute-done | bytes 65568 | tf_op jit(solution)/shard_map/ppermute | solution.py:65
  144.3 4.1 %late_backward.1 = (f32[128,1024]{1,0:T(8,128)S(1)}, f32[128,1024]{1,0:T(8,128)S(1)}, bf16[128,1024]{1,0:T(8,128)(2,1)S(1)}, bf16[128,1024]{1,0:T(8,128)(2,1)S(1)}, f32[64,15]{1,0:T(8,128)S(1)}) custom-call(f32[512,2048]{1,0:T(8,128)S(1)} %get-tuple-element.442.sharp_ref, f32[8,2048]{1,0:T(8,128)S(1)} %get-tuple-element.445.soft_ref, ...), custom_call_target="tpu_custom_call" | custom-call | flops 1 | bytes 1 | tf_op jit(solution)/shard_map/late_backward/pallas_call | solution.py:627
  150.7 3.9 %collective-permute-done.35 = f32[64,15]{1,0:T(8,128)S(1)} collective-permute-done((f32[64,15]{1,0:T(8,128)S(1)}, f32[64,15]{1,0:T(8,128)S(1)}, u32[]{:S(2)}, u32[]{:S(2)}) %collective-permute-start.35) | collective-permute-done | bytes 3872 | tf_op jit(solution)/shard_map/ppermute | solution.py:65
  154.6 3.9 %collective-permute-done.38.refs_2_ = bf16[128,1024]{1,0:T(8,128)(2,1)S(1)} collective-permute-done((bf16[128,1024]{1,0:T(8,128)(2,1)S(1)}, bf16[128,1024]{1,0:T(8,128)(2,1)S(1)}, u32[]{:S(2)}, u32[]{:S(2)}) %collective-permute-start.38) | collective-permute-done | bytes 262176 | tf_op jit(solution)/shard_map/ppermute | solution.py:65
  158.5 1.7 norm_two_back.1
  162.5 3.1 %collective-permute-done.39 = f32[64,15]{1,0:T(8,128)S(1)} collective-permute-done((f32[64,15]{1,0:T(8,128)S(1)}, f32[64,15]{1,0:T(8,128)S(1)}, u32[]{:S(2)}, u32[]{:S(2)}) %collective-permute-start.39) | collective-permute-done | bytes 3872 | tf_op jit(solution)/shard_map/ppermute | solution.py:65
  165.6 2.2 collective-permute-done.40.refs_1_
  170.2 2.4 feed_inner.1.dz_ref.dinner_ref
  172.6 2.6 collective-permute-done.45.refs_9_
  175.2 2.2 feed_back.1
  180.0 2.4 grad_down.1
  182.4 2.3 grad_up.1
  184.8 2.9 %collective-permute-done.50.refs_3_ = bf16[128,1024]{1,0:T(8,128)(2,1)S(1)} collective-permute-done((bf16[128,1024]{1,0:T(8,128)(2,1)S(1)}, bf16[128,1024]{1,0:T(8,128)(2,1)S(1)}, u32[]{:S(2)}, u32[]{:S(2)}) %collective-permute-start.50) | collective-permute-done | bytes 262176 | tf_op jit(solution)/shard_map/ppermute | solution.py:65
  189.4 7.4 %collective-permute-done.51.refs_1_ = bf16[144,1024]{1,0:T(8,128)(2,1)S(1)} collective-permute-done((bf16[144,1024]{1,0:T(8,128)(2,1)S(1)}, bf16[144,1024]{1,0:T(8,128)(2,1)S(1)}, u32[]{:S(2)}, u32[]{:S(2)}) %collective-permute-start.51) | collective-permute-done | bytes 294944 | tf_op jit(solution)/shard_map/ppermute | solution.py:65
  200.3 6.3 %attend_back.2 = (f32[512,256]{1,0:T(8,128)S(1)}, f32[512,256]{1,0:T(8,128)S(1)}, bf16[512,256]{1,0:T(8,128)(2,1)S(1)}) custom-call(bf16[1024,512]{1,0:T(8,128)(2,1)S(1)} %convolution_convert_fusion.q_ref.k_ref.refs_0_.refs_1_, bf16[1024,512]{1,0:T(8,128)(2,1)S(1)} %convolution_convert_fusion.q_ref.k_ref.refs_0_.refs_1_, ...), custom_call_target="tpu_custom_call" | custom-call | flops 1 | bytes 1 | tf_op jit(solution)/shard_map/attend_back/pallas_call | solution.py:373
  206.6 11.1 %collective-permute-done.54 = bf16[1,512,256]{2,1,0:T(8,128)(2,1)S(1)} collective-permute-done((bf16[1,512,256]{2,1,0:T(8,128)(2,1)S(1)}, bf16[1,512,256]{2,1,0:T(8,128)(2,1)S(1)}, u32[]{:S(2)}, u32[]{:S(2)}) %collective-permute-start.54) | collective-permute-done | bytes 262176 | tf_op jit(solution)/shard_map/ppermute | solution.py:65
  218.4 1.8 collective-permute-start.59
  220.9 4.9 %attend_back.3 = (bf16[512,512]{1,0:T(8,128)(2,1)S(1)}, bf16[512,256]{1,0:T(8,128)(2,1)S(1)}) custom-call(bf16[1024,512]{1,0:T(8,128)(2,1)S(1)} %convolution_convert_fusion.q_ref.k_ref.refs_0_.refs_1_, bf16[1024,512]{1,0:T(8,128)(2,1)S(1)} %convolution_convert_fusion.q_ref.k_ref.refs_0_.refs_1_, ...), custom_call_target="tpu_custom_call" | custom-call | flops 1 | bytes 1 | tf_op jit(solution)/shard_map/attend_back/pallas_call | solution.py:373
  234.5 4.0 %collective-permute-done.62.refs_3_ = bf16[128,1024]{1,0:T(8,128)(2,1)S(1)} collective-permute-done((bf16[128,1024]{1,0:T(8,128)(2,1)S(1)}, bf16[128,1024]{1,0:T(8,128)(2,1)S(1)}, u32[]{:S(2)}, u32[]{:S(2)}) %collective-permute-start.62) | collective-permute-done | bytes 262176 | tf_op jit(solution)/shard_map/ppermute | solution.py:65
  240.6 5.4 %collective-permute-done.58.other_low.other_high = bf16[4,528,128]{2,1,0:T(8,128)(2,1)S(1)} collective-permute-done((bf16[4,528,128]{2,1,0:T(8,128)(2,1)S(1)}, bf16[4,528,128]{2,1,0:T(8,128)(2,1)S(1)}, u32[]{:S(2)}, u32[]{:S(2)}) %collective-permute-start.58) | collective-permute-done | bytes 540704 | tf_op jit(solution)/shard_map/ppermute | solution.py:65
  252.6 2.0 place_rows.1
  254.6 9.8 %collective-permute-done.66.other_low.other_high = bf16[2,128,512]{2,1,0:T(8,128)(2,1)S(1)} collective-permute-done((bf16[2,128,512]{2,1,0:T(8,128)(2,1)}, bf16[2,128,512]{2,1,0:T(8,128)(2,1)S(1)}, u32[]{:S(2)}, u32[]{:S(2)}) %collective-permute-start.66) | collective-permute-done | bytes 262176 | tf_op jit(solution)/shard_map/ppermute | solution.py:65
  265.5 6.6 %collective-permute-done.71 = bf16[1,1024,128]{2,1,0:T(8,128)(2,1)} collective-permute-done((bf16[1,1024,128]{2,1,0:T(8,128)(2,1)}, bf16[1,1024,128]{2,1,0:T(8,128)(2,1)}, u32[]{:S(2)}, u32[]{:S(2)}) %collective-permute-start.71) | collective-permute-done | bytes 262176 | tf_op jit(solution)/shard_map/ppermute | solution.py:65
  273.0 1.8 add_bitcast_fusion
  275.5 5.0 %collective-permute-done.69 = bf16[1,528,128]{2,1,0:T(8,128)(2,1)S(1)} collective-permute-done((bf16[1,528,128]{2,1,0:T(8,128)(2,1)S(1)}, bf16[1,528,128]{2,1,0:T(8,128)(2,1)S(1)}, u32[]{:S(2)}, u32[]{:S(2)}) %collective-permute-start.69) | collective-permute-done | bytes 135200 | tf_op jit(solution)/shard_map/ppermute | solution.py:65
  (206 shorter events, 76.6 us)
Async XLA Ops:
  4.5 14.3 %collective-permute-start.1 = (bf16[1,1,1,128,512]{4,3,2,1,0:T(8,128)(2,1)}, bf16[1,1,1,128,512]{4,3,2,1,0:T(8,128)(2,1)S(1)}, u32[]{:S(2)}, u32[]{:S(2)}) collective-permute-start(bf16[1,1,1,128,512]{4,3,2,1,0:T(8,128)(2,1)} %bitcast.91), channel_id=1, source_target_pairs={{0,16},{4,20},{8,24},{12,28},{16,0},{20,4},{24,8},{28,12},{1,17},{... | collective-permute-start | bytes 393224 | tf_op jit(solution)/shard_map/ppermute | solution.py:65
  8.6 12.3 %collective-permute-start = (bf16[1,1,1,528,128]{4,3,2,1,0:T(8,128)(2,1)}, bf16[1,1,1,528,128]{4,3,2,1,0:T(8,128)(2,1)S(1)}, u32[]{:S(2)}, u32[]{:S(2)}) collective-permute-start(bf16[1,1,1,528,128]{4,3,2,1,0:T(8,128)(2,1)} %bitcast.89), channel_id=1, source_target_pairs={{0,16},{4,20},{8,24},{12,28},{16,0},{20,4},{24,8},{28,12},{1,17},{... | collective-permute-start | bytes 405512 | tf_op jit(solution)/shard_map/ppermute | solution.py:65
  8.6 17.4 %collective-permute-start.5 = (bf16[1,128,1024]{2,1,0:T(8,128)(2,1)}, bf16[1,128,1024]{2,1,0:T(8,128)(2,1)}, u32[]{:S(2)}, u32[]{:S(2)}) collective-permute-start(bf16[1,128,1024]{2,1,0:T(8,128)(2,1)} %bitcast.72), channel_id=1, source_target_pairs={{0,4},{4,0},{8,12},{12,8},{16,20},{20,16},{24,28},{28,24},{1,5},{5... | collective-permute-start | bytes 786440 | tf_op jit(solution)/shard_map/ppermute | solution.py:65
  10.4 15.7 %collective-permute-start.4 = (bf16[1,1,1,1024,128]{4,3,2,1,0:T(8,128)(2,1)}, bf16[1,1,1,1024,128]{4,3,2,1,0:T(8,128)(2,1)S(1)}, u32[]{:S(2)}, u32[]{:S(2)}) collective-permute-start(bf16[1,1,1,1024,128]{4,3,2,1,0:T(8,128)(2,1)} %bitcast.85), channel_id=1, source_target_pairs={{0,4},{4,0},{8,12},{12,8},{16,20},{20,16},{24,28},{28,24},{1,5},{5... | collective-permute-start | bytes 786440 | tf_op jit(solution)/shard_map/ppermute | solution.py:65
  19.8 16.3 %collective-permute-start.3 = (bf16[2,1,1,128,512]{4,3,2,1,0:T(8,128)(2,1)S(1)}, bf16[2,1,1,128,512]{4,3,2,1,0:T(8,128)(2,1)S(1)}, u32[]{:S(2)}, u32[]{:S(2)}) collective-permute-start(bf16[2,1,1,128,512]{4,3,2,1,0:T(8,128)(2,1)S(1)} %maximum_select_fusion.11), channel_id=1, source_target_pairs={{0,8},{4,12},{8,0},{12,4},{16,24},{20,28},{24,16},{28,20},{1,9},{5... | collective-permute-start | bytes 786440 | tf_op jit(solution)/shard_map/ppermute | solution.py:65
  21.9 17.5 %collective-permute-start.2 = (bf16[2,1,1,528,128]{4,3,2,1,0:T(8,128)(2,1)S(1)}, bf16[2,1,1,528,128]{4,3,2,1,0:T(8,128)(2,1)S(1)}, u32[]{:S(2)}, u32[]{:S(2)}) collective-permute-start(bf16[2,1,1,528,128]{4,3,2,1,0:T(8,128)(2,1)S(1)} %maximum_select_fusion.10), channel_id=1, source_target_pairs={{0,8},{4,12},{8,0},{12,4},{16,24},{20,28},{24,16},{28,20},{1,9},{5... | collective-permute-start | bytes 811016 | tf_op jit(solution)/shard_map/ppermute | solution.py:65
  23.0 16.4 %collective-permute-start.8 = (bf16[1,1,1,128,1280]{4,3,2,1,0:T(8,128)(2,1)S(1)}, bf16[1,1,1,128,1280]{4,3,2,1,0:T(8,128)(2,1)S(1)}, u32[]{:S(2)}, u32[]{:S(2)}) collective-permute-start(bf16[1,1,1,128,1280]{4,3,2,1,0:T(8,128)(2,1)S(1)} %bitcast.83), channel_id=1, source_target_pairs={{0,16},{4,20},{8,24},{12,28},{16,0},{20,4},{24,8},{28,12},{1,17},{... | collective-permute-start | bytes 983048 | tf_op jit(solution)/shard_map/ppermute | solution.py:65
  26.1 16.7 %collective-permute-start.10 = (bf16[1,128,1024]{2,1,0:T(8,128)(2,1)}, bf16[1,128,1024]{2,1,0:T(8,128)(2,1)}, u32[]{:S(2)}, u32[]{:S(2)}) collective-permute-start(bf16[1,128,1024]{2,1,0:T(8,128)(2,1)} %collective-permute-done.5), channel_id=1, source_target_pairs={{0,2},{1,3},{2,0},{3,1},{4,6},{5,7},{6,4},{7,5},{8,10},{9,11},{10,... | collective-permute-start | bytes 786440 | tf_op jit(solution)/shard_map/ppermute | solution.py:65
  39.6 26.6 %collective-permute-start.9 = (bf16[2,1,1,128,1280]{4,3,2,1,0:T(8,128)(2,1)S(1)}, bf16[2,1,1,128,1280]{4,3,2,1,0:T(8,128)(2,1)S(1)}, u32[]{:S(2)}, u32[]{:S(2)}) collective-permute-start(bf16[2,1,1,128,1280]{4,3,2,1,0:T(8,128)(2,1)S(1)} %maximum_select_fusion.6), channel_id=1, source_target_pairs={{0,8},{4,12},{8,0},{12,4},{16,24},{20,28},{24,16},{28,20},{1,9},{5... | collective-permute-start | bytes 1966088 | tf_op jit(solution)/shard_map/ppermute | solution.py:65
  43.3 23.2 %collective-permute-start.7 = (bf16[2,2,1,128,512]{4,3,2,1,0:T(8,128)(2,1)S(1)}, bf16[2,2,1,128,512]{4,3,2,1,0:T(8,128)(2,1)S(1)}, u32[]{:S(2)}, u32[]{:S(2)}) collective-permute-start(bf16[2,2,1,128,512]{4,3,2,1,0:T(8,128)(2,1)S(1)} %maximum_select_fusion.8), channel_id=1, source_target_pairs={{0,4},{4,0},{8,12},{12,8},{16,20},{20,16},{24,28},{28,24},{1,5},{5... | collective-permute-start | bytes 1572872 | tf_op jit(solution)/shard_map/ppermute | solution.py:65
  44.8 24.0 %collective-permute-start.6 = (bf16[2,2,1,528,128]{4,3,2,1,0:T(8,128)(2,1)S(1)}, bf16[2,2,1,528,128]{4,3,2,1,0:T(8,128)(2,1)S(1)}, u32[]{:S(2)}, u32[]{:S(2)}) collective-permute-start(bf16[2,2,1,528,128]{4,3,2,1,0:T(8,128)(2,1)S(1)} %maximum_select_fusion.7), channel_id=1, source_target_pairs={{0,4},{4,0},{8,12},{12,8},{16,20},{20,16},{24,28},{28,24},{1,5},{5... | collective-permute-start | bytes 1622024 | tf_op jit(solution)/shard_map/ppermute | solution.py:65
  45.4 25.5 %collective-permute-start.13 = (bf16[1,1,2,1024,128]{4,3,2,1,0:T(8,128)(2,1)S(1)}, bf16[1,1,2,1024,128]{4,3,2,1,0:T(8,128)(2,1)S(1)}, u32[]{:S(2)}, u32[]{:S(2)}) collective-permute-start(bf16[1,1,2,1024,128]{4,3,2,1,0:T(8,128)(2,1)S(1)} %maximum_select_fusion.9), channel_id=1, source_target_pairs={{0,16},{4,20},{8,24},{12,28},{16,0},{20,4},{24,8},{28,12},{1,17},{... | collective-permute-start | bytes 1572872 | tf_op jit(solution)/shard_map/ppermute | solution.py:65
  71.1 29.4 %collective-permute-start.17 = (bf16[2,2,1,128,1280]{4,3,2,1,0:T(8,128)(2,1)S(1)}, bf16[2,2,1,128,1280]{4,3,2,1,0:T(8,128)(2,1)S(1)}, u32[]{:S(2)}, u32[]{:S(2)}) collective-permute-start(bf16[2,2,1,128,1280]{4,3,2,1,0:T(8,128)(2,1)S(1)} %maximum_select_fusion.2), channel_id=1, source_target_pairs={{0,4},{4,0},{8,12},{12,8},{16,20},{20,16},{24,28},{28,24},{1,5},{5... | collective-permute-start | bytes 3932168 | tf_op jit(solution)/shard_map/ppermute | solution.py:65
  80.3 8.4 %collective-permute-start.16 = (bf16[128,1024]{1,0:T(8,128)(2,1)S(1)}, bf16[128,1024]{1,0:T(8,128)(2,1)S(1)}, u32[]{:S(2)}, u32[]{:S(2)}) collective-permute-start(bf16[128,1024]{1,0:T(8,128)(2,1)S(1)} %fold.5), channel_id=1, source_target_pairs={{0,2},{1,3},{2,0},{3,1},{4,6},{5,7},{6,4},{7,5},{8,10},{9,11},{10,... | collective-permute-start | bytes 786440 | tf_op jit(solution)/shard_map/ppermute | solution.py:65
  81.9 25.2 %collective-permute-start.20 = (bf16[2,1,2,1024,128]{4,3,2,1,0:T(8,128)(2,1)S(1)}, bf16[2,1,2,1024,128]{4,3,2,1,0:T(8,128)(2,1)S(1)}, u32[]{:S(2)}, u32[]{:S(2)}) collective-permute-start(bf16[2,1,2,1024,128]{4,3,2,1,0:T(8,128)(2,1)S(1)} %maximum_select_fusion.5), channel_id=1, source_target_pairs={{0,8},{4,12},{8,0},{12,4},{16,24},{20,28},{24,16},{28,20},{1,9},{5... | collective-permute-start | bytes 3145736 | tf_op jit(solution)/shard_map/ppermute | solution.py:65
  89.0 7.6 %collective-permute-start.18 = (bf16[128,1024]{1,0:T(8,128)(2,1)S(1)}, bf16[128,1024]{1,0:T(8,128)(2,1)S(1)}, u32[]{:S(2)}, u32[]{:S(2)}) collective-permute-start(bf16[128,1024]{1,0:T(8,128)(2,1)S(1)} %get-tuple-element.421.refs_0_), channel_id=1, source_target_pairs={{0,2},{1,3},{2,0},{3,1},{4,6},{5,7},{6,4},{7,5},{8,10},{9,11},{10,... | collective-permute-start | bytes 786440 | tf_op jit(solution)/shard_map/ppermute | solution.py:65
  100.9 11.6 %collective-permute-start.19 = (bf16[1024,256]{1,0:T(8,128)(2,1)S(1)}, bf16[1024,256]{1,0:T(8,128)(2,1)S(1)}, u32[]{:S(2)}, u32[]{:S(2)}) collective-permute-start(bf16[1024,256]{1,0:T(8,128)(2,1)S(1)} %slice.27.refs_5_.refs_8_), channel_id=1, source_target_pairs={{0,2},{1,3},{2,0},{3,1},{4,6},{5,7},{6,4},{7,5},{8,10},{9,11},{10,... | collective-permute-start | bytes 1572872 | tf_op jit(solution)/shard_map/ppermute | solution.py:65
  113.1 9.5 %collective-permute-start.27 = (bf16[1024,256]{1,0:T(8,128)(2,1)S(1)}, bf16[1024,256]{1,0:T(8,128)(2,1)S(1)}, u32[]{:S(2)}, u32[]{:S(2)}) collective-permute-start(bf16[1024,256]{1,0:T(8,128)(2,1)S(1)} %collective-permute-done.19.refs_6_.refs_9_), channel_id=1, source_target_pairs={{0,1},{1,0},{2,3},{3,2},{4,5},{5,4},{6,7},{7,6},{8,9},{9,8},{10,11... | collective-permute-start | bytes 1572872 | tf_op jit(solution)/shard_map/ppermute | solution.py:65
  114.2 8.4 %collective-permute-start.25 = (bf16[128,1024]{1,0:T(8,128)(2,1)S(1)}, bf16[128,1024]{1,0:T(8,128)(2,1)S(1)}, u32[]{:S(2)}, u32[]{:S(2)}) collective-permute-start(bf16[128,1024]{1,0:T(8,128)(2,1)S(1)} %fold.6), channel_id=1, source_target_pairs={{0,2},{1,3},{2,0},{3,1},{4,6},{5,7},{6,4},{7,5},{8,10},{9,11},{10,... | collective-permute-start | bytes 786440 | tf_op jit(solution)/shard_map/ppermute | solution.py:65
  123.9 7.9 %collective-permute-start.28 = (bf16[1,512,256]{2,1,0:T(8,128)(2,1)S(1)}, bf16[1,512,256]{2,1,0:T(8,128)(2,1)S(1)}, u32[]{:S(2)}, u32[]{:S(2)}) collective-permute-start(bf16[1,512,256]{2,1,0:T(8,128)(2,1)S(1)} %bitcast.64), channel_id=1, source_target_pairs={{0,4},{4,0},{8,12},{12,8},{16,20},{20,16},{24,28},{28,24},{1,5},{5... | collective-permute-start | bytes 786440 | tf_op jit(solution)/shard_map/ppermute | solution.py:65
  125.5 7.2 %collective-permute-start.30 = (bf16[128,1024]{1,0:T(8,128)(2,1)S(1)}, bf16[128,1024]{1,0:T(8,128)(2,1)S(1)}, u32[]{:S(2)}, u32[]{:S(2)}) collective-permute-start(bf16[128,1024]{1,0:T(8,128)(2,1)S(1)} %get-tuple-element.437.refs_0_), channel_id=1, source_target_pairs={{0,2},{1,3},{2,0},{3,1},{4,6},{5,7},{6,4},{7,5},{8,10},{9,11},{10,... | collective-permute-start | bytes 786440 | tf_op jit(solution)/shard_map/ppermute | solution.py:65
  138.5 9.9 %collective-permute-start.34 = (bf16[128,1024]{1,0:T(8,128)(2,1)S(1)}, bf16[128,1024]{1,0:T(8,128)(2,1)S(1)}, u32[]{:S(2)}, u32[]{:S(2)}) collective-permute-start(bf16[128,1024]{1,0:T(8,128)(2,1)S(1)} %get-tuple-element.505.refs_4_), channel_id=1, source_target_pairs={{0,2},{1,3},{2,0},{3,1},{4,6},{5,7},{6,4},{7,5},{8,10},{9,11},{10,... | collective-permute-start | bytes 786440 | tf_op jit(solution)/shard_map/ppermute | solution.py:65
  148.5 6.1 %collective-permute-start.36 = (bf16[128,1024]{1,0:T(8,128)(2,1)S(1)}, bf16[128,1024]{1,0:T(8,128)(2,1)S(1)}, u32[]{:S(2)}, u32[]{:S(2)}) collective-permute-start(bf16[128,1024]{1,0:T(8,128)(2,1)S(1)} %get-tuple-element.461), channel_id=1, source_target_pairs={{0,1},{1,0},{2,3},{3,2},{4,5},{5,4},{6,7},{7,6},{8,9},{9,8},{10,11... | collective-permute-start | bytes 786440 | tf_op jit(solution)/shard_map/ppermute | solution.py:65
  150.0 8.4 %collective-permute-start.38 = (bf16[128,1024]{1,0:T(8,128)(2,1)S(1)}, bf16[128,1024]{1,0:T(8,128)(2,1)S(1)}, u32[]{:S(2)}, u32[]{:S(2)}) collective-permute-start(bf16[128,1024]{1,0:T(8,128)(2,1)S(1)} %fold.7), channel_id=1, source_target_pairs={{0,2},{1,3},{2,0},{3,1},{4,6},{5,7},{6,4},{7,5},{8,10},{9,11},{10,... | collective-permute-start | bytes 786440 | tf_op jit(solution)/shard_map/ppermute | solution.py:65
  160.2 7.6 %collective-permute-start.40 = (bf16[128,1024]{1,0:T(8,128)(2,1)S(1)}, bf16[128,1024]{1,0:T(8,128)(2,1)S(1)}, u32[]{:S(2)}, u32[]{:S(2)}) collective-permute-start(bf16[128,1024]{1,0:T(8,128)(2,1)S(1)} %get-tuple-element.490.refs_0_), channel_id=1, source_target_pairs={{0,2},{1,3},{2,0},{3,1},{4,6},{5,7},{6,4},{7,5},{8,10},{9,11},{10,... | collective-permute-start | bytes 786440 | tf_op jit(solution)/shard_map/ppermute | solution.py:65
  162.0 6.3 %collective-permute-start.41 = (bf16[128,1024]{1,0:T(8,128)(2,1)S(1)}, bf16[128,1024]{1,0:T(8,128)(2,1)S(1)}, u32[]{:S(2)}, u32[]{:S(2)}) collective-permute-start(bf16[128,1024]{1,0:T(8,128)(2,1)S(1)} %get-tuple-element.505.refs_4_), channel_id=1, source_target_pairs={{0,1},{1,0},{2,3},{3,2},{4,5},{5,4},{6,7},{7,6},{8,9},{9,8},{10,11... | collective-permute-start | bytes 786440 | tf_op jit(solution)/shard_map/ppermute | solution.py:65
  162.0 6.3 %collective-permute-start.42 = (bf16[128,1024]{1,0:T(8,128)(2,1)S(1)}, bf16[128,1024]{1,0:T(8,128)(2,1)S(1)}, u32[]{:S(2)}, u32[]{:S(2)}) collective-permute-start(bf16[128,1024]{1,0:T(8,128)(2,1)S(1)} %collective-permute-done.34.refs_5_), channel_id=1, source_target_pairs={{0,1},{1,0},{2,3},{3,2},{4,5},{5,4},{6,7},{7,6},{8,9},{9,8},{10,11... | collective-permute-start | bytes 786440 | tf_op jit(solution)/shard_map/ppermute | solution.py:65
  169.7 5.5 %collective-permute-start.45 = (bf16[128,512]{1,0:T(8,128)(2,1)S(1)}, bf16[128,512]{1,0:T(8,128)(2,1)S(1)}, u32[]{:S(2)}, u32[]{:S(2)}) collective-permute-start(bf16[128,512]{1,0:T(8,128)(2,1)S(1)} %get-tuple-element.489), channel_id=1, source_target_pairs={{0,2},{1,3},{2,0},{3,1},{4,6},{5,7},{6,4},{7,5},{8,10},{9,11},{10,... | collective-permute-start | bytes 393224 | tf_op jit(solution)/shard_map/ppermute | solution.py:65
  179.4 8.3 %collective-permute-start.50 = (bf16[128,1024]{1,0:T(8,128)(2,1)S(1)}, bf16[128,1024]{1,0:T(8,128)(2,1)S(1)}, u32[]{:S(2)}, u32[]{:S(2)}) collective-permute-start(bf16[128,1024]{1,0:T(8,128)(2,1)S(1)} %fold.8), channel_id=1, source_target_pairs={{0,2},{1,3},{2,0},{3,1},{4,6},{5,7},{6,4},{7,5},{8,10},{9,11},{10,... | collective-permute-start | bytes 786440 | tf_op jit(solution)/shard_map/ppermute | solution.py:65
  187.7 30.0 %collective-permute-start.56 = (bf16[4,128,1280]{2,1,0:T(8,128)(2,1)S(1)}, bf16[4,128,1280]{2,1,0:T(8,128)(2,1)S(1)}, u32[]{:S(2)}, u32[]{:S(2)}) collective-permute-start(bf16[4,128,1280]{2,1,0:T(8,128)(2,1)S(1)} %get-tuple-element.529), channel_id=1, source_target_pairs={{0,8},{4,12},{8,0},{12,4},{16,24},{20,28},{24,16},{28,20},{1,9},{5... | collective-permute-start | bytes 3932168 | tf_op jit(solution)/shard_map/ppermute | solution.py:65
  187.7 30.4 %collective-permute-start.55 = (bf16[4,1024,128]{2,1,0:T(8,128)(2,1)S(1)}, bf16[4,1024,128]{2,1,0:T(8,128)(2,1)S(1)}, u32[]{:S(2)}, u32[]{:S(2)}) collective-permute-start(bf16[4,1024,128]{2,1,0:T(8,128)(2,1)S(1)} %get-tuple-element.527), channel_id=1, source_target_pairs={{0,4},{4,0},{8,12},{12,8},{16,20},{20,16},{24,28},{28,24},{1,5},{5... | collective-permute-start | bytes 3145736 | tf_op jit(solution)/shard_map/ppermute | solution.py:65
  188.8 8.0 %collective-permute-start.51 = (bf16[144,1024]{1,0:T(8,128)(2,1)S(1)}, bf16[144,1024]{1,0:T(8,128)(2,1)S(1)}, u32[]{:S(2)}, u32[]{:S(2)}) collective-permute-start(bf16[144,1024]{1,0:T(8,128)(2,1)S(1)} %get-tuple-element.517.refs_0_), channel_id=1, source_target_pairs={{0,2},{1,3},{2,0},{3,1},{4,6},{5,7},{6,4},{7,5},{8,10},{9,11},{10,... | collective-permute-start | bytes 884744 | tf_op jit(solution)/shard_map/ppermute | solution.py:65
  189.4 7.4 %collective-permute-start.52 = (bf16[144,1024]{1,0:T(8,128)(2,1)S(1)}, bf16[144,1024]{1,0:T(8,128)(2,1)S(1)}, u32[]{:S(2)}, u32[]{:S(2)}) collective-permute-start(bf16[144,1024]{1,0:T(8,128)(2,1)S(1)} %get-tuple-element.517.refs_0_), channel_id=1, source_target_pairs={{0,1},{1,0},{2,3},{3,2},{4,5},{5,4},{6,7},{7,6},{8,9},{9,8},{10,11... | collective-permute-start | bytes 884744 | tf_op jit(solution)/shard_map/ppermute | solution.py:65
  198.9 18.9 %collective-permute-start.54 = (bf16[1,512,256]{2,1,0:T(8,128)(2,1)S(1)}, bf16[1,512,256]{2,1,0:T(8,128)(2,1)S(1)}, u32[]{:S(2)}, u32[]{:S(2)}) collective-permute-start(bf16[1,512,256]{2,1,0:T(8,128)(2,1)S(1)} %bitcast.71), channel_id=1, source_target_pairs={{0,4},{4,0},{8,12},{12,8},{16,20},{20,16},{24,28},{28,24},{1,5},{5... | collective-permute-start | bytes 786440 | tf_op jit(solution)/shard_map/ppermute | solution.py:65
  218.4 13.8 %collective-permute-start.59 = (bf16[2,1024,128]{2,1,0:T(8,128)(2,1)S(1)}, bf16[2,1024,128]{2,1,0:T(8,128)(2,1)S(1)}, u32[]{:S(2)}, u32[]{:S(2)}) collective-permute-start(bf16[2,1024,128]{2,1,0:T(8,128)(2,1)S(1)} %get-tuple-element.551), channel_id=1, source_target_pairs={{0,8},{4,12},{8,0},{12,4},{16,24},{20,28},{24,16},{28,20},{1,9},{5... | collective-permute-start | bytes 1572872 | tf_op jit(solution)/shard_map/ppermute | solution.py:65
  220.2 18.2 %collective-permute-start.61 = (bf16[2,128,1280]{2,1,0:T(8,128)(2,1)S(1)}, bf16[2,128,1280]{2,1,0:T(8,128)(2,1)S(1)}, u32[]{:S(2)}, u32[]{:S(2)}) collective-permute-start(bf16[2,128,1280]{2,1,0:T(8,128)(2,1)S(1)} %get-tuple-element.559), channel_id=1, source_target_pairs={{0,4},{4,0},{8,12},{12,8},{16,20},{20,16},{24,28},{28,24},{1,5},{5... | collective-permute-start | bytes 1966088 | tf_op jit(solution)/shard_map/ppermute | solution.py:65
  230.0 16.0 %collective-permute-start.58 = (bf16[4,528,128]{2,1,0:T(8,128)(2,1)S(1)}, bf16[4,528,128]{2,1,0:T(8,128)(2,1)S(1)}, u32[]{:S(2)}, u32[]{:S(2)}) collective-permute-start(bf16[4,528,128]{2,1,0:T(8,128)(2,1)S(1)} %get-tuple-element.548), channel_id=1, source_target_pairs={{0,8},{4,12},{8,0},{12,4},{16,24},{20,28},{24,16},{28,20},{1,9},{5... | collective-permute-start | bytes 1622024 | tf_op jit(solution)/shard_map/ppermute | solution.py:65
  230.3 8.1 %collective-permute-start.62 = (bf16[128,1024]{1,0:T(8,128)(2,1)S(1)}, bf16[128,1024]{1,0:T(8,128)(2,1)S(1)}, u32[]{:S(2)}, u32[]{:S(2)}) collective-permute-start(bf16[128,1024]{1,0:T(8,128)(2,1)S(1)} %fold.9), channel_id=1, source_target_pairs={{0,2},{1,3},{2,0},{3,1},{4,6},{5,7},{6,4},{7,5},{8,10},{9,11},{10,... | collective-permute-start | bytes 786440 | tf_op jit(solution)/shard_map/ppermute | solution.py:65
  230.9 7.7 %collective-permute-start.60 = (bf16[128,1024]{1,0:T(8,128)(2,1)S(1)}, bf16[128,1024]{1,0:T(8,128)(2,1)S(1)}, u32[]{:S(2)}, u32[]{:S(2)}) collective-permute-start(bf16[128,1024]{1,0:T(8,128)(2,1)S(1)} %get-tuple-element.557), channel_id=1, source_target_pairs={{0,1},{1,0},{2,3},{3,2},{4,5},{5,4},{6,7},{7,6},{8,9},{9,8},{10,11... | collective-permute-start | bytes 786440 | tf_op jit(solution)/shard_map/ppermute | solution.py:65
  232.3 16.0 %collective-permute-start.65 = (bf16[4,128,512]{2,1,0:T(8,128)(2,1)S(1)}, bf16[4,128,512]{2,1,0:T(8,128)(2,1)S(1)}, u32[]{:S(2)}, u32[]{:S(2)}) collective-permute-start(bf16[4,128,512]{2,1,0:T(8,128)(2,1)S(1)} %get-tuple-element.573), channel_id=1, source_target_pairs={{0,4},{4,0},{8,12},{12,8},{16,20},{20,16},{24,28},{28,24},{1,5},{5... | collective-permute-start | bytes 1572872 | tf_op jit(solution)/shard_map/ppermute | solution.py:65
  238.8 7.3 %collective-permute-start.63 = (bf16[128,1024]{1,0:T(8,128)(2,1)S(1)}, bf16[128,1024]{1,0:T(8,128)(2,1)S(1)}, u32[]{:S(2)}, u32[]{:S(2)}) collective-permute-start(bf16[128,1024]{1,0:T(8,128)(2,1)S(1)} %close.1.refs_0_), channel_id=1, source_target_pairs={{0,2},{1,3},{2,0},{3,1},{4,6},{5,7},{6,4},{7,5},{8,10},{9,11},{10,... | collective-permute-start | bytes 786440 | tf_op jit(solution)/shard_map/ppermute | solution.py:65
  239.4 11.2 %collective-permute-start.67 = (bf16[128,1024]{1,0:T(8,128)(2,1)S(1)}, bf16[128,1024]{1,0:T(8,128)(2,1)S(1)}, u32[]{:S(2)}, u32[]{:S(2)}) collective-permute-start(bf16[128,1024]{1,0:T(8,128)(2,1)S(1)} %close.1.refs_0_), channel_id=1, source_target_pairs={{0,1},{1,0},{2,3},{3,2},{4,5},{5,4},{6,7},{7,6},{8,9},{9,8},{10,11... | collective-permute-start | bytes 786440 | tf_op jit(solution)/shard_map/ppermute | solution.py:65
  239.4 26.0 %collective-permute-start.72 = (bf16[1,128,1280]{2,1,0:T(8,128)(2,1)S(1)}, bf16[1,128,1280]{2,1,0:T(8,128)(2,1)S(1)}, u32[]{:S(2)}, u32[]{:S(2)}) collective-permute-start(bf16[1,128,1280]{2,1,0:T(8,128)(2,1)S(1)} %get-tuple-element.591), channel_id=1, source_target_pairs={{0,16},{4,20},{8,24},{12,28},{16,0},{20,4},{24,8},{28,12},{1,17},{... | collective-permute-start | bytes 983048 | tf_op jit(solution)/shard_map/ppermute | solution.py:65
  246.9 18.5 %collective-permute-start.64 = (bf16[2,528,128]{2,1,0:T(8,128)(2,1)}, bf16[2,528,128]{2,1,0:T(8,128)(2,1)S(1)}, u32[]{:S(2)}, u32[]{:S(2)}) collective-permute-start(bf16[2,528,128]{2,1,0:T(8,128)(2,1)} %get-tuple-element.569), channel_id=1, source_target_pairs={{0,4},{4,0},{8,12},{12,8},{16,20},{20,16},{24,28},{28,24},{1,5},{5... | collective-permute-start | bytes 811016 | tf_op jit(solution)/shard_map/ppermute | solution.py:65
  249.1 15.3 %collective-permute-start.66 = (bf16[2,128,512]{2,1,0:T(8,128)(2,1)}, bf16[2,128,512]{2,1,0:T(8,128)(2,1)S(1)}, u32[]{:S(2)}, u32[]{:S(2)}) collective-permute-start(bf16[2,128,512]{2,1,0:T(8,128)(2,1)} %get-tuple-element.579), channel_id=1, source_target_pairs={{0,8},{4,12},{8,0},{12,4},{16,24},{20,28},{24,16},{28,20},{1,9},{5... | collective-permute-start | bytes 786440 | tf_op jit(solution)/shard_map/ppermute | solution.py:65
  250.7 21.4 %collective-permute-start.71 = (bf16[1,1024,128]{2,1,0:T(8,128)(2,1)}, bf16[1,1024,128]{2,1,0:T(8,128)(2,1)}, u32[]{:S(2)}, u32[]{:S(2)}) collective-permute-start(bf16[1,1024,128]{2,1,0:T(8,128)(2,1)} %get-tuple-element.590), channel_id=1, source_target_pairs={{0,16},{4,20},{8,24},{12,28},{16,0},{20,4},{24,8},{28,12},{1,17},{... | collective-permute-start | bytes 786440 | tf_op jit(solution)/shard_map/ppermute | solution.py:65
  264.4 10.4 %collective-permute-start.70 = (bf16[1,128,512]{2,1,0:T(8,128)(2,1)S(1)}, bf16[1,128,512]{2,1,0:T(8,128)(2,1)S(1)}, u32[]{:S(2)}, u32[]{:S(2)}) collective-permute-start(bf16[1,128,512]{2,1,0:T(8,128)(2,1)S(1)} %get-tuple-element.589), channel_id=1, source_target_pairs={{0,16},{4,20},{8,24},{12,28},{16,0},{20,4},{24,8},{28,12},{1,17},{... | collective-permute-start | bytes 393224 | tf_op jit(solution)/shard_map/ppermute | solution.py:65
  272.1 8.4 %collective-permute-start.69 = (bf16[1,528,128]{2,1,0:T(8,128)(2,1)S(1)}, bf16[1,528,128]{2,1,0:T(8,128)(2,1)S(1)}, u32[]{:S(2)}, u32[]{:S(2)}) collective-permute-start(bf16[1,528,128]{2,1,0:T(8,128)(2,1)S(1)} %get-tuple-element.588), channel_id=1, source_target_pairs={{0,16},{4,20},{8,24},{12,28},{16,0},{20,4},{24,8},{28,12},{1,17},{... | collective-permute-start | bytes 405512 | tf_op jit(solution)/shard_map/ppermute | solution.py:65
  (33 other events, 195.4 us)
